TPU v7x, 256 devices: a whole 4x4x8 slice. The times are simulated.
256 devices in a mesh: gx: 16 (over x, z_lo), gy: 16 (over y, z_hi, core).
Axes of the slice: x: 4, y: 4, z: 8 (z_hi: 2, z_lo: 4; z = z_hi * 4 + z_lo), core: 2. Of those that a mesh axis runs over, the one named last changes fastest.
Arguments:
- features: bfloat16 [32, 64, 128, 256], P('gx', 'gy'), may hold values from -6 to 6
- coords: bfloat16 [32, 64, 3, 128], P('gx', 'gy'), may hold values from 0 to 1
- nbr_cells: int32 [32, 64, 9], P('gx', 'gy'), may hold values from 0 to 2047, as said below
- nbr_count: int32 [32, 64], P('gx', 'gy'), may hold values from 1 to 9
- miller: int32 [3, 1024], replicated, may hold values from -8 to 8
- gammas: float32 [8], replicated, may hold values from 0.3 to 6
- radial_filter: bfloat16 [8, 256], replicated, may hold values from -0.09375 to 0.09375
- reciprocal_filter: bfloat16 [1024, 256], P(('gx', 'gy')), may hold values from -0.00024414062 to 0.00024414062
- norm_gain: float32 [256], replicated, may hold values from 0.1 to 1.9
- w_in: bfloat16 [256, 512], replicated, may hold values from -0.375 to 0.375
- w_out: bfloat16 [512, 256], replicated, may hold values from -0.25 to 0.25
Outputs:
- updated: bfloat16 [32, 64, 128, 256], P('gx', 'gy')
Inputs may be any that keep to these rules, and one draw needn't show every extreme that they name: Every entry of nbr_cells names a cell at most one cell away in each of the first two directions, counting periodically; the first nbr_count entries of a list are distinct; the entries after them name the cell itself.
All inputs are finite; a program needn't handle non-finite values.
Results may differ from a plain program's by a relative error of at most 0.009.
Values may be sent and summed in bfloat16 or wider, within the bound.
No kernel may reach another device: no remote copies, remote signals or barrier semaphores. Data moves between devices by JAX's collectives and lax.ppermute only.
A program may use at most 64 MiB of HBM per device.

v0:
```python
import jax
import jax.numpy as jnp
from jax import lax
from jax.sharding import PartitionSpec as P

TWO_PI = 6.283185307179586
slab_depth = 2.0
epsilon = 1e-06


def with_halo(block, sides, width):
    for axis, dim in sides:
        count = lax.axis_size(axis)
        forward = [(i, i + 1) for i in range(count - 1)]
        forward.append((count - 1, 0))
        backward = [(target, source) for source, target in forward]
        low = lax.ppermute(
            lax.slice_in_dim(block, block.shape[dim] - width, None, axis=dim), axis, forward
        )
        high = lax.ppermute(lax.slice_in_dim(block, 0, width, axis=dim), axis, backward)
        block = jnp.concatenate([low, block, high], axis=dim)
    return block


def neighbour_weights(nbr_cells, nbr_count, cell_x, cell_y, total_x, total_y):
    slots = jnp.arange(9, dtype=jnp.int32)
    near_x = nbr_cells // total_y
    near_y = nbr_cells % total_y
    step_x = (near_x - cell_x[:, None, None] + 1) % total_x - 1
    step_y = (near_y - cell_y[None, :, None] + 1) % total_y - 1
    offset_code = (step_x + 1) * 3 + (step_y + 1)
    alive = slots[None, None, :] < nbr_count[:, :, None]
    match = (offset_code[..., None] == slots) & alive[..., None]
    return jnp.sum(jnp.where(match, 1.0, 0.0).astype(jnp.float32), axis=2)


def phase_lookup_tables(miller, along_x, along_y, along_z, total_x, total_y):
    indices = miller.astype(jnp.float32)
    angle = TWO_PI * (
        indices[0][:, None] * (along_x / total_x)[None, :]
        + indices[1][:, None] * (along_y / total_y)[None, :]
        + indices[2][:, None] * (along_z / slab_depth)[None, :]
    )
    return (jnp.cos(angle).astype(jnp.bfloat16), jnp.sin(angle).astype(jnp.bfloat16))


def radial(own_coords, near_feat, near_coords, weight, step_x, step_y, gammas, radial_filter):
    mine = own_coords.astype(jnp.float32)
    theirs = near_coords.astype(jnp.float32)
    delta_x = step_x + theirs[..., 0, None, :] - mine[..., 0, :, None]
    delta_y = step_y + theirs[..., 1, None, :] - mine[..., 1, :, None]
    delta_z = theirs[..., 2, None, :] - mine[..., 2, :, None]
    dist_sq = delta_x * delta_x + delta_y * delta_y + delta_z * delta_z
    kernel = jnp.exp(-gammas[:, None, None] * dist_sq[..., None, :, :]).astype(jnp.bfloat16)
    summed = jnp.einsum("xykij,xyjc->xykic", kernel, near_feat, preferred_element_type=jnp.float32)
    filtered = jnp.sum(summed * radial_filter.astype(jnp.float32)[:, None, :], axis=-3)
    return filtered * weight[..., None, None]


def per_device(
    features,
    coords,
    nbr_cells,
    nbr_count,
    miller,
    gammas,
    radial_filter,
    reciprocal_filter,
    norm_gain,
    w_in,
    w_out,
):
    cells_x, cells_y, atoms, width = features.shape
    groups_x = lax.axis_size("gx")
    groups_y = lax.axis_size("gy")
    total_x = cells_x * groups_x
    total_y = cells_y * groups_y
    cell_x = lax.axis_index("gx") * cells_x + jnp.arange(cells_x, dtype=jnp.int32)
    cell_y = lax.axis_index("gy") * cells_y + jnp.arange(cells_y, dtype=jnp.int32)
    weights = neighbour_weights(nbr_cells, nbr_count, cell_x, cell_y, total_x, total_y)
    around_feat, around_coords = (
        with_halo(features, (("gx", 0), ("gy", 1)), 1),
        with_halo(coords, (("gx", 0), ("gy", 1)), 1),
    )
    radial_sum = jnp.zeros(features.shape, jnp.float32)
    for offset in range(9):
        step_x = offset // 3 - 1
        step_y = offset % 3 - 1
        near_feat = around_feat[
            1 + step_x : 1 + step_x + cells_x, 1 + step_y : 1 + step_y + cells_y
        ]
        near_coords = around_coords[
            1 + step_x : 1 + step_x + cells_x, 1 + step_y : 1 + step_y + cells_y
        ]
        radial_sum = radial_sum + radial(
            coords,
            near_feat,
            near_coords,
            weights[:, :, offset],
            step_x,
            step_y,
            gammas,
            radial_filter,
        )
    coord_float = coords.astype(jnp.float32)
    along_x = (cell_x.astype(jnp.float32)[:, None, None] + coord_float[:, :, 0, :]).reshape(-1)
    along_y = (cell_y.astype(jnp.float32)[None, :, None] + coord_float[:, :, 1, :]).reshape(-1)
    along_z = coord_float[:, :, 2, :].reshape(-1)
    cos_table, sin_table = phase_lookup_tables(miller, along_x, along_y, along_z, total_x, total_y)
    own_rows = features.reshape(-1, width)
    dims = (((0,), (0,)), ((), ()))
    partial_sums = jnp.stack(
        [
            jnp.dot(cos_table, own_rows, preferred_element_type=jnp.float32),
            jnp.dot(sin_table, own_rows, preferred_element_type=jnp.float32),
        ],
        axis=1,
    )
    sums = lax.psum(partial_sums, ("gx", "gy"))
    whole_filter = lax.all_gather(reciprocal_filter, ("gx", "gy"), axis=0, tiled=True)
    coefficients = (sums * whole_filter.astype(jnp.float32)[:, None, :]).astype(jnp.bfloat16)
    recip = lax.dot_general(cos_table, coefficients[:, 0], dims, preferred_element_type=jnp.float32)
    recip = recip + lax.dot_general(
        sin_table, coefficients[:, 1], dims, preferred_element_type=jnp.float32
    )
    mixed = features.astype(jnp.float32).reshape(-1, width) + radial_sum.reshape(-1, width) + recip
    normed = (
        mixed * lax.rsqrt(jnp.mean(mixed * mixed, axis=-1, keepdims=True) + epsilon) * norm_gain
    ).astype(jnp.bfloat16)
    hidden = jax.nn.silu(jnp.dot(normed, w_in, preferred_element_type=jnp.float32)).astype(
        jnp.bfloat16
    )
    updated = mixed + jnp.dot(hidden, w_out, preferred_element_type=jnp.float32)
    return updated.astype(jnp.bfloat16).reshape(features.shape)


def solution(mesh):
    in_specs = (
        P("gx", "gy", None, None),
        P("gx", "gy", None, None),
        P("gx", "gy", None),
        P("gx", "gy"),
        P(),
        P(),
        P(),
        P(("gx", "gy"), None),
        P(),
        P(),
        P(),
    )
    out_specs = P("gx", "gy", None, None)
    return jax.shard_map(
        per_device, mesh=mesh, in_specs=in_specs, out_specs=out_specs, check_vma=False
    )
```

profile of v0, /device:TPU:1, one launch (start us, length us, event | category | flops | bytes accessed | tf_op | source)
XLA Modules:
  0.0 706.9 jit_solution(16048404796254962886)
XLA Ops:
  6.5 0.8 fusion.112
  7.3 2.5 collective-permute-start
  9.8 5.0 collective-permute-start.1
  14.8 1.1 fusion.108
  15.9 5.4 collective-permute-start.4
  21.3 0.7 fusion.111
  22.0 0.8 fusion.75
  23.6 0.7 convert_element_type.133
  24.3 348.2 %all-gather = bf16[256,4,256]{2,1,0:T(4,128)(2,1)S(1)} all-gather(bf16[1,4,256]{2,1,0:T(4,128)(2,1)} %bitcast.219), channel_id=1, replica_groups=mesh['gx'=16,'gy'=16] {'gx','gy'}, dimensions={0}, use_global_device_ids=true | all-gather | bytes 526336 | tf_op jit(solution)/shard_map/all_gather | solution.py:120
  374.5 15.0 %fusion.22 = f32[1024,1,256]{2,0,1:T(8,128)S(1)} fusion(bf16[1024,256]{1,0:T(8,128)(2,1)S(1)} %bitcast.188, f32[1024]{0:T(1024)S(1)} %bitcast.203, f32[1024]{0:T(1024)S(1)} %bitcast.211, f32[1024]{0:T(1024)S(1)} %add_multiply_fusion.1, f32[1024]{0:T(1024)S(1)} %bitcast.215, f32[1024]{0:T(1024)S(1)} %add_multiply_fusion.2, f32[1024]{0:T(1024)S(1)} %bitcast.207), kind=kOutput, calls=%fused_computation.50 | convolution fusion | flops 544210944 | bytes 1597440 | tf_op jit(solution)/shard_map/dot_general | solution.py:115
  389.4 14.7 %fusion.23 = f32[1024,1,256]{2,0,1:T(8,128)S(1)} fusion(bf16[1024,256]{1,0:T(8,128)(2,1)S(1)} %bitcast.189, f32[1024]{0:T(1024)S(1)} %bitcast.204, f32[1024]{0:T(1024)S(1)} %bitcast.212, f32[1024]{0:T(1024)S(1)} %add_multiply_fusion.1, f32[1024]{0:T(1024)S(1)} %bitcast.216, f32[1024]{0:T(1024)S(1)} %add_multiply_fusion.2, f32[1024]{0:T(1024)S(1)} %bitcast.208), kind=kOutput, calls=%fused_computation.51 | convolution fusion | flops 544210944 | bytes 1597440 | tf_op jit(solution)/shard_map/dot_general | solution.py:114
  404.2 1.7 collective-permute-start.2
  405.8 1.4 pad_maximum_fusion
  407.3 5.8 collective-permute-done.6
  413.2 1.1 multiply_add_fusion.8
  414.3 1.3 multiply_reduce_fusion.4
  416.5 1.1 collective-permute-start.7
  417.5 1.4 multiply_reduce_fusion.7
  418.9 1.4 multiply_reduce_fusion.1
  420.5 1.4 multiply_reduce_fusion.8
  421.9 1.4 multiply_reduce_fusion.5
  423.3 1.4 multiply_reduce_fusion.2
  424.6 6.6 collective-permute-done.7
  431.2 1.4 multiply_reduce_fusion.6
  432.6 1.4 multiply_reduce_fusion
  434.0 1.4 multiply_reduce_fusion.3
  436.0 2.7 fusion.28
  438.7 227.3 %all-reduce.2.cloned.1.call-done = f32[1024,2,256]{2,0,1:T(8,128)} async-done(((f32[1024,2,256]{2,0,1:T(8,128)}), f32[1024,2,256]{2,0,1:T(8,128)}) %all-reduce.2.cloned.1.call-update) | async-done | bytes 2097168 | tf_op jit(solution)/shard_map/psum | solution.py:119
  666.0 1.8 multiply_convert_fusion.1
  667.8 14.9 %fusion.18 = f32[1024,256]{1,0:T(8,128)S(1)} fusion(f32[1024]{0:T(1024)S(1)} %bitcast.205, f32[1024]{0:T(1024)S(1)} %bitcast.213, f32[1024]{0:T(1024)S(1)} %add_multiply_fusion.1, f32[1024]{0:T(1024)S(1)} %bitcast.217, f32[1024]{0:T(1024)S(1)} %add_multiply_fusion.2, f32[1024]{0:T(1024)S(1)} %bitcast.209, bf16[1024,2,256]{2,0,1:T(8,128)(2,1)S(1)} %multiply_convert_fusion.1), kind=kOutput, calls=%fused_computation.46 | convolution fusion | flops 544210944 | bytes 1597440 | tf_op jit(solution)/shard_map/dot_general | solution.py:122
  682.8 15.3 %multiply_reduce_fusion.9 = (f32[1024]{0:T(1024)S(1)}, f32[1024,256]{1,0:T(8,128)S(1)}) fusion(f32[1024,256]{1,0:T(8,128)S(1)} %fusion.28, f32[1024,256]{1,0:T(8,128)S(1)} %fusion.18, bf16[1024,2,256]{2,0,1:T(8,128)(2,1)S(1)} %multiply_convert_fusion.1, f32[1024]{0:T(1024)S(1)} %bitcast.206, f32[1024]{0:T(1024)S(1)} %bitcast.214, ...), kind=kOutput, calls=%fused_computation.80 | convolution fusion | flops 545258496 | bytes 3698688 | tf_op jit(solution)/shard_map/dot_general | solution.py:123
  698.1 1.7 fusion.26
  (60 shorter events, 4.5 us)
Async XLA Ops:
  6.5 691.6 %copy-start = (bf16[512,256]{1,0:T(8,128)(2,1)S(1)}, bf16[512,256]{1,0:T(8,128)(2,1)}, u32[]{:S(2)}) copy-start(bf16[512,256]{1,0:T(8,128)(2,1)} %param.21) | copy-start | bytes 786436
  6.5 367.9 %copy-start.2 = (bf16[2,4,3,128]{3,1,2,0:T(4,128)(2,1)S(1)}, bf16[2,4,3,128]{3,1,2,0:T(4,128)(2,1)}, u32[]{:S(2)}) copy-start(bf16[2,4,3,128]{3,1,2,0:T(4,128)(2,1)} %param.12) | copy-start | bytes 18436
  6.5 367.9 %copy-start.1 = (bf16[2,4,128,256]{3,2,1,0:T(8,128)(2,1)S(1)}, bf16[2,4,128,256]{3,2,1,0:T(8,128)(2,1)}, u32[]{:S(2)}) copy-start(bf16[2,4,128,256]{3,2,1,0:T(8,128)(2,1)} %param.11) | copy-start | bytes 1572868
  6.5 659.4 %all-reduce.2.cloned.1.call-start = ((), (), s32[]{:S(2)}) async-start(), calls=%async_computation | async-start | bytes 4194304 | tf_op jit(solution)/shard_map/psum | solution.py:119
  7.3 367.1 %collective-permute-start = (bf16[1,4,3,128]{3,1,2,0:T(4,128)(2,1)S(1)}, bf16[1,4,3,128]{3,1,2,0:T(4,128)(2,1)S(1)}, u32[]{:S(2)}, u32[]{:S(2)}) collective-permute-start(bf16[1,4,3,128]{3,1,2,0:T(4,128)(2,1)S(1)} %get-tuple-element.76), channel_id=1, source_target_pairs={{0,16},{16,32},{32,48},{48,64},{64,80},{80,96},{96,112},{112,128},... | collective-permute-start | bytes 9224 | tf_op jit(solution)/shard_map/ppermute | solution.py:17
  9.8 364.6 %collective-permute-start.1 = (bf16[1,4,3,128]{3,1,2,0:T(4,128)(2,1)S(1)}, bf16[1,4,3,128]{3,1,2,0:T(4,128)(2,1)S(1)}, u32[]{:S(2)}, u32[]{:S(2)}) collective-permute-start(bf16[1,4,3,128]{3,1,2,0:T(4,128)(2,1)S(1)} %get-tuple-element.75), channel_id=1, source_target_pairs={{16,0},{32,16},{48,32},{64,48},{80,64},{96,80},{112,96},{128,112},... | collective-permute-start | bytes 9224 | tf_op jit(solution)/shard_map/ppermute | solution.py:20
  15.8 400.4 %collective-permute-start.3 = (bf16[1,4,128,256]{3,2,1,0:T(8,128)(2,1)S(1)}, bf16[1,4,128,256]{3,2,1,0:T(8,128)(2,1)S(1)}, u32[]{:S(2)}, u32[]{:S(2)}) collective-permute-start(bf16[1,4,128,256]{3,2,1,0:T(8,128)(2,1)S(1)} %get-tuple-element.17), channel_id=1, source_target_pairs={{0,16},{16,32},{32,48},{48,64},{64,80},{80,96},{96,112},{112,128},... | collective-permute-start | bytes 786440 | tf_op jit(solution)/shard_map/ppermute | solution.py:17
  15.9 400.4 %collective-permute-start.4 = (bf16[1,4,128,256]{3,2,1,0:T(8,128)(2,1)S(1)}, bf16[1,4,128,256]{3,2,1,0:T(8,128)(2,1)S(1)}, u32[]{:S(2)}, u32[]{:S(2)}) collective-permute-start(bf16[1,4,128,256]{3,2,1,0:T(8,128)(2,1)S(1)} %get-tuple-element.16), channel_id=1, source_target_pairs={{16,0},{32,16},{48,32},{64,48},{80,64},{96,80},{112,96},{128,112},... | collective-permute-start | bytes 786440 | tf_op jit(solution)/shard_map/ppermute | solution.py:20
  404.2 3.1 collective-permute-start.2
  405.8 7.3 %collective-permute-start.6 = (bf16[4,1,3,128]{3,1,2,0:T(2,128)(2,1)S(1)}, bf16[4,1,3,128]{3,1,2,0:T(2,128)(2,1)S(1)}, u32[]{:S(2)}, u32[]{:S(2)}) collective-permute-start(bf16[4,1,3,128]{3,1,2,0:T(2,128)(2,1)S(1)} %get-tuple-element.62), channel_id=1, source_target_pairs={{1,0},{2,1},{3,2},{4,3},{5,4},{6,5},{7,6},{8,7},{9,8},{10,9},{11,1... | collective-permute-start | bytes 9224 | tf_op jit(solution)/shard_map/ppermute | solution.py:20
  416.4 4.1 collective-permute-start.5
  416.5 14.8 %collective-permute-start.7 = (bf16[4,1,128,256]{3,2,1,0:T(8,128)(2,1)S(1)}, bf16[4,1,128,256]{3,2,1,0:T(8,128)(2,1)S(1)}, u32[]{:S(2)}, u32[]{:S(2)}) collective-permute-start(bf16[4,1,128,256]{3,2,1,0:T(8,128)(2,1)S(1)} %get-tuple-element.15), channel_id=1, source_target_pairs={{1,0},{2,1},{3,2},{4,3},{5,4},{6,5},{7,6},{8,7},{9,8},{10,9},{11,1... | collective-permute-start | bytes 786440 | tf_op jit(solution)/shard_map/ppermute | solution.py:20
  682.7 15.4 %copy-start.3 = (bf16[256,512]{1,0:T(8,128)(2,1)S(1)}, bf16[256,512]{1,0:T(8,128)(2,1)}, u32[]{:S(2)}) copy-start(bf16[256,512]{1,0:T(8,128)(2,1)} %param.20) | copy-start | bytes 786436
  682.8 15.4 %copy-start.4 = (f32[256]{0:T(256)S(1)}, f32[256]{0:T(256)}, u32[]{:S(2)}) copy-start(f32[256]{0:T(256)} %param.19) | copy-start | bytes 3076
Sparse Core Ops, SparseCore 0:
  407.4 258.5 all-reduce.1
where the time goes:
time: 711 us; the launch traced here: 707 us
  blocking collectives  348 us (49%)
  waiting for transfers between devices  240 us (34%)
  matrix products  73.8 us (10%)
  starting transfers between devices  15.7 us (2%)
  between operations  14 us (2%)
  other arithmetic  11.3 us (2%)
    all_gather x1, blocking collectives, per_device(): lax.all_gather(reciprocal_filter, ('gx', 'gy'), axis=0, tiled=True)  348 us
    psum x1, waiting for transfers between devices, per_device(): sums = lax.psum(partial_sums, ('gx', 'gy'))  227 us
    dot_general x1, matrix products, per_device(): lax.dot_general(sin_table, coefficients[:, 1], dims, preferred_element_ty...  15.3 us
    dot_general x1, matrix products, per_device(): jnp.dot(sin_table, own_rows, preferred_element_type=jnp.float32)  15 us
    dot_general x1, matrix products, per_device(): lax.dot_general(cos_table, coefficients[:, 0], dims, preferred_element_ty...  14.9 us
    dot_general x1, matrix products, per_device(): jnp.dot(cos_table, own_rows, preferred_element_type=jnp.float32)  14.7 us
  transfers between devices with their start and end apart: 9, of which 4 were waited for; matrix products, arithmetic and copies ran while one was open for 8% of the time, Pallas kernels for 0%

commit v1 on v0

v1 whole, which is shorter than its diff:
```python
import functools

import jax
import jax.numpy as jnp
from jax import lax
from jax.experimental import pallas as pl
from jax.experimental.pallas import tpu as pltpu
from jax.sharding import PartitionSpec as P

slab_depth = 2.0
epsilon = 1e-06
LOG2E = 1.4426950408889634
AXES = ("gx", "gy")
F32 = jnp.float32
BF16 = jnp.bfloat16
CX, CY, ATOMS, WIDTH = 2, 4, 128, 256
PACK = 136
VMEM = pltpu.VMEM

SIN_COEF = (3.14159264, -5.16771008, 2.55007752, -0.59829129, 0.07765766)
COS_COEF = (0.99999995, -4.93479283, 4.05841135, -1.33187657, 0.21968961)


def linear(x, y, z, core):
    return (x * 4 + z % 4) * 16 + y * 4 + (z // 4) * 2 + core


def partner_list(step):
    pairs = []
    for x in range(4):
        for y in range(4):
            for z in range(8):
                for core in range(2):
                    pairs.append((linear(x, y, z, core), linear(*step(x, y, z, core))))
    return pairs


def flip_core(x, y, z, core):
    return x, y, z, 1 - core


def flip_plane(first, second):
    def step(x, y, z, core):
        if core == 0:
            return x ^ first, y ^ second, z, core
        return x ^ second, y ^ first, z, core

    return step


def flip_z(which):
    table = ((1, 0, 3, 2, 5, 4, 7, 6), (7, 2, 1, 4, 3, 6, 5, 0), (3, 6, 5, 0, 7, 2, 1, 4))[which]

    def step(x, y, z, core):
        return x, y, table[z], core

    return step


HALVING = (flip_core, flip_plane(1, 0), flip_plane(3, 0), flip_plane(0, 1))
DOUBLING = (flip_plane(0, 3), flip_z(0), flip_z(1), flip_z(2))
CHUNK = 64


def permute(value, step):
    return lax.ppermute(value, AXES, partner_list(step))


def my_place():
    gx, gy = lax.axis_index("gx"), lax.axis_index("gy")
    return gx // 4, gy // 4, (gx % 4) + 4 * ((gy // 2) % 2), gy % 2


def vector_order():
    x, y, z, core = my_place()
    pos = lax.broadcasted_iota(jnp.int32, (1, 1024), 1)
    rest = pos % 4
    mz = (pos // 4) % 8
    mb = (pos // 32) % 2
    b3 = (pos // 64) % 2
    b2 = (pos // 128) % 2
    b1 = (pos // 256) % 2
    owner = core ^ (pos // 512)
    main = jnp.where(owner == 0, x, y) ^ b1 ^ (3 * b2)
    other = jnp.where(owner == 0, y, x)
    coset = (other ^ (other >> 1)) & 1
    side = (coset ^ b3) ^ (3 * mb)
    ox = jnp.where(owner == 0, main, side)
    oy = jnp.where(owner == 0, side, main)
    return linear(ox, oy, mz, owner) * 4 + rest


def wave_kernel(place, coords, features, miller, order, cos_ref, sin_ref, send_ref, keep_ref, turned):
    number = miller[...].astype(F32)
    five = jnp.concatenate([number, number[0:2], jnp.zeros((3, 1024), F32)], axis=0).astype(BF16)
    natural = lax.broadcasted_iota(jnp.int32, (1024, 1024), 0)
    pick = jnp.where(natural == order[...], 1.0, 0.0).astype(BF16)
    placed = jnp.dot(five, pick, preferred_element_type=F32).astype(BF16)
    turned[...] = features[...].astype(F32).T.astype(BF16)
    ones = jnp.ones((1, ATOMS), F32)

    for cell in range(CX * CY):
        block = coords[cell].astype(F32)
        along = (place[0] * CX + cell // CY).astype(F32) / 32.0
        across = (place[1] * CY + cell % CY).astype(F32) / 64.0
        rows = jnp.concatenate(
            [
                block[0:1] / 32.0,
                block[1:2] / 64.0,
                block[2:3] / slab_depth,
                along * ones,
                across * ones,
                jnp.zeros((3, ATOMS), F32),
            ],
            axis=0,
        )
        columns = rows.T.astype(BF16)

        for j in range(4):
            lanes = slice(j * 256, (j + 1) * 256)
            angle = jnp.dot(columns, placed[:, lanes], preferred_element_type=F32)
            r = angle - jnp.round(angle)
            s = r * r
            sine = SIN_COEF[4]
            cosine = COS_COEF[4]
            for a in (3, 2, 1, 0):
                sine = sine * s + SIN_COEF[a]
            for a in (3, 2, 1, 0):
                cosine = cosine * s + COS_COEF[a]
            sine = sine * r
            double = sine + sine
            rows_at = pl.ds(cell * ATOMS, ATOMS)
            cos_ref[rows_at, lanes] = (1.0 - double * sine).astype(BF16)
            sin_ref[rows_at, lanes] = (double * cosine).astype(BF16)

    for half, target in ((0, keep_ref), (1, send_ref)):
        lanes = slice(half * 512, half * 512 + 512)
        for col, table in ((0, cos_ref), (1, sin_ref)):
            total = jnp.dot(turned[...], table[:, lanes], preferred_element_type=F32)
            target[:, col * WIDTH : (col + 1) * WIDTH] = total.T.astype(target.dtype)


def waves(place, coords, features, miller, order):
    vm = pl.BlockSpec(memory_space=VMEM)
    return pl.pallas_call(
        wave_kernel,
        out_shape=(
            jax.ShapeDtypeStruct((1024, 1024), BF16),
            jax.ShapeDtypeStruct((1024, 1024), BF16),
            jax.ShapeDtypeStruct((512, 512), BF16),
            jax.ShapeDtypeStruct((512, 512), F32),
        ),
        in_specs=[pl.BlockSpec(memory_space=pltpu.SMEM), vm, vm, vm, vm],
        out_specs=(vm, vm, vm, vm),
        scratch_shapes=[VMEM((WIDTH, 1024), BF16)],
        compiler_params=pltpu.CompilerParams(vmem_limit_bytes=40 * 1024 * 1024),
        cost_estimate=pl.CostEstimate(flops=4_000_000_000, bytes_accessed=6_000_000, transcendentals=0),
        name="wave_tables",
    )(place, coords, features, miller, order)


def mark_live(place, near_list, near_count, live):
    def clear(i, carry):
        live[i] = 0
        return carry

    lax.fori_loop(0, 72, clear, 0)

    def mark(i, carry):
        cell = i // 9
        entry = near_list[i]
        step_x = ((entry >> 6) - (place[0] * CX + cell // CY) + 1) & 31
        step_y = ((entry & 63) - (place[1] * CY + cell % CY) + 1) & 63

        @pl.when(i % 9 < near_count[cell])
        def _():
            live[cell * 9 + step_x * 3 + step_y] = 1

        return carry

    lax.fori_loop(0, 72, mark, 0)


def own_columns(own, mine):
    for cell in range(CX * CY):
        rows = own[cell // CY, cell % CY, ATOMS:PACK, 0:ATOMS].astype(F32)
        mine[cell] = rows.T


def scaled_features(block, filters, scaled):
    values = block[0:ATOMS, :].astype(F32)
    for k in range(8):
        scaled[k * ATOMS : (k + 1) * ATOMS, :] = (values * filters[k : k + 1, :].astype(F32)).astype(BF16)


def pair(acc, mine, scaled, near, rates, cell, u, v):
    here = mine[cell]
    dx = (near[0:1] + u) - here[:, 0:1]
    dy = (near[1:2] + v) - here[:, 1:2]
    dz = near[2:3] - here[:, 2:3]
    dist = dx * dx + dy * dy + dz * dz
    kernel = jnp.concatenate([jnp.exp2(dist * (rates[k] * -LOG2E)).astype(BF16) for k in range(8)], axis=1)
    acc[cell] += jnp.dot(kernel, scaled[...], preferred_element_type=F32)


def near_rows(block):
    return block[ATOMS:PACK, 0:ATOMS].astype(F32)


def inner_kernel(place, near_list, near_count, rates, filters, own, acc, live, mine, scaled):
    mark_live(place, near_list, near_count, live)
    own_columns(own, mine)
    acc[...] = jnp.zeros_like(acc)

    def one(nb, carry):
        ja, jb = nb // CY, nb % CY
        block = own.at[ja, jb]
        scaled_features(block, filters, scaled)
        near = near_rows(block)

        def inner(p, carry):
            ia, v = p // 3, p % 3 - 1
            ib = jb - v
            u = ja - ia
            cell = jnp.clip(ia * CY + ib, 0, CX * CY - 1)
            ok = (ib >= 0) & (ib < CY) & (live[cell * 9 + (u + 1) * 3 + v + 1] > 0)

            @pl.when(ok)
            def _():
                pair(acc, mine, scaled, near_rows(block), rates, cell, u.astype(F32), v.astype(F32))

            return carry

        return lax.fori_loop(0, 6, inner, carry)

    lax.fori_loop(0, CX * CY, one, 0)


def outer_kernel(along_x, place, near_list, near_count, rates, filters, own, low, high, start, acc, live, mine, scaled):
    mark_live(place, near_list, near_count, live)
    own_columns(own, mine)
    acc[...] = start[...]
    for side, ref in ((-1, low), (1, high)):

        def one(j, carry, side=side, ref=ref):
            block = ref.at[0, j] if along_x else ref.at[j, 0]
            scaled_features(block, filters, scaled)

            def inner(p, carry):
                t = p - 1
                if along_x:
                    u, v = side, t
                    ia, ib = (0 if side < 0 else CX - 1), j - t
                    inside = (ib >= 0) & (ib < CY)
                else:
                    u, v = t, side
                    ia, ib = j - 1 - t, (0 if side < 0 else CY - 1)
                    inside = (ia >= 0) & (ia < CX)
                cell = jnp.clip(ia * CY + ib, 0, CX * CY - 1)
                ok = inside & (live[cell * 9 + (u + 1) * 3 + v + 1] > 0)

                @pl.when(ok)
                def _():
                    pair(acc, mine, scaled, near_rows(block), rates, cell,
                         jnp.asarray(u, F32), jnp.asarray(v, F32))

                return carry

            return lax.fori_loop(0, 3, inner, carry)

        lax.fori_loop(0, CY, one, 0)


def radial_call(kernel, scalars, arrays, name, pairs, alias):
    vm = pl.BlockSpec(memory_space=VMEM)
    sm = pl.BlockSpec(memory_space=pltpu.SMEM)
    count = len(scalars) + len(arrays)
    return pl.pallas_call(
        kernel,
        out_shape=jax.ShapeDtypeStruct((CX * CY, ATOMS, WIDTH), F32),
        in_specs=[sm] * len(scalars) + [vm] * len(arrays),
        out_specs=vm,
        scratch_shapes=[
            pltpu.SMEM((72,), jnp.int32),
            VMEM((CX * CY, ATOMS, 8), F32),
            VMEM((8 * ATOMS, WIDTH), BF16),
        ],
        input_output_aliases={count - 1: 0} if alias else {},
        compiler_params=pltpu.CompilerParams(vmem_limit_bytes=24 * 1024 * 1024),
        cost_estimate=pl.CostEstimate(flops=pairs * 200_000_000, bytes_accessed=2_000_000, transcendentals=0),
        name=name,
    )(*scalars, *arrays)


def final_kernel(cos_ref, sin_ref, first, second, features, radial, gain, w_in, w_out, out):
    recip = jnp.dot(cos_ref[:, 0:512], first[:, 0:WIDTH], preferred_element_type=F32)
    recip += jnp.dot(sin_ref[:, 0:512], first[:, WIDTH:], preferred_element_type=F32)
    recip += jnp.dot(cos_ref[:, 512:], second[:, 0:WIDTH], preferred_element_type=F32)
    recip += jnp.dot(sin_ref[:, 512:], second[:, WIDTH:], preferred_element_type=F32)
    mixed = features[...].astype(F32) + radial[...] + recip
    power = jnp.mean(mixed * mixed, axis=-1, keepdims=True)
    normed = (mixed * lax.rsqrt(power + epsilon) * gain[...]).astype(BF16)
    v = jnp.dot(normed, w_in[...], preferred_element_type=F32)
    hidden = (v / (1.0 + jnp.exp(-v))).astype(BF16)
    out[...] = (mixed + jnp.dot(hidden, w_out[...], preferred_element_type=F32)).astype(BF16)


def final(cos_table, sin_table, first, second, features, radial, gain, w_in, w_out):
    rows = 256
    whole = pl.BlockSpec(memory_space=VMEM)
    table = pl.BlockSpec((rows, 1024), lambda i: (i, 0))
    block = pl.BlockSpec((rows, WIDTH), lambda i: (i, 0))
    return pl.pallas_call(
        final_kernel,
        grid=(1024 // rows,),
        out_shape=jax.ShapeDtypeStruct((1024, WIDTH), BF16),
        in_specs=[table, table, whole, whole, block, block, whole, whole, whole],
        out_specs=block,
        compiler_params=pltpu.CompilerParams(vmem_limit_bytes=32 * 1024 * 1024),
        cost_estimate=pl.CostEstimate(flops=3_000_000_000, bytes_accessed=8_000_000, transcendentals=0),
        name="mix_and_network",
    )(cos_table, sin_table, first, second, features, radial, gain, w_in, w_out)


def shifted(value, axis, by):
    count = lax.axis_size(axis)
    return lax.ppermute(value, axis, [(i, (i + by) % count) for i in range(count)])


def per_device(
    features,
    coords,
    nbr_cells,
    nbr_count,
    miller,
    gammas,
    radial_filter,
    reciprocal_filter,
    norm_gain,
    w_in,
    w_out,
):
    packed = jnp.concatenate([features, jnp.pad(coords, ((0, 0), (0, 0), (0, 5), (0, 128)))], axis=2)
    low = shifted(packed[1:2], "gx", 1)
    high = shifted(packed[0:1], "gx", -1)

    gx, gy = lax.axis_index("gx"), lax.axis_index("gy")
    place = jnp.stack([gx, gy]).astype(jnp.int32)
    own_rows = features.reshape(1024, WIDTH)
    cos_table, sin_table, send, keep = waves(
        place, coords.reshape(CX * CY, 3, ATOMS), own_rows, miller, vector_order()
    )

    got = permute(send, HALVING[0])
    for step, height in ((1, 256), (2, 128), (3, 64)):
        send = (keep[height:].astype(F32) + got[height:].astype(F32)).astype(BF16)
        fresh = permute(send, HALVING[step])
        keep = keep[:height] + got[:height].astype(F32)
        got = fresh
    x, y, z, core = my_place()
    other = jnp.where(core == 0, y, x)
    member = (other >> 1) * 8 + z
    slots = lax.broadcasted_iota(jnp.int32, (CHUNK, WIDTH), 0) // 4
    filters = jnp.where(slots == member, jnp.tile(reciprocal_filter, (CHUNK // 4, 1)).astype(F32), 0.0)
    total = jnp.concatenate([keep + got.astype(F32), filters], axis=1)
    for step in range(4):
        total = total + permute(total.astype(BF16), DOUBLING[step]).astype(F32)
    scale = total[:, 2 * WIDTH :]
    chunk = jnp.concatenate([total[:, :WIDTH] * scale, total[:, WIDTH : 2 * WIDTH] * scale], axis=1).astype(BF16)
    for step in (3, 2, 1):
        chunk = jnp.concatenate([chunk, permute(chunk, HALVING[step])], axis=0)
    second = permute(chunk, HALVING[0])

    left = shifted(jnp.concatenate([low[:, 3:4], packed[:, 3:4], high[:, 3:4]], axis=0), "gy", 1)
    right = shifted(jnp.concatenate([low[:, 0:1], packed[:, 0:1], high[:, 0:1]], axis=0), "gy", -1)

    scalars = (place, nbr_cells.reshape(72), nbr_count.reshape(8), gammas)
    acc = radial_call(inner_kernel, scalars, (radial_filter, packed), "radial_own", 40, False)
    acc = radial_call(
        functools.partial(outer_kernel, True), scalars, (radial_filter, packed, low, high, acc), "radial_rows", 20, True
    )
    acc = radial_call(
        functools.partial(outer_kernel, False), scalars, (radial_filter, packed, left, right, acc), "radial_columns", 12, True
    )

    out = final(
        cos_table,
        sin_table,
        chunk,
        second,
        own_rows,
        acc.reshape(1024, WIDTH),
        norm_gain.reshape(1, WIDTH),
        w_in,
        w_out,
    )
    return out.reshape(features.shape)


def solution(mesh):
    in_specs = (
        P("gx", "gy", None, None),
        P("gx", "gy", None, None),
        P("gx", "gy", None),
        P("gx", "gy"),
        P(),
        P(),
        P(),
        P(("gx", "gy"), None),
        P(),
        P(),
        P(),
    )
    out_specs = P("gx", "gy", None, None)
    return jax.shard_map(
        per_device, mesh=mesh, in_specs=in_specs, out_specs=out_specs, check_vma=False
    )
```

time: 711 us -> 110 us (0.15)
  blocking collectives: 348 us -> 0 us
  waiting for transfers between devices: 240 us -> 28.4 us
  matrix products: 73.8 us -> 0 us
  Pallas kernels: 0 us -> 35 us
  starting transfers between devices: 15.7 us -> 39.5 us
  between operations: 14 us -> 0.45 us
  other arithmetic: 11.3 us -> 0.88 us
    all_gather x1 -> x0, blocking collectives: 348 us -> none  [per_device(): lax.all_gather(reciprocal_filter, ('gx', 'gy'), axis=0, tiled=True)]
    psum x1 -> x0, waiting for transfers between devices: 227 us -> none  [per_device(): sums = lax.psum(partial_sums, ('gx', 'gy'))]
    dot_general x14 -> x0, matrix products: 73.8 us -> none  [the longest x1 15.3 us: per_device(): lax.dot_general(sin_table, coefficients[:, 1], dims, preferred_element_ty...]
    pallas_call x0 -> x5, Pallas kernels: none -> 35 us  [the longest x3 24.6 us: radial_call(): pl.pallas_call(kernel, out_shape=jax.ShapeDtypeStruct((CX * CY, ATOMS, WI...]
    ppermute x8 -> x16, starting transfers between devices: 15.7 us -> 39.5 us  [the longest x12 22.1 us: permute(): return lax.ppermute(value, AXES, partner_list(step))]
    ppermute x8 -> x16, waiting for transfers between devices: 12.6 us -> 28.4 us  [the longest x12 27.2 us: permute(): return lax.ppermute(value, AXES, partner_list(step))]
  transfers between devices with their start and end apart: 9 -> 16, of which waited for: 4 -> 9; matrix products, arithmetic and copies ran while one was open for 8% -> 1% of each run, Pallas kernels for 0% -> 23%
where the time goes in v1:
time: 110 us; the launch traced here: 108 us
  starting transfers between devices  39.5 us (36%)
  Pallas kernels  35 us (32%)
  waiting for transfers between devices  28.4 us (26%)
  local copies, waits for them, and re-layouts  4.15 us (4%)
    ppermute x12, waiting for transfers between devices, permute(): return lax.ppermute(value, AXES, partner_list(step))  27.2 us
    pallas_call x3, Pallas kernels, radial_call(): pl.pallas_call(kernel, out_shape=jax.ShapeDtypeStruct((CX * CY, ATOMS, WI...  24.6 us
    ppermute x12, starting transfers between devices, permute(): return lax.ppermute(value, AXES, partner_list(step))  22.1 us
    ppermute x4, starting transfers between devices, shifted(): lax.ppermute(value, axis, [(i, (i + by) % count) for i in range(count)])  17.4 us
    pallas_call x1, Pallas kernels, waves(): pl.pallas_call(wave_kernel, out_shape=(jax.ShapeDtypeStruct((1024, 1024),...  5.8 us
    pallas_call x1, Pallas kernels, final(): pl.pallas_call(final_kernel, grid=(1024 // rows,), out_shape=jax.ShapeDty...  4.59 us
    unnamed x31, local copies, waits for them, and re-layouts  3.87 us
  transfers between devices with their start and end apart: 16, of which 9 were waited for; matrix products, arithmetic and copies ran while one was open for 1% of the time, Pallas kernels for 23%

profile of v1, /device:TPU:1, one launch (start us, length us, event | category | flops | bytes accessed | tf_op | source)
XLA Modules:
  0.0 108.4 jit_solution(15630443745162374686)
XLA Ops:
  0.0 0.7 copy.14
  0.9 1.0 copy-done
  1.9 0.7 copy-done.4
  2.6 5.8 %wave_tables.1 = (bf16[1024,1024]{1,0:T(8,128)(2,1)S(1)}, bf16[1024,1024]{1,0:T(8,128)(2,1)S(1)}, bf16[512,512]{1,0:T(8,128)(2,1)S(1)}, f32[512,512]{1,0:T(8,128)S(1)}) custom-call(s32[2]{0:T(128)S(1)} %pad_add_fusion.place, bf16[8,3,128]{2,1,0:T(4,128)(2,1)S(1)} %bitcast.9, bf16[1024,256]{1,0:T(8,128)(2,1)S(1)} %bitcast.7, s32[3,1024]{1,0:T(4,128)S(1)} %copy-done.4, ...), custom_call_target="tpu_custom_call" | custom-call | flops 4000000000 | bytes 6000000 | tf_op jit(solution)/shard_map/wave_tables/pallas_call | solution.py:145
  8.4 1.4 %copy-done.10 = bf16[1024,1024]{1,0:T(8,128)(2,1)} copy-done((bf16[1024,1024]{1,0:T(8,128)(2,1)}, bf16[1024,1024]{1,0:T(8,128)(2,1)S(1)}, u32[]{:S(2)}) %copy-start.10) | copy-done | bytes 2097176
  9.8 3.2 %collective-permute-start = (bf16[512,512]{1,0:T(8,128)(2,1)S(1)}, bf16[512,512]{1,0:T(8,128)(2,1)S(1)}, u32[]{:S(2)}, u32[]{:S(2)}) collective-permute-start(bf16[512,512]{1,0:T(8,128)(2,1)S(1)} %get-tuple-element.12), channel_id=1, source_target_pairs={{0,1},{1,0},{16,17},{17,16},{32,33},{33,32},{48,49},{49,48},{2,3},... | collective-permute-start | bytes 1572872 | tf_op jit(solution)/shard_map/ppermute | solution.py:66
  13.0 1.5 %collective-permute-done = bf16[512,512]{1,0:T(8,128)(2,1)S(1)} collective-permute-done((bf16[512,512]{1,0:T(8,128)(2,1)S(1)}, bf16[512,512]{1,0:T(8,128)(2,1)S(1)}, u32[]{:S(2)}, u32[]{:S(2)}) %collective-permute-start) | collective-permute-done | bytes 524320 | tf_op jit(solution)/shard_map/ppermute | solution.py:66
  14.6 0.1 add_convert_fusion
  14.8 5.5 %collective-permute-done.1 = bf16[256,512]{1,0:T(8,128)(2,1)S(1)} collective-permute-done((bf16[256,512]{1,0:T(8,128)(2,1)S(1)}, bf16[256,512]{1,0:T(8,128)(2,1)S(1)}, u32[]{:S(2)}, u32[]{:S(2)}) %collective-permute-start.1) | collective-permute-done | bytes 262176 | tf_op jit(solution)/shard_map/ppermute | solution.py:66
  20.4 1.1 %collective-permute-start.2 = (bf16[128,512]{1,0:T(8,128)(2,1)S(1)}, bf16[128,512]{1,0:T(8,128)(2,1)S(1)}, u32[]{:S(2)}, u32[]{:S(2)}) collective-permute-start(bf16[128,512]{1,0:T(8,128)(2,1)S(1)} %get-tuple-element.15), channel_id=1, source_target_pairs={{0,192},{1,13},{16,208},{17,29},{32,224},{33,45},{48,240},{49,61},... | collective-permute-start | bytes 393224 | tf_op jit(solution)/shard_map/ppermute | solution.py:66
  21.6 3.9 %collective-permute-done.2 = bf16[128,512]{1,0:T(8,128)(2,1)S(1)} collective-permute-done((bf16[128,512]{1,0:T(8,128)(2,1)S(1)}, bf16[128,512]{1,0:T(8,128)(2,1)S(1)}, u32[]{:S(2)}, u32[]{:S(2)}) %collective-permute-start.2) | collective-permute-done | bytes 131104 | tf_op jit(solution)/shard_map/ppermute | solution.py:66
  25.7 0.1 fusion.10
  25.8 3.0 %collective-permute-done.3 = bf16[64,512]{1,0:T(8,128)(2,1)S(1)} collective-permute-done((bf16[64,512]{1,0:T(8,128)(2,1)S(1)}, bf16[64,512]{1,0:T(8,128)(2,1)S(1)}, u32[]{:S(2)}, u32[]{:S(2)}) %collective-permute-start.3) | collective-permute-done | bytes 65568 | tf_op jit(solution)/shard_map/ppermute | solution.py:66
  28.8 0.9 collective-permute-start.4
  29.7 3.9 %collective-permute-done.4 = bf16[64,768]{1,0:T(8,128)(2,1)S(1)} collective-permute-done((bf16[64,768]{1,0:T(8,128)(2,1)S(1)}, bf16[64,768]{1,0:T(8,128)(2,1)S(1)}, u32[]{:S(2)}, u32[]{:S(2)}) %collective-permute-start.4) | collective-permute-done | bytes 98336 | tf_op jit(solution)/shard_map/ppermute | solution.py:66
  33.6 0.1 collective-permute-start.5
  33.8 3.7 %collective-permute-done.5 = bf16[64,768]{1,0:T(8,128)(2,1)S(1)} collective-permute-done((bf16[64,768]{1,0:T(8,128)(2,1)S(1)}, bf16[64,768]{1,0:T(8,128)(2,1)S(1)}, u32[]{:S(2)}, u32[]{:S(2)}) %collective-permute-start.5) | collective-permute-done | bytes 98336 | tf_op jit(solution)/shard_map/ppermute | solution.py:66
  37.5 4.0 %collective-permute-start.6 = (bf16[64,768]{1,0:T(8,128)(2,1)S(1)}, bf16[64,768]{1,0:T(8,128)(2,1)S(1)}, u32[]{:S(2)}, u32[]{:S(2)}) collective-permute-start(bf16[64,768]{1,0:T(8,128)(2,1)S(1)} %fusion.4), channel_id=1, source_target_pairs={{0,50},{1,51},{16,32},{17,33},{32,16},{33,17},{48,2},{49,3},{2,48}... | collective-permute-start | bytes 294920 | tf_op jit(solution)/shard_map/ppermute | solution.py:66
  41.6 5.4 %collective-permute-start.13 = (bf16[1,4,136,256]{3,2,1,0:T(8,128)(2,1)S(1)}, bf16[1,4,136,256]{3,2,1,0:T(8,128)(2,1)S(1)}, u32[]{:S(2)}, u32[]{:S(2)}) collective-permute-start(bf16[1,4,136,256]{3,2,1,0:T(8,128)(2,1)S(1)} %get-tuple-element.20), channel_id=1, source_target_pairs={{0,240},{16,0},{32,16},{48,32},{64,48},{80,64},{96,80},{112,96},{1... | collective-permute-start | bytes 835592 | tf_op jit(solution)/shard_map/ppermute | solution.py:327
  47.2 0.3 collective-permute-start.7
  47.5 11.4 %radial_own.1.start = f32[8,128,256]{2,1,0:T(8,128)S(1)} custom-call(s32[2]{0:T(128)S(1)} %pad_add_fusion.place, s32[72]{0:T(128)S(1)} %reshape.726.near_list, s32[8]{0:T(128)S(1)} %reshape.727.near_count, f32[8]{0:T(128)S(1)} %copy-done.7, bf16[8,256]{1,0:T(8,128)(2,1)S(1)} %copy-done.5, bf16[2,4,136,256]{3,2,1,0:T(8,128)(2,1)S(1)} %fusion.1.own), custom_call_target="tpu_custom_call" | custom-call | flops 8000000000 | bytes 2000000 | tf_op jit(solution)/shard_map/radial_own/pallas_call | solution.py:278
  59.2 3.4 %collective-permute-done.8 = bf16[64,512]{1,0:T(8,128)(2,1)S(1)} collective-permute-done((bf16[64,512]{1,0:T(8,128)(2,1)S(1)}, bf16[64,512]{1,0:T(8,128)(2,1)S(1)}, u32[]{:S(2)}, u32[]{:S(2)}) %collective-permute-start.8) | collective-permute-done | bytes 65568 | tf_op jit(solution)/shard_map/ppermute | solution.py:66
  62.6 3.1 %collective-permute-start.9 = (bf16[128,512]{1,0:T(8,128)(2,1)S(1)}, bf16[128,512]{1,0:T(8,128)(2,1)S(1)}, u32[]{:S(2)}, u32[]{:S(2)}) collective-permute-start(bf16[128,512]{1,0:T(8,128)(2,1)S(1)} %pad_maximum_fusion.5), channel_id=1, source_target_pairs={{0,192},{1,13},{16,208},{17,29},{32,224},{33,45},{48,240},{49,61},... | collective-permute-start | bytes 393224 | tf_op jit(solution)/shard_map/ppermute | solution.py:66
  65.7 2.3 %collective-permute-done.9 = bf16[128,512]{1,0:T(8,128)(2,1)S(1)} collective-permute-done((bf16[128,512]{1,0:T(8,128)(2,1)S(1)}, bf16[128,512]{1,0:T(8,128)(2,1)S(1)}, u32[]{:S(2)}, u32[]{:S(2)}) %collective-permute-start.9) | collective-permute-done | bytes 131104 | tf_op jit(solution)/shard_map/ppermute | solution.py:66
  68.1 1.3 %collective-permute-start.10 = (bf16[256,512]{1,0:T(8,128)(2,1)S(1)}, bf16[256,512]{1,0:T(8,128)(2,1)S(1)}, u32[]{:S(2)}, u32[]{:S(2)}) collective-permute-start(bf16[256,512]{1,0:T(8,128)(2,1)S(1)} %pad_maximum_fusion.3), channel_id=1, source_target_pairs={{0,64},{1,5},{16,80},{17,21},{32,96},{33,37},{48,112},{49,53},{2,6... | collective-permute-start | bytes 786440 | tf_op jit(solution)/shard_map/ppermute | solution.py:66
  69.4 11.6 %collective-permute-start.14 = (bf16[4,1,136,256]{3,2,1,0:T(8,128)(2,1)S(1)}, bf16[4,1,136,256]{3,2,1,0:T(8,128)(2,1)S(1)}, u32[]{:S(2)}, u32[]{:S(2)}) collective-permute-start(bf16[4,1,136,256]{3,2,1,0:T(8,128)(2,1)S(1)} %pad_maximum_fusion.1), channel_id=1, source_target_pairs={{0,1},{1,2},{2,3},{3,4},{4,5},{5,6},{6,7},{7,8},{8,9},{9,10},{10,1... | collective-permute-start | bytes 835592 | tf_op jit(solution)/shard_map/ppermute | solution.py:327
  81.0 0.4 collective-permute-start.15
  81.5 7.8 %collective-permute-start.11 = (bf16[512,512]{1,0:T(8,128)(2,1)S(1)}, bf16[512,512]{1,0:T(8,128)(2,1)S(1)}, u32[]{:S(2)}, u32[]{:S(2)}) collective-permute-start(bf16[512,512]{1,0:T(8,128)(2,1)S(1)} %pad_maximum_fusion.first), channel_id=1, source_target_pairs={{0,1},{1,0},{16,17},{17,16},{32,33},{33,32},{48,49},{49,48},{2,3},... | collective-permute-start | bytes 1572872 | tf_op jit(solution)/shard_map/ppermute | solution.py:66
  89.3 7.7 %radial_rows.1.start = f32[8,128,256]{2,1,0:T(8,128)S(1)} custom-call(s32[2]{0:T(128)S(1)} %pad_add_fusion.place, s32[72]{0:T(128)S(1)} %reshape.726.near_list, s32[8]{0:T(128)S(1)} %reshape.727.near_count, f32[8]{0:T(128)S(1)} %copy-done.7, bf16[8,256]{1,0:T(8,128)(2,1)S(1)} %copy-done.5, ...), custom_call_target="tpu_custom_call", output_to_operand_aliasing={{}: (8, {})} | custom-call | flops 4000000000 | bytes 2000000 | tf_op jit(solution)/shard_map/radial_rows/pallas_call | solution.py:278
  97.1 1.2 %collective-permute-done.15.high = bf16[4,1,136,256]{3,2,1,0:T(8,128)(2,1)S(1)} collective-permute-done((bf16[4,1,136,256]{3,2,1,0:T(8,128)(2,1)S(1)}, bf16[4,1,136,256]{3,2,1,0:T(8,128)(2,1)S(1)}, u32[]{:S(2)}, u32[]{:S(2)}) %collective-permute-start.15) | collective-permute-done | bytes 278560 | tf_op jit(solution)/shard_map/ppermute | solution.py:327
  98.2 5.5 %radial_columns.1 = f32[8,128,256]{2,1,0:T(8,128)S(1)} custom-call(s32[2]{0:T(128)S(1)} %pad_add_fusion.place, s32[72]{0:T(128)S(1)} %reshape.726.near_list, s32[8]{0:T(128)S(1)} %reshape.727.near_count, f32[8]{0:T(128)S(1)} %copy-done.7, bf16[8,256]{1,0:T(8,128)(2,1)S(1)} %copy-done.5, ...), custom_call_target="tpu_custom_call", output_to_operand_aliasing={{}: (8, {})} | custom-call | flops 2400000000 | bytes 2000000 | tf_op jit(solution)/shard_map/radial_columns/pallas_call | solution.py:278
  103.8 4.6 %mix_and_network.1 = bf16[1024,256]{1,0:T(8,128)(2,1)} custom-call(bf16[1024,1024]{1,0:T(8,128)(2,1)S(1)} %copy-done.9, bf16[1024,1024]{1,0:T(8,128)(2,1)S(1)} %copy-done.11, bf16[512,512]{1,0:T(8,128)(2,1)S(1)} %pad_maximum_fusion.first, bf16[512,512]{1,0:T(8,128)(2,1)S(1)} %collective-permute-done.11.second, bf16[1024,256]{1,0:T(8,128)(2,1)S(1)} %bitcast.8, ...), custom_call_target="tpu_custom_call" | custom-call | flops 3000000000 | bytes 8000000 | tf_op jit(solution)/shard_map/mix_and_network/pallas_call | solution.py:313
  (66 shorter events, 1.4 us)
Async XLA Ops:
  0.9 1.0 copy-start
  1.9 0.7 copy-start.4
  8.4 1.4 %copy-start.10 = (bf16[1024,1024]{1,0:T(8,128)(2,1)}, bf16[1024,1024]{1,0:T(8,128)(2,1)S(1)}, u32[]{:S(2)}) copy-start(bf16[1024,1024]{1,0:T(8,128)(2,1)S(1)} %get-tuple-element.10.sin_ref) | copy-start | bytes 6291460
  9.8 4.9 %copy-start.8 = (bf16[1024,1024]{1,0:T(8,128)(2,1)}, bf16[1024,1024]{1,0:T(8,128)(2,1)S(1)}, u32[]{:S(2)}) copy-start(bf16[1024,1024]{1,0:T(8,128)(2,1)S(1)} %get-tuple-element.9.cos_ref) | copy-start | bytes 6291460
  9.8 4.8 %collective-permute-start = (bf16[512,512]{1,0:T(8,128)(2,1)S(1)}, bf16[512,512]{1,0:T(8,128)(2,1)S(1)}, u32[]{:S(2)}, u32[]{:S(2)}) collective-permute-start(bf16[512,512]{1,0:T(8,128)(2,1)S(1)} %get-tuple-element.12), channel_id=1, source_target_pairs={{0,1},{1,0},{16,17},{17,16},{32,33},{33,32},{48,49},{49,48},{2,3},... | collective-permute-start | bytes 1572872 | tf_op jit(solution)/shard_map/ppermute | solution.py:66
  14.7 6.8 %copy-start.13 = (bf16[4,256]{1,0:T(4,128)(2,1)S(1)}, bf16[4,256]{1,0:T(4,128)(2,1)}, u32[]{:S(2)}) copy-start(bf16[4,256]{1,0:T(4,128)(2,1)} %param.18) | copy-start | bytes 6148
  14.7 5.6 %collective-permute-start.1 = (bf16[256,512]{1,0:T(8,128)(2,1)S(1)}, bf16[256,512]{1,0:T(8,128)(2,1)S(1)}, u32[]{:S(2)}, u32[]{:S(2)}) collective-permute-start(bf16[256,512]{1,0:T(8,128)(2,1)S(1)} %get-tuple-element.13), channel_id=1, source_target_pairs={{0,64},{1,5},{16,80},{17,21},{32,96},{33,37},{48,112},{49,53},{2,6... | collective-permute-start | bytes 786440 | tf_op jit(solution)/shard_map/ppermute | solution.py:66
  20.4 13.3 %copy-start.1 = (bf16[2,4,128,256]{3,2,1,0:T(8,128)(2,1)S(1)}, bf16[2,4,128,256]{3,2,1,0:T(8,128)(2,1)}, u32[]{:S(2)}) copy-start(bf16[2,4,128,256]{3,2,1,0:T(8,128)(2,1)} %param.11) | copy-start | bytes 1572868
  20.4 5.1 %collective-permute-start.2 = (bf16[128,512]{1,0:T(8,128)(2,1)S(1)}, bf16[128,512]{1,0:T(8,128)(2,1)S(1)}, u32[]{:S(2)}, u32[]{:S(2)}) collective-permute-start(bf16[128,512]{1,0:T(8,128)(2,1)S(1)} %get-tuple-element.15), channel_id=1, source_target_pairs={{0,192},{1,13},{16,208},{17,29},{32,224},{33,45},{48,240},{49,61},... | collective-permute-start | bytes 393224 | tf_op jit(solution)/shard_map/ppermute | solution.py:66
  25.6 3.2 %collective-permute-start.3 = (bf16[64,512]{1,0:T(8,128)(2,1)S(1)}, bf16[64,512]{1,0:T(8,128)(2,1)S(1)}, u32[]{:S(2)}, u32[]{:S(2)}) collective-permute-start(bf16[64,512]{1,0:T(8,128)(2,1)S(1)} %fusion.5), channel_id=1, source_target_pairs={{0,4},{1,65},{16,20},{17,81},{32,36},{33,97},{48,52},{49,113},{2,6... | collective-permute-start | bytes 196616 | tf_op jit(solution)/shard_map/ppermute | solution.py:66
  28.8 4.8 %collective-permute-start.4 = (bf16[64,768]{1,0:T(8,128)(2,1)S(1)}, bf16[64,768]{1,0:T(8,128)(2,1)S(1)}, u32[]{:S(2)}, u32[]{:S(2)}) collective-permute-start(bf16[64,768]{1,0:T(8,128)(2,1)S(1)} %fusion.3), channel_id=1, source_target_pairs={{0,12},{1,193},{16,28},{17,209},{32,44},{33,225},{48,60},{49,241},... | collective-permute-start | bytes 294920 | tf_op jit(solution)/shard_map/ppermute | solution.py:66
  33.6 13.4 %copy-start.12 = (s32[2,4,9]{2,1,0:T(4,128)S(1)}, s32[2,4,9]{2,1,0:T(4,128)}, u32[]{:S(2)}) copy-start(s32[2,4,9]{2,1,0:T(4,128)} %param.13) | copy-start | bytes 868
  33.6 13.5 %copy-start.14 = (s32[2,4]{1,0:T(2,128)S(1)}, s32[2,4]{1,0:T(2,128)}, u32[]{:S(2)}) copy-start(s32[2,4]{1,0:T(2,128)} %param.14) | copy-start | bytes 100
  33.6 3.8 %collective-permute-start.5 = (bf16[64,768]{1,0:T(8,128)(2,1)S(1)}, bf16[64,768]{1,0:T(8,128)(2,1)S(1)}, u32[]{:S(2)}, u32[]{:S(2)}) collective-permute-start(bf16[64,768]{1,0:T(8,128)(2,1)S(1)} %fusion.27), channel_id=1, source_target_pairs={{0,16},{1,17},{16,0},{17,1},{32,48},{33,49},{48,32},{49,33},{2,18}... | collective-permute-start | bytes 294920 | tf_op jit(solution)/shard_map/ppermute | solution.py:66
  33.8 13.7 %copy-start.5 = (bf16[8,256]{1,0:T(8,128)(2,1)S(1)}, bf16[8,256]{1,0:T(8,128)(2,1)}, u32[]{:S(2)}) copy-start(bf16[8,256]{1,0:T(8,128)(2,1)} %filters.5) | copy-start | bytes 12292
  33.8 13.7 %copy-start.7 = (f32[8]{0:T(128)S(1)}, f32[8]{0:T(128)}, u32[]{:S(2)}) copy-start(f32[8]{0:T(128)} %rates.5) | copy-start | bytes 100
  37.5 9.7 %collective-permute-start.6 = (bf16[64,768]{1,0:T(8,128)(2,1)S(1)}, bf16[64,768]{1,0:T(8,128)(2,1)S(1)}, u32[]{:S(2)}, u32[]{:S(2)}) collective-permute-start(bf16[64,768]{1,0:T(8,128)(2,1)S(1)} %fusion.4), channel_id=1, source_target_pairs={{0,50},{1,51},{16,32},{17,33},{32,16},{33,17},{48,2},{49,3},{2,48}... | collective-permute-start | bytes 294920 | tf_op jit(solution)/shard_map/ppermute | solution.py:66
  41.5 24.1 %collective-permute-start.12 = (bf16[1,4,136,256]{3,2,1,0:T(8,128)(2,1)S(1)}, bf16[1,4,136,256]{3,2,1,0:T(8,128)(2,1)S(1)}, u32[]{:S(2)}, u32[]{:S(2)}) collective-permute-start(bf16[1,4,136,256]{3,2,1,0:T(8,128)(2,1)S(1)} %get-tuple-element.19), channel_id=1, source_target_pairs={{0,16},{16,32},{32,48},{48,64},{64,80},{80,96},{96,112},{112,128},... | collective-permute-start | bytes 835592 | tf_op jit(solution)/shard_map/ppermute | solution.py:327
  41.6 27.7 %collective-permute-start.13 = (bf16[1,4,136,256]{3,2,1,0:T(8,128)(2,1)S(1)}, bf16[1,4,136,256]{3,2,1,0:T(8,128)(2,1)S(1)}, u32[]{:S(2)}, u32[]{:S(2)}) collective-permute-start(bf16[1,4,136,256]{3,2,1,0:T(8,128)(2,1)S(1)} %get-tuple-element.20), channel_id=1, source_target_pairs={{0,240},{16,0},{32,16},{48,32},{64,48},{80,64},{96,80},{112,96},{1... | collective-permute-start | bytes 835592 | tf_op jit(solution)/shard_map/ppermute | solution.py:327
  47.2 11.8 %collective-permute-start.7 = (bf16[64,768]{1,0:T(8,128)(2,1)S(1)}, bf16[64,768]{1,0:T(8,128)(2,1)S(1)}, u32[]{:S(2)}, u32[]{:S(2)}) collective-permute-start(bf16[64,768]{1,0:T(8,128)(2,1)S(1)} %fusion.7), channel_id=1, source_target_pairs={{0,48},{1,49},{16,34},{17,35},{32,18},{33,19},{48,0},{49,1},{2,50}... | collective-permute-start | bytes 294920 | tf_op jit(solution)/shard_map/ppermute | solution.py:66
  59.1 3.5 %collective-permute-start.8 = (bf16[64,512]{1,0:T(8,128)(2,1)S(1)}, bf16[64,512]{1,0:T(8,128)(2,1)S(1)}, u32[]{:S(2)}, u32[]{:S(2)}) collective-permute-start(bf16[64,512]{1,0:T(8,128)(2,1)S(1)} %pad_maximum_fusion.6), channel_id=1, source_target_pairs={{0,4},{1,65},{16,20},{17,81},{32,36},{33,97},{48,52},{49,113},{2,6... | collective-permute-start | bytes 196616 | tf_op jit(solution)/shard_map/ppermute | solution.py:66
  62.6 5.4 %collective-permute-start.9 = (bf16[128,512]{1,0:T(8,128)(2,1)S(1)}, bf16[128,512]{1,0:T(8,128)(2,1)S(1)}, u32[]{:S(2)}, u32[]{:S(2)}) collective-permute-start(bf16[128,512]{1,0:T(8,128)(2,1)S(1)} %pad_maximum_fusion.5), channel_id=1, source_target_pairs={{0,192},{1,13},{16,208},{17,29},{32,224},{33,45},{48,240},{49,61},... | collective-permute-start | bytes 393224 | tf_op jit(solution)/shard_map/ppermute | solution.py:66
  68.1 13.4 %collective-permute-start.10 = (bf16[256,512]{1,0:T(8,128)(2,1)S(1)}, bf16[256,512]{1,0:T(8,128)(2,1)S(1)}, u32[]{:S(2)}, u32[]{:S(2)}) collective-permute-start(bf16[256,512]{1,0:T(8,128)(2,1)S(1)} %pad_maximum_fusion.3), channel_id=1, source_target_pairs={{0,64},{1,5},{16,80},{17,21},{32,96},{33,37},{48,112},{49,53},{2,6... | collective-permute-start | bytes 786440 | tf_op jit(solution)/shard_map/ppermute | solution.py:66
  69.4 27.7 %collective-permute-start.14 = (bf16[4,1,136,256]{3,2,1,0:T(8,128)(2,1)S(1)}, bf16[4,1,136,256]{3,2,1,0:T(8,128)(2,1)S(1)}, u32[]{:S(2)}, u32[]{:S(2)}) collective-permute-start(bf16[4,1,136,256]{3,2,1,0:T(8,128)(2,1)S(1)} %pad_maximum_fusion.1), channel_id=1, source_target_pairs={{0,1},{1,2},{2,3},{3,4},{4,5},{5,6},{6,7},{7,8},{8,9},{9,10},{10,1... | collective-permute-start | bytes 835592 | tf_op jit(solution)/shard_map/ppermute | solution.py:327
  81.0 17.2 %collective-permute-start.15 = (bf16[4,1,136,256]{3,2,1,0:T(8,128)(2,1)S(1)}, bf16[4,1,136,256]{3,2,1,0:T(8,128)(2,1)S(1)}, u32[]{:S(2)}, u32[]{:S(2)}) collective-permute-start(bf16[4,1,136,256]{3,2,1,0:T(8,128)(2,1)S(1)} %pad_maximum_fusion.2), channel_id=1, source_target_pairs={{0,15},{1,0},{2,1},{3,2},{4,3},{5,4},{6,5},{7,6},{8,7},{9,8},{10,9... | collective-permute-start | bytes 835592 | tf_op jit(solution)/shard_map/ppermute | solution.py:327
  81.5 22.2 %collective-permute-start.11 = (bf16[512,512]{1,0:T(8,128)(2,1)S(1)}, bf16[512,512]{1,0:T(8,128)(2,1)S(1)}, u32[]{:S(2)}, u32[]{:S(2)}) collective-permute-start(bf16[512,512]{1,0:T(8,128)(2,1)S(1)} %pad_maximum_fusion.first), channel_id=1, source_target_pairs={{0,1},{1,0},{16,17},{17,16},{32,33},{33,32},{48,49},{49,48},{2,3},... | collective-permute-start | bytes 1572872 | tf_op jit(solution)/shard_map/ppermute | solution.py:66
  97.0 6.7 %copy-start.2 = (bf16[256,512]{1,0:T(8,128)(2,1)S(1)}, bf16[256,512]{1,0:T(8,128)(2,1)}, u32[]{:S(2)}) copy-start(bf16[256,512]{1,0:T(8,128)(2,1)} %w_in.1) | copy-start | bytes 786436
  97.0 6.7 %copy-start.3 = (bf16[512,256]{1,0:T(8,128)(2,1)S(1)}, bf16[512,256]{1,0:T(8,128)(2,1)}, u32[]{:S(2)}) copy-start(bf16[512,256]{1,0:T(8,128)(2,1)} %w_out.1) | copy-start | bytes 786436
  97.0 6.7 %copy-start.6 = (f32[256]{0:T(256)S(1)}, f32[256]{0:T(256)}, u32[]{:S(2)}) copy-start(f32[256]{0:T(256)} %param.19) | copy-start | bytes 3076
  97.0 6.7 %copy-start.9 = (bf16[1024,1024]{1,0:T(8,128)(2,1)S(1)}, bf16[1024,1024]{1,0:T(8,128)(2,1)}, u32[]{:S(2)}) copy-start(bf16[1024,1024]{1,0:T(8,128)(2,1)} %copy-done.8) | copy-start | bytes 6291460
  97.1 6.7 %copy-start.11 = (bf16[1024,1024]{1,0:T(8,128)(2,1)S(1)}, bf16[1024,1024]{1,0:T(8,128)(2,1)}, u32[]{:S(2)}) copy-start(bf16[1024,1024]{1,0:T(8,128)(2,1)} %copy-done.10) | copy-start | bytes 6291460

commit v2 on v1

--- a/solution.py
+++ b/solution.py
@@ -90,7 +90,9 @@
     return linear(ox, oy, mz, owner) * 4 + rest
 
 
-def wave_kernel(place, coords, features, miller, order, cos_ref, sin_ref, send_ref, keep_ref, turned):
+def wave_kernel(
+    place, coords, features, miller, order, cos_out, sin_out, send_ref, keep_ref, turned, cos_ref, sin_ref, sems
+):
     number = miller[...].astype(F32)
     five = jnp.concatenate([number, number[0:2], jnp.zeros((3, 1024), F32)], axis=0).astype(BF16)
     natural = lax.broadcasted_iota(jnp.int32, (1024, 1024), 0)
@@ -98,16 +100,18 @@
     placed = jnp.dot(five, pick, preferred_element_type=F32).astype(BF16)
     turned[...] = features[...].astype(F32).T.astype(BF16)
     ones = jnp.ones((1, ATOMS), F32)
+    copies = []
 
     for cell in range(CX * CY):
-        block = coords[cell].astype(F32)
+        ia, ib = cell // CY, cell % CY
+        block = [coords[ia, d, ib : ib + 1, :].astype(F32) for d in range(3)]
         along = (place[0] * CX + cell // CY).astype(F32) / 32.0
         across = (place[1] * CY + cell % CY).astype(F32) / 64.0
         rows = jnp.concatenate(
             [
-                block[0:1] / 32.0,
-                block[1:2] / 64.0,
-                block[2:3] / slab_depth,
+                block[0] / 32.0,
+                block[1] / 64.0,
+                block[2] / slab_depth,
                 along * ones,
                 across * ones,
                 jnp.zeros((3, ATOMS), F32),
@@ -132,28 +136,41 @@
             rows_at = pl.ds(cell * ATOMS, ATOMS)
             cos_ref[rows_at, lanes] = (1.0 - double * sine).astype(BF16)
             sin_ref[rows_at, lanes] = (double * cosine).astype(BF16)
+        for i, (source, target) in enumerate(((cos_ref, cos_out), (sin_ref, sin_out))):
+            rows_at = pl.ds(cell * ATOMS, ATOMS)
+            copy = pltpu.make_async_copy(source.at[rows_at], target.at[rows_at], sems.at[i, cell])
+            copy.start()
+            copies.append(copy)
 
     for half, target in ((0, keep_ref), (1, send_ref)):
         lanes = slice(half * 512, half * 512 + 512)
         for col, table in ((0, cos_ref), (1, sin_ref)):
             total = jnp.dot(turned[...], table[:, lanes], preferred_element_type=F32)
             target[:, col * WIDTH : (col + 1) * WIDTH] = total.T.astype(target.dtype)
+    for copy in copies:
+        copy.wait()
 
 
 def waves(place, coords, features, miller, order):
     vm = pl.BlockSpec(memory_space=VMEM)
+    hbm = pl.BlockSpec(memory_space=pltpu.MemorySpace.HBM)
     return pl.pallas_call(
         wave_kernel,
         out_shape=(
-            jax.ShapeDtypeStruct((1024, 1024), BF16),
-            jax.ShapeDtypeStruct((1024, 1024), BF16),
+            pltpu.MemorySpace.HBM((1024, 1024), BF16),
+            pltpu.MemorySpace.HBM((1024, 1024), BF16),
             jax.ShapeDtypeStruct((512, 512), BF16),
             jax.ShapeDtypeStruct((512, 512), F32),
         ),
         in_specs=[pl.BlockSpec(memory_space=pltpu.SMEM), vm, vm, vm, vm],
-        out_specs=(vm, vm, vm, vm),
-        scratch_shapes=[VMEM((WIDTH, 1024), BF16)],
-        compiler_params=pltpu.CompilerParams(vmem_limit_bytes=40 * 1024 * 1024),
+        out_specs=(hbm, hbm, vm, vm),
+        scratch_shapes=[
+            VMEM((WIDTH, 1024), BF16),
+            VMEM((1024, 1024), BF16),
+            VMEM((1024, 1024), BF16),
+            pltpu.SemaphoreType.DMA((2, CX * CY)),
+        ],
+        compiler_params=pltpu.CompilerParams(vmem_limit_bytes=16 * 1024 * 1024),
         cost_estimate=pl.CostEstimate(flops=4_000_000_000, bytes_accessed=6_000_000, transcendentals=0),
         name="wave_tables",
     )(place, coords, features, miller, order)
@@ -181,10 +198,29 @@
     lax.fori_loop(0, 72, mark, 0)
 
 
-def own_columns(own, mine):
+def prepare_kernel(place, near_list, near_count, coords, live, mine):
+    mark_live(place, near_list, near_count, live)
     for cell in range(CX * CY):
-        rows = own[cell // CY, cell % CY, ATOMS:PACK, 0:ATOMS].astype(F32)
-        mine[cell] = rows.T
+        ia, ib = cell // CY, cell % CY
+        rows = [coords[ia, d, ib : ib + 1, :].astype(F32) for d in range(3)]
+        mine[cell] = jnp.concatenate(rows + [jnp.zeros((5, ATOMS), F32)], axis=0).T
+
+
+def prepare(place, near_list, near_count, coords):
+    vm = pl.BlockSpec(memory_space=VMEM)
+    sm = pl.BlockSpec(memory_space=pltpu.SMEM)
+    return pl.pallas_call(
+        prepare_kernel,
+        out_shape=(
+            jax.ShapeDtypeStruct((72,), jnp.int32),
+            jax.ShapeDtypeStruct((CX * CY, ATOMS, 8), F32),
+        ),
+        in_specs=[sm, sm, sm, vm],
+        out_specs=(sm, vm),
+        compiler_params=pltpu.CompilerParams(vmem_limit_bytes=4 * 1024 * 1024),
+        cost_estimate=pl.CostEstimate(flops=500_000_000, bytes_accessed=100_000, transcendentals=0),
+        name="radial_prepare",
+    )(place, near_list, near_count, coords)
 
 
 def scaled_features(block, filters, scaled):
@@ -207,16 +243,13 @@
     return block[ATOMS:PACK, 0:ATOMS].astype(F32)
 
 
-def inner_kernel(place, near_list, near_count, rates, filters, own, acc, live, mine, scaled):
-    mark_live(place, near_list, near_count, live)
-    own_columns(own, mine)
-    acc[...] = jnp.zeros_like(acc)
-
-    def one(nb, carry):
-        ja, jb = nb // CY, nb % CY
+def inner_kernel(jb, live, rates, filters, mine, own, *rest):
+    acc, scaled = rest[-2:]
+    acc[...] = jnp.zeros_like(acc) if jb == 0 else rest[0][...]
+
+    def one(ja, carry):
         block = own.at[ja, jb]
         scaled_features(block, filters, scaled)
-        near = near_rows(block)
 
         def inner(p, carry):
             ia, v = p // 3, p % 3 - 1
@@ -233,42 +266,38 @@
 
         return lax.fori_loop(0, 6, inner, carry)
 
-    lax.fori_loop(0, CX * CY, one, 0)
-
-
-def outer_kernel(along_x, place, near_list, near_count, rates, filters, own, low, high, start, acc, live, mine, scaled):
-    mark_live(place, near_list, near_count, live)
-    own_columns(own, mine)
+    lax.fori_loop(0, CX, one, 0)
+
+
+def outer_kernel(along_x, side, live, rates, filters, mine, edge, start, acc, scaled):
     acc[...] = start[...]
-    for side, ref in ((-1, low), (1, high)):
-
-        def one(j, carry, side=side, ref=ref):
-            block = ref.at[0, j] if along_x else ref.at[j, 0]
-            scaled_features(block, filters, scaled)
-
-            def inner(p, carry):
-                t = p - 1
-                if along_x:
-                    u, v = side, t
-                    ia, ib = (0 if side < 0 else CX - 1), j - t
-                    inside = (ib >= 0) & (ib < CY)
-                else:
-                    u, v = t, side
-                    ia, ib = j - 1 - t, (0 if side < 0 else CY - 1)
-                    inside = (ia >= 0) & (ia < CX)
-                cell = jnp.clip(ia * CY + ib, 0, CX * CY - 1)
-                ok = inside & (live[cell * 9 + (u + 1) * 3 + v + 1] > 0)
-
-                @pl.when(ok)
-                def _():
-                    pair(acc, mine, scaled, near_rows(block), rates, cell,
-                         jnp.asarray(u, F32), jnp.asarray(v, F32))
-
-                return carry
-
-            return lax.fori_loop(0, 3, inner, carry)
-
-        lax.fori_loop(0, CY, one, 0)
+
+    def one(j, carry):
+        block = edge.at[0, j] if along_x else edge.at[j, 0]
+        scaled_features(block, filters, scaled)
+
+        def inner(p, carry):
+            t = p - 1
+            if along_x:
+                u, v = side, t
+                ia, ib = (0 if side < 0 else CX - 1), j - t
+                inside = (ib >= 0) & (ib < CY)
+            else:
+                u, v = t, side
+                ia, ib = j - 1 - t, (0 if side < 0 else CY - 1)
+                inside = (ia >= 0) & (ia < CX)
+            cell = jnp.clip(ia * CY + ib, 0, CX * CY - 1)
+            ok = inside & (live[cell * 9 + (u + 1) * 3 + v + 1] > 0)
+
+            @pl.when(ok)
+            def _():
+                pair(acc, mine, scaled, near_rows(block), rates, cell, jnp.asarray(u, F32), jnp.asarray(v, F32))
+
+            return carry
+
+        return lax.fori_loop(0, 3, inner, carry)
+
+    lax.fori_loop(0, CY, one, 0)
 
 
 def radial_call(kernel, scalars, arrays, name, pairs, alias):
@@ -280,13 +309,9 @@
         out_shape=jax.ShapeDtypeStruct((CX * CY, ATOMS, WIDTH), F32),
         in_specs=[sm] * len(scalars) + [vm] * len(arrays),
         out_specs=vm,
-        scratch_shapes=[
-            pltpu.SMEM((72,), jnp.int32),
-            VMEM((CX * CY, ATOMS, 8), F32),
-            VMEM((8 * ATOMS, WIDTH), BF16),
-        ],
+        scratch_shapes=[VMEM((8 * ATOMS, WIDTH), BF16)],
         input_output_aliases={count - 1: 0} if alias else {},
-        compiler_params=pltpu.CompilerParams(vmem_limit_bytes=24 * 1024 * 1024),
+        compiler_params=pltpu.CompilerParams(vmem_limit_bytes=8 * 1024 * 1024),
         cost_estimate=pl.CostEstimate(flops=pairs * 200_000_000, bytes_accessed=2_000_000, transcendentals=0),
         name=name,
     )(*scalars, *arrays)
@@ -316,7 +341,7 @@
         out_shape=jax.ShapeDtypeStruct((1024, WIDTH), BF16),
         in_specs=[table, table, whole, whole, block, block, whole, whole, whole],
         out_specs=block,
-        compiler_params=pltpu.CompilerParams(vmem_limit_bytes=32 * 1024 * 1024),
+        compiler_params=pltpu.CompilerParams(vmem_limit_bytes=16 * 1024 * 1024),
         cost_estimate=pl.CostEstimate(flops=3_000_000_000, bytes_accessed=8_000_000, transcendentals=0),
         name="mix_and_network",
     )(cos_table, sin_table, first, second, features, radial, gain, w_in, w_out)
@@ -347,14 +372,42 @@
     gx, gy = lax.axis_index("gx"), lax.axis_index("gy")
     place = jnp.stack([gx, gy]).astype(jnp.int32)
     own_rows = features.reshape(1024, WIDTH)
-    cos_table, sin_table, send, keep = waves(
-        place, coords.reshape(CX * CY, 3, ATOMS), own_rows, miller, vector_order()
-    )
-
+    turned = coords.transpose(0, 2, 1, 3)
+    cos_table, sin_table, send, keep = waves(place, turned, own_rows, miller, vector_order())
+
+    scalars, acc = None, None
+
+    def own_piece(jb, acc):
+        arrays = (radial_filter, mine, packed) + (() if jb == 0 else (acc,))
+        return radial_call(
+            functools.partial(inner_kernel, jb), scalars, arrays, "radial_own", 10 if jb in (0, 3) else 12, jb > 0
+        )
+
+    def edge_piece(along_x, side, edge, acc):
+        return radial_call(
+            functools.partial(outer_kernel, along_x, side),
+            scalars,
+            (radial_filter, mine, edge, acc),
+            "radial_edge",
+            10 if along_x else 6,
+            True,
+        )
+
+    send, low, high = lax.optimization_barrier((send, low, high))
     got = permute(send, HALVING[0])
+    place, send = lax.optimization_barrier((place, send))
+    live, mine = prepare(place, nbr_cells.reshape(72), nbr_count.reshape(8), turned)
+    scalars = (live, gammas)
+    left = shifted(jnp.concatenate([low[:, 3:4], packed[:, 3:4], high[:, 3:4]], axis=0), "gy", 1)
+    right = shifted(jnp.concatenate([low[:, 0:1], packed[:, 0:1], high[:, 0:1]], axis=0), "gy", -1)
     for step, height in ((1, 256), (2, 128), (3, 64)):
         send = (keep[height:].astype(F32) + got[height:].astype(F32)).astype(BF16)
+        if step == 1:
+            send, mine = lax.optimization_barrier((send, mine))
+        else:
+            send, acc = lax.optimization_barrier((send, acc))
         fresh = permute(send, HALVING[step])
+        acc = own_piece(step - 1, acc)
         keep = keep[:height] + got[:height].astype(F32)
         got = fresh
     x, y, z, core = my_place()
@@ -364,24 +417,27 @@
     filters = jnp.where(slots == member, jnp.tile(reciprocal_filter, (CHUNK // 4, 1)).astype(F32), 0.0)
     total = jnp.concatenate([keep + got.astype(F32), filters], axis=1)
     for step in range(4):
-        total = total + permute(total.astype(BF16), DOUBLING[step]).astype(F32)
+        total, acc = lax.optimization_barrier((total, acc))
+        fresh = permute(total.astype(BF16), DOUBLING[step])
+        if step == 0:
+            acc = own_piece(3, acc)
+        elif step == 1:
+            acc = edge_piece(True, -1, low, acc)
+        elif step == 2:
+            acc = edge_piece(True, 1, high, acc)
+        else:
+            left, right, acc = lax.optimization_barrier((left, right, acc))
+            acc = edge_piece(False, -1, left, acc)
+        total = total + fresh.astype(F32)
     scale = total[:, 2 * WIDTH :]
     chunk = jnp.concatenate([total[:, :WIDTH] * scale, total[:, WIDTH : 2 * WIDTH] * scale], axis=1).astype(BF16)
     for step in (3, 2, 1):
-        chunk = jnp.concatenate([chunk, permute(chunk, HALVING[step])], axis=0)
+        chunk, acc = lax.optimization_barrier((chunk, acc))
+        fresh = permute(chunk, HALVING[step])
+        if step == 3:
+            acc = edge_piece(False, 1, right, acc)
+        chunk = jnp.concatenate([chunk, fresh], axis=0)
     second = permute(chunk, HALVING[0])
-
-    left = shifted(jnp.concatenate([low[:, 3:4], packed[:, 3:4], high[:, 3:4]], axis=0), "gy", 1)
-    right = shifted(jnp.concatenate([low[:, 0:1], packed[:, 0:1], high[:, 0:1]], axis=0), "gy", -1)
-
-    scalars = (place, nbr_cells.reshape(72), nbr_count.reshape(8), gammas)
-    acc = radial_call(inner_kernel, scalars, (radial_filter, packed), "radial_own", 40, False)
-    acc = radial_call(
-        functools.partial(outer_kernel, True), scalars, (radial_filter, packed, low, high, acc), "radial_rows", 20, True
-    )
-    acc = radial_call(
-        functools.partial(outer_kernel, False), scalars, (radial_filter, packed, left, right, acc), "radial_columns", 12, True
-    )
 
     out = final(
         cos_table,

time: 110 us -> 97.3 us (0.88)
  waiting for transfers between devices: 28.4 us -> 14.7 us
  other arithmetic: 0.88 us -> 2.77 us
  Pallas kernels: 35 us -> 36.5 us
  starting transfers between devices: 39.5 us -> 38 us
    ppermute x12, waiting for transfers between devices: 27.2 us -> 14.6 us  [permute(): return lax.ppermute(value, AXES, partner_list(step))]
    ppermute x4, starting transfers between devices: 17.4 us -> 13.1 us  [shifted(): lax.ppermute(value, axis, [(i, (i + by) % count) for i in range(count)])]
    pallas_call x1 -> x2, Pallas kernels: 5.8 us -> 9.21 us  [the longest x1 5.99 us: waves(): pl.pallas_call(wave_kernel, out_shape=(pltpu.MemorySpace.HBM((1024, 1024)...]
    unnamed x31 -> x28, local copies, waits for them, and re-layouts: 3.87 us -> 0.78 us
    ppermute x12, starting transfers between devices: 22.1 us -> 25 us  [permute(): return lax.ppermute(value, AXES, partner_list(step))]
    pallas_call x3 -> x8, Pallas kernels: 24.6 us -> 22.6 us  [radial_call(): pl.pallas_call(kernel, out_shape=jax.ShapeDtypeStruct((CX * CY, ATOMS, WI...]
    convert_element_type x1, local copies, waits for them, and re-layouts: 0.02 us -> 1.48 us  [per_device(): jnp.tile(reciprocal_filter, (CHUNK // 4, 1)).astype(F32)]
    ppermute x4, waiting for transfers between devices: 1.18 us -> 0.06 us  [shifted(): lax.ppermute(value, axis, [(i, (i + by) % count) for i in range(count)])]
  transfers between devices with their start and end apart: 16 -> 16, of which waited for: 9 -> 5; matrix products, arithmetic and copies ran while one was open for 1% -> 4% of each run, Pallas kernels for 23% -> 33%
where the time goes in v2:
time: 97.3 us; the launch traced here: 96.3 us
  starting transfers between devices  38 us (39%)
  Pallas kernels  36.5 us (38%)
  waiting for transfers between devices  14.7 us (15%)
  local copies, waits for them, and re-layouts  3.85 us (4%)
  other arithmetic  2.77 us (3%)
    ppermute x12, starting transfers between devices, permute(): return lax.ppermute(value, AXES, partner_list(step))  25 us
    pallas_call x8, Pallas kernels, radial_call(): pl.pallas_call(kernel, out_shape=jax.ShapeDtypeStruct((CX * CY, ATOMS, WI...  22.6 us
    ppermute x12, waiting for transfers between devices, permute(): return lax.ppermute(value, AXES, partner_list(step))  14.6 us
    ppermute x4, starting transfers between devices, shifted(): lax.ppermute(value, axis, [(i, (i + by) % count) for i in range(count)])  13.1 us
    pallas_call x1, Pallas kernels, waves(): pl.pallas_call(wave_kernel, out_shape=(pltpu.MemorySpace.HBM((1024, 1024)...  5.99 us
    pallas_call x1, Pallas kernels, final(): pl.pallas_call(final_kernel, grid=(1024 // rows,), out_shape=jax.ShapeDty...  4.62 us
    pallas_call x1, Pallas kernels, prepare(): pl.pallas_call(prepare_kernel, out_shape=(jax.ShapeDtypeStruct((72,), jnp...  3.22 us
  transfers between devices with their start and end apart: 16, of which 5 were waited for; matrix products, arithmetic and copies ran while one was open for 4% of the time, Pallas kernels for 33%

profile of v2, /device:TPU:1, one launch (start us, length us, event | category | flops | bytes accessed | tf_op | source)
XLA Modules:
  0.0 96.3 jit_solution(8026598998810523753)
XLA Ops:
  0.0 0.7 copy.19
  0.7 1.1 %fusion.1.own = bf16[2,4,136,256]{3,2,1,0:T(8,128)(2,1)S(1)} fusion(bf16[2,4,3,128]{3,2,1,0:T(4,128)(2,1)S(1)} %copy.19, bf16[2,4,128,256]{3,2,1,0:T(8,128)(2,1)} %param.11), kind=kLoop, calls=%fused_computation.2 | loop fusion | flops 1671168 | bytes 1087488 | tf_op jit(solution)/shard_map/concatenate | solution.py:368
  1.9 0.7 fusion.25
  2.6 2.5 %collective-permute-start = (bf16[1,4,136,256]{3,2,1,0:T(8,128)(2,1)}, bf16[1,4,136,256]{3,2,1,0:T(8,128)(2,1)S(1)}, u32[]{:S(2)}, u32[]{:S(2)}) collective-permute-start(bf16[1,4,136,256]{3,2,1,0:T(8,128)(2,1)} %get-tuple-element.78), channel_id=1, source_target_pairs={{0,16},{16,32},{32,48},{48,64},{64,80},{80,96},{96,112},{112,128},... | collective-permute-start | bytes 835592 | tf_op jit(solution)/shard_map/ppermute | solution.py:352
  5.1 4.9 %collective-permute-start.1 = (bf16[1,4,136,256]{3,2,1,0:T(8,128)(2,1)S(1)}, bf16[1,4,136,256]{3,2,1,0:T(8,128)(2,1)S(1)}, u32[]{:S(2)}, u32[]{:S(2)}) collective-permute-start(bf16[1,4,136,256]{3,2,1,0:T(8,128)(2,1)S(1)} %get-tuple-element.77), channel_id=1, source_target_pairs={{0,240},{16,0},{32,16},{48,32},{64,48},{80,64},{96,80},{112,96},{1... | collective-permute-start | bytes 835592 | tf_op jit(solution)/shard_map/ppermute | solution.py:352
  10.2 6.0 %wave_tables.1 = (bf16[1024,1024]{1,0:T(8,128)(2,1)}, bf16[1024,1024]{1,0:T(8,128)(2,1)}, bf16[512,512]{1,0:T(8,128)(2,1)S(1)}, f32[512,512]{1,0:T(8,128)S(1)}) custom-call(s32[2]{0:T(128)S(1)} %pad_add_fusion.place, bf16[2,3,4,128]{3,2,1,0:T(4,128)(2,1)S(1)} %bitcast.9, bf16[1024,256]{1,0:T(8,128)(2,1)S(1)} %bitcast.7, s32[3,1024]{1,0:T(4,128)S(1)} %copy-done.4, ...), custom_call_target="tpu_custom_call" | custom-call | flops 4000000000 | bytes 6000000 | tf_op jit(solution)/shard_map/wave_tables/pallas_call | solution.py:157
  16.9 1.5 %convert_element_type.75 = f32[64,256]{1,0:T(8,128)} reshape(f32[16,4,256]{2,1,0:T(4,128)} %tile.2) | data formatting | bytes 131072 | tf_op jit(solution)/shard_map/convert_element_type | solution.py:417
  18.6 1.9 %collective-permute-start.2 = (bf16[512,512]{1,0:T(8,128)(2,1)S(1)}, bf16[512,512]{1,0:T(8,128)(2,1)S(1)}, u32[]{:S(2)}, u32[]{:S(2)}) collective-permute-start(bf16[512,512]{1,0:T(8,128)(2,1)S(1)} %get-tuple-element.42), channel_id=1, source_target_pairs={{0,1},{1,0},{16,17},{17,16},{32,33},{33,32},{48,49},{49,48},{2,3},... | collective-permute-start | bytes 1572872 | tf_op jit(solution)/shard_map/ppermute | solution.py:66
  20.5 0.9 fusion.7
  21.5 5.6 %collective-permute-start.10 = (bf16[4,1,136,256]{3,2,1,0:T(8,128)(2,1)S(1)}, bf16[4,1,136,256]{3,2,1,0:T(8,128)(2,1)S(1)}, u32[]{:S(2)}, u32[]{:S(2)}) collective-permute-start(bf16[4,1,136,256]{3,2,1,0:T(8,128)(2,1)S(1)} %pad_maximum_fusion), channel_id=1, source_target_pairs={{0,1},{1,2},{2,3},{3,4},{4,5},{5,6},{6,7},{7,8},{8,9},{9,10},{10,1... | collective-permute-start | bytes 835592 | tf_op jit(solution)/shard_map/ppermute | solution.py:352
  27.1 3.2 %radial_prepare.1 = (s32[72]{0:T(128)S(1)}, f32[8,128,8]{2,1,0:T(8,128)S(1)}) custom-call(s32[2]{0:T(128)S(1)} %pad_add_fusion.place, s32[72]{0:T(128)S(1)} %reshape.722.near_list, s32[8]{0:T(128)S(1)} %reshape.723.near_count, bf16[2,3,4,128]{3,2,1,0:T(4,128)(2,1)S(1)} %bitcast.10), custom_call_target="tpu_custom_call" | custom-call | flops 500000000 | bytes 100000 | tf_op jit(solution)/shard_map/radial_prepare/pallas_call | solution.py:212
  30.5 1.4 %collective-permute-start.3 = (bf16[256,512]{1,0:T(8,128)(2,1)S(1)}, bf16[256,512]{1,0:T(8,128)(2,1)S(1)}, u32[]{:S(2)}, u32[]{:S(2)}) collective-permute-start(bf16[256,512]{1,0:T(8,128)(2,1)S(1)} %get-tuple-element.45), channel_id=1, source_target_pairs={{0,64},{1,5},{16,80},{17,21},{32,96},{33,37},{48,112},{49,53},{2,6... | collective-permute-start | bytes 786440 | tf_op jit(solution)/shard_map/ppermute | solution.py:66
  32.1 2.7 %radial_own.4.rest_0_ = f32[8,128,256]{2,1,0:T(8,128)S(1)} custom-call(s32[72]{0:T(128)S(1)} %get-tuple-element.46.live, f32[8]{0:T(128)S(1)} %copy-done.7, bf16[8,256]{1,0:T(8,128)(2,1)S(1)} %copy-done.5, f32[8,128,8]{2,1,0:T(8,128)S(1)} %get-tuple-element.47.mine, bf16[2,4,136,256]{3,2,1,0:T(8,128)(2,1)S(1)} %fusion.1.own), custom_call_target="tpu_custom_call" | custom-call | flops 2000000000 | bytes 2000000 | tf_op jit(solution)/shard_map/radial_own/pallas_call | solution.py:307
  34.8 1.0 %collective-permute-done.3 = bf16[256,512]{1,0:T(8,128)(2,1)S(1)} collective-permute-done((bf16[256,512]{1,0:T(8,128)(2,1)S(1)}, bf16[256,512]{1,0:T(8,128)(2,1)S(1)}, u32[]{:S(2)}, u32[]{:S(2)}) %collective-permute-start.3) | collective-permute-done | bytes 262176 | tf_op jit(solution)/shard_map/ppermute | solution.py:66
  35.9 2.8 %collective-permute-start.4 = (bf16[128,512]{1,0:T(8,128)(2,1)S(1)}, bf16[128,512]{1,0:T(8,128)(2,1)S(1)}, u32[]{:S(2)}, u32[]{:S(2)}) collective-permute-start(bf16[128,512]{1,0:T(8,128)(2,1)S(1)} %get-tuple-element.48), channel_id=1, source_target_pairs={{0,192},{1,13},{16,208},{17,29},{32,224},{33,45},{48,240},{49,61},... | collective-permute-start | bytes 393224 | tf_op jit(solution)/shard_map/ppermute | solution.py:66
  38.7 3.4 %radial_own.5.rest_0_ = f32[8,128,256]{2,1,0:T(8,128)S(1)} custom-call(s32[72]{0:T(128)S(1)} %get-tuple-element.46.live, f32[8]{0:T(128)S(1)} %copy-done.7, bf16[8,256]{1,0:T(8,128)(2,1)S(1)} %copy-done.5, f32[8,128,8]{2,1,0:T(8,128)S(1)} %get-tuple-element.47.mine, bf16[2,4,136,256]{3,2,1,0:T(8,128)(2,1)S(1)} %fusion.1.own, ...), custom_call_target="tpu_custom_call", output_to_operand_aliasing={{}: (5, {})} | custom-call | flops 2400000000 | bytes 2000000 | tf_op jit(solution)/shard_map/radial_own/pallas_call | solution.py:307
  42.7 3.4 %radial_own.6.rest_0_ = f32[8,128,256]{2,1,0:T(8,128)S(1)} custom-call(s32[72]{0:T(128)S(1)} %get-tuple-element.46.live, f32[8]{0:T(128)S(1)} %copy-done.7, bf16[8,256]{1,0:T(8,128)(2,1)S(1)} %copy-done.5, f32[8,128,8]{2,1,0:T(8,128)S(1)} %get-tuple-element.47.mine, bf16[2,4,136,256]{3,2,1,0:T(8,128)(2,1)S(1)} %fusion.1.own, ...), custom_call_target="tpu_custom_call", output_to_operand_aliasing={{}: (5, {})} | custom-call | flops 2400000000 | bytes 2000000 | tf_op jit(solution)/shard_map/radial_own/pallas_call | solution.py:307
  46.2 4.2 %collective-permute-start.6 = (bf16[64,768]{1,0:T(8,128)(2,1)S(1)}, bf16[64,768]{1,0:T(8,128)(2,1)S(1)}, u32[]{:S(2)}, u32[]{:S(2)}) collective-permute-start(bf16[64,768]{1,0:T(8,128)(2,1)S(1)} %convert_element_type.76), channel_id=1, source_target_pairs={{0,12},{1,193},{16,28},{17,209},{32,44},{33,225},{48,60},{49,241},... | collective-permute-start | bytes 294920 | tf_op jit(solution)/shard_map/ppermute | solution.py:66
  50.4 2.5 %radial_own.7.start = f32[8,128,256]{2,1,0:T(8,128)S(1)} custom-call(s32[72]{0:T(128)S(1)} %get-tuple-element.46.live, f32[8]{0:T(128)S(1)} %copy-done.7, bf16[8,256]{1,0:T(8,128)(2,1)S(1)} %copy-done.5, f32[8,128,8]{2,1,0:T(8,128)S(1)} %get-tuple-element.47.mine, bf16[2,4,136,256]{3,2,1,0:T(8,128)(2,1)S(1)} %fusion.1.own, ...), custom_call_target="tpu_custom_call", output_to_operand_aliasing={{}: (5, {})} | custom-call | flops 2000000000 | bytes 2000000 | tf_op jit(solution)/shard_map/radial_own/pallas_call | solution.py:307
  53.0 2.0 %collective-permute-start.7 = (bf16[64,768]{1,0:T(8,128)(2,1)S(1)}, bf16[64,768]{1,0:T(8,128)(2,1)S(1)}, u32[]{:S(2)}, u32[]{:S(2)}) collective-permute-start(bf16[64,768]{1,0:T(8,128)(2,1)S(1)} %convert_element_type.78), channel_id=1, source_target_pairs={{0,16},{1,17},{16,0},{17,1},{32,48},{33,49},{48,32},{49,33},{2,18}... | collective-permute-start | bytes 294920 | tf_op jit(solution)/shard_map/ppermute | solution.py:66
  55.0 2.8 %radial_edge.4.start = f32[8,128,256]{2,1,0:T(8,128)S(1)} custom-call(s32[72]{0:T(128)S(1)} %get-tuple-element.46.live, f32[8]{0:T(128)S(1)} %copy-done.7, bf16[8,256]{1,0:T(8,128)(2,1)S(1)} %copy-done.5, f32[8,128,8]{2,1,0:T(8,128)S(1)} %get-tuple-element.47.mine, ...), custom_call_target="tpu_custom_call", output_to_operand_aliasing={{}: (5, {})} | custom-call | flops 2000000000 | bytes 2000000 | tf_op jit(solution)/shard_map/radial_edge/pallas_call | solution.py:307
  57.9 2.8 %radial_edge.5.start = f32[8,128,256]{2,1,0:T(8,128)S(1)} custom-call(s32[72]{0:T(128)S(1)} %get-tuple-element.46.live, f32[8]{0:T(128)S(1)} %copy-done.7, bf16[8,256]{1,0:T(8,128)(2,1)S(1)} %copy-done.5, f32[8,128,8]{2,1,0:T(8,128)S(1)} %get-tuple-element.47.mine, ...), custom_call_target="tpu_custom_call", output_to_operand_aliasing={{}: (5, {})} | custom-call | flops 2000000000 | bytes 2000000 | tf_op jit(solution)/shard_map/radial_edge/pallas_call | solution.py:307
  60.7 1.8 %collective-permute-done.8 = bf16[64,768]{1,0:T(8,128)(2,1)S(1)} collective-permute-done((bf16[64,768]{1,0:T(8,128)(2,1)S(1)}, bf16[64,768]{1,0:T(8,128)(2,1)S(1)}, u32[]{:S(2)}, u32[]{:S(2)}) %collective-permute-start.8) | collective-permute-done | bytes 98336 | tf_op jit(solution)/shard_map/ppermute | solution.py:66
  62.6 2.9 %collective-permute-start.9 = (bf16[64,768]{1,0:T(8,128)(2,1)S(1)}, bf16[64,768]{1,0:T(8,128)(2,1)S(1)}, u32[]{:S(2)}, u32[]{:S(2)}) collective-permute-start(bf16[64,768]{1,0:T(8,128)(2,1)S(1)} %convert_element_type.82), channel_id=1, source_target_pairs={{0,48},{1,49},{16,34},{17,35},{32,18},{33,19},{48,0},{49,1},{2,50}... | collective-permute-start | bytes 294920 | tf_op jit(solution)/shard_map/ppermute | solution.py:66
  65.6 2.5 %radial_edge.6.start = f32[8,128,256]{2,1,0:T(8,128)S(1)} custom-call(s32[72]{0:T(128)S(1)} %get-tuple-element.46.live, f32[8]{0:T(128)S(1)} %copy-done.7, bf16[8,256]{1,0:T(8,128)(2,1)S(1)} %copy-done.5, f32[8,128,8]{2,1,0:T(8,128)S(1)} %get-tuple-element.47.mine, ...), custom_call_target="tpu_custom_call", output_to_operand_aliasing={{}: (5, {})} | custom-call | flops 1200000000 | bytes 2000000 | tf_op jit(solution)/shard_map/radial_edge/pallas_call | solution.py:307
  68.1 4.3 %collective-permute-start.12 = (bf16[64,512]{1,0:T(8,128)(2,1)S(1)}, bf16[64,512]{1,0:T(8,128)(2,1)S(1)}, u32[]{:S(2)}, u32[]{:S(2)}) collective-permute-start(bf16[64,512]{1,0:T(8,128)(2,1)S(1)} %pad_maximum_fusion.5), channel_id=1, source_target_pairs={{0,4},{1,65},{16,20},{17,81},{32,36},{33,97},{48,52},{49,113},{2,6... | collective-permute-start | bytes 196616 | tf_op jit(solution)/shard_map/ppermute | solution.py:66
  72.4 2.5 %radial_edge.7 = f32[8,128,256]{2,1,0:T(8,128)S(1)} custom-call(s32[72]{0:T(128)S(1)} %get-tuple-element.46.live, f32[8]{0:T(128)S(1)} %copy-done.7, bf16[8,256]{1,0:T(8,128)(2,1)S(1)} %copy-done.5, f32[8,128,8]{2,1,0:T(8,128)S(1)} %get-tuple-element.47.mine, ...), custom_call_target="tpu_custom_call", output_to_operand_aliasing={{}: (5, {})} | custom-call | flops 1200000000 | bytes 2000000 | tf_op jit(solution)/shard_map/radial_edge/pallas_call | solution.py:307
  75.1 5.0 %collective-permute-done.13 = bf16[128,512]{1,0:T(8,128)(2,1)S(1)} collective-permute-done((bf16[128,512]{1,0:T(8,128)(2,1)S(1)}, bf16[128,512]{1,0:T(8,128)(2,1)S(1)}, u32[]{:S(2)}, u32[]{:S(2)}) %collective-permute-start.13) | collective-permute-done | bytes 131104 | tf_op jit(solution)/shard_map/ppermute | solution.py:66
  80.2 5.2 %collective-permute-done.14 = bf16[256,512]{1,0:T(8,128)(2,1)S(1)} collective-permute-done((bf16[256,512]{1,0:T(8,128)(2,1)S(1)}, bf16[256,512]{1,0:T(8,128)(2,1)S(1)}, u32[]{:S(2)}, u32[]{:S(2)}) %collective-permute-start.14) | collective-permute-done | bytes 262176 | tf_op jit(solution)/shard_map/ppermute | solution.py:66
  85.5 4.7 %collective-permute-start.15 = (bf16[512,512]{1,0:T(8,128)(2,1)S(1)}, bf16[512,512]{1,0:T(8,128)(2,1)S(1)}, u32[]{:S(2)}, u32[]{:S(2)}) collective-permute-start(bf16[512,512]{1,0:T(8,128)(2,1)S(1)} %constant_dynamic-update-slice_fusion.first), channel_id=1, source_target_pairs={{0,1},{1,0},{16,17},{17,16},{32,33},{33,32},{48,49},{49,48},{2,3},... | collective-permute-start | bytes 1572872 | tf_op jit(solution)/shard_map/ppermute | solution.py:66
  90.2 1.5 %collective-permute-done.15.second = bf16[512,512]{1,0:T(8,128)(2,1)S(1)} collective-permute-done((bf16[512,512]{1,0:T(8,128)(2,1)S(1)}, bf16[512,512]{1,0:T(8,128)(2,1)S(1)}, u32[]{:S(2)}, u32[]{:S(2)}) %collective-permute-start.15) | collective-permute-done | bytes 524320 | tf_op jit(solution)/shard_map/ppermute | solution.py:66
  91.7 4.6 %mix_and_network.1 = bf16[1024,256]{1,0:T(8,128)(2,1)} custom-call(bf16[1024,1024]{1,0:T(8,128)(2,1)S(1)} %copy-done.8, bf16[1024,1024]{1,0:T(8,128)(2,1)S(1)} %copy-done.9, bf16[512,512]{1,0:T(8,128)(2,1)S(1)} %constant_dynamic-update-slice_fusion.first, bf16[512,512]{1,0:T(8,128)(2,1)S(1)} %collective-permute-done.15.second, ...), custom_call_target="tpu_custom_call" | custom-call | flops 3000000000 | bytes 8000000 | tf_op jit(solution)/shard_map/mix_and_network/pallas_call | solution.py:338
  (72 shorter events, 2.6 us)
Async XLA Ops:
  0.7 9.4 %copy-start = (bf16[2,4,128,256]{3,2,1,0:T(8,128)(2,1)S(1)}, bf16[2,4,128,256]{3,2,1,0:T(8,128)(2,1)}, u32[]{:S(2)}) copy-start(bf16[2,4,128,256]{3,2,1,0:T(8,128)(2,1)} %param.11) | copy-start | bytes 1572868
  0.7 9.4 %copy-start.1 = (bf16[2,4,3,128]{3,1,2,0:T(4,128)(2,1)S(1)}, bf16[2,4,3,128]{3,1,2,0:T(4,128)(2,1)}, u32[]{:S(2)}) copy-start(bf16[2,4,3,128]{3,1,2,0:T(4,128)(2,1)} %param.12) | copy-start | bytes 18436
  0.7 9.5 %copy-start.4 = (s32[3,1024]{1,0:T(4,128)S(1)}, s32[3,1024]{1,0:T(4,128)}, u32[]{:S(2)}) copy-start(s32[3,1024]{1,0:T(4,128)} %miller.1) | copy-start | bytes 36868
  2.6 16.0 %collective-permute-start = (bf16[1,4,136,256]{3,2,1,0:T(8,128)(2,1)}, bf16[1,4,136,256]{3,2,1,0:T(8,128)(2,1)S(1)}, u32[]{:S(2)}, u32[]{:S(2)}) collective-permute-start(bf16[1,4,136,256]{3,2,1,0:T(8,128)(2,1)} %get-tuple-element.78), channel_id=1, source_target_pairs={{0,16},{16,32},{32,48},{48,64},{64,80},{80,96},{96,112},{112,128},... | collective-permute-start | bytes 835592 | tf_op jit(solution)/shard_map/ppermute | solution.py:352
  5.1 13.5 %collective-permute-start.1 = (bf16[1,4,136,256]{3,2,1,0:T(8,128)(2,1)S(1)}, bf16[1,4,136,256]{3,2,1,0:T(8,128)(2,1)S(1)}, u32[]{:S(2)}, u32[]{:S(2)}) collective-permute-start(bf16[1,4,136,256]{3,2,1,0:T(8,128)(2,1)S(1)} %get-tuple-element.77), channel_id=1, source_target_pairs={{0,240},{16,0},{32,16},{48,32},{64,48},{80,64},{96,80},{112,96},{1... | collective-permute-start | bytes 835592 | tf_op jit(solution)/shard_map/ppermute | solution.py:352
  10.2 6.1 %copy-start.11 = (bf16[4,256]{1,0:T(4,128)(2,1)S(1)}, bf16[4,256]{1,0:T(4,128)(2,1)}, u32[]{:S(2)}) copy-start(bf16[4,256]{1,0:T(4,128)(2,1)} %param.18) | copy-start | bytes 6148
  10.2 8.2 %copy-start.10 = (s32[2,4,9]{2,1,0:T(4,128)S(1)}, s32[2,4,9]{2,1,0:T(4,128)}, u32[]{:S(2)}) copy-start(s32[2,4,9]{2,1,0:T(4,128)} %param.13) | copy-start | bytes 868
  10.2 8.3 %copy-start.12 = (s32[2,4]{1,0:T(2,128)S(1)}, s32[2,4]{1,0:T(2,128)}, u32[]{:S(2)}) copy-start(s32[2,4]{1,0:T(2,128)} %param.14) | copy-start | bytes 100
  18.6 11.7 %collective-permute-start.2 = (bf16[512,512]{1,0:T(8,128)(2,1)S(1)}, bf16[512,512]{1,0:T(8,128)(2,1)S(1)}, u32[]{:S(2)}, u32[]{:S(2)}) collective-permute-start(bf16[512,512]{1,0:T(8,128)(2,1)S(1)} %get-tuple-element.42), channel_id=1, source_target_pairs={{0,1},{1,0},{16,17},{17,16},{32,33},{33,32},{48,49},{49,48},{2,3},... | collective-permute-start | bytes 1572872 | tf_op jit(solution)/shard_map/ppermute | solution.py:66
  21.5 44.1 %collective-permute-start.10 = (bf16[4,1,136,256]{3,2,1,0:T(8,128)(2,1)S(1)}, bf16[4,1,136,256]{3,2,1,0:T(8,128)(2,1)S(1)}, u32[]{:S(2)}, u32[]{:S(2)}) collective-permute-start(bf16[4,1,136,256]{3,2,1,0:T(8,128)(2,1)S(1)} %pad_maximum_fusion), channel_id=1, source_target_pairs={{0,1},{1,2},{2,3},{3,4},{4,5},{5,6},{6,7},{7,8},{8,9},{9,10},{10,1... | collective-permute-start | bytes 835592 | tf_op jit(solution)/shard_map/ppermute | solution.py:352
  30.3 1.7 %copy-start.5 = (bf16[8,256]{1,0:T(8,128)(2,1)S(1)}, bf16[8,256]{1,0:T(8,128)(2,1)}, u32[]{:S(2)}) copy-start(bf16[8,256]{1,0:T(8,128)(2,1)} %filters.15) | copy-start | bytes 12292
  30.4 1.7 %copy-start.7 = (f32[8]{0:T(128)S(1)}, f32[8]{0:T(128)}, u32[]{:S(2)}) copy-start(f32[8]{0:T(128)} %rates.15) | copy-start | bytes 100
  30.5 5.3 %collective-permute-start.3 = (bf16[256,512]{1,0:T(8,128)(2,1)S(1)}, bf16[256,512]{1,0:T(8,128)(2,1)S(1)}, u32[]{:S(2)}, u32[]{:S(2)}) collective-permute-start(bf16[256,512]{1,0:T(8,128)(2,1)S(1)} %get-tuple-element.45), channel_id=1, source_target_pairs={{0,64},{1,5},{16,80},{17,21},{32,96},{33,37},{48,112},{49,53},{2,6... | collective-permute-start | bytes 786440 | tf_op jit(solution)/shard_map/ppermute | solution.py:66
  31.9 33.6 %collective-permute-start.11 = (bf16[4,1,136,256]{3,2,1,0:T(8,128)(2,1)S(1)}, bf16[4,1,136,256]{3,2,1,0:T(8,128)(2,1)S(1)}, u32[]{:S(2)}, u32[]{:S(2)}) collective-permute-start(bf16[4,1,136,256]{3,2,1,0:T(8,128)(2,1)S(1)} %pad_maximum_fusion.1), channel_id=1, source_target_pairs={{0,15},{1,0},{2,1},{3,2},{4,3},{5,4},{6,5},{7,6},{8,7},{9,8},{10,9... | collective-permute-start | bytes 835592 | tf_op jit(solution)/shard_map/ppermute | solution.py:352
  35.9 6.3 %collective-permute-start.4 = (bf16[128,512]{1,0:T(8,128)(2,1)S(1)}, bf16[128,512]{1,0:T(8,128)(2,1)S(1)}, u32[]{:S(2)}, u32[]{:S(2)}) collective-permute-start(bf16[128,512]{1,0:T(8,128)(2,1)S(1)} %get-tuple-element.48), channel_id=1, source_target_pairs={{0,192},{1,13},{16,208},{17,29},{32,224},{33,45},{48,240},{49,61},... | collective-permute-start | bytes 393224 | tf_op jit(solution)/shard_map/ppermute | solution.py:66
  42.2 4.0 %collective-permute-start.5 = (bf16[64,512]{1,0:T(8,128)(2,1)S(1)}, bf16[64,512]{1,0:T(8,128)(2,1)S(1)}, u32[]{:S(2)}, u32[]{:S(2)}) collective-permute-start(bf16[64,512]{1,0:T(8,128)(2,1)S(1)} %fusion.3), channel_id=1, source_target_pairs={{0,4},{1,65},{16,20},{17,81},{32,36},{33,97},{48,52},{49,113},{2,6... | collective-permute-start | bytes 196616 | tf_op jit(solution)/shard_map/ppermute | solution.py:66
  46.2 6.7 %collective-permute-start.6 = (bf16[64,768]{1,0:T(8,128)(2,1)S(1)}, bf16[64,768]{1,0:T(8,128)(2,1)S(1)}, u32[]{:S(2)}, u32[]{:S(2)}) collective-permute-start(bf16[64,768]{1,0:T(8,128)(2,1)S(1)} %convert_element_type.76), channel_id=1, source_target_pairs={{0,12},{1,193},{16,28},{17,209},{32,44},{33,225},{48,60},{49,241},... | collective-permute-start | bytes 294920 | tf_op jit(solution)/shard_map/ppermute | solution.py:66
  53.0 4.8 %collective-permute-start.7 = (bf16[64,768]{1,0:T(8,128)(2,1)S(1)}, bf16[64,768]{1,0:T(8,128)(2,1)S(1)}, u32[]{:S(2)}, u32[]{:S(2)}) collective-permute-start(bf16[64,768]{1,0:T(8,128)(2,1)S(1)} %convert_element_type.78), channel_id=1, source_target_pairs={{0,16},{1,17},{16,0},{17,1},{32,48},{33,49},{48,32},{49,33},{2,18}... | collective-permute-start | bytes 294920 | tf_op jit(solution)/shard_map/ppermute | solution.py:66
  57.8 4.8 %collective-permute-start.8 = (bf16[64,768]{1,0:T(8,128)(2,1)S(1)}, bf16[64,768]{1,0:T(8,128)(2,1)S(1)}, u32[]{:S(2)}, u32[]{:S(2)}) collective-permute-start(bf16[64,768]{1,0:T(8,128)(2,1)S(1)} %convert_element_type.80), channel_id=1, source_target_pairs={{0,50},{1,51},{16,32},{17,33},{32,16},{33,17},{48,2},{49,3},{2,48}... | collective-permute-start | bytes 294920 | tf_op jit(solution)/shard_map/ppermute | solution.py:66
  62.6 5.4 %collective-permute-start.9 = (bf16[64,768]{1,0:T(8,128)(2,1)S(1)}, bf16[64,768]{1,0:T(8,128)(2,1)S(1)}, u32[]{:S(2)}, u32[]{:S(2)}) collective-permute-start(bf16[64,768]{1,0:T(8,128)(2,1)S(1)} %convert_element_type.82), channel_id=1, source_target_pairs={{0,48},{1,49},{16,34},{17,35},{32,18},{33,19},{48,0},{49,1},{2,50}... | collective-permute-start | bytes 294920 | tf_op jit(solution)/shard_map/ppermute | solution.py:66
  68.1 6.9 %collective-permute-start.12 = (bf16[64,512]{1,0:T(8,128)(2,1)S(1)}, bf16[64,512]{1,0:T(8,128)(2,1)S(1)}, u32[]{:S(2)}, u32[]{:S(2)}) collective-permute-start(bf16[64,512]{1,0:T(8,128)(2,1)S(1)} %pad_maximum_fusion.5), channel_id=1, source_target_pairs={{0,4},{1,65},{16,20},{17,81},{32,36},{33,97},{48,52},{49,113},{2,6... | collective-permute-start | bytes 196616 | tf_op jit(solution)/shard_map/ppermute | solution.py:66
  72.4 19.3 %copy-start.8 = (bf16[1024,1024]{1,0:T(8,128)(2,1)S(1)}, bf16[1024,1024]{1,0:T(8,128)(2,1)}, u32[]{:S(2)}) copy-start(bf16[1024,1024]{1,0:T(8,128)(2,1)} %get-tuple-element.38.cos_ref) | copy-start | bytes 6291460
  72.4 19.3 %copy-start.9 = (bf16[1024,1024]{1,0:T(8,128)(2,1)S(1)}, bf16[1024,1024]{1,0:T(8,128)(2,1)}, u32[]{:S(2)}) copy-start(bf16[1024,1024]{1,0:T(8,128)(2,1)} %get-tuple-element.39.sin_ref) | copy-start | bytes 6291460
  74.9 16.8 %copy-start.2 = (bf16[256,512]{1,0:T(8,128)(2,1)S(1)}, bf16[256,512]{1,0:T(8,128)(2,1)}, u32[]{:S(2)}) copy-start(bf16[256,512]{1,0:T(8,128)(2,1)} %w_in.1) | copy-start | bytes 786436
  74.9 16.8 %copy-start.3 = (bf16[512,256]{1,0:T(8,128)(2,1)S(1)}, bf16[512,256]{1,0:T(8,128)(2,1)}, u32[]{:S(2)}) copy-start(bf16[512,256]{1,0:T(8,128)(2,1)} %w_out.1) | copy-start | bytes 786436
  74.9 16.8 %copy-start.6 = (f32[256]{0:T(256)S(1)}, f32[256]{0:T(256)}, u32[]{:S(2)}) copy-start(f32[256]{0:T(256)} %param.19) | copy-start | bytes 3076
  75.0 5.1 %collective-permute-start.13 = (bf16[128,512]{1,0:T(8,128)(2,1)S(1)}, bf16[128,512]{1,0:T(8,128)(2,1)S(1)}, u32[]{:S(2)}, u32[]{:S(2)}) collective-permute-start(bf16[128,512]{1,0:T(8,128)(2,1)S(1)} %pad_maximum_fusion.4), channel_id=1, source_target_pairs={{0,192},{1,13},{16,208},{17,29},{32,224},{33,45},{48,240},{49,61},... | collective-permute-start | bytes 393224 | tf_op jit(solution)/shard_map/ppermute | solution.py:66
  80.1 5.3 %collective-permute-start.14 = (bf16[256,512]{1,0:T(8,128)(2,1)S(1)}, bf16[256,512]{1,0:T(8,128)(2,1)S(1)}, u32[]{:S(2)}, u32[]{:S(2)}) collective-permute-start(bf16[256,512]{1,0:T(8,128)(2,1)S(1)} %pad_maximum_fusion.2), channel_id=1, source_target_pairs={{0,64},{1,5},{16,80},{17,21},{32,96},{33,37},{48,112},{49,53},{2,6... | collective-permute-start | bytes 786440 | tf_op jit(solution)/shard_map/ppermute | solution.py:66
  85.5 6.2 %collective-permute-start.15 = (bf16[512,512]{1,0:T(8,128)(2,1)S(1)}, bf16[512,512]{1,0:T(8,128)(2,1)S(1)}, u32[]{:S(2)}, u32[]{:S(2)}) collective-permute-start(bf16[512,512]{1,0:T(8,128)(2,1)S(1)} %constant_dynamic-update-slice_fusion.first), channel_id=1, source_target_pairs={{0,1},{1,0},{16,17},{17,16},{32,33},{33,32},{48,49},{49,48},{2,3},... | collective-permute-start | bytes 1572872 | tf_op jit(solution)/shard_map/ppermute | solution.py:66

commit v3 on v2

v3 whole, which is shorter than its diff:
```python
import functools

import jax
import jax.numpy as jnp
from jax import lax
from jax.experimental import pallas as pl
from jax.experimental.pallas import tpu as pltpu
from jax.sharding import PartitionSpec as P

slab_depth = 2.0
epsilon = 1e-06
LOG2E = 1.4426950408889634
AXES = ("gx", "gy")
F32 = jnp.float32
BF16 = jnp.bfloat16
CX, CY, ATOMS, WIDTH = 2, 4, 128, 256
PACK = 144
VMEM = pltpu.VMEM

SIN_COEF = (3.14159264, -5.16771008, 2.55007752, -0.59829129, 0.07765766)
COS_COEF = (0.99999995, -4.93479283, 4.05841135, -1.33187657, 0.21968961)


def linear(x, y, z, core):
    return (x * 4 + z % 4) * 16 + y * 4 + (z // 4) * 2 + core


def partner_list(step):
    pairs = []
    for x in range(4):
        for y in range(4):
            for z in range(8):
                for core in range(2):
                    pairs.append((linear(x, y, z, core), linear(*step(x, y, z, core))))
    return pairs


def flip_core(x, y, z, core):
    return x, y, z, 1 - core


def flip_plane(first, second):
    def step(x, y, z, core):
        if core == 0:
            return x ^ first, y ^ second, z, core
        return x ^ second, y ^ first, z, core

    return step


def flip_z(which):
    table = ((1, 0, 3, 2, 5, 4, 7, 6), (7, 2, 1, 4, 3, 6, 5, 0), (3, 6, 5, 0, 7, 2, 1, 4))[which]

    def step(x, y, z, core):
        return x, y, table[z], core

    return step


HALVING = (flip_core, flip_plane(1, 0), flip_plane(3, 0), flip_plane(0, 1))
DOUBLING = (flip_plane(0, 3), flip_z(0), flip_z(1), flip_z(2))
CHUNK = 64


def permute(value, step):
    return lax.ppermute(value, AXES, partner_list(step))


def my_place():
    gx, gy = lax.axis_index("gx"), lax.axis_index("gy")
    return gx // 4, gy // 4, (gx % 4) + 4 * ((gy // 2) % 2), gy % 2


def vector_order():
    x, y, z, core = my_place()
    pos = lax.broadcasted_iota(jnp.int32, (1, 1024), 1)
    rest = pos % 4
    mz = (pos // 4) % 8
    mb = (pos // 32) % 2
    b3 = (pos // 64) % 2
    b2 = (pos // 128) % 2
    b1 = (pos // 256) % 2
    owner = core ^ (pos // 512)
    main = jnp.where(owner == 0, x, y) ^ b1 ^ (3 * b2)
    other = jnp.where(owner == 0, y, x)
    coset = (other ^ (other >> 1)) & 1
    side = (coset ^ b3) ^ (3 * mb)
    ox = jnp.where(owner == 0, main, side)
    oy = jnp.where(owner == 0, side, main)
    return linear(ox, oy, mz, owner) * 4 + rest


HALF = 512


def wave_kernel(first, place, coords, miller, order, source, cos_out, sin_out, sums, *rest):
    cos_ref, sin_ref, sems = rest[-3:]
    if first:
        turned, packed, features = rest[0], rest[1:3], rest[3]
        load = pltpu.make_async_copy(source, features, sems.at[2, 0])
        load.start()
    else:
        turned = source
    number = miller[...].astype(F32)
    five = jnp.concatenate([number, number[0:2], jnp.zeros((3, 1024), F32)], axis=0).astype(BF16)
    natural = lax.broadcasted_iota(jnp.int32, (1024, HALF), 0)
    pick = jnp.where(natural == order[...], 1.0, 0.0).astype(BF16)
    placed = jnp.dot(five, pick, preferred_element_type=F32).astype(BF16)
    ones = jnp.ones((1, ATOMS), F32)
    copies = []

    for cell in range(CX * CY):
        ia, ib = cell // CY, cell % CY
        block = [coords[ia, d, ib : ib + 1, :].astype(F32) for d in range(3)]
        along = (place[0] * CX + ia).astype(F32) / 32.0
        across = (place[1] * CY + ib).astype(F32) / 64.0
        rows = jnp.concatenate(
            [
                block[0] / 32.0,
                block[1] / 64.0,
                block[2] / slab_depth,
                along * ones,
                across * ones,
                jnp.zeros((3, ATOMS), F32),
            ],
            axis=0,
        )
        columns = rows.T.astype(BF16)
        rows_at = pl.ds(cell * ATOMS, ATOMS)
        for j in range(HALF // 256):
            lanes = slice(j * 256, (j + 1) * 256)
            angle = jnp.dot(columns, placed[:, lanes], preferred_element_type=F32)
            r = angle - jnp.round(angle)
            s = r * r
            sine = SIN_COEF[4]
            cosine = COS_COEF[4]
            for a in (3, 2, 1, 0):
                sine = sine * s + SIN_COEF[a]
            for a in (3, 2, 1, 0):
                cosine = cosine * s + COS_COEF[a]
            sine = sine * r
            double = sine + sine
            cos_ref[rows_at, lanes] = (1.0 - double * sine).astype(BF16)
            sin_ref[rows_at, lanes] = (double * cosine).astype(BF16)
        for i, (source, target) in enumerate(((cos_ref, cos_out), (sin_ref, sin_out))):
            copy = pltpu.make_async_copy(source.at[rows_at], target.at[rows_at], sems.at[i, cell])
            copy.start()
            copies.append(copy)

    if first:
        load.wait()
        turned[...] = features[...].astype(F32).T.astype(BF16)
        for cell in range(CX * CY):
            ia, ib = cell // CY, cell % CY
            packed[ia][ib, 0:ATOMS, :] = features[cell * ATOMS : (cell + 1) * ATOMS, :]
            rows = [coords[ia, d, ib : ib + 1, :].astype(F32) for d in range(3)]
            rows = jnp.concatenate(rows + [jnp.zeros((PACK - ATOMS - 3, ATOMS), F32)], axis=0).astype(BF16)
            packed[ia][ib, ATOMS:PACK, :] = jnp.concatenate([rows, jnp.zeros_like(rows)], axis=1)
    for col, table in ((0, cos_ref), (1, sin_ref)):
        total = jnp.dot(turned[...], table[...], preferred_element_type=F32)
        sums[:, col * WIDTH : (col + 1) * WIDTH] = total.T.astype(sums.dtype)
    for copy in copies:
        copy.wait()


def waves(place, coords, miller, order, source, first):
    vm = pl.BlockSpec(memory_space=VMEM)
    hbm = pl.BlockSpec(memory_space=pl.ANY)
    out_shape = [
        pltpu.MemorySpace.HBM((1024, HALF), BF16),
        pltpu.MemorySpace.HBM((1024, HALF), BF16),
        jax.ShapeDtypeStruct((HALF, 2 * WIDTH), BF16 if first else F32),
    ]
    scratch = [VMEM((1024, HALF), BF16), VMEM((1024, HALF), BF16), pltpu.SemaphoreType.DMA((3, CX * CY))]
    if first:
        source = pltpu.with_memory_space_constraint(source, pltpu.MemorySpace.HBM)
        out_shape.append(jax.ShapeDtypeStruct((WIDTH, 1024), BF16))
        out_shape += [jax.ShapeDtypeStruct((CY, PACK, WIDTH), BF16)] * CX
        scratch.insert(0, VMEM((1024, WIDTH), BF16))
    return pl.pallas_call(
        functools.partial(wave_kernel, first),
        out_shape=out_shape,
        in_specs=[pl.BlockSpec(memory_space=pltpu.SMEM), vm, vm, vm, hbm if first else vm],
        out_specs=[hbm, hbm] + [vm] * (len(out_shape) - 2),
        scratch_shapes=scratch,
        compiler_params=pltpu.CompilerParams(vmem_limit_bytes=14 * 1024 * 1024),
        cost_estimate=pl.CostEstimate(flops=2_000_000_000, bytes_accessed=3_000_000, transcendentals=0),
        name="wave_tables",
    )(place, coords, miller, order, source)


def prepare_kernel(place, near_count, near_list, coords, row_filter, live, mine, filters):
    shape = (CX * CY, 9)
    cell = lax.broadcasted_iota(jnp.int32, shape, 0)
    slot = lax.broadcasted_iota(jnp.int32, shape, 1)
    entry = near_list[...]
    step_x = ((entry >> 6) - (place[0] * CX + cell // CY) + 1) & 31
    step_y = ((entry & 63) - (place[1] * CY + cell % CY) + 1) & 63
    count = jnp.zeros(shape, jnp.int32)
    for c in range(CX * CY):
        count = jnp.where(cell == c, near_count[c], count)
    code = jnp.where(slot < count, step_x * 3 + step_y, -1)
    for o in range(9):
        live[:, o : o + 1] = jnp.max(jnp.where(code == o, 1.0, 0.0), axis=1, keepdims=True)
    for c in range(CX * CY):
        ia, ib = c // CY, c % CY
        rows = [coords[ia, d, ib : ib + 1, :].astype(F32) for d in range(3)]
        columns = jnp.concatenate(rows + [jnp.zeros((5, ATOMS), F32)], axis=0).T
        for d in range(3):
            mine[c, d] = jnp.broadcast_to(columns[:, d : d + 1], (ATOMS, ATOMS))
    x, z = place[0] // 4, place[0] % 4 + 4 * ((place[1] // 2) % 2)
    y, core = place[1] // 4, place[1] % 2
    member = (jnp.where(core == 0, y, x) // 2) * 8 + z
    whole = jnp.concatenate([row_filter[...].astype(F32)] * (CHUNK // 4), axis=0)
    slots = lax.broadcasted_iota(jnp.int32, (CHUNK, WIDTH), 0) // 4
    filters[...] = jnp.where(slots == member, whole, 0.0)


def prepare(place, near_count, near_list, coords, row_filter):
    vm = pl.BlockSpec(memory_space=VMEM)
    sm = pl.BlockSpec(memory_space=pltpu.SMEM)
    return pl.pallas_call(
        prepare_kernel,
        out_shape=(
            jax.ShapeDtypeStruct((CX * CY, 9), F32),
            jax.ShapeDtypeStruct((CX * CY, 3, ATOMS, ATOMS), F32),
            jax.ShapeDtypeStruct((CHUNK, WIDTH), F32),
        ),
        in_specs=[sm, sm, vm, vm, vm],
        out_specs=(vm, vm, vm),
        compiler_params=pltpu.CompilerParams(vmem_limit_bytes=6 * 1024 * 1024),
        cost_estimate=pl.CostEstimate(flops=500_000_000, bytes_accessed=100_000, transcendentals=0),
        name="radial_prepare",
    )(place, near_count, near_list, coords, row_filter)


def radial_kernel(near_cells, fresh, rates, live, filters, mine, *rest):
    acc, scaled = rest[-2:]
    start = rest[-3]
    done = set()
    for i, ((na, nb), (source, at)) in enumerate(near_cells):
        cell_block = rest[source].at[at]
        values = cell_block[0:ATOMS, :]
        for k in range(8):
            scaled[i % 2, k * ATOMS : (k + 1) * ATOMS, :] = values * filters[k : k + 1, :]
        near = cell_block[ATOMS:PACK, 0:ATOMS].astype(F32)
        for ia in range(max(0, na - 1), min(CX, na + 2)):
            for ib in range(max(0, nb - 1), min(CY, nb + 2)):
                u, v = na - ia, nb - ib
                cell = ia * CY + ib
                dx = (near[0:1] + float(u)) - mine[cell, 0]
                dy = (near[1:2] + float(v)) - mine[cell, 1]
                dz = near[2:3] - mine[cell, 2]
                dist = dx * dx + dy * dy + dz * dz
                kernel = jnp.concatenate(
                    [jnp.exp2(dist * (rates[k] * -LOG2E)).astype(BF16) for k in range(8)], axis=1
                )
                o = (u + 1) * 3 + v + 1
                part = jnp.dot(kernel, scaled[i % 2], preferred_element_type=F32) * live[cell : cell + 1, o : o + 1]
                if cell in done:
                    acc[cell] += part
                elif fresh:
                    acc[cell] = part
                else:
                    acc[cell] = start[cell] + part
                done.add(cell)
    for cell in range(CX * CY):
        if cell not in done:
            acc[cell] = jnp.zeros((ATOMS, WIDTH), F32) if fresh else start[cell]


def radial_piece(near_cells, gammas, live, filters, mine, blocks, acc):
    vm = pl.BlockSpec(memory_space=VMEM)
    sm = pl.BlockSpec(memory_space=pltpu.SMEM)
    fresh = acc is None
    arrays = (gammas, live, filters, mine) + blocks + (() if fresh else (acc,))
    return pl.pallas_call(
        functools.partial(radial_kernel, near_cells, fresh),
        out_shape=jax.ShapeDtypeStruct((CX * CY, ATOMS, WIDTH), F32),
        in_specs=[sm] + [vm] * (len(arrays) - 1),
        out_specs=vm,
        scratch_shapes=[VMEM((2, 8 * ATOMS, WIDTH), BF16)],
        input_output_aliases={} if fresh else {len(arrays) - 1: 0},
        compiler_params=pltpu.CompilerParams(vmem_limit_bytes=10 * 1024 * 1024),
        cost_estimate=pl.CostEstimate(flops=2_000_000_000, bytes_accessed=2_000_000, transcendentals=0),
        name="radial_piece",
    )(*arrays)


def recip_kernel(low, high, cos_ref, sin_ref, coef, start, acc):
    lanes = slice(low, high)
    for row in range(4):
        rows = slice(row * 256, row * 256 + 256)
        acc[rows] = (
            start[rows]
            + jnp.dot(cos_ref[rows, lanes], coef[lanes, 0:WIDTH], preferred_element_type=F32)
            + jnp.dot(sin_ref[rows, lanes], coef[lanes, WIDTH:], preferred_element_type=F32)
        )


def recip_piece(low, high, cos_table, sin_table, coef, acc):
    vm = pl.BlockSpec(memory_space=VMEM)
    return pl.pallas_call(
        functools.partial(recip_kernel, low, high),
        out_shape=jax.ShapeDtypeStruct((1024, WIDTH), F32),
        in_specs=[vm] * 4,
        out_specs=vm,
        input_output_aliases={3: 0},
        compiler_params=pltpu.CompilerParams(vmem_limit_bytes=10 * 1024 * 1024),
        cost_estimate=pl.CostEstimate(flops=1_000_000_000, bytes_accessed=2_000_000, transcendentals=0),
        name="recip_piece",
    )(cos_table, sin_table, coef, acc)


def final_kernel(cos_ref, sin_ref, coef, features, acc, gain, w_in, w_out, out):
    rows = pl.ds(pl.multiple_of(pl.program_id(0) * 256, 256), 256)
    recip = jnp.dot(cos_ref[rows, :], coef[:, 0:WIDTH], preferred_element_type=F32)
    recip += jnp.dot(sin_ref[rows, :], coef[:, WIDTH:], preferred_element_type=F32)
    mixed = features[rows, :].astype(F32) + acc[rows, :] + recip
    power = jnp.mean(mixed * mixed, axis=-1, keepdims=True)
    normed = (mixed * lax.rsqrt(power + epsilon) * gain[...]).astype(BF16)
    v = jnp.dot(normed, w_in[...], preferred_element_type=F32)
    hidden = (v / (1.0 + jnp.exp(-v))).astype(BF16)
    out[...] = (mixed + jnp.dot(hidden, w_out[...], preferred_element_type=F32)).astype(BF16)


def final(cos_table, sin_table, coef, features, acc, gain, w_in, w_out):
    whole = pl.BlockSpec(memory_space=VMEM)
    return pl.pallas_call(
        final_kernel,
        grid=(4,),
        out_shape=jax.ShapeDtypeStruct((1024, WIDTH), BF16),
        in_specs=[whole] * 8,
        out_specs=pl.BlockSpec((256, WIDTH), lambda i: (i, 0)),
        compiler_params=pltpu.CompilerParams(vmem_limit_bytes=14 * 1024 * 1024),
        cost_estimate=pl.CostEstimate(flops=3_000_000_000, bytes_accessed=8_000_000, transcendentals=0),
        name="mix_and_network",
    )(cos_table, sin_table, coef, features, acc, gain, w_in, w_out)


def shifted(value, axis, by):
    count = lax.axis_size(axis)
    return lax.ppermute(value, axis, [(i, (i + by) % count) for i in range(count)])


def per_device(
    features,
    coords,
    nbr_cells,
    nbr_count,
    miller,
    gammas,
    radial_filter,
    reciprocal_filter,
    norm_gain,
    w_in,
    w_out,
):
    gx, gy = lax.axis_index("gx"), lax.axis_index("gy")
    place = jnp.stack([gx, gy]).astype(jnp.int32)
    own_rows = features.reshape(1024, WIDTH)
    turned = coords.transpose(0, 2, 1, 3)
    order = vector_order()
    barrier = lax.optimization_barrier

    cos_far, sin_far, send, across, upper, lower = waves(place, turned, miller, order[:, HALF:], own_rows, True)
    got = permute(send, HALVING[0])
    low = shifted(lower, "gx", 1)
    high = shifted(upper, "gx", -1)
    cos_near, sin_near, keep = waves(place, turned, miller, order[:, :HALF], across, False)

    acc = None

    def piece(near_cells, blocks, acc):
        return radial_piece(near_cells, gammas, live, radial_filter, mine, blocks, acc)

    for step, height in ((1, 256), (2, 128), (3, 64)):
        send = (keep[height:].astype(F32) + got[height:].astype(F32)).astype(BF16)
        if step == 2:
            send, live, mine, filters = barrier((send, live, mine, filters))
        elif step == 3:
            send, acc = barrier((send, acc))
        fresh = permute(send, HALVING[step])
        if step == 1:
            place, send = barrier((place, send))
            live, mine, filters = prepare(
                place, nbr_count.reshape(8), nbr_cells.reshape(8, 9), turned, reciprocal_filter
            )
        else:
            jbs = (0, 1) if step == 2 else (2, 3)
            acc = piece(tuple(((ja, jb), (ja, jb)) for jb in jbs for ja in range(CX)), (upper, lower), acc)
        keep = keep[:height] + got[:height].astype(F32)
        got = fresh
    total = jnp.concatenate([keep + got.astype(F32), filters], axis=1)
    for step in range(4):
        total, acc, low, high = barrier((total, acc, low, high))
        fresh = permute(total.astype(BF16), DOUBLING[step])
        if step == 0:
            left = shifted(jnp.concatenate([low[3:4], upper[3:4], lower[3:4], high[3:4]], axis=0), "gy", 1)
            right = shifted(jnp.concatenate([low[0:1], upper[0:1], lower[0:1], high[0:1]], axis=0), "gy", -1)
            acc = piece(tuple(((-1, jb), (0, jb)) for jb in range(CY)), (low,), acc)
        elif step == 1:
            acc = piece(tuple(((CX, jb), (0, jb)) for jb in range(CY)), (high,), acc)
        total = total + fresh.astype(F32)
    scale = total[:, 2 * WIDTH :]
    chunk = jnp.concatenate([total[:, :WIDTH] * scale, total[:, WIDTH : 2 * WIDTH] * scale], axis=1).astype(BF16)
    flat = (1024, WIDTH)
    for step, low_at, high_at in ((3, 0, 0), (2, 0, 128), (1, 128, 256), (0, 256, 512)):
        chunk, acc = barrier((chunk, acc))
        if step == 3:
            chunk, left = barrier((chunk, left))
        elif step == 2:
            chunk, right = barrier((chunk, right))
        fresh = permute(chunk, HALVING[step])
        if step == 3:
            acc = piece(tuple(((ja - 1, -1), (0, ja)) for ja in range(CX + 2)), (left,), acc)
        elif step == 2:
            acc = piece(tuple(((ja - 1, CY), (0, ja)) for ja in range(CX + 2)), (right,), acc)
            acc = acc.reshape(flat)
        if high_at:
            acc = recip_piece(low_at, high_at, cos_near, sin_near, chunk, acc)
        if step:
            chunk = jnp.concatenate([chunk, fresh], axis=0)

    out = final(
        cos_far, sin_far, fresh, own_rows, acc, norm_gain.reshape(1, WIDTH), w_in, w_out
    )
    return out.reshape(CX, CY, ATOMS, WIDTH)


def solution(mesh):
    in_specs = (
        P("gx", "gy", None, None),
        P("gx", "gy", None, None),
        P("gx", "gy", None),
        P("gx", "gy"),
        P(),
        P(),
        P(),
        P(("gx", "gy"), None),
        P(),
        P(),
        P(),
    )
    out_specs = P("gx", "gy", None, None)
    return jax.shard_map(
        per_device, mesh=mesh, in_specs=in_specs, out_specs=out_specs, check_vma=False
    )
```

time: 97.3 us -> 99.4 us (1.022)
  waiting for transfers between devices: 14.7 us -> 29.8 us
  Pallas kernels: 36.5 us -> 25.4 us
  starting transfers between devices: 38 us -> 41.1 us
  local copies, waits for them, and re-layouts: 3.85 us -> 1.61 us
  other arithmetic: 2.77 us -> 0.77 us
    ppermute x12, waiting for transfers between devices: 14.6 us -> 26.3 us  [permute(): return lax.ppermute(value, AXES, partner_list(step))]
    pallas_call x11 -> x13, Pallas kernels: 36.5 us -> 25.4 us  [the longest x6 11.4 us: radial_piece(): pl.pallas_call(functools.partial(radial_kernel, near_cells, fresh), out_s...]
    ppermute x4, starting transfers between devices: 13.1 us -> 19.9 us  [shifted(): lax.ppermute(value, axis, [(i, (i + by) % count) for i in range(count)])]
    ppermute x12, starting transfers between devices: 25 us -> 21.2 us  [permute(): return lax.ppermute(value, AXES, partner_list(step))]
    ppermute x4, waiting for transfers between devices: 0.06 us -> 3.45 us  [shifted(): lax.ppermute(value, axis, [(i, (i + by) % count) for i in range(count)])]
    convert_element_type x1 -> x0, local copies, waits for them, and re-layouts: 1.48 us -> none  [per_device(): jnp.tile(reciprocal_filter, (CHUNK // 4, 1)).astype(F32)]
    concatenate x3 -> x2, other arithmetic: 1.21 us -> 0.08 us  [the longest x1 0.04 us: per_device(): jnp.concatenate([low[3:4], upper[3:4], lower[3:4], high[3:4]], axis=0)]
  transfers between devices with their start and end apart: 16 -> 16, of which waited for: 5 -> 11; matrix products, arithmetic and copies ran while one was open for 4% -> 1% of each run, Pallas kernels for 33% -> 18%
where the time goes in v3:
time: 99.4 us; the launch traced here: 99.1 us
  starting transfers between devices  41.1 us (41%)
  waiting for transfers between devices  29.8 us (30%)
  Pallas kernels  25.4 us (26%)
  local copies, waits for them, and re-layouts  1.61 us (2%)
    ppermute x12, waiting for transfers between devices, permute(): return lax.ppermute(value, AXES, partner_list(step))  26.3 us
    ppermute x12, starting transfers between devices, permute(): return lax.ppermute(value, AXES, partner_list(step))  21.2 us
    ppermute x4, starting transfers between devices, shifted(): lax.ppermute(value, axis, [(i, (i + by) % count) for i in range(count)])  19.9 us
    pallas_call x6, Pallas kernels, radial_piece(): pl.pallas_call(functools.partial(radial_kernel, near_cells, fresh), out_s...  11.4 us
    pallas_call x2, Pallas kernels, waves(): pl.pallas_call(functools.partial(wave_kernel, first), out_shape=out_shape...  7.32 us
    pallas_call x1, Pallas kernels, final(): pl.pallas_call(final_kernel, grid=(4,), out_shape=jax.ShapeDtypeStruct((1...  4.07 us
    ppermute x4, waiting for transfers between devices, shifted(): lax.ppermute(value, axis, [(i, (i + by) % count) for i in range(count)])  3.45 us
  transfers between devices with their start and end apart: 16, of which 11 were waited for; matrix products, arithmetic and copies ran while one was open for 1% of the time, Pallas kernels for 18%

profile of v3, /device:TPU:1, one launch (start us, length us, event | category | flops | bytes accessed | tf_op | source)
XLA Modules:
  0.0 99.1 jit_solution(11600628084394032240)
XLA Ops:
  0.2 0.7 copy-done.5
  0.9 0.7 copy-done.7
  1.6 3.7 %wave_tables.2 = (bf16[1024,512]{1,0:T(8,128)(2,1)}, bf16[1024,512]{1,0:T(8,128)(2,1)}, bf16[512,512]{1,0:T(8,128)(2,1)S(1)}, bf16[256,1024]{1,0:T(8,128)(2,1)S(...) custom-call(s32[2]{0:T(128)S(1)} %pad_add_fusion.place, bf16[2,3,4,128]{3,2,1,0:T(4,128)(2,1)S(1)} %bitcast.11, ...), custom_call_target="tpu_custom_call" | custom-call | flops 2000000000 | bytes 3000000 | tf_op jit(solution)/shard_map/wave_tables/pallas_call | solution.py:180
  5.3 3.3 %collective-permute-start = (bf16[512,512]{1,0:T(8,128)(2,1)S(1)}, bf16[512,512]{1,0:T(8,128)(2,1)S(1)}, u32[]{:S(2)}, u32[]{:S(2)}) collective-permute-start(bf16[512,512]{1,0:T(8,128)(2,1)S(1)} %get-tuple-element.51), channel_id=1, source_target_pairs={{0,1},{1,0},{16,17},{17,16},{32,33},{33,32},{48,49},{49,48},{2,3},... | collective-permute-start | bytes 1572872 | tf_op jit(solution)/shard_map/ppermute | solution.py:66
  8.6 5.4 %collective-permute-start.5 = (bf16[4,144,256]{2,1,0:T(8,128)(2,1)S(1)}, bf16[4,144,256]{2,1,0:T(8,128)(2,1)S(1)}, u32[]{:S(2)}, u32[]{:S(2)}) collective-permute-start(bf16[4,144,256]{2,1,0:T(8,128)(2,1)S(1)} %get-tuple-element.59.rest_0_), channel_id=1, source_target_pairs={{0,240},{16,0},{32,16},{48,32},{64,48},{80,64},{96,80},{112,96},{1... | collective-permute-start | bytes 884744 | tf_op jit(solution)/shard_map/ppermute | solution.py:343
  14.1 3.6 %wave_tables.3 = (bf16[1024,512]{1,0:T(8,128)(2,1)}, bf16[1024,512]{1,0:T(8,128)(2,1)}, f32[512,512]{1,0:T(8,128)S(1)}) custom-call(s32[2]{0:T(128)S(1)} %pad_add_fusion.place, bf16[2,3,4,128]{3,2,1,0:T(4,128)(2,1)S(1)} %bitcast.12, s32[3,1024]{1,0:T(4,128)S(1)} %copy-done.6, s32[1,512]{1,0:T(1,128)S(1)} %get-tuple-element.103.order, ...), custom_call_target="tpu_custom_call" | custom-call | flops 2000000000 | bytes 3000000 | tf_op jit(solution)/shard_map/wave_tables/pallas_call | solution.py:180
  17.9 0.8 collective-permute-start.1
  18.8 1.3 %radial_prepare.1 = (f32[8,9]{1,0:T(8,128)S(1)}, f32[8,3,128,128]{3,2,1,0:T(8,128)S(1)}, f32[64,256]{1,0:T(8,128)S(1)}) custom-call(s32[2]{0:T(128)S(1)} %pad_add_fusion.place, s32[8]{0:T(128)S(1)} %reshape.717.near_count, s32[8,9]{1,0:T(8,128)S(1)} %bitcast.14, bf16[2,3,4,128]{3,2,1,0:T(4,128)(2,1)S(1)} %bitcast.13, bf16[4,256]{1,0:T(4,128)(2,1)S(1)} %copy-done.11), custom_call_target="tpu_custom_call" | custom-call | flops 500000000 | bytes 100000 | tf_op jit(solution)/shard_map/radial_prepare/pallas_call | solution.py:222
  20.1 3.5 %collective-permute-done.1 = bf16[256,512]{1,0:T(8,128)(2,1)S(1)} collective-permute-done((bf16[256,512]{1,0:T(8,128)(2,1)S(1)}, bf16[256,512]{1,0:T(8,128)(2,1)S(1)}, u32[]{:S(2)}, u32[]{:S(2)}) %collective-permute-start.1) | collective-permute-done | bytes 262176 | tf_op jit(solution)/shard_map/ppermute | solution.py:66
  23.6 2.2 %collective-permute-start.2 = (bf16[128,512]{1,0:T(8,128)(2,1)S(1)}, bf16[128,512]{1,0:T(8,128)(2,1)S(1)}, u32[]{:S(2)}, u32[]{:S(2)}) collective-permute-start(bf16[128,512]{1,0:T(8,128)(2,1)S(1)} %get-tuple-element.56), channel_id=1, source_target_pairs={{0,192},{1,13},{16,208},{17,29},{32,224},{33,45},{48,240},{49,61},... | collective-permute-start | bytes 393224 | tf_op jit(solution)/shard_map/ppermute | solution.py:66
  25.9 2.4 %radial_piece.6.rest_2_ = f32[8,128,256]{2,1,0:T(8,128)S(1)} custom-call(f32[8]{0:T(128)S(1)} %copy-done.13, f32[8,9]{1,0:T(8,128)S(1)} %get-tuple-element.57.live, bf16[8,256]{1,0:T(8,128)(2,1)S(1)} %copy-done.10, f32[8,3,128,128]{3,2,1,0:T(8,128)S(1)} %get-tuple-element.58.mine, bf16[4,144,256]{2,1,0:T(8,128)(2,1)S(1)} %get-tuple-element.59.rest_0_, ...), custom_call_target="tpu_custom_call" | custom-call | flops 2000000000 | bytes 2000000 | tf_op jit(solution)/shard_map/radial_piece/pallas_call | solution.py:277
  29.0 2.6 %radial_piece.7.rest_1_ = f32[8,128,256]{2,1,0:T(8,128)S(1)} custom-call(f32[8]{0:T(128)S(1)} %copy-done.13, f32[8,9]{1,0:T(8,128)S(1)} %get-tuple-element.57.live, bf16[8,256]{1,0:T(8,128)(2,1)S(1)} %copy-done.10, f32[8,3,128,128]{3,2,1,0:T(8,128)S(1)} %get-tuple-element.58.mine, ...), custom_call_target="tpu_custom_call", output_to_operand_aliasing={{}: (6, {})} | custom-call | flops 2000000000 | bytes 2000000 | tf_op jit(solution)/shard_map/radial_piece/pallas_call | solution.py:277
  31.6 0.5 collective-permute-done.3
  32.5 1.8 %radial_piece.8.rest_1_ = f32[8,128,256]{2,1,0:T(8,128)S(1)} custom-call(f32[8]{0:T(128)S(1)} %copy-done.13, f32[8,9]{1,0:T(8,128)S(1)} %get-tuple-element.57.live, bf16[8,256]{1,0:T(8,128)(2,1)S(1)} %copy-done.10, f32[8,3,128,128]{3,2,1,0:T(8,128)S(1)} %get-tuple-element.58.mine, ...), custom_call_target="tpu_custom_call", output_to_operand_aliasing={{}: (5, {})} | custom-call | flops 2000000000 | bytes 2000000 | tf_op jit(solution)/shard_map/radial_piece/pallas_call | solution.py:277
  34.3 2.7 %collective-permute-done.6 = bf16[64,768]{1,0:T(8,128)(2,1)S(1)} collective-permute-done((bf16[64,768]{1,0:T(8,128)(2,1)S(1)}, bf16[64,768]{1,0:T(8,128)(2,1)S(1)}, u32[]{:S(2)}, u32[]{:S(2)}) %collective-permute-start.6) | collective-permute-done | bytes 98336 | tf_op jit(solution)/shard_map/ppermute | solution.py:66
  37.2 1.8 %radial_piece.9.rest_1_ = f32[8,128,256]{2,1,0:T(8,128)S(1)} custom-call(f32[8]{0:T(128)S(1)} %copy-done.13, f32[8,9]{1,0:T(8,128)S(1)} %get-tuple-element.57.live, bf16[8,256]{1,0:T(8,128)(2,1)S(1)} %copy-done.10, f32[8,3,128,128]{3,2,1,0:T(8,128)S(1)} %get-tuple-element.58.mine, ...), custom_call_target="tpu_custom_call", output_to_operand_aliasing={{}: (5, {})} | custom-call | flops 2000000000 | bytes 2000000 | tf_op jit(solution)/shard_map/radial_piece/pallas_call | solution.py:277
  39.0 1.9 %collective-permute-done.7 = bf16[64,768]{1,0:T(8,128)(2,1)S(1)} collective-permute-done((bf16[64,768]{1,0:T(8,128)(2,1)S(1)}, bf16[64,768]{1,0:T(8,128)(2,1)S(1)}, u32[]{:S(2)}, u32[]{:S(2)}) %collective-permute-start.7) | collective-permute-done | bytes 98336 | tf_op jit(solution)/shard_map/ppermute | solution.py:66
  40.9 1.9 %collective-permute-start.8 = (bf16[64,768]{1,0:T(8,128)(2,1)S(1)}, bf16[64,768]{1,0:T(8,128)(2,1)S(1)}, u32[]{:S(2)}, u32[]{:S(2)}) collective-permute-start(bf16[64,768]{1,0:T(8,128)(2,1)S(1)} %convert_element_type.69), channel_id=1, source_target_pairs={{0,50},{1,51},{16,32},{17,33},{32,16},{33,17},{48,2},{49,3},{2,48}... | collective-permute-start | bytes 294920 | tf_op jit(solution)/shard_map/ppermute | solution.py:66
  42.9 12.2 %collective-permute-start.10 = (bf16[4,144,256]{2,1,0:T(8,128)(2,1)S(1)}, bf16[4,144,256]{2,1,0:T(8,128)(2,1)S(1)}, u32[]{:S(2)}, u32[]{:S(2)}) collective-permute-start(bf16[4,144,256]{2,1,0:T(8,128)(2,1)S(1)} %pad_maximum_fusion.1), channel_id=1, source_target_pairs={{0,1},{1,2},{2,3},{3,4},{4,5},{5,6},{6,7},{7,8},{8,9},{9,10},{10,1... | collective-permute-start | bytes 884744 | tf_op jit(solution)/shard_map/ppermute | solution.py:343
  55.2 2.8 %collective-permute-start.9 = (bf16[64,768]{1,0:T(8,128)(2,1)S(1)}, bf16[64,768]{1,0:T(8,128)(2,1)S(1)}, u32[]{:S(2)}, u32[]{:S(2)}) collective-permute-start(bf16[64,768]{1,0:T(8,128)(2,1)S(1)} %convert_element_type.71), channel_id=1, source_target_pairs={{0,48},{1,49},{16,34},{17,35},{32,18},{33,19},{48,0},{49,1},{2,50}... | collective-permute-start | bytes 294920 | tf_op jit(solution)/shard_map/ppermute | solution.py:66
  58.0 2.3 %collective-permute-start.12 = (bf16[4,144,256]{2,1,0:T(8,128)(2,1)S(1)}, bf16[4,144,256]{2,1,0:T(8,128)(2,1)S(1)}, u32[]{:S(2)}, u32[]{:S(2)}) collective-permute-start(bf16[4,144,256]{2,1,0:T(8,128)(2,1)S(1)} %pad_maximum_fusion.2), channel_id=1, source_target_pairs={{0,15},{1,0},{2,1},{3,2},{4,3},{5,4},{6,5},{7,6},{8,7},{9,8},{10,9... | collective-permute-start | bytes 884744 | tf_op jit(solution)/shard_map/ppermute | solution.py:343
  60.3 8.9 %collective-permute-done.9 = bf16[64,768]{1,0:T(8,128)(2,1)S(1)} collective-permute-done((bf16[64,768]{1,0:T(8,128)(2,1)S(1)}, bf16[64,768]{1,0:T(8,128)(2,1)S(1)}, u32[]{:S(2)}, u32[]{:S(2)}) %collective-permute-start.9) | collective-permute-done | bytes 98336 | tf_op jit(solution)/shard_map/ppermute | solution.py:66
  69.4 1.4 %radial_piece.10.rest_1_ = f32[8,128,256]{2,1,0:T(8,128)S(1)} custom-call(f32[8]{0:T(128)S(1)} %copy-done.13, f32[8,9]{1,0:T(8,128)S(1)} %get-tuple-element.57.live, bf16[8,256]{1,0:T(8,128)(2,1)S(1)} %copy-done.10, f32[8,3,128,128]{3,2,1,0:T(8,128)S(1)} %get-tuple-element.58.mine, ...), custom_call_target="tpu_custom_call", output_to_operand_aliasing={{}: (5, {})} | custom-call | flops 2000000000 | bytes 2000000 | tf_op jit(solution)/shard_map/radial_piece/pallas_call | solution.py:277
  70.8 2.0 %collective-permute-done.11 = bf16[64,512]{1,0:T(8,128)(2,1)S(1)} collective-permute-done((bf16[64,512]{1,0:T(8,128)(2,1)S(1)}, bf16[64,512]{1,0:T(8,128)(2,1)S(1)}, u32[]{:S(2)}, u32[]{:S(2)}) %collective-permute-start.11) | collective-permute-done | bytes 65568 | tf_op jit(solution)/shard_map/ppermute | solution.py:66
  72.8 3.4 %collective-permute-done.12.rest_0_ = bf16[4,144,256]{2,1,0:T(8,128)(2,1)S(1)} collective-permute-done((bf16[4,144,256]{2,1,0:T(8,128)(2,1)S(1)}, bf16[4,144,256]{2,1,0:T(8,128)(2,1)S(1)}, u32[]{:S(2)}, u32[]{:S(2)}) %collective-permute-start.12) | collective-permute-done | bytes 294944 | tf_op jit(solution)/shard_map/ppermute | solution.py:343
  76.3 2.9 %collective-permute-start.13 = (bf16[128,512]{1,0:T(8,128)(2,1)S(1)}, bf16[128,512]{1,0:T(8,128)(2,1)S(1)}, u32[]{:S(2)}, u32[]{:S(2)}) collective-permute-start(bf16[128,512]{1,0:T(8,128)(2,1)S(1)} %pad_maximum_fusion.5.coef), channel_id=1, source_target_pairs={{0,192},{1,13},{16,208},{17,29},{32,224},{33,45},{48,240},{49,61},... | collective-permute-start | bytes 393224 | tf_op jit(solution)/shard_map/ppermute | solution.py:66
  79.2 1.4 %radial_piece.11 = f32[8,128,256]{2,1,0:T(8,128)S(1)} custom-call(f32[8]{0:T(128)S(1)} %copy-done.13, f32[8,9]{1,0:T(8,128)S(1)} %get-tuple-element.57.live, bf16[8,256]{1,0:T(8,128)(2,1)S(1)} %copy-done.10, f32[8,3,128,128]{3,2,1,0:T(8,128)S(1)} %get-tuple-element.58.mine, ...), custom_call_target="tpu_custom_call", output_to_operand_aliasing={{}: (5, {})} | custom-call | flops 2000000000 | bytes 2000000 | tf_op jit(solution)/shard_map/radial_piece/pallas_call | solution.py:277
  81.0 0.5 collective-permute-done.13
  82.1 4.8 %collective-permute-done.14 = bf16[256,512]{1,0:T(8,128)(2,1)S(1)} collective-permute-done((bf16[256,512]{1,0:T(8,128)(2,1)S(1)}, bf16[256,512]{1,0:T(8,128)(2,1)S(1)}, u32[]{:S(2)}, u32[]{:S(2)}) %collective-permute-start.14) | collective-permute-done | bytes 262176 | tf_op jit(solution)/shard_map/ppermute | solution.py:66
  87.0 6.5 %collective-permute-start.15 = (bf16[512,512]{1,0:T(8,128)(2,1)S(1)}, bf16[512,512]{1,0:T(8,128)(2,1)S(1)}, u32[]{:S(2)}, u32[]{:S(2)}) collective-permute-start(bf16[512,512]{1,0:T(8,128)(2,1)S(1)} %pad_maximum_fusion.coef), channel_id=1, source_target_pairs={{0,1},{1,0},{16,17},{17,16},{32,33},{33,32},{48,49},{49,48},{2,3},... | collective-permute-start | bytes 1572872 | tf_op jit(solution)/shard_map/ppermute | solution.py:66
  93.9 1.1 %collective-permute-done.15.coef = bf16[512,512]{1,0:T(8,128)(2,1)S(1)} collective-permute-done((bf16[512,512]{1,0:T(8,128)(2,1)S(1)}, bf16[512,512]{1,0:T(8,128)(2,1)S(1)}, u32[]{:S(2)}, u32[]{:S(2)}) %collective-permute-start.15) | collective-permute-done | bytes 524320 | tf_op jit(solution)/shard_map/ppermute | solution.py:66
  95.0 4.1 %mix_and_network.1 = bf16[1024,256]{1,0:T(8,128)(2,1)} custom-call(bf16[1024,512]{1,0:T(8,128)(2,1)S(1)} %copy-done.14, bf16[1024,512]{1,0:T(8,128)(2,1)S(1)} %copy-done.15, bf16[512,512]{1,0:T(8,128)(2,1)S(1)} %collective-permute-done.15.coef, bf16[1024,256]{1,0:T(8,128)(2,1)S(1)} %bitcast.10, f32[1024,256]{1,0:T(8,128)S(1)} %recip_piece.5.acc, ...), custom_call_target="tpu_custom_call" | custom-call | flops 3000000000 | bytes 8000000 | tf_op jit(solution)/shard_map/mix_and_network/pallas_call | solution.py:329
  (73 shorter events, 3.5 us)
Async XLA Ops:
  0.2 0.7 copy-start.5
  1.6 12.5 %copy-start.16 = (s32[2,4]{1,0:T(2,128)S(1)}, s32[2,4]{1,0:T(2,128)}, u32[]{:S(2)}) copy-start(s32[2,4]{1,0:T(2,128)} %param.14) | copy-start | bytes 100
  1.6 12.5 %copy-start.6 = (s32[3,1024]{1,0:T(4,128)S(1)}, s32[3,1024]{1,0:T(4,128)}, u32[]{:S(2)}) copy-start(s32[3,1024]{1,0:T(4,128)} %miller.3) | copy-start | bytes 36868
  1.6 12.5 %copy-start.8 = (bf16[2,4,3,128]{3,1,2,0:T(4,128)(2,1)S(1)}, bf16[2,4,3,128]{3,1,2,0:T(4,128)(2,1)}, u32[]{:S(2)}) copy-start(bf16[2,4,3,128]{3,1,2,0:T(4,128)(2,1)} %param.12) | copy-start | bytes 18436
  5.3 12.4 %collective-permute-start = (bf16[512,512]{1,0:T(8,128)(2,1)S(1)}, bf16[512,512]{1,0:T(8,128)(2,1)S(1)}, u32[]{:S(2)}, u32[]{:S(2)}) collective-permute-start(bf16[512,512]{1,0:T(8,128)(2,1)S(1)} %get-tuple-element.51), channel_id=1, source_target_pairs={{0,1},{1,0},{16,17},{17,16},{32,33},{33,32},{48,49},{49,48},{2,3},... | collective-permute-start | bytes 1572872 | tf_op jit(solution)/shard_map/ppermute | solution.py:66
  8.6 23.6 %collective-permute-start.4 = (bf16[4,144,256]{2,1,0:T(8,128)(2,1)S(1)}, bf16[4,144,256]{2,1,0:T(8,128)(2,1)S(1)}, u32[]{:S(2)}, u32[]{:S(2)}) collective-permute-start(bf16[4,144,256]{2,1,0:T(8,128)(2,1)S(1)} %get-tuple-element.60.rest_1_), channel_id=1, source_target_pairs={{0,16},{16,32},{32,48},{48,64},{64,80},{80,96},{96,112},{112,128},... | collective-permute-start | bytes 884744 | tf_op jit(solution)/shard_map/ppermute | solution.py:343
  8.6 23.6 %collective-permute-start.5 = (bf16[4,144,256]{2,1,0:T(8,128)(2,1)S(1)}, bf16[4,144,256]{2,1,0:T(8,128)(2,1)S(1)}, u32[]{:S(2)}, u32[]{:S(2)}) collective-permute-start(bf16[4,144,256]{2,1,0:T(8,128)(2,1)S(1)} %get-tuple-element.59.rest_0_), channel_id=1, source_target_pairs={{0,240},{16,0},{32,16},{48,32},{64,48},{80,64},{96,80},{112,96},{1... | collective-permute-start | bytes 884744 | tf_op jit(solution)/shard_map/ppermute | solution.py:343
  17.7 1.1 %copy-start.9 = (s32[2,4,9]{2,1,0:T(4,128)S(1)}, s32[2,4,9]{2,1,0:T(4,128)}, u32[]{:S(2)}) copy-start(s32[2,4,9]{2,1,0:T(4,128)} %param.13) | copy-start | bytes 868
  17.7 1.1 %copy-start.11 = (bf16[4,256]{1,0:T(4,128)(2,1)S(1)}, bf16[4,256]{1,0:T(4,128)(2,1)}, u32[]{:S(2)}) copy-start(bf16[4,256]{1,0:T(4,128)(2,1)} %row_filter.1) | copy-start | bytes 6148
  17.9 5.6 %collective-permute-start.1 = (bf16[256,512]{1,0:T(8,128)(2,1)S(1)}, bf16[256,512]{1,0:T(8,128)(2,1)S(1)}, u32[]{:S(2)}, u32[]{:S(2)}) collective-permute-start(bf16[256,512]{1,0:T(8,128)(2,1)S(1)} %get-tuple-element.89), channel_id=1, source_target_pairs={{0,64},{1,5},{16,80},{17,21},{32,96},{33,37},{48,112},{49,53},{2,6... | collective-permute-start | bytes 786440 | tf_op jit(solution)/shard_map/ppermute | solution.py:66
  18.8 7.1 %copy-start.10 = (bf16[8,256]{1,0:T(8,128)(2,1)S(1)}, bf16[8,256]{1,0:T(8,128)(2,1)}, u32[]{:S(2)}) copy-start(bf16[8,256]{1,0:T(8,128)(2,1)} %filters.11) | copy-start | bytes 12292
  18.8 7.1 %copy-start.13 = (f32[8]{0:T(128)S(1)}, f32[8]{0:T(128)}, u32[]{:S(2)}) copy-start(f32[8]{0:T(128)} %rates.11) | copy-start | bytes 100
  23.6 5.1 %collective-permute-start.2 = (bf16[128,512]{1,0:T(8,128)(2,1)S(1)}, bf16[128,512]{1,0:T(8,128)(2,1)S(1)}, u32[]{:S(2)}, u32[]{:S(2)}) collective-permute-start(bf16[128,512]{1,0:T(8,128)(2,1)S(1)} %get-tuple-element.56), channel_id=1, source_target_pairs={{0,192},{1,13},{16,208},{17,29},{32,224},{33,45},{48,240},{49,61},... | collective-permute-start | bytes 393224 | tf_op jit(solution)/shard_map/ppermute | solution.py:66
  28.8 3.4 %collective-permute-start.3 = (bf16[64,512]{1,0:T(8,128)(2,1)S(1)}, bf16[64,512]{1,0:T(8,128)(2,1)S(1)}, u32[]{:S(2)}, u32[]{:S(2)}) collective-permute-start(bf16[64,512]{1,0:T(8,128)(2,1)S(1)} %fusion.1), channel_id=1, source_target_pairs={{0,4},{1,65},{16,20},{17,81},{32,36},{33,97},{48,52},{49,113},{2,6... | collective-permute-start | bytes 196616 | tf_op jit(solution)/shard_map/ppermute | solution.py:66
  32.2 4.8 %collective-permute-start.6 = (bf16[64,768]{1,0:T(8,128)(2,1)S(1)}, bf16[64,768]{1,0:T(8,128)(2,1)S(1)}, u32[]{:S(2)}, u32[]{:S(2)}) collective-permute-start(bf16[64,768]{1,0:T(8,128)(2,1)S(1)} %convert_element_type.65), channel_id=1, source_target_pairs={{0,12},{1,193},{16,28},{17,209},{32,44},{33,225},{48,60},{49,241},... | collective-permute-start | bytes 294920 | tf_op jit(solution)/shard_map/ppermute | solution.py:66
  37.1 3.8 %collective-permute-start.7 = (bf16[64,768]{1,0:T(8,128)(2,1)S(1)}, bf16[64,768]{1,0:T(8,128)(2,1)S(1)}, u32[]{:S(2)}, u32[]{:S(2)}) collective-permute-start(bf16[64,768]{1,0:T(8,128)(2,1)S(1)} %convert_element_type.67), channel_id=1, source_target_pairs={{0,16},{1,17},{16,0},{17,1},{32,48},{33,49},{48,32},{49,33},{2,18}... | collective-permute-start | bytes 294920 | tf_op jit(solution)/shard_map/ppermute | solution.py:66
  40.9 14.2 %collective-permute-start.8 = (bf16[64,768]{1,0:T(8,128)(2,1)S(1)}, bf16[64,768]{1,0:T(8,128)(2,1)S(1)}, u32[]{:S(2)}, u32[]{:S(2)}) collective-permute-start(bf16[64,768]{1,0:T(8,128)(2,1)S(1)} %convert_element_type.69), channel_id=1, source_target_pairs={{0,50},{1,51},{16,32},{17,33},{32,16},{33,17},{48,2},{49,3},{2,48}... | collective-permute-start | bytes 294920 | tf_op jit(solution)/shard_map/ppermute | solution.py:66
  42.9 26.4 %collective-permute-start.10 = (bf16[4,144,256]{2,1,0:T(8,128)(2,1)S(1)}, bf16[4,144,256]{2,1,0:T(8,128)(2,1)S(1)}, u32[]{:S(2)}, u32[]{:S(2)}) collective-permute-start(bf16[4,144,256]{2,1,0:T(8,128)(2,1)S(1)} %pad_maximum_fusion.1), channel_id=1, source_target_pairs={{0,1},{1,2},{2,3},{3,4},{4,5},{5,6},{6,7},{7,8},{8,9},{9,10},{10,1... | collective-permute-start | bytes 884744 | tf_op jit(solution)/shard_map/ppermute | solution.py:343
  55.2 14.1 %collective-permute-start.9 = (bf16[64,768]{1,0:T(8,128)(2,1)S(1)}, bf16[64,768]{1,0:T(8,128)(2,1)S(1)}, u32[]{:S(2)}, u32[]{:S(2)}) collective-permute-start(bf16[64,768]{1,0:T(8,128)(2,1)S(1)} %convert_element_type.71), channel_id=1, source_target_pairs={{0,48},{1,49},{16,34},{17,35},{32,18},{33,19},{48,0},{49,1},{2,50}... | collective-permute-start | bytes 294920 | tf_op jit(solution)/shard_map/ppermute | solution.py:66
  58.0 18.3 %collective-permute-start.12 = (bf16[4,144,256]{2,1,0:T(8,128)(2,1)S(1)}, bf16[4,144,256]{2,1,0:T(8,128)(2,1)S(1)}, u32[]{:S(2)}, u32[]{:S(2)}) collective-permute-start(bf16[4,144,256]{2,1,0:T(8,128)(2,1)S(1)} %pad_maximum_fusion.2), channel_id=1, source_target_pairs={{0,15},{1,0},{2,1},{3,2},{4,3},{5,4},{6,5},{7,6},{8,7},{9,8},{10,9... | collective-permute-start | bytes 884744 | tf_op jit(solution)/shard_map/ppermute | solution.py:343
  69.3 3.5 %collective-permute-start.11 = (bf16[64,512]{1,0:T(8,128)(2,1)S(1)}, bf16[64,512]{1,0:T(8,128)(2,1)S(1)}, u32[]{:S(2)}, u32[]{:S(2)}) collective-permute-start(bf16[64,512]{1,0:T(8,128)(2,1)S(1)} %pad_maximum_fusion.6), channel_id=1, source_target_pairs={{0,4},{1,65},{16,20},{17,81},{32,36},{33,97},{48,52},{49,113},{2,6... | collective-permute-start | bytes 196616 | tf_op jit(solution)/shard_map/ppermute | solution.py:66
  72.8 7.8 %copy-start = (bf16[1024,512]{1,0:T(8,128)(2,1)S(1)}, bf16[1024,512]{1,0:T(8,128)(2,1)}, u32[]{:S(2)}) copy-start(bf16[1024,512]{1,0:T(8,128)(2,1)} %get-tuple-element.81.cos_ref) | copy-start | bytes 3145732
  72.8 7.8 %copy-start.1 = (bf16[1024,512]{1,0:T(8,128)(2,1)S(1)}, bf16[1024,512]{1,0:T(8,128)(2,1)}, u32[]{:S(2)}) copy-start(bf16[1024,512]{1,0:T(8,128)(2,1)} %get-tuple-element.82.sin_ref) | copy-start | bytes 3145732
  76.3 5.3 %collective-permute-start.13 = (bf16[128,512]{1,0:T(8,128)(2,1)S(1)}, bf16[128,512]{1,0:T(8,128)(2,1)S(1)}, u32[]{:S(2)}, u32[]{:S(2)}) collective-permute-start(bf16[128,512]{1,0:T(8,128)(2,1)S(1)} %pad_maximum_fusion.5.coef), channel_id=1, source_target_pairs={{0,192},{1,13},{16,208},{17,29},{32,224},{33,45},{48,240},{49,61},... | collective-permute-start | bytes 393224 | tf_op jit(solution)/shard_map/ppermute | solution.py:66
  81.6 5.3 %collective-permute-start.14 = (bf16[256,512]{1,0:T(8,128)(2,1)S(1)}, bf16[256,512]{1,0:T(8,128)(2,1)S(1)}, u32[]{:S(2)}, u32[]{:S(2)}) collective-permute-start(bf16[256,512]{1,0:T(8,128)(2,1)S(1)} %pad_maximum_fusion.3.coef), channel_id=1, source_target_pairs={{0,64},{1,5},{16,80},{17,21},{32,96},{33,37},{48,112},{49,53},{2,6... | collective-permute-start | bytes 786440 | tf_op jit(solution)/shard_map/ppermute | solution.py:66
  86.9 8.1 %copy-start.2 = (bf16[2,4,128,256]{3,2,1,0:T(8,128)(2,1)S(1)}, bf16[2,4,128,256]{3,2,1,0:T(8,128)(2,1)}, u32[]{:S(2)}) copy-start(bf16[2,4,128,256]{3,2,1,0:T(8,128)(2,1)} %param.11) | copy-start | bytes 1572868
  86.9 8.1 %copy-start.3 = (bf16[256,512]{1,0:T(8,128)(2,1)S(1)}, bf16[256,512]{1,0:T(8,128)(2,1)}, u32[]{:S(2)}) copy-start(bf16[256,512]{1,0:T(8,128)(2,1)} %w_in.1) | copy-start | bytes 786436
  86.9 8.1 %copy-start.4 = (bf16[512,256]{1,0:T(8,128)(2,1)S(1)}, bf16[512,256]{1,0:T(8,128)(2,1)}, u32[]{:S(2)}) copy-start(bf16[512,256]{1,0:T(8,128)(2,1)} %w_out.1) | copy-start | bytes 786436
  87.0 8.1 %copy-start.12 = (f32[256]{0:T(256)S(1)}, f32[256]{0:T(256)}, u32[]{:S(2)}) copy-start(f32[256]{0:T(256)} %param.19) | copy-start | bytes 3076
  87.0 8.0 %copy-start.14 = (bf16[1024,512]{1,0:T(8,128)(2,1)S(1)}, bf16[1024,512]{1,0:T(8,128)(2,1)}, u32[]{:S(2)}) copy-start(bf16[1024,512]{1,0:T(8,128)(2,1)} %get-tuple-element.47.cos_ref) | copy-start | bytes 3145732
  87.0 8.0 %copy-start.15 = (bf16[1024,512]{1,0:T(8,128)(2,1)S(1)}, bf16[1024,512]{1,0:T(8,128)(2,1)}, u32[]{:S(2)}) copy-start(bf16[1024,512]{1,0:T(8,128)(2,1)} %get-tuple-element.48.sin_ref) | copy-start | bytes 3145732
  87.0 8.0 %collective-permute-start.15 = (bf16[512,512]{1,0:T(8,128)(2,1)S(1)}, bf16[512,512]{1,0:T(8,128)(2,1)S(1)}, u32[]{:S(2)}, u32[]{:S(2)}) collective-permute-start(bf16[512,512]{1,0:T(8,128)(2,1)S(1)} %pad_maximum_fusion.coef), channel_id=1, source_target_pairs={{0,1},{1,0},{16,17},{17,16},{32,33},{33,32},{48,49},{49,48},{2,3},... | collective-permute-start | bytes 1572872 | tf_op jit(solution)/shard_map/ppermute | solution.py:66
  (1 other events, 0.7 us)

commit v4 on v3

--- a/solution.py
+++ b/solution.py
@@ -17,8 +17,8 @@
 PACK = 144
 VMEM = pltpu.VMEM
 
-SIN_COEF = (3.14159264, -5.16771008, 2.55007752, -0.59829129, 0.07765766)
-COS_COEF = (0.99999995, -4.93479283, 4.05841135, -1.33187657, 0.21968961)
+SIN_COEF = (3.14159027, -5.16740673, 2.54401052, -0.55946246)
+COS_COEF = (0.99999325, -4.93393467, 4.0412481, -1.22203176)
 
 
 def linear(x, y, z, core):
@@ -132,11 +132,10 @@
             angle = jnp.dot(columns, placed[:, lanes], preferred_element_type=F32)
             r = angle - jnp.round(angle)
             s = r * r
-            sine = SIN_COEF[4]
-            cosine = COS_COEF[4]
-            for a in (3, 2, 1, 0):
+            sine = SIN_COEF[3]
+            cosine = COS_COEF[3]
+            for a in (2, 1, 0):
                 sine = sine * s + SIN_COEF[a]
-            for a in (3, 2, 1, 0):
                 cosine = cosine * s + COS_COEF[a]
             sine = sine * r
             double = sine + sine
@@ -312,26 +311,33 @@
     )(cos_table, sin_table, coef, acc)
 
 
-def final_kernel(cos_ref, sin_ref, coef, features, acc, gain, w_in, w_out, out):
-    rows = pl.ds(pl.multiple_of(pl.program_id(0) * 256, 256), 256)
-    recip = jnp.dot(cos_ref[rows, :], coef[:, 0:WIDTH], preferred_element_type=F32)
-    recip += jnp.dot(sin_ref[rows, :], coef[:, WIDTH:], preferred_element_type=F32)
-    mixed = features[rows, :].astype(F32) + acc[rows, :] + recip
-    power = jnp.mean(mixed * mixed, axis=-1, keepdims=True)
-    normed = (mixed * lax.rsqrt(power + epsilon) * gain[...]).astype(BF16)
-    v = jnp.dot(normed, w_in[...], preferred_element_type=F32)
-    hidden = (v / (1.0 + jnp.exp(-v))).astype(BF16)
-    out[...] = (mixed + jnp.dot(hidden, w_out[...], preferred_element_type=F32)).astype(BF16)
+def final_kernel(cos_ref, sin_ref, coef, features, acc, gain, w_in, w_out, out, result, sems):
+    copies = []
+    for block in range(4):
+        rows = pl.ds(block * 256, 256)
+        recip = jnp.dot(cos_ref[rows, :], coef[:, 0:WIDTH], preferred_element_type=F32)
+        recip += jnp.dot(sin_ref[rows, :], coef[:, WIDTH:], preferred_element_type=F32)
+        mixed = features[rows, :].astype(F32) + acc[rows, :] + recip
+        power = jnp.mean(mixed * mixed, axis=-1, keepdims=True)
+        normed = (mixed * lax.rsqrt(power + epsilon) * gain[...]).astype(BF16)
+        v = jnp.dot(normed, w_in[...], preferred_element_type=F32)
+        hidden = (v / (1.0 + jnp.exp(-v))).astype(BF16)
+        result[rows, :] = (mixed + jnp.dot(hidden, w_out[...], preferred_element_type=F32)).astype(BF16)
+        copy = pltpu.make_async_copy(result.at[rows], out.at[rows], sems.at[block])
+        copy.start()
+        copies.append(copy)
+    for copy in copies:
+        copy.wait()
 
 
 def final(cos_table, sin_table, coef, features, acc, gain, w_in, w_out):
     whole = pl.BlockSpec(memory_space=VMEM)
     return pl.pallas_call(
         final_kernel,
-        grid=(4,),
-        out_shape=jax.ShapeDtypeStruct((1024, WIDTH), BF16),
+        out_shape=pltpu.MemorySpace.HBM((1024, WIDTH), BF16),
         in_specs=[whole] * 8,
-        out_specs=pl.BlockSpec((256, WIDTH), lambda i: (i, 0)),
+        out_specs=pl.BlockSpec(memory_space=pl.ANY),
+        scratch_shapes=[VMEM((1024, WIDTH), BF16), pltpu.SemaphoreType.DMA((4,))],
         compiler_params=pltpu.CompilerParams(vmem_limit_bytes=14 * 1024 * 1024),
         cost_estimate=pl.CostEstimate(flops=3_000_000_000, bytes_accessed=8_000_000, transcendentals=0),
         name="mix_and_network",
@@ -377,10 +383,13 @@
     for step, height in ((1, 256), (2, 128), (3, 64)):
         send = (keep[height:].astype(F32) + got[height:].astype(F32)).astype(BF16)
         if step == 2:
-            send, live, mine, filters = barrier((send, live, mine, filters))
+            send, low, high, live, mine, filters = barrier((send, low, high, live, mine, filters))
         elif step == 3:
             send, acc = barrier((send, acc))
         fresh = permute(send, HALVING[step])
+        if step == 2:
+            left = shifted(jnp.concatenate([low[3:4], upper[3:4], lower[3:4], high[3:4]], axis=0), "gy", 1)
+            right = shifted(jnp.concatenate([low[0:1], upper[0:1], lower[0:1], high[0:1]], axis=0), "gy", -1)
         if step == 1:
             place, send = barrier((place, send))
             live, mine, filters = prepare(
@@ -393,30 +402,25 @@
         got = fresh
     total = jnp.concatenate([keep + got.astype(F32), filters], axis=1)
     for step in range(4):
-        total, acc, low, high = barrier((total, acc, low, high))
+        total, acc = barrier((total, acc))
+        if step == 1:
+            total, left, right = barrier((total, left, right))
         fresh = permute(total.astype(BF16), DOUBLING[step])
         if step == 0:
-            left = shifted(jnp.concatenate([low[3:4], upper[3:4], lower[3:4], high[3:4]], axis=0), "gy", 1)
-            right = shifted(jnp.concatenate([low[0:1], upper[0:1], lower[0:1], high[0:1]], axis=0), "gy", -1)
             acc = piece(tuple(((-1, jb), (0, jb)) for jb in range(CY)), (low,), acc)
         elif step == 1:
             acc = piece(tuple(((CX, jb), (0, jb)) for jb in range(CY)), (high,), acc)
+        elif step == 2:
+            acc = piece(tuple(((ja - 1, -1), (0, ja)) for ja in range(CX + 2)), (left,), acc)
+        else:
+            acc = piece(tuple(((ja - 1, CY), (0, ja)) for ja in range(CX + 2)), (right,), acc)
         total = total + fresh.astype(F32)
     scale = total[:, 2 * WIDTH :]
     chunk = jnp.concatenate([total[:, :WIDTH] * scale, total[:, WIDTH : 2 * WIDTH] * scale], axis=1).astype(BF16)
-    flat = (1024, WIDTH)
+    acc = acc.reshape(1024, WIDTH)
     for step, low_at, high_at in ((3, 0, 0), (2, 0, 128), (1, 128, 256), (0, 256, 512)):
         chunk, acc = barrier((chunk, acc))
-        if step == 3:
-            chunk, left = barrier((chunk, left))
-        elif step == 2:
-            chunk, right = barrier((chunk, right))
         fresh = permute(chunk, HALVING[step])
-        if step == 3:
-            acc = piece(tuple(((ja - 1, -1), (0, ja)) for ja in range(CX + 2)), (left,), acc)
-        elif step == 2:
-            acc = piece(tuple(((ja - 1, CY), (0, ja)) for ja in range(CX + 2)), (right,), acc)
-            acc = acc.reshape(flat)
         if high_at:
             acc = recip_piece(low_at, high_at, cos_near, sin_near, chunk, acc)
         if step:

time: 99.4 us -> 89.6 us (0.901)
  waiting for transfers between devices: 29.8 us -> 24.9 us
  starting transfers between devices: 41.1 us -> 38.3 us
  Pallas kernels: 25.4 us -> 23.3 us
    ppermute x4, starting transfers between devices: 19.9 us -> 12.5 us  [shifted(): lax.ppermute(value, axis, [(i, (i + by) % count) for i in range(count)])]
    ppermute x12, starting transfers between devices: 21.2 us -> 25.8 us  [permute(): return lax.ppermute(value, AXES, partner_list(step))]
    ppermute x12, waiting for transfers between devices: 26.3 us -> 22.4 us  [permute(): return lax.ppermute(value, AXES, partner_list(step))]
    pallas_call x1, Pallas kernels: 4.07 us -> 2.45 us  [final(): pl.pallas_call(final_kernel, out_shape=pltpu.MemorySpace.HBM((1024, WIDTH...]
  transfers between devices with their start and end apart: 16 -> 16, of which waited for: 11 -> 12; matrix products, arithmetic and copies ran while one was open for 1% -> 1% of each run, Pallas kernels for 18% -> 19%
where the time goes in v4:
time: 89.6 us; the launch traced here: 89.4 us
  starting transfers between devices  38.3 us (43%)
  waiting for transfers between devices  24.9 us (28%)
  Pallas kernels  23.3 us (26%)
  local copies, waits for them, and re-layouts  1.61 us (2%)
    ppermute x12, starting transfers between devices, permute(): return lax.ppermute(value, AXES, partner_list(step))  25.8 us
    ppermute x12, waiting for transfers between devices, permute(): return lax.ppermute(value, AXES, partner_list(step))  22.4 us
    ppermute x4, starting transfers between devices, shifted(): lax.ppermute(value, axis, [(i, (i + by) % count) for i in range(count)])  12.5 us
    pallas_call x6, Pallas kernels, radial_piece(): pl.pallas_call(functools.partial(radial_kernel, near_cells, fresh), out_s...  11.5 us
    pallas_call x2, Pallas kernels, waves(): pl.pallas_call(functools.partial(wave_kernel, first), out_shape=out_shape...  6.75 us
    ppermute x4, waiting for transfers between devices, shifted(): lax.ppermute(value, axis, [(i, (i + by) % count) for i in range(count)])  2.46 us
    pallas_call x1, Pallas kernels, final(): pl.pallas_call(final_kernel, out_shape=pltpu.MemorySpace.HBM((1024, WIDTH...  2.45 us
  transfers between devices with their start and end apart: 16, of which 12 were waited for; matrix products, arithmetic and copies ran while one was open for 1% of the time, Pallas kernels for 19%

profile of v4, /device:TPU:1, one launch (start us, length us, event | category | flops | bytes accessed | tf_op | source)
XLA Modules:
  0.0 89.4 jit_solution(867893755483070658)
XLA Ops:
  0.2 0.7 copy-done.5
  0.9 0.7 copy-done.6
  1.6 3.5 %wave_tables.2 = (bf16[1024,512]{1,0:T(8,128)(2,1)}, bf16[1024,512]{1,0:T(8,128)(2,1)}, bf16[512,512]{1,0:T(8,128)(2,1)S(1)}, bf16[256,1024]{1,0:T(8,128)(2,1)S(...) custom-call(s32[2]{0:T(128)S(1)} %pad_add_fusion.place, bf16[2,3,4,128]{3,2,1,0:T(4,128)(2,1)S(1)} %bitcast.11, ...), custom_call_target="tpu_custom_call" | custom-call | flops 2000000000 | bytes 3000000 | tf_op jit(solution)/shard_map/wave_tables/pallas_call | solution.py:179
  5.0 3.3 %collective-permute-start = (bf16[512,512]{1,0:T(8,128)(2,1)S(1)}, bf16[512,512]{1,0:T(8,128)(2,1)S(1)}, u32[]{:S(2)}, u32[]{:S(2)}) collective-permute-start(bf16[512,512]{1,0:T(8,128)(2,1)S(1)} %get-tuple-element.49), channel_id=1, source_target_pairs={{0,1},{1,0},{16,17},{17,16},{32,33},{33,32},{48,49},{49,48},{2,3},... | collective-permute-start | bytes 1572872 | tf_op jit(solution)/shard_map/ppermute | solution.py:66
  8.4 5.4 %collective-permute-start.3 = (bf16[4,144,256]{2,1,0:T(8,128)(2,1)S(1)}, bf16[4,144,256]{2,1,0:T(8,128)(2,1)S(1)}, u32[]{:S(2)}, u32[]{:S(2)}) collective-permute-start(bf16[4,144,256]{2,1,0:T(8,128)(2,1)S(1)} %get-tuple-element.51.rest_0_), channel_id=1, source_target_pairs={{0,240},{16,0},{32,16},{48,32},{64,48},{80,64},{96,80},{112,96},{1... | collective-permute-start | bytes 884744 | tf_op jit(solution)/shard_map/ppermute | solution.py:349
  13.8 3.3 %wave_tables.3 = (bf16[1024,512]{1,0:T(8,128)(2,1)}, bf16[1024,512]{1,0:T(8,128)(2,1)}, f32[512,512]{1,0:T(8,128)S(1)}) custom-call(s32[2]{0:T(128)S(1)} %pad_add_fusion.place, bf16[2,3,4,128]{3,2,1,0:T(4,128)(2,1)S(1)} %bitcast.12, s32[3,1024]{1,0:T(4,128)S(1)} %copy-done.5, s32[1,512]{1,0:T(1,128)S(1)} %get-tuple-element.99.order, ...), custom_call_target="tpu_custom_call" | custom-call | flops 2000000000 | bytes 3000000 | tf_op jit(solution)/shard_map/wave_tables/pallas_call | solution.py:179
  17.3 0.8 collective-permute-start.1
  18.2 1.3 %radial_prepare.1 = (f32[8,9]{1,0:T(8,128)S(1)}, f32[8,3,128,128]{3,2,1,0:T(8,128)S(1)}, f32[64,256]{1,0:T(8,128)S(1)}) custom-call(s32[2]{0:T(128)S(1)} %pad_add_fusion.place, s32[8]{0:T(128)S(1)} %reshape.717.near_count, s32[8,9]{1,0:T(8,128)S(1)} %bitcast.14, bf16[2,3,4,128]{3,2,1,0:T(4,128)(2,1)S(1)} %bitcast.13, bf16[4,256]{1,0:T(4,128)(2,1)S(1)} %copy-done.10), custom_call_target="tpu_custom_call" | custom-call | flops 500000000 | bytes 100000 | tf_op jit(solution)/shard_map/radial_prepare/pallas_call | solution.py:221
  19.5 3.4 %collective-permute-done.1 = bf16[256,512]{1,0:T(8,128)(2,1)S(1)} collective-permute-done((bf16[256,512]{1,0:T(8,128)(2,1)S(1)}, bf16[256,512]{1,0:T(8,128)(2,1)S(1)}, u32[]{:S(2)}, u32[]{:S(2)}) %collective-permute-start.1) | collective-permute-done | bytes 262176 | tf_op jit(solution)/shard_map/ppermute | solution.py:66
  23.2 2.7 %collective-permute-start.4 = (bf16[128,512]{1,0:T(8,128)(2,1)S(1)}, bf16[128,512]{1,0:T(8,128)(2,1)S(1)}, u32[]{:S(2)}, u32[]{:S(2)}) collective-permute-start(bf16[128,512]{1,0:T(8,128)(2,1)S(1)} %get-tuple-element.56), channel_id=1, source_target_pairs={{0,192},{1,13},{16,208},{17,29},{32,224},{33,45},{48,240},{49,61},... | collective-permute-start | bytes 393224 | tf_op jit(solution)/shard_map/ppermute | solution.py:66
  26.0 6.8 %collective-permute-start.7 = (bf16[4,144,256]{2,1,0:T(8,128)(2,1)S(1)}, bf16[4,144,256]{2,1,0:T(8,128)(2,1)S(1)}, u32[]{:S(2)}, u32[]{:S(2)}) collective-permute-start(bf16[4,144,256]{2,1,0:T(8,128)(2,1)S(1)} %pad_maximum_fusion.1), channel_id=1, source_target_pairs={{0,1},{1,2},{2,3},{3,4},{4,5},{5,6},{6,7},{7,8},{8,9},{9,10},{10,1... | collective-permute-start | bytes 884744 | tf_op jit(solution)/shard_map/ppermute | solution.py:349
  33.2 2.5 %radial_piece.6.rest_2_ = f32[8,128,256]{2,1,0:T(8,128)S(1)} custom-call(f32[8]{0:T(128)S(1)} %copy-done.12, f32[8,9]{1,0:T(8,128)S(1)} %get-tuple-element.57.live, bf16[8,256]{1,0:T(8,128)(2,1)S(1)} %copy-done.9, f32[8,3,128,128]{3,2,1,0:T(8,128)S(1)} %get-tuple-element.58.mine, bf16[4,144,256]{2,1,0:T(8,128)(2,1)S(1)} %get-tuple-element.51.rest_0_, ...), custom_call_target="tpu_custom_call" | custom-call | flops 2000000000 | bytes 2000000 | tf_op jit(solution)/shard_map/radial_piece/pallas_call | solution.py:276
  35.7 2.6 %radial_piece.7.rest_1_ = f32[8,128,256]{2,1,0:T(8,128)S(1)} custom-call(f32[8]{0:T(128)S(1)} %copy-done.12, f32[8,9]{1,0:T(8,128)S(1)} %get-tuple-element.57.live, bf16[8,256]{1,0:T(8,128)(2,1)S(1)} %copy-done.9, f32[8,3,128,128]{3,2,1,0:T(8,128)S(1)} %get-tuple-element.58.mine, ...), custom_call_target="tpu_custom_call", output_to_operand_aliasing={{}: (6, {})} | custom-call | flops 2000000000 | bytes 2000000 | tf_op jit(solution)/shard_map/radial_piece/pallas_call | solution.py:276
  39.5 1.8 %radial_piece.8.rest_1_ = f32[8,128,256]{2,1,0:T(8,128)S(1)} custom-call(f32[8]{0:T(128)S(1)} %copy-done.12, f32[8,9]{1,0:T(8,128)S(1)} %get-tuple-element.57.live, bf16[8,256]{1,0:T(8,128)(2,1)S(1)} %copy-done.9, f32[8,3,128,128]{3,2,1,0:T(8,128)S(1)} %get-tuple-element.58.mine, ...), custom_call_target="tpu_custom_call", output_to_operand_aliasing={{}: (5, {})} | custom-call | flops 2000000000 | bytes 2000000 | tf_op jit(solution)/shard_map/radial_piece/pallas_call | solution.py:276
  41.4 2.4 %collective-permute-done.6 = bf16[64,768]{1,0:T(8,128)(2,1)S(1)} collective-permute-done((bf16[64,768]{1,0:T(8,128)(2,1)S(1)}, bf16[64,768]{1,0:T(8,128)(2,1)S(1)}, u32[]{:S(2)}, u32[]{:S(2)}) %collective-permute-start.6) | collective-permute-done | bytes 98336 | tf_op jit(solution)/shard_map/ppermute | solution.py:66
  43.7 2.2 %collective-permute-done.8.rest_0_ = bf16[4,144,256]{2,1,0:T(8,128)(2,1)S(1)} collective-permute-done((bf16[4,144,256]{2,1,0:T(8,128)(2,1)S(1)}, bf16[4,144,256]{2,1,0:T(8,128)(2,1)S(1)}, u32[]{:S(2)}, u32[]{:S(2)}) %collective-permute-start.8) | collective-permute-done | bytes 294944 | tf_op jit(solution)/shard_map/ppermute | solution.py:349
  46.3 1.8 %radial_piece.9.rest_1_ = f32[8,128,256]{2,1,0:T(8,128)S(1)} custom-call(f32[8]{0:T(128)S(1)} %copy-done.12, f32[8,9]{1,0:T(8,128)S(1)} %get-tuple-element.57.live, bf16[8,256]{1,0:T(8,128)(2,1)S(1)} %copy-done.9, f32[8,3,128,128]{3,2,1,0:T(8,128)S(1)} %get-tuple-element.58.mine, ...), custom_call_target="tpu_custom_call", output_to_operand_aliasing={{}: (5, {})} | custom-call | flops 2000000000 | bytes 2000000 | tf_op jit(solution)/shard_map/radial_piece/pallas_call | solution.py:276
  48.1 1.5 %collective-permute-done.9 = bf16[64,768]{1,0:T(8,128)(2,1)S(1)} collective-permute-done((bf16[64,768]{1,0:T(8,128)(2,1)S(1)}, bf16[64,768]{1,0:T(8,128)(2,1)S(1)}, u32[]{:S(2)}, u32[]{:S(2)}) %collective-permute-start.9) | collective-permute-done | bytes 98336 | tf_op jit(solution)/shard_map/ppermute | solution.py:66
  49.6 6.7 %collective-permute-start.10 = (bf16[64,768]{1,0:T(8,128)(2,1)S(1)}, bf16[64,768]{1,0:T(8,128)(2,1)S(1)}, u32[]{:S(2)}, u32[]{:S(2)}) collective-permute-start(bf16[64,768]{1,0:T(8,128)(2,1)S(1)} %convert_element_type.69), channel_id=1, source_target_pairs={{0,50},{1,51},{16,32},{17,33},{32,16},{33,17},{48,2},{49,3},{2,48}... | collective-permute-start | bytes 294920 | tf_op jit(solution)/shard_map/ppermute | solution.py:66
  56.3 1.4 %radial_piece.10.rest_1_ = f32[8,128,256]{2,1,0:T(8,128)S(1)} custom-call(f32[8]{0:T(128)S(1)} %copy-done.12, f32[8,9]{1,0:T(8,128)S(1)} %get-tuple-element.57.live, bf16[8,256]{1,0:T(8,128)(2,1)S(1)} %copy-done.9, f32[8,3,128,128]{3,2,1,0:T(8,128)S(1)} %get-tuple-element.58.mine, ...), custom_call_target="tpu_custom_call", output_to_operand_aliasing={{}: (5, {})} | custom-call | flops 2000000000 | bytes 2000000 | tf_op jit(solution)/shard_map/radial_piece/pallas_call | solution.py:276
  57.7 1.1 %collective-permute-done.10 = bf16[64,768]{1,0:T(8,128)(2,1)S(1)} collective-permute-done((bf16[64,768]{1,0:T(8,128)(2,1)S(1)}, bf16[64,768]{1,0:T(8,128)(2,1)S(1)}, u32[]{:S(2)}, u32[]{:S(2)}) %collective-permute-start.10) | collective-permute-done | bytes 98336 | tf_op jit(solution)/shard_map/ppermute | solution.py:66
  58.9 0.6 collective-permute-start.11
  59.4 1.4 %radial_piece.11 = f32[8,128,256]{2,1,0:T(8,128)S(1)} custom-call(f32[8]{0:T(128)S(1)} %copy-done.12, f32[8,9]{1,0:T(8,128)S(1)} %get-tuple-element.57.live, bf16[8,256]{1,0:T(8,128)(2,1)S(1)} %copy-done.9, f32[8,3,128,128]{3,2,1,0:T(8,128)S(1)} %get-tuple-element.58.mine, ...), custom_call_target="tpu_custom_call", output_to_operand_aliasing={{}: (5, {})} | custom-call | flops 2000000000 | bytes 2000000 | tf_op jit(solution)/shard_map/radial_piece/pallas_call | solution.py:276
  60.8 3.5 %collective-permute-done.11 = bf16[64,768]{1,0:T(8,128)(2,1)S(1)} collective-permute-done((bf16[64,768]{1,0:T(8,128)(2,1)S(1)}, bf16[64,768]{1,0:T(8,128)(2,1)S(1)}, u32[]{:S(2)}, u32[]{:S(2)}) %collective-permute-start.11) | collective-permute-done | bytes 98336 | tf_op jit(solution)/shard_map/ppermute | solution.py:66
  64.5 3.1 %collective-permute-done.12 = bf16[64,512]{1,0:T(8,128)(2,1)S(1)} collective-permute-done((bf16[64,512]{1,0:T(8,128)(2,1)S(1)}, bf16[64,512]{1,0:T(8,128)(2,1)S(1)}, u32[]{:S(2)}, u32[]{:S(2)}) %collective-permute-start.12) | collective-permute-done | bytes 65568 | tf_op jit(solution)/shard_map/ppermute | solution.py:66
  67.6 2.3 %collective-permute-start.13 = (bf16[128,512]{1,0:T(8,128)(2,1)S(1)}, bf16[128,512]{1,0:T(8,128)(2,1)S(1)}, u32[]{:S(2)}, u32[]{:S(2)}) collective-permute-start(bf16[128,512]{1,0:T(8,128)(2,1)S(1)} %pad_maximum_fusion.5.coef), channel_id=1, source_target_pairs={{0,192},{1,13},{16,208},{17,29},{32,224},{33,45},{48,240},{49,61},... | collective-permute-start | bytes 393224 | tf_op jit(solution)/shard_map/ppermute | solution.py:66
  70.4 2.5 %collective-permute-done.13 = bf16[128,512]{1,0:T(8,128)(2,1)S(1)} collective-permute-done((bf16[128,512]{1,0:T(8,128)(2,1)S(1)}, bf16[128,512]{1,0:T(8,128)(2,1)S(1)}, u32[]{:S(2)}, u32[]{:S(2)}) %collective-permute-start.13) | collective-permute-done | bytes 131104 | tf_op jit(solution)/shard_map/ppermute | solution.py:66
  73.0 3.0 %collective-permute-start.14 = (bf16[256,512]{1,0:T(8,128)(2,1)S(1)}, bf16[256,512]{1,0:T(8,128)(2,1)S(1)}, u32[]{:S(2)}, u32[]{:S(2)}) collective-permute-start(bf16[256,512]{1,0:T(8,128)(2,1)S(1)} %pad_maximum_fusion.3.coef), channel_id=1, source_target_pairs={{0,64},{1,5},{16,80},{17,21},{32,96},{33,37},{48,112},{49,53},{2,6... | collective-permute-start | bytes 786440 | tf_op jit(solution)/shard_map/ppermute | solution.py:66
  76.4 3.3 %collective-permute-done.14 = bf16[256,512]{1,0:T(8,128)(2,1)S(1)} collective-permute-done((bf16[256,512]{1,0:T(8,128)(2,1)S(1)}, bf16[256,512]{1,0:T(8,128)(2,1)S(1)}, u32[]{:S(2)}, u32[]{:S(2)}) %collective-permute-start.14) | collective-permute-done | bytes 262176 | tf_op jit(solution)/shard_map/ppermute | solution.py:66
  79.8 5.4 %collective-permute-start.15 = (bf16[512,512]{1,0:T(8,128)(2,1)S(1)}, bf16[512,512]{1,0:T(8,128)(2,1)S(1)}, u32[]{:S(2)}, u32[]{:S(2)}) collective-permute-start(bf16[512,512]{1,0:T(8,128)(2,1)S(1)} %pad_maximum_fusion.coef), channel_id=1, source_target_pairs={{0,1},{1,0},{16,17},{17,16},{32,33},{33,32},{48,49},{49,48},{2,3},... | collective-permute-start | bytes 1572872 | tf_op jit(solution)/shard_map/ppermute | solution.py:66
  85.6 1.1 %collective-permute-done.15.coef = bf16[512,512]{1,0:T(8,128)(2,1)S(1)} collective-permute-done((bf16[512,512]{1,0:T(8,128)(2,1)S(1)}, bf16[512,512]{1,0:T(8,128)(2,1)S(1)}, u32[]{:S(2)}, u32[]{:S(2)}) %collective-permute-start.15) | collective-permute-done | bytes 524320 | tf_op jit(solution)/shard_map/ppermute | solution.py:66
  86.7 2.5 %mix_and_network.1 = bf16[1024,256]{1,0:T(8,128)(2,1)} custom-call(bf16[1024,512]{1,0:T(8,128)(2,1)S(1)} %copy-done.13, bf16[1024,512]{1,0:T(8,128)(2,1)S(1)} %copy-done.14, bf16[512,512]{1,0:T(8,128)(2,1)S(1)} %collective-permute-done.15.coef, bf16[1024,256]{1,0:T(8,128)(2,1)S(1)} %bitcast.10, f32[1024,256]{1,0:T(8,128)S(1)} %recip_piece.5.acc, ...), custom_call_target="tpu_custom_call" | custom-call | flops 3000000000 | bytes 8000000 | tf_op jit(solution)/shard_map/mix_and_network/pallas_call | solution.py:335
  (71 shorter events, 4.3 us)
Async XLA Ops:
  0.2 0.7 copy-start.5
  0.9 0.7 copy-start.6
  5.0 12.1 %collective-permute-start = (bf16[512,512]{1,0:T(8,128)(2,1)S(1)}, bf16[512,512]{1,0:T(8,128)(2,1)S(1)}, u32[]{:S(2)}, u32[]{:S(2)}) collective-permute-start(bf16[512,512]{1,0:T(8,128)(2,1)S(1)} %get-tuple-element.49), channel_id=1, source_target_pairs={{0,1},{1,0},{16,17},{17,16},{32,33},{33,32},{48,49},{49,48},{2,3},... | collective-permute-start | bytes 1572872 | tf_op jit(solution)/shard_map/ppermute | solution.py:66
  8.4 14.6 %collective-permute-start.2 = (bf16[4,144,256]{2,1,0:T(8,128)(2,1)S(1)}, bf16[4,144,256]{2,1,0:T(8,128)(2,1)S(1)}, u32[]{:S(2)}, u32[]{:S(2)}) collective-permute-start(bf16[4,144,256]{2,1,0:T(8,128)(2,1)S(1)} %get-tuple-element.50.rest_1_), channel_id=1, source_target_pairs={{0,16},{16,32},{32,48},{48,64},{64,80},{80,96},{96,112},{112,128},... | collective-permute-start | bytes 884744 | tf_op jit(solution)/shard_map/ppermute | solution.py:349
  8.4 14.8 %collective-permute-start.3 = (bf16[4,144,256]{2,1,0:T(8,128)(2,1)S(1)}, bf16[4,144,256]{2,1,0:T(8,128)(2,1)S(1)}, u32[]{:S(2)}, u32[]{:S(2)}) collective-permute-start(bf16[4,144,256]{2,1,0:T(8,128)(2,1)S(1)} %get-tuple-element.51.rest_0_), channel_id=1, source_target_pairs={{0,240},{16,0},{32,16},{48,32},{64,48},{80,64},{96,80},{112,96},{1... | collective-permute-start | bytes 884744 | tf_op jit(solution)/shard_map/ppermute | solution.py:349
  17.1 1.1 %copy-start.15 = (s32[2,4]{1,0:T(2,128)S(1)}, s32[2,4]{1,0:T(2,128)}, u32[]{:S(2)}) copy-start(s32[2,4]{1,0:T(2,128)} %param.14) | copy-start | bytes 100
  17.1 1.2 %copy-start.7 = (bf16[2,4,3,128]{3,1,2,0:T(4,128)(2,1)S(1)}, bf16[2,4,3,128]{3,1,2,0:T(4,128)(2,1)}, u32[]{:S(2)}) copy-start(bf16[2,4,3,128]{3,1,2,0:T(4,128)(2,1)} %param.12) | copy-start | bytes 18436
  17.1 1.1 %copy-start.8 = (s32[2,4,9]{2,1,0:T(4,128)S(1)}, s32[2,4,9]{2,1,0:T(4,128)}, u32[]{:S(2)}) copy-start(s32[2,4,9]{2,1,0:T(4,128)} %param.13) | copy-start | bytes 868
  17.1 1.1 %copy-start.10 = (bf16[4,256]{1,0:T(4,128)(2,1)S(1)}, bf16[4,256]{1,0:T(4,128)(2,1)}, u32[]{:S(2)}) copy-start(bf16[4,256]{1,0:T(4,128)(2,1)} %row_filter.1) | copy-start | bytes 6148
  17.3 5.6 %collective-permute-start.1 = (bf16[256,512]{1,0:T(8,128)(2,1)S(1)}, bf16[256,512]{1,0:T(8,128)(2,1)S(1)}, u32[]{:S(2)}, u32[]{:S(2)}) collective-permute-start(bf16[256,512]{1,0:T(8,128)(2,1)S(1)} %get-tuple-element.85), channel_id=1, source_target_pairs={{0,64},{1,5},{16,80},{17,21},{32,96},{33,37},{48,112},{49,53},{2,6... | collective-permute-start | bytes 786440 | tf_op jit(solution)/shard_map/ppermute | solution.py:66
  19.5 13.6 %copy-start.9 = (bf16[8,256]{1,0:T(8,128)(2,1)S(1)}, bf16[8,256]{1,0:T(8,128)(2,1)}, u32[]{:S(2)}) copy-start(bf16[8,256]{1,0:T(8,128)(2,1)} %filters.11) | copy-start | bytes 12292
  19.5 13.6 %copy-start.12 = (f32[8]{0:T(128)S(1)}, f32[8]{0:T(128)}, u32[]{:S(2)}) copy-start(f32[8]{0:T(128)} %rates.11) | copy-start | bytes 100
  23.2 12.4 %collective-permute-start.4 = (bf16[128,512]{1,0:T(8,128)(2,1)S(1)}, bf16[128,512]{1,0:T(8,128)(2,1)S(1)}, u32[]{:S(2)}, u32[]{:S(2)}) collective-permute-start(bf16[128,512]{1,0:T(8,128)(2,1)S(1)} %get-tuple-element.56), channel_id=1, source_target_pairs={{0,192},{1,13},{16,208},{17,29},{32,224},{33,45},{48,240},{49,61},... | collective-permute-start | bytes 393224 | tf_op jit(solution)/shard_map/ppermute | solution.py:66
  26.0 17.7 %collective-permute-start.7 = (bf16[4,144,256]{2,1,0:T(8,128)(2,1)S(1)}, bf16[4,144,256]{2,1,0:T(8,128)(2,1)S(1)}, u32[]{:S(2)}, u32[]{:S(2)}) collective-permute-start(bf16[4,144,256]{2,1,0:T(8,128)(2,1)S(1)} %pad_maximum_fusion.1), channel_id=1, source_target_pairs={{0,1},{1,2},{2,3},{3,4},{4,5},{5,6},{6,7},{7,8},{8,9},{9,10},{10,1... | collective-permute-start | bytes 884744 | tf_op jit(solution)/shard_map/ppermute | solution.py:349
  32.9 13.1 %collective-permute-start.8 = (bf16[4,144,256]{2,1,0:T(8,128)(2,1)S(1)}, bf16[4,144,256]{2,1,0:T(8,128)(2,1)S(1)}, u32[]{:S(2)}, u32[]{:S(2)}) collective-permute-start(bf16[4,144,256]{2,1,0:T(8,128)(2,1)S(1)} %pad_maximum_fusion.2), channel_id=1, source_target_pairs={{0,15},{1,0},{2,1},{3,2},{4,3},{5,4},{6,5},{7,6},{8,7},{9,8},{10,9... | collective-permute-start | bytes 884744 | tf_op jit(solution)/shard_map/ppermute | solution.py:349
  35.6 3.2 %collective-permute-start.5 = (bf16[64,512]{1,0:T(8,128)(2,1)S(1)}, bf16[64,512]{1,0:T(8,128)(2,1)S(1)}, u32[]{:S(2)}, u32[]{:S(2)}) collective-permute-start(bf16[64,512]{1,0:T(8,128)(2,1)S(1)} %fusion.1), channel_id=1, source_target_pairs={{0,4},{1,65},{16,20},{17,81},{32,36},{33,97},{48,52},{49,113},{2,6... | collective-permute-start | bytes 196616 | tf_op jit(solution)/shard_map/ppermute | solution.py:66
  38.9 4.8 %collective-permute-start.6 = (bf16[64,768]{1,0:T(8,128)(2,1)S(1)}, bf16[64,768]{1,0:T(8,128)(2,1)S(1)}, u32[]{:S(2)}, u32[]{:S(2)}) collective-permute-start(bf16[64,768]{1,0:T(8,128)(2,1)S(1)} %convert_element_type.65), channel_id=1, source_target_pairs={{0,12},{1,193},{16,28},{17,209},{32,44},{33,225},{48,60},{49,241},... | collective-permute-start | bytes 294920 | tf_op jit(solution)/shard_map/ppermute | solution.py:66
  46.0 3.6 %collective-permute-start.9 = (bf16[64,768]{1,0:T(8,128)(2,1)S(1)}, bf16[64,768]{1,0:T(8,128)(2,1)S(1)}, u32[]{:S(2)}, u32[]{:S(2)}) collective-permute-start(bf16[64,768]{1,0:T(8,128)(2,1)S(1)} %convert_element_type.67), channel_id=1, source_target_pairs={{0,16},{1,17},{16,0},{17,1},{32,48},{33,49},{48,32},{49,33},{2,18}... | collective-permute-start | bytes 294920 | tf_op jit(solution)/shard_map/ppermute | solution.py:66
  49.6 9.2 %collective-permute-start.10 = (bf16[64,768]{1,0:T(8,128)(2,1)S(1)}, bf16[64,768]{1,0:T(8,128)(2,1)S(1)}, u32[]{:S(2)}, u32[]{:S(2)}) collective-permute-start(bf16[64,768]{1,0:T(8,128)(2,1)S(1)} %convert_element_type.69), channel_id=1, source_target_pairs={{0,50},{1,51},{16,32},{17,33},{32,16},{33,17},{48,2},{49,3},{2,48}... | collective-permute-start | bytes 294920 | tf_op jit(solution)/shard_map/ppermute | solution.py:66
  58.9 5.5 %collective-permute-start.11 = (bf16[64,768]{1,0:T(8,128)(2,1)S(1)}, bf16[64,768]{1,0:T(8,128)(2,1)S(1)}, u32[]{:S(2)}, u32[]{:S(2)}) collective-permute-start(bf16[64,768]{1,0:T(8,128)(2,1)S(1)} %convert_element_type.71), channel_id=1, source_target_pairs={{0,48},{1,49},{16,34},{17,35},{32,18},{33,19},{48,0},{49,1},{2,50}... | collective-permute-start | bytes 294920 | tf_op jit(solution)/shard_map/ppermute | solution.py:66
  59.4 10.5 %copy-start.1 = (bf16[1024,512]{1,0:T(8,128)(2,1)S(1)}, bf16[1024,512]{1,0:T(8,128)(2,1)}, u32[]{:S(2)}) copy-start(bf16[1024,512]{1,0:T(8,128)(2,1)} %get-tuple-element.79.sin_ref) | copy-start | bytes 3145732
  60.8 9.1 %copy-start = (bf16[1024,512]{1,0:T(8,128)(2,1)S(1)}, bf16[1024,512]{1,0:T(8,128)(2,1)}, u32[]{:S(2)}) copy-start(bf16[1024,512]{1,0:T(8,128)(2,1)} %get-tuple-element.78.cos_ref) | copy-start | bytes 3145732
  64.4 3.2 %collective-permute-start.12 = (bf16[64,512]{1,0:T(8,128)(2,1)S(1)}, bf16[64,512]{1,0:T(8,128)(2,1)S(1)}, u32[]{:S(2)}, u32[]{:S(2)}) collective-permute-start(bf16[64,512]{1,0:T(8,128)(2,1)S(1)} %pad_maximum_fusion.6), channel_id=1, source_target_pairs={{0,4},{1,65},{16,20},{17,81},{32,36},{33,97},{48,52},{49,113},{2,6... | collective-permute-start | bytes 196616 | tf_op jit(solution)/shard_map/ppermute | solution.py:66
  67.6 5.3 %collective-permute-start.13 = (bf16[128,512]{1,0:T(8,128)(2,1)S(1)}, bf16[128,512]{1,0:T(8,128)(2,1)S(1)}, u32[]{:S(2)}, u32[]{:S(2)}) collective-permute-start(bf16[128,512]{1,0:T(8,128)(2,1)S(1)} %pad_maximum_fusion.5.coef), channel_id=1, source_target_pairs={{0,192},{1,13},{16,208},{17,29},{32,224},{33,45},{48,240},{49,61},... | collective-permute-start | bytes 393224 | tf_op jit(solution)/shard_map/ppermute | solution.py:66
  73.0 6.7 %collective-permute-start.14 = (bf16[256,512]{1,0:T(8,128)(2,1)S(1)}, bf16[256,512]{1,0:T(8,128)(2,1)S(1)}, u32[]{:S(2)}, u32[]{:S(2)}) collective-permute-start(bf16[256,512]{1,0:T(8,128)(2,1)S(1)} %pad_maximum_fusion.3.coef), channel_id=1, source_target_pairs={{0,64},{1,5},{16,80},{17,21},{32,96},{33,37},{48,112},{49,53},{2,6... | collective-permute-start | bytes 786440 | tf_op jit(solution)/shard_map/ppermute | solution.py:66
  79.7 7.0 %copy-start.2 = (bf16[2,4,128,256]{3,2,1,0:T(8,128)(2,1)S(1)}, bf16[2,4,128,256]{3,2,1,0:T(8,128)(2,1)}, u32[]{:S(2)}) copy-start(bf16[2,4,128,256]{3,2,1,0:T(8,128)(2,1)} %param.11) | copy-start | bytes 1572868
  79.8 7.0 %copy-start.3 = (bf16[256,512]{1,0:T(8,128)(2,1)S(1)}, bf16[256,512]{1,0:T(8,128)(2,1)}, u32[]{:S(2)}) copy-start(bf16[256,512]{1,0:T(8,128)(2,1)} %w_in.1) | copy-start | bytes 786436
  79.8 6.9 %copy-start.4 = (bf16[512,256]{1,0:T(8,128)(2,1)S(1)}, bf16[512,256]{1,0:T(8,128)(2,1)}, u32[]{:S(2)}) copy-start(bf16[512,256]{1,0:T(8,128)(2,1)} %w_out.1) | copy-start | bytes 786436
  79.8 6.9 %copy-start.11 = (f32[256]{0:T(256)S(1)}, f32[256]{0:T(256)}, u32[]{:S(2)}) copy-start(f32[256]{0:T(256)} %param.19) | copy-start | bytes 3076
  79.8 6.9 %copy-start.13 = (bf16[1024,512]{1,0:T(8,128)(2,1)S(1)}, bf16[1024,512]{1,0:T(8,128)(2,1)}, u32[]{:S(2)}) copy-start(bf16[1024,512]{1,0:T(8,128)(2,1)} %get-tuple-element.45.cos_ref) | copy-start | bytes 3145732
  79.8 6.9 %copy-start.14 = (bf16[1024,512]{1,0:T(8,128)(2,1)S(1)}, bf16[1024,512]{1,0:T(8,128)(2,1)}, u32[]{:S(2)}) copy-start(bf16[1024,512]{1,0:T(8,128)(2,1)} %get-tuple-element.46.sin_ref) | copy-start | bytes 3145732
  79.8 6.9 %collective-permute-start.15 = (bf16[512,512]{1,0:T(8,128)(2,1)S(1)}, bf16[512,512]{1,0:T(8,128)(2,1)S(1)}, u32[]{:S(2)}, u32[]{:S(2)}) collective-permute-start(bf16[512,512]{1,0:T(8,128)(2,1)S(1)} %pad_maximum_fusion.coef), channel_id=1, source_target_pairs={{0,1},{1,0},{16,17},{17,16},{32,33},{33,32},{48,49},{49,48},{2,3},... | collective-permute-start | bytes 1572872 | tf_op jit(solution)/shard_map/ppermute | solution.py:66

commit v5 on v4

--- a/solution.py
+++ b/solution.py
@@ -52,7 +52,7 @@
     table = ((1, 0, 3, 2, 5, 4, 7, 6), (7, 2, 1, 4, 3, 6, 5, 0), (3, 6, 5, 0, 7, 2, 1, 4))[which]
 
     def step(x, y, z, core):
-        return x, y, table[z], core
+        return x, y, table[z] if core == 0 else (table[(z - 1) % 8] + 1) % 8, core
 
     return step
 
@@ -97,13 +97,23 @@
     cos_ref, sin_ref, sems = rest[-3:]
     if first:
         turned, packed, features = rest[0], rest[1:3], rest[3]
+        coords_in, miller_in = coords, miller
+        coords, miller = rest[4:6]
+        fetch = [
+            pltpu.make_async_copy(coords_in, coords, sems.at[2, 1]),
+            pltpu.make_async_copy(miller_in, miller, sems.at[2, 2]),
+        ]
         load = pltpu.make_async_copy(source, features, sems.at[2, 0])
-        load.start()
+        for copy in fetch + [load]:
+            copy.start()
+        for copy in fetch:
+            copy.wait()
     else:
         turned = source
     number = miller[...].astype(F32)
     five = jnp.concatenate([number, number[0:2], jnp.zeros((3, 1024), F32)], axis=0).astype(BF16)
-    natural = lax.broadcasted_iota(jnp.int32, (1024, HALF), 0)
+    size = order.shape[1]
+    natural = lax.broadcasted_iota(jnp.int32, (1024, size), 0)
     pick = jnp.where(natural == order[...], 1.0, 0.0).astype(BF16)
     placed = jnp.dot(five, pick, preferred_element_type=F32).astype(BF16)
     ones = jnp.ones((1, ATOMS), F32)
@@ -127,7 +137,7 @@
         )
         columns = rows.T.astype(BF16)
         rows_at = pl.ds(cell * ATOMS, ATOMS)
-        for j in range(HALF // 256):
+        for j in range(size // 256):
             lanes = slice(j * 256, (j + 1) * 256)
             angle = jnp.dot(columns, placed[:, lanes], preferred_element_type=F32)
             r = angle - jnp.round(angle)
@@ -165,25 +175,29 @@
 def waves(place, coords, miller, order, source, first):
     vm = pl.BlockSpec(memory_space=VMEM)
     hbm = pl.BlockSpec(memory_space=pl.ANY)
+    place_of = hbm if first else vm
+    size = order.shape[1]
     out_shape = [
-        pltpu.MemorySpace.HBM((1024, HALF), BF16),
-        pltpu.MemorySpace.HBM((1024, HALF), BF16),
-        jax.ShapeDtypeStruct((HALF, 2 * WIDTH), BF16 if first else F32),
+        pltpu.MemorySpace.HBM((1024, size), BF16),
+        pltpu.MemorySpace.HBM((1024, size), BF16),
+        jax.ShapeDtypeStruct((size, 2 * WIDTH), BF16 if first else F32),
     ]
-    scratch = [VMEM((1024, HALF), BF16), VMEM((1024, HALF), BF16), pltpu.SemaphoreType.DMA((3, CX * CY))]
+    scratch = [VMEM((1024, size), BF16), VMEM((1024, size), BF16), pltpu.SemaphoreType.DMA((3, CX * CY))]
     if first:
-        source = pltpu.with_memory_space_constraint(source, pltpu.MemorySpace.HBM)
+        source, coords, miller = (
+            pltpu.with_memory_space_constraint(value, pltpu.MemorySpace.HBM) for value in (source, coords, miller)
+        )
         out_shape.append(jax.ShapeDtypeStruct((WIDTH, 1024), BF16))
         out_shape += [jax.ShapeDtypeStruct((CY, PACK, WIDTH), BF16)] * CX
-        scratch.insert(0, VMEM((1024, WIDTH), BF16))
+        scratch = [VMEM((1024, WIDTH), BF16), VMEM(coords.shape, BF16), VMEM(miller.shape, jnp.int32)] + scratch
     return pl.pallas_call(
         functools.partial(wave_kernel, first),
         out_shape=out_shape,
-        in_specs=[pl.BlockSpec(memory_space=pltpu.SMEM), vm, vm, vm, hbm if first else vm],
+        in_specs=[pl.BlockSpec(memory_space=pltpu.SMEM), place_of, place_of, vm, place_of],
         out_specs=[hbm, hbm] + [vm] * (len(out_shape) - 2),
         scratch_shapes=scratch,
         compiler_params=pltpu.CompilerParams(vmem_limit_bytes=14 * 1024 * 1024),
-        cost_estimate=pl.CostEstimate(flops=2_000_000_000, bytes_accessed=3_000_000, transcendentals=0),
+        cost_estimate=pl.CostEstimate(flops=size * 4_000_000, bytes_accessed=3_000_000, transcendentals=0),
         name="wave_tables",
     )(place, coords, miller, order, source)
 
@@ -287,13 +301,14 @@
 
 
 def recip_kernel(low, high, cos_ref, sin_ref, coef, start, acc):
-    lanes = slice(low, high)
+    at = slice(low, high)
+    lanes = slice(low % 256, (high - 1) % 256 + 1)
     for row in range(4):
         rows = slice(row * 256, row * 256 + 256)
         acc[rows] = (
             start[rows]
-            + jnp.dot(cos_ref[rows, lanes], coef[lanes, 0:WIDTH], preferred_element_type=F32)
-            + jnp.dot(sin_ref[rows, lanes], coef[lanes, WIDTH:], preferred_element_type=F32)
+            + jnp.dot(cos_ref[rows, lanes], coef[at, 0:WIDTH], preferred_element_type=F32)
+            + jnp.dot(sin_ref[rows, lanes], coef[at, WIDTH:], preferred_element_type=F32)
         )
 
 
@@ -373,7 +388,7 @@
     got = permute(send, HALVING[0])
     low = shifted(lower, "gx", 1)
     high = shifted(upper, "gx", -1)
-    cos_near, sin_near, keep = waves(place, turned, miller, order[:, :HALF], across, False)
+    cos_next, sin_next, keep_next = waves(place, turned, miller, order[:, 256:HALF], across, False)
 
     acc = None
 
@@ -381,17 +396,18 @@
         return radial_piece(near_cells, gammas, live, radial_filter, mine, blocks, acc)
 
     for step, height in ((1, 256), (2, 128), (3, 64)):
-        send = (keep[height:].astype(F32) + got[height:].astype(F32)).astype(BF16)
+        send = ((keep_next if step == 1 else keep[height:]) + got[height:].astype(F32)).astype(BF16)
         if step == 2:
-            send, low, high, live, mine, filters = barrier((send, low, high, live, mine, filters))
+            send, live, mine, filters = barrier((send, live, mine, filters))
         elif step == 3:
-            send, acc = barrier((send, acc))
+            send, acc, low, high = barrier((send, acc, low, high))
         fresh = permute(send, HALVING[step])
-        if step == 2:
+        if step == 3:
             left = shifted(jnp.concatenate([low[3:4], upper[3:4], lower[3:4], high[3:4]], axis=0), "gy", 1)
             right = shifted(jnp.concatenate([low[0:1], upper[0:1], lower[0:1], high[0:1]], axis=0), "gy", -1)
         if step == 1:
-            place, send = barrier((place, send))
+            across, place, send = barrier((across, place, send))
+            cos_near, sin_near, keep = waves(place, turned, miller, order[:, :256], across, False)
             live, mine, filters = prepare(
                 place, nbr_count.reshape(8), nbr_cells.reshape(8, 9), turned, reciprocal_filter
             )
@@ -403,7 +419,7 @@
     total = jnp.concatenate([keep + got.astype(F32), filters], axis=1)
     for step in range(4):
         total, acc = barrier((total, acc))
-        if step == 1:
+        if step == 2:
             total, left, right = barrier((total, left, right))
         fresh = permute(total.astype(BF16), DOUBLING[step])
         if step == 0:
@@ -422,7 +438,8 @@
         chunk, acc = barrier((chunk, acc))
         fresh = permute(chunk, HALVING[step])
         if high_at:
-            acc = recip_piece(low_at, high_at, cos_near, sin_near, chunk, acc)
+            tables = (cos_near, sin_near) if high_at <= 256 else (cos_next, sin_next)
+            acc = recip_piece(low_at, high_at, *tables, chunk, acc)
         if step:
             chunk = jnp.concatenate([chunk, fresh], axis=0)
 

time: 89.6 us -> 91.4 us (1.020)
  Pallas kernels: 23.3 us -> 25.8 us
  local copies, waits for them, and re-layouts: 1.61 us -> 0.55 us
    ppermute x12, waiting for transfers between devices: 22.4 us -> 25.8 us  [permute(): return lax.ppermute(value, AXES, partner_list(step))]
    ppermute x12, starting transfers between devices: 25.8 us -> 23 us  [permute(): return lax.ppermute(value, AXES, partner_list(step))]
    pallas_call x2 -> x3, Pallas kernels: 6.75 us -> 9.35 us  [waves(): pl.pallas_call(functools.partial(wave_kernel, first), out_shape=out_shape...]
    ppermute x4, waiting for transfers between devices: 2.46 us -> 0.01 us  [shifted(): lax.ppermute(value, axis, [(i, (i + by) % count) for i in range(count)])]
    ppermute x4, starting transfers between devices: 12.5 us -> 14.8 us  [shifted(): lax.ppermute(value, axis, [(i, (i + by) % count) for i in range(count)])]
    unnamed x32 -> x34, local copies, waits for them, and re-layouts: 1.49 us -> 0.42 us
  transfers between devices with their start and end apart: 16 -> 16, of which waited for: 12 -> 10; matrix products, arithmetic and copies ran while one was open for 1% -> 1% of each run, Pallas kernels for 19% -> 21%
where the time goes in v5:
time: 91.4 us; the launch traced here: 91.3 us
  starting transfers between devices  37.8 us (41%)
  Pallas kernels  25.8 us (28%)
  waiting for transfers between devices  25.8 us (28%)
    ppermute x12, waiting for transfers between devices, permute(): return lax.ppermute(value, AXES, partner_list(step))  25.8 us
    ppermute x12, starting transfers between devices, permute(): return lax.ppermute(value, AXES, partner_list(step))  23 us
    ppermute x4, starting transfers between devices, shifted(): lax.ppermute(value, axis, [(i, (i + by) % count) for i in range(count)])  14.8 us
    pallas_call x6, Pallas kernels, radial_piece(): pl.pallas_call(functools.partial(radial_kernel, near_cells, fresh), out_s...  11.4 us
    pallas_call x3, Pallas kernels, waves(): pl.pallas_call(functools.partial(wave_kernel, first), out_shape=out_shape...  9.35 us
    pallas_call x1, Pallas kernels, final(): pl.pallas_call(final_kernel, out_shape=pltpu.MemorySpace.HBM((1024, WIDTH...  2.42 us
  transfers between devices with their start and end apart: 16, of which 10 were waited for; matrix products, arithmetic and copies ran while one was open for 1% of the time, Pallas kernels for 21%

profile of v5, /device:TPU:1, one launch (start us, length us, event | category | flops | bytes accessed | tf_op | source)
XLA Modules:
  0.0 91.3 jit_solution(11702667773683121353)
XLA Ops:
  0.2 4.2 %wave_tables.3 = (bf16[1024,512]{1,0:T(8,128)(2,1)}, bf16[1024,512]{1,0:T(8,128)(2,1)}, bf16[512,512]{1,0:T(8,128)(2,1)S(1)}, bf16[256,1024]{1,0:T(8,128)(2,1)S(...) custom-call(s32[2]{0:T(128)S(1)} %pad_add_fusion.place, bf16[2,3,4,128]{3,2,1,0:T(4,128)(2,1)} %bitcast.10, ...), custom_call_target="tpu_custom_call" | custom-call | flops 2048000000 | bytes 3000000 | tf_op jit(solution)/shard_map/wave_tables/pallas_call | solution.py:193
  4.4 3.3 %collective-permute-start = (bf16[512,512]{1,0:T(8,128)(2,1)S(1)}, bf16[512,512]{1,0:T(8,128)(2,1)S(1)}, u32[]{:S(2)}, u32[]{:S(2)}) collective-permute-start(bf16[512,512]{1,0:T(8,128)(2,1)S(1)} %get-tuple-element.53), channel_id=1, source_target_pairs={{0,1},{1,0},{16,17},{17,16},{32,33},{33,32},{48,49},{49,48},{2,3},... | collective-permute-start | bytes 1572872 | tf_op jit(solution)/shard_map/ppermute | solution.py:66
  7.7 5.4 %collective-permute-start.4 = (bf16[4,144,256]{2,1,0:T(8,128)(2,1)S(1)}, bf16[4,144,256]{2,1,0:T(8,128)(2,1)S(1)}, u32[]{:S(2)}, u32[]{:S(2)}) collective-permute-start(bf16[4,144,256]{2,1,0:T(8,128)(2,1)S(1)} %get-tuple-element.63.rest_0_), channel_id=1, source_target_pairs={{0,240},{16,0},{32,16},{48,32},{64,48},{80,64},{96,80},{112,96},{1... | collective-permute-start | bytes 884744 | tf_op jit(solution)/shard_map/ppermute | solution.py:364
  13.2 2.6 %wave_tables.4 = (bf16[1024,256]{1,0:T(8,128)(2,1)}, bf16[1024,256]{1,0:T(8,128)(2,1)}, f32[256,512]{1,0:T(8,128)S(1)}) custom-call(s32[2]{0:T(128)S(1)} %pad_add_fusion.place, bf16[2,3,4,128]{3,2,1,0:T(4,128)(2,1)S(1)} %bitcast.11, s32[3,1024]{1,0:T(4,128)S(1)} %copy-done.3, s32[1,256]{1,0:T(1,128)S(1)} %get-tuple-element.106.order, ...), custom_call_target="tpu_custom_call" | custom-call | flops 1024000000 | bytes 3000000 | tf_op jit(solution)/shard_map/wave_tables/pallas_call | solution.py:193
  15.9 0.8 collective-permute-start.1
  16.7 2.6 %wave_tables.5 = (bf16[1024,256]{1,0:T(8,128)(2,1)}, bf16[1024,256]{1,0:T(8,128)(2,1)}, f32[256,512]{1,0:T(8,128)S(1)}) custom-call(s32[2]{0:T(128)S(1)} %pad_add_fusion.place, bf16[2,3,4,128]{3,2,1,0:T(4,128)(2,1)S(1)} %bitcast.12, s32[3,1024]{1,0:T(4,128)S(1)} %copy-done.3, s32[1,256]{1,0:T(1,128)S(1)} %get-tuple-element.105.order, ...), custom_call_target="tpu_custom_call" | custom-call | flops 1024000000 | bytes 3000000 | tf_op jit(solution)/shard_map/wave_tables/pallas_call | solution.py:193
  19.3 1.3 %radial_prepare.1 = (f32[8,9]{1,0:T(8,128)S(1)}, f32[8,3,128,128]{3,2,1,0:T(8,128)S(1)}, f32[64,256]{1,0:T(8,128)S(1)}) custom-call(s32[2]{0:T(128)S(1)} %pad_add_fusion.place, s32[8]{0:T(128)S(1)} %reshape.717.near_count, s32[8,9]{1,0:T(8,128)S(1)} %bitcast.14, bf16[2,3,4,128]{3,2,1,0:T(4,128)(2,1)S(1)} %bitcast.13, bf16[4,256]{1,0:T(4,128)(2,1)S(1)} %copy-done.7), custom_call_target="tpu_custom_call" | custom-call | flops 500000000 | bytes 100000 | tf_op jit(solution)/shard_map/radial_prepare/pallas_call | solution.py:235
  20.7 0.8 collective-permute-done.1
  21.6 2.2 %collective-permute-start.2 = (bf16[128,512]{1,0:T(8,128)(2,1)S(1)}, bf16[128,512]{1,0:T(8,128)(2,1)S(1)}, u32[]{:S(2)}, u32[]{:S(2)}) collective-permute-start(bf16[128,512]{1,0:T(8,128)(2,1)S(1)} %get-tuple-element.60), channel_id=1, source_target_pairs={{0,192},{1,13},{16,208},{17,29},{32,224},{33,45},{48,240},{49,61},... | collective-permute-start | bytes 393224 | tf_op jit(solution)/shard_map/ppermute | solution.py:66
  23.8 2.4 %radial_piece.6.rest_2_ = f32[8,128,256]{2,1,0:T(8,128)S(1)} custom-call(f32[8]{0:T(128)S(1)} %copy-done.9, f32[8,9]{1,0:T(8,128)S(1)} %get-tuple-element.61.live, bf16[8,256]{1,0:T(8,128)(2,1)S(1)} %copy-done.6, f32[8,3,128,128]{3,2,1,0:T(8,128)S(1)} %get-tuple-element.62.mine, bf16[4,144,256]{2,1,0:T(8,128)(2,1)S(1)} %get-tuple-element.63.rest_0_, ...), custom_call_target="tpu_custom_call" | custom-call | flops 2000000000 | bytes 2000000 | tf_op jit(solution)/shard_map/radial_piece/pallas_call | solution.py:290
  26.2 0.5 collective-permute-done.2
  27.0 2.6 %radial_piece.7.rest_1_ = f32[8,128,256]{2,1,0:T(8,128)S(1)} custom-call(f32[8]{0:T(128)S(1)} %copy-done.9, f32[8,9]{1,0:T(8,128)S(1)} %get-tuple-element.61.live, bf16[8,256]{1,0:T(8,128)(2,1)S(1)} %copy-done.6, f32[8,3,128,128]{3,2,1,0:T(8,128)S(1)} %get-tuple-element.62.mine, ...), custom_call_target="tpu_custom_call", output_to_operand_aliasing={{}: (6, {})} | custom-call | flops 2000000000 | bytes 2000000 | tf_op jit(solution)/shard_map/radial_piece/pallas_call | solution.py:290
  29.7 9.3 %collective-permute-start.8 = (bf16[4,144,256]{2,1,0:T(8,128)(2,1)S(1)}, bf16[4,144,256]{2,1,0:T(8,128)(2,1)S(1)}, u32[]{:S(2)}, u32[]{:S(2)}) collective-permute-start(bf16[4,144,256]{2,1,0:T(8,128)(2,1)S(1)} %pad_maximum_fusion.1), channel_id=1, source_target_pairs={{0,1},{1,2},{2,3},{3,4},{4,5},{5,6},{6,7},{7,8},{8,9},{9,10},{10,1... | collective-permute-start | bytes 884744 | tf_op jit(solution)/shard_map/ppermute | solution.py:364
  39.2 2.4 %collective-permute-start.6 = (bf16[64,768]{1,0:T(8,128)(2,1)S(1)}, bf16[64,768]{1,0:T(8,128)(2,1)S(1)}, u32[]{:S(2)}, u32[]{:S(2)}) collective-permute-start(bf16[64,768]{1,0:T(8,128)(2,1)S(1)} %convert_element_type.65), channel_id=1, source_target_pairs={{0,12},{1,193},{16,28},{17,209},{32,44},{33,225},{48,60},{49,241},... | collective-permute-start | bytes 294920 | tf_op jit(solution)/shard_map/ppermute | solution.py:66
  41.6 1.8 %radial_piece.8.rest_1_ = f32[8,128,256]{2,1,0:T(8,128)S(1)} custom-call(f32[8]{0:T(128)S(1)} %copy-done.9, f32[8,9]{1,0:T(8,128)S(1)} %get-tuple-element.61.live, bf16[8,256]{1,0:T(8,128)(2,1)S(1)} %copy-done.6, f32[8,3,128,128]{3,2,1,0:T(8,128)S(1)} %get-tuple-element.62.mine, ...), custom_call_target="tpu_custom_call", output_to_operand_aliasing={{}: (5, {})} | custom-call | flops 2000000000 | bytes 2000000 | tf_op jit(solution)/shard_map/radial_piece/pallas_call | solution.py:290
  43.4 0.9 collective-permute-done.6
  44.3 1.9 %collective-permute-start.7 = (bf16[64,768]{1,0:T(8,128)(2,1)S(1)}, bf16[64,768]{1,0:T(8,128)(2,1)S(1)}, u32[]{:S(2)}, u32[]{:S(2)}) collective-permute-start(bf16[64,768]{1,0:T(8,128)(2,1)S(1)} %convert_element_type.67), channel_id=1, source_target_pairs={{0,16},{1,51},{16,0},{17,33},{32,48},{33,17},{48,32},{49,3},{2,18}... | collective-permute-start | bytes 294920 | tf_op jit(solution)/shard_map/ppermute | solution.py:66
  46.2 1.8 %radial_piece.9.rest_1_ = f32[8,128,256]{2,1,0:T(8,128)S(1)} custom-call(f32[8]{0:T(128)S(1)} %copy-done.9, f32[8,9]{1,0:T(8,128)S(1)} %get-tuple-element.61.live, bf16[8,256]{1,0:T(8,128)(2,1)S(1)} %copy-done.6, f32[8,3,128,128]{3,2,1,0:T(8,128)S(1)} %get-tuple-element.62.mine, ...), custom_call_target="tpu_custom_call", output_to_operand_aliasing={{}: (5, {})} | custom-call | flops 2000000000 | bytes 2000000 | tf_op jit(solution)/shard_map/radial_piece/pallas_call | solution.py:290
  48.1 5.8 %collective-permute-done.7 = bf16[64,768]{1,0:T(8,128)(2,1)S(1)} collective-permute-done((bf16[64,768]{1,0:T(8,128)(2,1)S(1)}, bf16[64,768]{1,0:T(8,128)(2,1)S(1)}, u32[]{:S(2)}, u32[]{:S(2)}) %collective-permute-start.7) | collective-permute-done | bytes 98336 | tf_op jit(solution)/shard_map/ppermute | solution.py:66
  54.0 1.4 %radial_piece.10.rest_1_ = f32[8,128,256]{2,1,0:T(8,128)S(1)} custom-call(f32[8]{0:T(128)S(1)} %copy-done.9, f32[8,9]{1,0:T(8,128)S(1)} %get-tuple-element.61.live, bf16[8,256]{1,0:T(8,128)(2,1)S(1)} %copy-done.6, f32[8,3,128,128]{3,2,1,0:T(8,128)S(1)} %get-tuple-element.62.mine, ...), custom_call_target="tpu_custom_call", output_to_operand_aliasing={{}: (5, {})} | custom-call | flops 2000000000 | bytes 2000000 | tf_op jit(solution)/shard_map/radial_piece/pallas_call | solution.py:290
  55.4 2.1 %collective-permute-done.10 = bf16[64,768]{1,0:T(8,128)(2,1)S(1)} collective-permute-done((bf16[64,768]{1,0:T(8,128)(2,1)S(1)}, bf16[64,768]{1,0:T(8,128)(2,1)S(1)}, u32[]{:S(2)}, u32[]{:S(2)}) %collective-permute-start.10) | collective-permute-done | bytes 98336 | tf_op jit(solution)/shard_map/ppermute | solution.py:66
  57.5 1.1 %collective-permute-start.11 = (bf16[64,768]{1,0:T(8,128)(2,1)S(1)}, bf16[64,768]{1,0:T(8,128)(2,1)S(1)}, u32[]{:S(2)}, u32[]{:S(2)}) collective-permute-start(bf16[64,768]{1,0:T(8,128)(2,1)S(1)} %convert_element_type.71), channel_id=1, source_target_pairs={{0,48},{1,19},{16,34},{17,3},{32,18},{33,51},{48,0},{49,35},{2,50}... | collective-permute-start | bytes 294920 | tf_op jit(solution)/shard_map/ppermute | solution.py:66
  58.6 1.4 %radial_piece.11 = f32[8,128,256]{2,1,0:T(8,128)S(1)} custom-call(f32[8]{0:T(128)S(1)} %copy-done.9, f32[8,9]{1,0:T(8,128)S(1)} %get-tuple-element.61.live, bf16[8,256]{1,0:T(8,128)(2,1)S(1)} %copy-done.6, f32[8,3,128,128]{3,2,1,0:T(8,128)S(1)} %get-tuple-element.62.mine, ...), custom_call_target="tpu_custom_call", output_to_operand_aliasing={{}: (5, {})} | custom-call | flops 2000000000 | bytes 2000000 | tf_op jit(solution)/shard_map/radial_piece/pallas_call | solution.py:290
  60.0 4.1 %collective-permute-done.11 = bf16[64,768]{1,0:T(8,128)(2,1)S(1)} collective-permute-done((bf16[64,768]{1,0:T(8,128)(2,1)S(1)}, bf16[64,768]{1,0:T(8,128)(2,1)S(1)}, u32[]{:S(2)}, u32[]{:S(2)}) %collective-permute-start.11) | collective-permute-done | bytes 98336 | tf_op jit(solution)/shard_map/ppermute | solution.py:66
  64.2 3.1 %collective-permute-done.12 = bf16[64,512]{1,0:T(8,128)(2,1)S(1)} collective-permute-done((bf16[64,512]{1,0:T(8,128)(2,1)S(1)}, bf16[64,512]{1,0:T(8,128)(2,1)S(1)}, u32[]{:S(2)}, u32[]{:S(2)}) %collective-permute-start.12) | collective-permute-done | bytes 65568 | tf_op jit(solution)/shard_map/ppermute | solution.py:66
  67.4 2.1 %collective-permute-start.13 = (bf16[128,512]{1,0:T(8,128)(2,1)S(1)}, bf16[128,512]{1,0:T(8,128)(2,1)S(1)}, u32[]{:S(2)}, u32[]{:S(2)}) collective-permute-start(bf16[128,512]{1,0:T(8,128)(2,1)S(1)} %pad_maximum_fusion.5.coef), channel_id=1, source_target_pairs={{0,192},{1,13},{16,208},{17,29},{32,224},{33,45},{48,240},{49,61},... | collective-permute-start | bytes 393224 | tf_op jit(solution)/shard_map/ppermute | solution.py:66
  69.9 2.5 %collective-permute-done.13 = bf16[128,512]{1,0:T(8,128)(2,1)S(1)} collective-permute-done((bf16[128,512]{1,0:T(8,128)(2,1)S(1)}, bf16[128,512]{1,0:T(8,128)(2,1)S(1)}, u32[]{:S(2)}, u32[]{:S(2)}) %collective-permute-start.13) | collective-permute-done | bytes 131104 | tf_op jit(solution)/shard_map/ppermute | solution.py:66
  73.3 5.1 %collective-permute-done.14 = bf16[256,512]{1,0:T(8,128)(2,1)S(1)} collective-permute-done((bf16[256,512]{1,0:T(8,128)(2,1)S(1)}, bf16[256,512]{1,0:T(8,128)(2,1)S(1)}, u32[]{:S(2)}, u32[]{:S(2)}) %collective-permute-start.14) | collective-permute-done | bytes 262176 | tf_op jit(solution)/shard_map/ppermute | solution.py:66
  78.4 8.4 %collective-permute-start.15 = (bf16[512,512]{1,0:T(8,128)(2,1)S(1)}, bf16[512,512]{1,0:T(8,128)(2,1)S(1)}, u32[]{:S(2)}, u32[]{:S(2)}) collective-permute-start(bf16[512,512]{1,0:T(8,128)(2,1)S(1)} %pad_maximum_fusion.coef), channel_id=1, source_target_pairs={{0,1},{1,0},{16,17},{17,16},{32,33},{33,32},{48,49},{49,48},{2,3},... | collective-permute-start | bytes 1572872 | tf_op jit(solution)/shard_map/ppermute | solution.py:66
  86.8 0.5 recip_piece.5.acc
  87.3 1.0 %collective-permute-done.15.coef = bf16[512,512]{1,0:T(8,128)(2,1)S(1)} collective-permute-done((bf16[512,512]{1,0:T(8,128)(2,1)S(1)}, bf16[512,512]{1,0:T(8,128)(2,1)S(1)}, u32[]{:S(2)}, u32[]{:S(2)}) %collective-permute-start.15) | collective-permute-done | bytes 524320 | tf_op jit(solution)/shard_map/ppermute | solution.py:66
  88.7 2.4 %mix_and_network.1 = bf16[1024,256]{1,0:T(8,128)(2,1)} custom-call(bf16[1024,512]{1,0:T(8,128)(2,1)S(1)} %copy-done.14, bf16[1024,512]{1,0:T(8,128)(2,1)S(1)} %copy-done.15, bf16[512,512]{1,0:T(8,128)(2,1)S(1)} %collective-permute-done.15.coef, bf16[1024,256]{1,0:T(8,128)(2,1)S(1)} %bitcast.9, f32[1024,256]{1,0:T(8,128)S(1)} %recip_piece.5.acc, ...), custom_call_target="tpu_custom_call" | custom-call | flops 3000000000 | bytes 8000000 | tf_op jit(solution)/shard_map/mix_and_network/pallas_call | solution.py:350
  (76 shorter events, 3.0 us)
Async XLA Ops:
  0.2 12.9 %copy-start.16 = (s32[2,4]{1,0:T(2,128)S(1)}, s32[2,4]{1,0:T(2,128)}, u32[]{:S(2)}) copy-start(s32[2,4]{1,0:T(2,128)} %param.14) | copy-start | bytes 100
  0.2 13.0 %copy-start.3 = (s32[3,1024]{1,0:T(4,128)S(1)}, s32[3,1024]{1,0:T(4,128)}, u32[]{:S(2)}) copy-start(s32[3,1024]{1,0:T(4,128)} %miller.5) | copy-start | bytes 36868
  0.2 13.0 %copy-start.4 = (bf16[2,4,3,128]{3,1,2,0:T(4,128)(2,1)S(1)}, bf16[2,4,3,128]{3,1,2,0:T(4,128)(2,1)}, u32[]{:S(2)}) copy-start(bf16[2,4,3,128]{3,1,2,0:T(4,128)(2,1)} %param.12) | copy-start | bytes 18436
  4.4 11.4 %collective-permute-start = (bf16[512,512]{1,0:T(8,128)(2,1)S(1)}, bf16[512,512]{1,0:T(8,128)(2,1)S(1)}, u32[]{:S(2)}, u32[]{:S(2)}) collective-permute-start(bf16[512,512]{1,0:T(8,128)(2,1)S(1)} %get-tuple-element.53), channel_id=1, source_target_pairs={{0,1},{1,0},{16,17},{17,16},{32,33},{33,32},{48,49},{49,48},{2,3},... | collective-permute-start | bytes 1572872 | tf_op jit(solution)/shard_map/ppermute | solution.py:66
  7.7 19.0 %collective-permute-start.3 = (bf16[4,144,256]{2,1,0:T(8,128)(2,1)S(1)}, bf16[4,144,256]{2,1,0:T(8,128)(2,1)S(1)}, u32[]{:S(2)}, u32[]{:S(2)}) collective-permute-start(bf16[4,144,256]{2,1,0:T(8,128)(2,1)S(1)} %get-tuple-element.64.rest_1_), channel_id=1, source_target_pairs={{0,16},{16,32},{32,48},{48,64},{64,80},{80,96},{96,112},{112,128},... | collective-permute-start | bytes 884744 | tf_op jit(solution)/shard_map/ppermute | solution.py:364
  7.7 19.0 %collective-permute-start.4 = (bf16[4,144,256]{2,1,0:T(8,128)(2,1)S(1)}, bf16[4,144,256]{2,1,0:T(8,128)(2,1)S(1)}, u32[]{:S(2)}, u32[]{:S(2)}) collective-permute-start(bf16[4,144,256]{2,1,0:T(8,128)(2,1)S(1)} %get-tuple-element.63.rest_0_), channel_id=1, source_target_pairs={{0,240},{16,0},{32,16},{48,32},{64,48},{80,64},{96,80},{112,96},{1... | collective-permute-start | bytes 884744 | tf_op jit(solution)/shard_map/ppermute | solution.py:364
  15.9 5.6 %collective-permute-start.1 = (bf16[256,512]{1,0:T(8,128)(2,1)S(1)}, bf16[256,512]{1,0:T(8,128)(2,1)S(1)}, u32[]{:S(2)}, u32[]{:S(2)}) collective-permute-start(bf16[256,512]{1,0:T(8,128)(2,1)S(1)} %add_convert_fusion), channel_id=1, source_target_pairs={{0,64},{1,5},{16,80},{17,21},{32,96},{33,37},{48,112},{49,53},{2,6... | collective-permute-start | bytes 786440 | tf_op jit(solution)/shard_map/ppermute | solution.py:66
  16.7 2.6 %copy-start.5 = (s32[2,4,9]{2,1,0:T(4,128)S(1)}, s32[2,4,9]{2,1,0:T(4,128)}, u32[]{:S(2)}) copy-start(s32[2,4,9]{2,1,0:T(4,128)} %param.13) | copy-start | bytes 868
  16.7 2.6 %copy-start.7 = (bf16[4,256]{1,0:T(4,128)(2,1)S(1)}, bf16[4,256]{1,0:T(4,128)(2,1)}, u32[]{:S(2)}) copy-start(bf16[4,256]{1,0:T(4,128)(2,1)} %row_filter.1) | copy-start | bytes 6148
  20.6 3.3 %copy-start.6 = (bf16[8,256]{1,0:T(8,128)(2,1)S(1)}, bf16[8,256]{1,0:T(8,128)(2,1)}, u32[]{:S(2)}) copy-start(bf16[8,256]{1,0:T(8,128)(2,1)} %filters.11) | copy-start | bytes 12292
  20.6 3.2 %copy-start.9 = (f32[8]{0:T(128)S(1)}, f32[8]{0:T(128)}, u32[]{:S(2)}) copy-start(f32[8]{0:T(128)} %rates.11) | copy-start | bytes 100
  21.6 5.1 %collective-permute-start.2 = (bf16[128,512]{1,0:T(8,128)(2,1)S(1)}, bf16[128,512]{1,0:T(8,128)(2,1)S(1)}, u32[]{:S(2)}, u32[]{:S(2)}) collective-permute-start(bf16[128,512]{1,0:T(8,128)(2,1)S(1)} %get-tuple-element.60), channel_id=1, source_target_pairs={{0,192},{1,13},{16,208},{17,29},{32,224},{33,45},{48,240},{49,61},... | collective-permute-start | bytes 393224 | tf_op jit(solution)/shard_map/ppermute | solution.py:66
  26.7 12.4 %collective-permute-start.5 = (bf16[64,512]{1,0:T(8,128)(2,1)S(1)}, bf16[64,512]{1,0:T(8,128)(2,1)S(1)}, u32[]{:S(2)}, u32[]{:S(2)}) collective-permute-start(bf16[64,512]{1,0:T(8,128)(2,1)S(1)} %fusion.1), channel_id=1, source_target_pairs={{0,4},{1,65},{16,20},{17,81},{32,36},{33,97},{48,52},{49,113},{2,6... | collective-permute-start | bytes 196616 | tf_op jit(solution)/shard_map/ppermute | solution.py:66
  29.7 24.2 %collective-permute-start.8 = (bf16[4,144,256]{2,1,0:T(8,128)(2,1)S(1)}, bf16[4,144,256]{2,1,0:T(8,128)(2,1)S(1)}, u32[]{:S(2)}, u32[]{:S(2)}) collective-permute-start(bf16[4,144,256]{2,1,0:T(8,128)(2,1)S(1)} %pad_maximum_fusion.1), channel_id=1, source_target_pairs={{0,1},{1,2},{2,3},{3,4},{4,5},{5,6},{6,7},{7,8},{8,9},{9,10},{10,1... | collective-permute-start | bytes 884744 | tf_op jit(solution)/shard_map/ppermute | solution.py:364
  39.0 14.8 %collective-permute-start.9 = (bf16[4,144,256]{2,1,0:T(8,128)(2,1)S(1)}, bf16[4,144,256]{2,1,0:T(8,128)(2,1)S(1)}, u32[]{:S(2)}, u32[]{:S(2)}) collective-permute-start(bf16[4,144,256]{2,1,0:T(8,128)(2,1)S(1)} %pad_maximum_fusion.2), channel_id=1, source_target_pairs={{0,15},{1,0},{2,1},{3,2},{4,3},{5,4},{6,5},{7,6},{8,7},{9,8},{10,9... | collective-permute-start | bytes 884744 | tf_op jit(solution)/shard_map/ppermute | solution.py:364
  39.2 5.1 %collective-permute-start.6 = (bf16[64,768]{1,0:T(8,128)(2,1)S(1)}, bf16[64,768]{1,0:T(8,128)(2,1)S(1)}, u32[]{:S(2)}, u32[]{:S(2)}) collective-permute-start(bf16[64,768]{1,0:T(8,128)(2,1)S(1)} %convert_element_type.65), channel_id=1, source_target_pairs={{0,12},{1,193},{16,28},{17,209},{32,44},{33,225},{48,60},{49,241},... | collective-permute-start | bytes 294920 | tf_op jit(solution)/shard_map/ppermute | solution.py:66
  44.3 9.5 %collective-permute-start.7 = (bf16[64,768]{1,0:T(8,128)(2,1)S(1)}, bf16[64,768]{1,0:T(8,128)(2,1)S(1)}, u32[]{:S(2)}, u32[]{:S(2)}) collective-permute-start(bf16[64,768]{1,0:T(8,128)(2,1)S(1)} %convert_element_type.67), channel_id=1, source_target_pairs={{0,16},{1,51},{16,0},{17,33},{32,48},{33,17},{48,32},{49,3},{2,18}... | collective-permute-start | bytes 294920 | tf_op jit(solution)/shard_map/ppermute | solution.py:66
  53.9 3.6 %collective-permute-start.10 = (bf16[64,768]{1,0:T(8,128)(2,1)S(1)}, bf16[64,768]{1,0:T(8,128)(2,1)S(1)}, u32[]{:S(2)}, u32[]{:S(2)}) collective-permute-start(bf16[64,768]{1,0:T(8,128)(2,1)S(1)} %convert_element_type.69), channel_id=1, source_target_pairs={{0,50},{1,17},{16,32},{17,1},{32,16},{33,49},{48,2},{49,33},{2,48}... | collective-permute-start | bytes 294920 | tf_op jit(solution)/shard_map/ppermute | solution.py:66
  57.5 12.0 %copy-start.12 = (bf16[1024,256]{1,0:T(8,128)(2,1)S(1)}, bf16[1024,256]{1,0:T(8,128)(2,1)}, u32[]{:S(2)}) copy-start(bf16[1024,256]{1,0:T(8,128)(2,1)} %get-tuple-element.84.cos_ref) | copy-start | bytes 1572868
  57.5 12.0 %copy-start.13 = (bf16[1024,256]{1,0:T(8,128)(2,1)S(1)}, bf16[1024,256]{1,0:T(8,128)(2,1)}, u32[]{:S(2)}) copy-start(bf16[1024,256]{1,0:T(8,128)(2,1)} %get-tuple-element.85.sin_ref) | copy-start | bytes 1572868
  57.5 6.6 %collective-permute-start.11 = (bf16[64,768]{1,0:T(8,128)(2,1)S(1)}, bf16[64,768]{1,0:T(8,128)(2,1)S(1)}, u32[]{:S(2)}, u32[]{:S(2)}) collective-permute-start(bf16[64,768]{1,0:T(8,128)(2,1)S(1)} %convert_element_type.71), channel_id=1, source_target_pairs={{0,48},{1,19},{16,34},{17,3},{32,18},{33,51},{48,0},{49,35},{2,50}... | collective-permute-start | bytes 294920 | tf_op jit(solution)/shard_map/ppermute | solution.py:66
  64.1 3.2 %collective-permute-start.12 = (bf16[64,512]{1,0:T(8,128)(2,1)S(1)}, bf16[64,512]{1,0:T(8,128)(2,1)S(1)}, u32[]{:S(2)}, u32[]{:S(2)}) collective-permute-start(bf16[64,512]{1,0:T(8,128)(2,1)S(1)} %pad_maximum_fusion.6), channel_id=1, source_target_pairs={{0,4},{1,65},{16,20},{17,81},{32,36},{33,97},{48,52},{49,113},{2,6... | collective-permute-start | bytes 196616 | tf_op jit(solution)/shard_map/ppermute | solution.py:66
  67.4 5.1 %collective-permute-start.13 = (bf16[128,512]{1,0:T(8,128)(2,1)S(1)}, bf16[128,512]{1,0:T(8,128)(2,1)S(1)}, u32[]{:S(2)}, u32[]{:S(2)}) collective-permute-start(bf16[128,512]{1,0:T(8,128)(2,1)S(1)} %pad_maximum_fusion.5.coef), channel_id=1, source_target_pairs={{0,192},{1,13},{16,208},{17,29},{32,224},{33,45},{48,240},{49,61},... | collective-permute-start | bytes 393224 | tf_op jit(solution)/shard_map/ppermute | solution.py:66
  72.5 14.3 %copy-start.10 = (bf16[1024,256]{1,0:T(8,128)(2,1)S(1)}, bf16[1024,256]{1,0:T(8,128)(2,1)}, u32[]{:S(2)}) copy-start(bf16[1024,256]{1,0:T(8,128)(2,1)} %get-tuple-element.90.cos_ref) | copy-start | bytes 1572868
  72.5 14.3 %copy-start.11 = (bf16[1024,256]{1,0:T(8,128)(2,1)S(1)}, bf16[1024,256]{1,0:T(8,128)(2,1)}, u32[]{:S(2)}) copy-start(bf16[1024,256]{1,0:T(8,128)(2,1)} %get-tuple-element.91.sin_ref) | copy-start | bytes 1572868
  72.5 5.8 %collective-permute-start.14 = (bf16[256,512]{1,0:T(8,128)(2,1)S(1)}, bf16[256,512]{1,0:T(8,128)(2,1)S(1)}, u32[]{:S(2)}, u32[]{:S(2)}) collective-permute-start(bf16[256,512]{1,0:T(8,128)(2,1)S(1)} %pad_maximum_fusion.3.coef), channel_id=1, source_target_pairs={{0,64},{1,5},{16,80},{17,21},{32,96},{33,37},{48,112},{49,53},{2,6... | collective-permute-start | bytes 786440 | tf_op jit(solution)/shard_map/ppermute | solution.py:66
  78.4 9.9 %collective-permute-start.15 = (bf16[512,512]{1,0:T(8,128)(2,1)S(1)}, bf16[512,512]{1,0:T(8,128)(2,1)S(1)}, u32[]{:S(2)}, u32[]{:S(2)}) collective-permute-start(bf16[512,512]{1,0:T(8,128)(2,1)S(1)} %pad_maximum_fusion.coef), channel_id=1, source_target_pairs={{0,1},{1,0},{16,17},{17,16},{32,33},{33,32},{48,49},{49,48},{2,3},... | collective-permute-start | bytes 1572872 | tf_op jit(solution)/shard_map/ppermute | solution.py:66
  86.8 1.5 %copy-start = (bf16[2,4,128,256]{3,2,1,0:T(8,128)(2,1)S(1)}, bf16[2,4,128,256]{3,2,1,0:T(8,128)(2,1)}, u32[]{:S(2)}) copy-start(bf16[2,4,128,256]{3,2,1,0:T(8,128)(2,1)} %param.11) | copy-start | bytes 1572868
  86.8 1.5 %copy-start.1 = (bf16[256,512]{1,0:T(8,128)(2,1)S(1)}, bf16[256,512]{1,0:T(8,128)(2,1)}, u32[]{:S(2)}) copy-start(bf16[256,512]{1,0:T(8,128)(2,1)} %w_in.1) | copy-start | bytes 786436
  86.8 1.5 %copy-start.2 = (bf16[512,256]{1,0:T(8,128)(2,1)S(1)}, bf16[512,256]{1,0:T(8,128)(2,1)}, u32[]{:S(2)}) copy-start(bf16[512,256]{1,0:T(8,128)(2,1)} %w_out.1) | copy-start | bytes 786436
  86.8 1.5 %copy-start.14 = (bf16[1024,512]{1,0:T(8,128)(2,1)S(1)}, bf16[1024,512]{1,0:T(8,128)(2,1)}, u32[]{:S(2)}) copy-start(bf16[1024,512]{1,0:T(8,128)(2,1)} %get-tuple-element.49.cos_ref) | copy-start | bytes 3145732
  86.8 1.8 %copy-start.15 = (bf16[1024,512]{1,0:T(8,128)(2,1)S(1)}, bf16[1024,512]{1,0:T(8,128)(2,1)}, u32[]{:S(2)}) copy-start(bf16[1024,512]{1,0:T(8,128)(2,1)} %get-tuple-element.50.sin_ref) | copy-start | bytes 3145732
  (1 other events, 1.5 us)

commit v6 on v5

--- a/solution.py
+++ b/solution.py
@@ -300,6 +300,77 @@
     )(*arrays)
 
 
+def edge_kernel(along_x, which, sides, rates, live, filters, mine, block, start, acc, scaled):
+    low_side = sides[which] < 0
+    step = jnp.where(low_side, -1.0, 1.0)
+    across = CY if along_x else CX
+    totals = [None] * across
+    places = []
+    for own in range(across):
+        at = (own, (CX - 1) * CY + own) if along_x else (own * CY, own * CY + CY - 1)
+        places.append((at, jnp.where(low_side, at[0], at[1])))
+    for i in range(CY if along_x else CX + 2):
+        line = i if along_x else i - 1
+        values = block[i, 0:ATOMS, :]
+        for k in range(8):
+            scaled[i % 2, k * ATOMS : (k + 1) * ATOMS, :] = values * filters[k : k + 1, :]
+        near = block[i, ATOMS:PACK, 0:ATOMS].astype(F32)
+        for own in range(max(0, line - 1), min(across, line + 2)):
+            shift = line - own
+            (cell_low, cell_high), cell = places[own]
+            u, v = (step, float(shift)) if along_x else (float(shift), step)
+            dx = (near[0:1] + u) - mine[cell, 0]
+            dy = (near[1:2] + v) - mine[cell, 1]
+            dz = near[2:3] - mine[cell, 2]
+            dist = dx * dx + dy * dy + dz * dz
+            kernel = jnp.concatenate([jnp.exp2(dist * (rates[k] * -LOG2E)).astype(BF16) for k in range(8)], axis=1)
+            o_low, o_high = (shift + 1, 7 + shift) if along_x else (3 * shift + 3, 3 * shift + 5)
+            weight = jnp.where(
+                low_side,
+                live[cell_low : cell_low + 1, o_low : o_low + 1],
+                live[cell_high : cell_high + 1, o_high : o_high + 1],
+            )
+            part = jnp.dot(kernel, scaled[i % 2], preferred_element_type=F32) * weight
+            totals[own] = part if totals[own] is None else totals[own] + part
+            if line == min(across - 1 + (0 if along_x else 1), own + 1):
+                acc[cell] = start[cell] + totals[own]
+    for cell in range(CX * CY):
+        at_low = cell < CY if along_x else cell % CY == 0
+        at_high = cell >= CY if along_x else cell % CY == CY - 1
+        if along_x:
+            keep_it = jnp.logical_not(low_side) if at_low else low_side
+        elif at_low:
+            keep_it = jnp.logical_not(low_side)
+        elif at_high:
+            keep_it = low_side
+        else:
+            keep_it = None
+
+        def keep_cell(cell=cell):
+            acc[cell] = start[cell]
+
+        if keep_it is None:
+            keep_cell()
+        else:
+            pl.when(keep_it)(keep_cell)
+
+
+def edge_piece(along_x, which, sides, gammas, live, filters, mine, block, acc):
+    vm = pl.BlockSpec(memory_space=VMEM)
+    sm = pl.BlockSpec(memory_space=pltpu.SMEM)
+    return pl.pallas_call(
+        functools.partial(edge_kernel, along_x, which),
+        out_shape=jax.ShapeDtypeStruct((CX * CY, ATOMS, WIDTH), F32),
+        in_specs=[sm, sm] + [vm] * 5,
+        out_specs=vm,
+        scratch_shapes=[VMEM((2, 8 * ATOMS, WIDTH), BF16)],
+        input_output_aliases={6: 0},
+        compiler_params=pltpu.CompilerParams(vmem_limit_bytes=10 * 1024 * 1024),
+        cost_estimate=pl.CostEstimate(flops=2_000_000_000, bytes_accessed=2_000_000, transcendentals=0),
+        name="radial_edge",
+    )(sides, gammas, live, filters, mine, block, acc)
+
+
 def recip_kernel(low, high, cos_ref, sin_ref, coef, start, acc):
     at = slice(low, high)
     lanes = slice(low % 256, (high - 1) % 256 + 1)
@@ -359,9 +430,15 @@
     )(cos_table, sin_table, coef, features, acc, gain, w_in, w_out)
 
 
-def shifted(value, axis, by):
-    count = lax.axis_size(axis)
-    return lax.ppermute(value, axis, [(i, (i + by) % count) for i in range(count)])
+def row_pairs(first):
+    def other(gx):
+        return (gx + 1) % 16 if (gx % 2 == 0) == first else (gx - 1) % 16
+
+    return [(i, other(i)) for i in range(16)]
+
+
+def column_pairs(first):
+    return row_pairs(first)
 
 
 def per_device(
@@ -386,25 +463,30 @@
 
     cos_far, sin_far, send, across, upper, lower = waves(place, turned, miller, order[:, HALF:], own_rows, True)
     got = permute(send, HALVING[0])
-    low = shifted(lower, "gx", 1)
-    high = shifted(upper, "gx", -1)
+    even_x, even_y = gx % 2 == 0, gy % 2 == 0
+    sides = jnp.stack(
+        [jnp.where(even_x, 1, -1), jnp.where(even_x, -1, 1), jnp.where(even_y, 1, -1), jnp.where(even_y, -1, 1)]
+    ).astype(jnp.int32)
+    row_a = lax.ppermute(jnp.where(even_x, lower, upper), "gx", row_pairs(True))
+    row_b = lax.ppermute(jnp.where(even_x, upper, lower), "gx", row_pairs(False))
     cos_next, sin_next, keep_next = waves(place, turned, miller, order[:, 256:HALF], across, False)
 
     acc = None
 
-    def piece(near_cells, blocks, acc):
-        return radial_piece(near_cells, gammas, live, radial_filter, mine, blocks, acc)
+    def own_piece(jb, acc):
+        near_cells = tuple(((ja, jb), (ja, jb)) for ja in range(CX))
+        return radial_piece(near_cells, gammas, live, radial_filter, mine, (upper, lower), acc)
+
+    def beyond(along_x, which, block, acc):
+        return edge_piece(along_x, which, sides, gammas, live, radial_filter, mine, block, acc)
 
     for step, height in ((1, 256), (2, 128), (3, 64)):
         send = ((keep_next if step == 1 else keep[height:]) + got[height:].astype(F32)).astype(BF16)
         if step == 2:
             send, live, mine, filters = barrier((send, live, mine, filters))
         elif step == 3:
-            send, acc, low, high = barrier((send, acc, low, high))
+            send, acc = barrier((send, acc))
         fresh = permute(send, HALVING[step])
-        if step == 3:
-            left = shifted(jnp.concatenate([low[3:4], upper[3:4], lower[3:4], high[3:4]], axis=0), "gy", 1)
-            right = shifted(jnp.concatenate([low[0:1], upper[0:1], lower[0:1], high[0:1]], axis=0), "gy", -1)
         if step == 1:
             across, place, send = barrier((across, place, send))
             cos_near, sin_near, keep = waves(place, turned, miller, order[:, :256], across, False)
@@ -412,36 +494,48 @@
                 place, nbr_count.reshape(8), nbr_cells.reshape(8, 9), turned, reciprocal_filter
             )
         else:
-            jbs = (0, 1) if step == 2 else (2, 3)
-            acc = piece(tuple(((ja, jb), (ja, jb)) for jb in jbs for ja in range(CX)), (upper, lower), acc)
+            acc = own_piece(step - 2, acc)
         keep = keep[:height] + got[:height].astype(F32)
         got = fresh
     total = jnp.concatenate([keep + got.astype(F32), filters], axis=1)
     for step in range(4):
         total, acc = barrier((total, acc))
-        if step == 2:
-            total, left, right = barrier((total, left, right))
         fresh = permute(total.astype(BF16), DOUBLING[step])
-        if step == 0:
-            acc = piece(tuple(((-1, jb), (0, jb)) for jb in range(CY)), (low,), acc)
-        elif step == 1:
-            acc = piece(tuple(((CX, jb), (0, jb)) for jb in range(CY)), (high,), acc)
-        elif step == 2:
-            acc = piece(tuple(((ja - 1, -1), (0, ja)) for ja in range(CX + 2)), (left,), acc)
+        if step < 2:
+            acc = own_piece(step + 2, acc)
         else:
-            acc = piece(tuple(((ja - 1, CY), (0, ja)) for ja in range(CX + 2)), (right,), acc)
+            acc = beyond(True, step - 2, row_a if step == 2 else row_b, acc)
         total = total + fresh.astype(F32)
     scale = total[:, 2 * WIDTH :]
     chunk = jnp.concatenate([total[:, :WIDTH] * scale, total[:, WIDTH : 2 * WIDTH] * scale], axis=1).astype(BF16)
-    acc = acc.reshape(1024, WIDTH)
+    chunk, row_a, row_b = barrier((chunk, row_a, row_b))
     for step, low_at, high_at in ((3, 0, 0), (2, 0, 128), (1, 128, 256), (0, 256, 512)):
         chunk, acc = barrier((chunk, acc))
         fresh = permute(chunk, HALVING[step])
+        if step == 3:
+            ends = [
+                (jnp.where(even_x, row_b[b : b + 1], row_a[b : b + 1]), jnp.where(even_x, row_a[b : b + 1], row_b[b : b + 1]))
+                for b in (0, CY - 1)
+            ]
+            left, right = (
+                jnp.concatenate([low, upper[b : b + 1], lower[b : b + 1], high], axis=0)
+                for b, (low, high) in zip((0, CY - 1), ends)
+            )
+            column_b = lax.ppermute(jnp.where(even_y, left, right), "gy", column_pairs(False))
+            near_send = jnp.where(even_y, right, left)
+        elif step == 2:
+            near_send, chunk = barrier((near_send, chunk))
+            column_a = lax.ppermute(near_send, "gy", column_pairs(True))
+        elif step == 1:
+            acc = beyond(False, 2, column_a, acc)
+        elif step == 0:
+            acc = beyond(False, 3, column_b, acc)
         if high_at:
             tables = (cos_near, sin_near) if high_at <= 256 else (cos_next, sin_next)
-            acc = recip_piece(low_at, high_at, *tables, chunk, acc)
+            acc = recip_piece(low_at, high_at, *tables, chunk, acc.reshape(1024, WIDTH)).reshape(CX * CY, ATOMS, WIDTH)
         if step:
             chunk = jnp.concatenate([chunk, fresh], axis=0)
+    acc = acc.reshape(1024, WIDTH)
 
     out = final(
         cos_far, sin_far, fresh, own_rows, acc, norm_gain.reshape(1, WIDTH), w_in, w_out

time: 91.4 us -> 94.9 us (1.038)
  starting transfers between devices: 37.8 us -> 42.9 us
  waiting for transfers between devices: 25.8 us -> 21.3 us
  Pallas kernels: 25.8 us -> 27.6 us
  local copies, waits for them, and re-layouts: 0.55 us -> 1.53 us
    ppermute x12, waiting for transfers between devices: 25.8 us -> 13.8 us  [permute(): return lax.ppermute(value, AXES, partner_list(step))]
    ppermute x4, starting transfers between devices: 14.8 us -> 22.8 us  [the longest x1 14.3 us: per_device(): column_a = lax.ppermute(near_send, 'gy', column_pairs(True))]
    ppermute x4, waiting for transfers between devices: 0.01 us -> 7.57 us  [the longest x1 7.56 us: per_device(): lax.ppermute(jnp.where(even_y, left, right), 'gy', column_pairs(False))]
    pallas_call x0 -> x4, Pallas kernels: none -> 6.48 us  [edge_piece(): pl.pallas_call(functools.partial(edge_kernel, along_x, which), out_shape=...]
    pallas_call x6 -> x4, Pallas kernels: 11.4 us -> 6.72 us  [radial_piece(): pl.pallas_call(functools.partial(radial_kernel, near_cells, fresh), out_s...]
    ppermute x12, starting transfers between devices: 23 us -> 20.1 us  [permute(): return lax.ppermute(value, AXES, partner_list(step))]
    unnamed x34, local copies, waits for them, and re-layouts: 0.42 us -> 1.42 us
  transfers between devices with their start and end apart: 16 -> 16, of which waited for: 10 -> 10; matrix products, arithmetic and copies ran while one was open for 1% -> 1% of each run, Pallas kernels for 21% -> 22%
where the time goes in v6:
time: 94.9 us; the launch traced here: 94.8 us
  starting transfers between devices  42.9 us (45%)
  Pallas kernels  27.6 us (29%)
  waiting for transfers between devices  21.3 us (22%)
  local copies, waits for them, and re-layouts  1.53 us (2%)
    ppermute x12, starting transfers between devices, permute(): return lax.ppermute(value, AXES, partner_list(step))  20.1 us
    ppermute x1, starting transfers between devices, per_device(): column_a = lax.ppermute(near_send, 'gy', column_pairs(True))  14.3 us
    ppermute x12, waiting for transfers between devices, permute(): return lax.ppermute(value, AXES, partner_list(step))  13.8 us
    pallas_call x3, Pallas kernels, waves(): pl.pallas_call(functools.partial(wave_kernel, first), out_shape=out_shape...  9.35 us
    ppermute x1, waiting for transfers between devices, per_device(): lax.ppermute(jnp.where(even_y, left, right), 'gy', column_pairs(False))  7.56 us
    pallas_call x4, Pallas kernels, radial_piece(): pl.pallas_call(functools.partial(radial_kernel, near_cells, fresh), out_s...  6.72 us
    pallas_call x4, Pallas kernels, edge_piece(): pl.pallas_call(functools.partial(edge_kernel, along_x, which), out_shape=...  6.48 us
    ppermute x1, starting transfers between devices, per_device(): lax.ppermute(jnp.where(even_x, upper, lower), 'gx', row_pairs(False))  4.89 us
  transfers between devices with their start and end apart: 16, of which 10 were waited for; matrix products, arithmetic and copies ran while one was open for 1% of the time, Pallas kernels for 22%

profile of v6, /device:TPU:1, one launch (start us, length us, event | category | flops | bytes accessed | tf_op | source)
XLA Modules:
  0.0 94.8 jit_solution(11496655637375853135)
XLA Ops:
  0.2 4.2 %wave_tables.3 = (bf16[1024,512]{1,0:T(8,128)(2,1)}, bf16[1024,512]{1,0:T(8,128)(2,1)}, bf16[512,512]{1,0:T(8,128)(2,1)S(1)}, bf16[256,1024]{1,0:T(8,128)(2,1)S(...) custom-call(s32[2]{0:T(128)S(1)} %pad_add_fusion.place, bf16[2,3,4,128]{3,2,1,0:T(4,128)(2,1)} %bitcast.18, ...), custom_call_target="tpu_custom_call" | custom-call | flops 2048000000 | bytes 3000000 | tf_op jit(solution)/shard_map/wave_tables/pallas_call | solution.py:193
  4.4 3.3 %collective-permute-start = (bf16[512,512]{1,0:T(8,128)(2,1)S(1)}, bf16[512,512]{1,0:T(8,128)(2,1)S(1)}, u32[]{:S(2)}, u32[]{:S(2)}) collective-permute-start(bf16[512,512]{1,0:T(8,128)(2,1)S(1)} %get-tuple-element.53), channel_id=1, source_target_pairs={{0,1},{1,0},{16,17},{17,16},{32,33},{33,32},{48,49},{49,48},{2,3},... | collective-permute-start | bytes 1572872 | tf_op jit(solution)/shard_map/ppermute | solution.py:66
  7.8 4.9 %collective-permute-start.9 = (bf16[4,144,256]{2,1,0:T(8,128)(2,1)S(1)}, bf16[4,144,256]{2,1,0:T(8,128)(2,1)S(1)}, u32[]{:S(2)}, u32[]{:S(2)}) collective-permute-start(bf16[4,144,256]{2,1,0:T(8,128)(2,1)S(1)} %get-tuple-element.101), channel_id=1, source_target_pairs={{0,240},{16,32},{32,16},{48,64},{64,48},{80,96},{96,80},{112,128},... | collective-permute-start | bytes 884744 | tf_op jit(solution)/shard_map/ppermute | solution.py:471
  12.8 2.6 %wave_tables.4 = (bf16[1024,256]{1,0:T(8,128)(2,1)}, bf16[1024,256]{1,0:T(8,128)(2,1)}, f32[256,512]{1,0:T(8,128)S(1)}) custom-call(s32[2]{0:T(128)S(1)} %pad_add_fusion.place, bf16[2,3,4,128]{3,2,1,0:T(4,128)(2,1)S(1)} %bitcast.19, s32[3,1024]{1,0:T(4,128)S(1)} %copy-done.3, s32[1,256]{1,0:T(1,128)S(1)} %get-tuple-element.110.order, ...), custom_call_target="tpu_custom_call" | custom-call | flops 1024000000 | bytes 3000000 | tf_op jit(solution)/shard_map/wave_tables/pallas_call | solution.py:193
  15.6 1.4 %collective-permute-start.1 = (bf16[256,512]{1,0:T(8,128)(2,1)S(1)}, bf16[256,512]{1,0:T(8,128)(2,1)S(1)}, u32[]{:S(2)}, u32[]{:S(2)}) collective-permute-start(bf16[256,512]{1,0:T(8,128)(2,1)S(1)} %add_convert_fusion), channel_id=1, source_target_pairs={{0,64},{1,5},{16,80},{17,21},{32,96},{33,37},{48,112},{49,53},{2,6... | collective-permute-start | bytes 786440 | tf_op jit(solution)/shard_map/ppermute | solution.py:66
  17.0 2.6 %wave_tables.5 = (bf16[1024,256]{1,0:T(8,128)(2,1)}, bf16[1024,256]{1,0:T(8,128)(2,1)}, f32[256,512]{1,0:T(8,128)S(1)}) custom-call(s32[2]{0:T(128)S(1)} %pad_add_fusion.place, bf16[2,3,4,128]{3,2,1,0:T(4,128)(2,1)S(1)} %bitcast.20, s32[3,1024]{1,0:T(4,128)S(1)} %copy-done.3, s32[1,256]{1,0:T(1,128)S(1)} %get-tuple-element.109.order, ...), custom_call_target="tpu_custom_call" | custom-call | flops 1024000000 | bytes 3000000 | tf_op jit(solution)/shard_map/wave_tables/pallas_call | solution.py:193
  19.6 1.3 %radial_prepare.1 = (f32[8,9]{1,0:T(8,128)S(1)}, f32[8,3,128,128]{3,2,1,0:T(8,128)S(1)}, f32[64,256]{1,0:T(8,128)S(1)}) custom-call(s32[2]{0:T(128)S(1)} %pad_add_fusion.place, s32[8]{0:T(128)S(1)} %reshape.729.near_count, s32[8,9]{1,0:T(8,128)S(1)} %bitcast.22, bf16[2,3,4,128]{3,2,1,0:T(4,128)(2,1)S(1)} %bitcast.21, bf16[4,256]{1,0:T(4,128)(2,1)S(1)} %copy-done.7), custom_call_target="tpu_custom_call" | custom-call | flops 500000000 | bytes 100000 | tf_op jit(solution)/shard_map/radial_prepare/pallas_call | solution.py:235
  21.3 2.8 %collective-permute-start.2 = (bf16[128,512]{1,0:T(8,128)(2,1)S(1)}, bf16[128,512]{1,0:T(8,128)(2,1)S(1)}, u32[]{:S(2)}, u32[]{:S(2)}) collective-permute-start(bf16[128,512]{1,0:T(8,128)(2,1)S(1)} %get-tuple-element.60), channel_id=1, source_target_pairs={{0,192},{1,13},{16,208},{17,29},{32,224},{33,45},{48,240},{49,61},... | collective-permute-start | bytes 393224 | tf_op jit(solution)/shard_map/ppermute | solution.py:66
  24.1 1.4 %radial_piece.4.rest_2_ = f32[8,128,256]{2,1,0:T(8,128)S(1)} custom-call(f32[8]{0:T(128)S(1)} %copy-done.9, f32[8,9]{1,0:T(8,128)S(1)} %get-tuple-element.61.live, bf16[8,256]{1,0:T(8,128)(2,1)S(1)} %copy-done.6, f32[8,3,128,128]{3,2,1,0:T(8,128)S(1)} %get-tuple-element.62.mine, bf16[4,144,256]{2,1,0:T(8,128)(2,1)S(1)} %get-tuple-element.63.rest_0_, ...), custom_call_target="tpu_custom_call" | custom-call | flops 2000000000 | bytes 2000000 | tf_op jit(solution)/shard_map/radial_piece/pallas_call | solution.py:290
  25.5 1.1 %collective-permute-done.2 = bf16[128,512]{1,0:T(8,128)(2,1)S(1)} collective-permute-done((bf16[128,512]{1,0:T(8,128)(2,1)S(1)}, bf16[128,512]{1,0:T(8,128)(2,1)S(1)}, u32[]{:S(2)}, u32[]{:S(2)}) %collective-permute-start.2) | collective-permute-done | bytes 131104 | tf_op jit(solution)/shard_map/ppermute | solution.py:66
  26.7 1.9 %radial_piece.5.rest_2_ = f32[8,128,256]{2,1,0:T(8,128)S(1)} custom-call(f32[8]{0:T(128)S(1)} %copy-done.9, f32[8,9]{1,0:T(8,128)S(1)} %get-tuple-element.61.live, bf16[8,256]{1,0:T(8,128)(2,1)S(1)} %copy-done.6, f32[8,3,128,128]{3,2,1,0:T(8,128)S(1)} %get-tuple-element.62.mine, ...), custom_call_target="tpu_custom_call", output_to_operand_aliasing={{}: (6, {})} | custom-call | flops 2000000000 | bytes 2000000 | tf_op jit(solution)/shard_map/radial_piece/pallas_call | solution.py:290
  28.6 1.2 %collective-permute-done.3 = bf16[64,512]{1,0:T(8,128)(2,1)S(1)} collective-permute-done((bf16[64,512]{1,0:T(8,128)(2,1)S(1)}, bf16[64,512]{1,0:T(8,128)(2,1)S(1)}, u32[]{:S(2)}, u32[]{:S(2)}) %collective-permute-start.3) | collective-permute-done | bytes 65568 | tf_op jit(solution)/shard_map/ppermute | solution.py:66
  30.7 1.9 %radial_piece.6.rest_2_ = f32[8,128,256]{2,1,0:T(8,128)S(1)} custom-call(f32[8]{0:T(128)S(1)} %copy-done.9, f32[8,9]{1,0:T(8,128)S(1)} %get-tuple-element.61.live, bf16[8,256]{1,0:T(8,128)(2,1)S(1)} %copy-done.6, f32[8,3,128,128]{3,2,1,0:T(8,128)S(1)} %get-tuple-element.62.mine, ...), custom_call_target="tpu_custom_call", output_to_operand_aliasing={{}: (6, {})} | custom-call | flops 2000000000 | bytes 2000000 | tf_op jit(solution)/shard_map/radial_piece/pallas_call | solution.py:290
  32.6 2.2 %collective-permute-done.4 = bf16[64,768]{1,0:T(8,128)(2,1)S(1)} collective-permute-done((bf16[64,768]{1,0:T(8,128)(2,1)S(1)}, bf16[64,768]{1,0:T(8,128)(2,1)S(1)}, u32[]{:S(2)}, u32[]{:S(2)}) %collective-permute-start.4) | collective-permute-done | bytes 98336 | tf_op jit(solution)/shard_map/ppermute | solution.py:66
  34.8 3.3 %collective-permute-start.5 = (bf16[64,768]{1,0:T(8,128)(2,1)S(1)}, bf16[64,768]{1,0:T(8,128)(2,1)S(1)}, u32[]{:S(2)}, u32[]{:S(2)}) collective-permute-start(bf16[64,768]{1,0:T(8,128)(2,1)S(1)} %convert_element_type.67), channel_id=1, source_target_pairs={{0,16},{1,51},{16,0},{17,33},{32,48},{33,17},{48,32},{49,3},{2,18}... | collective-permute-start | bytes 294920 | tf_op jit(solution)/shard_map/ppermute | solution.py:66
  38.1 1.6 %radial_piece.7.start = f32[8,128,256]{2,1,0:T(8,128)S(1)} custom-call(f32[8]{0:T(128)S(1)} %copy-done.9, f32[8,9]{1,0:T(8,128)S(1)} %get-tuple-element.61.live, bf16[8,256]{1,0:T(8,128)(2,1)S(1)} %copy-done.6, f32[8,3,128,128]{3,2,1,0:T(8,128)S(1)} %get-tuple-element.62.mine, ...), custom_call_target="tpu_custom_call", output_to_operand_aliasing={{}: (6, {})} | custom-call | flops 2000000000 | bytes 2000000 | tf_op jit(solution)/shard_map/radial_piece/pallas_call | solution.py:290
  40.3 1.8 %radial_edge.4.start = f32[8,128,256]{2,1,0:T(8,128)S(1)} custom-call(s32[4]{0:T(128)S(1)} %pad_add_fusion.1.sides, f32[8]{0:T(128)S(1)} %copy-done.9, f32[8,9]{1,0:T(8,128)S(1)} %get-tuple-element.61.live, bf16[8,256]{1,0:T(8,128)(2,1)S(1)} %copy-done.6, f32[8,3,128,128]{3,2,1,0:T(8,128)S(1)} %get-tuple-element.62.mine, ...), custom_call_target="tpu_custom_call", output_to_operand_aliasing={{}: (6, {})} | custom-call | flops 2000000000 | bytes 2000000 | tf_op jit(solution)/shard_map/radial_edge/pallas_call | solution.py:361
  42.1 1.6 %collective-permute-done.6 = bf16[64,768]{1,0:T(8,128)(2,1)S(1)} collective-permute-done((bf16[64,768]{1,0:T(8,128)(2,1)S(1)}, bf16[64,768]{1,0:T(8,128)(2,1)S(1)}, u32[]{:S(2)}, u32[]{:S(2)}) %collective-permute-start.6) | collective-permute-done | bytes 98336 | tf_op jit(solution)/shard_map/ppermute | solution.py:66
  43.8 3.3 %collective-permute-start.8 = (bf16[64,768]{1,0:T(8,128)(2,1)S(1)}, bf16[64,768]{1,0:T(8,128)(2,1)S(1)}, u32[]{:S(2)}, u32[]{:S(2)}) collective-permute-start(bf16[64,768]{1,0:T(8,128)(2,1)S(1)} %convert_element_type.71), channel_id=1, source_target_pairs={{0,48},{1,19},{16,34},{17,3},{32,18},{33,51},{48,0},{49,35},{2,50}... | collective-permute-start | bytes 294920 | tf_op jit(solution)/shard_map/ppermute | solution.py:66
  47.1 1.8 %radial_edge.5 = f32[8,128,256]{2,1,0:T(8,128)S(1)} custom-call(s32[4]{0:T(128)S(1)} %pad_add_fusion.1.sides, f32[8]{0:T(128)S(1)} %copy-done.9, f32[8,9]{1,0:T(8,128)S(1)} %get-tuple-element.61.live, bf16[8,256]{1,0:T(8,128)(2,1)S(1)} %copy-done.6, f32[8,3,128,128]{3,2,1,0:T(8,128)S(1)} %get-tuple-element.62.mine, ...), custom_call_target="tpu_custom_call", output_to_operand_aliasing={{}: (6, {})} | custom-call | flops 2000000000 | bytes 2000000 | tf_op jit(solution)/shard_map/radial_edge/pallas_call | solution.py:361
  48.9 1.4 %collective-permute-done.8 = bf16[64,768]{1,0:T(8,128)(2,1)S(1)} collective-permute-done((bf16[64,768]{1,0:T(8,128)(2,1)S(1)}, bf16[64,768]{1,0:T(8,128)(2,1)S(1)}, u32[]{:S(2)}, u32[]{:S(2)}) %collective-permute-start.8) | collective-permute-done | bytes 98336 | tf_op jit(solution)/shard_map/ppermute | solution.py:66
  50.6 3.0 %collective-permute-done.10 = bf16[64,512]{1,0:T(8,128)(2,1)S(1)} collective-permute-done((bf16[64,512]{1,0:T(8,128)(2,1)S(1)}, bf16[64,512]{1,0:T(8,128)(2,1)S(1)}, u32[]{:S(2)}, u32[]{:S(2)}) %collective-permute-start.10) | collective-permute-done | bytes 65568 | tf_op jit(solution)/shard_map/ppermute | solution.py:66
  53.6 14.3 %collective-permute-start.13 = (bf16[4,144,256]{2,1,0:T(8,128)(2,1)S(1)}, bf16[4,144,256]{2,1,0:T(8,128)(2,1)S(1)}, u32[]{:S(2)}, u32[]{:S(2)}) collective-permute-start(bf16[4,144,256]{2,1,0:T(8,128)(2,1)S(1)} %get-tuple-element.87), channel_id=1, source_target_pairs={{0,1},{1,0},{2,3},{3,2},{4,5},{5,4},{6,7},{7,6},{8,9},{9,8},{10,11... | collective-permute-start | bytes 884744 | tf_op jit(solution)/shard_map/ppermute | solution.py:528
  67.9 2.7 %collective-permute-start.11 = (bf16[128,512]{1,0:T(8,128)(2,1)S(1)}, bf16[128,512]{1,0:T(8,128)(2,1)S(1)}, u32[]{:S(2)}, u32[]{:S(2)}) collective-permute-start(bf16[128,512]{1,0:T(8,128)(2,1)S(1)} %pad_maximum_fusion.5.coef), channel_id=1, source_target_pairs={{0,192},{1,13},{16,208},{17,29},{32,224},{33,45},{48,240},{49,61},... | collective-permute-start | bytes 393224 | tf_op jit(solution)/shard_map/ppermute | solution.py:66
  70.7 3.5 %collective-permute-start.15 = (bf16[4,144,256]{2,1,0:T(8,128)(2,1)S(1)}, bf16[4,144,256]{2,1,0:T(8,128)(2,1)S(1)}, u32[]{:S(2)}, u32[]{:S(2)}) collective-permute-start(bf16[4,144,256]{2,1,0:T(8,128)(2,1)S(1)} %get-tuple-element.95), channel_id=1, source_target_pairs={{0,15},{1,2},{2,1},{3,4},{4,3},{5,6},{6,5},{7,8},{8,7},{9,10},{10,... | collective-permute-start | bytes 884744 | tf_op jit(solution)/shard_map/ppermute | solution.py:524
  74.6 1.1 %collective-permute-start.12 = (bf16[256,512]{1,0:T(8,128)(2,1)S(1)}, bf16[256,512]{1,0:T(8,128)(2,1)S(1)}, u32[]{:S(2)}, u32[]{:S(2)}) collective-permute-start(bf16[256,512]{1,0:T(8,128)(2,1)S(1)} %pad_maximum_fusion.3.coef), channel_id=1, source_target_pairs={{0,64},{1,5},{16,80},{17,21},{32,96},{33,37},{48,112},{49,53},{2,6... | collective-permute-start | bytes 786440 | tf_op jit(solution)/shard_map/ppermute | solution.py:66
  75.7 1.4 %radial_edge.6 = f32[8,128,256]{2,1,0:T(8,128)S(1)} custom-call(s32[4]{0:T(128)S(1)} %pad_add_fusion.1.sides, f32[8]{0:T(128)S(1)} %copy-done.9, f32[8,9]{1,0:T(8,128)S(1)} %get-tuple-element.61.live, bf16[8,256]{1,0:T(8,128)(2,1)S(1)} %copy-done.6, f32[8,3,128,128]{3,2,1,0:T(8,128)S(1)} %get-tuple-element.62.mine, ...), custom_call_target="tpu_custom_call", output_to_operand_aliasing={{}: (6, {})} | custom-call | flops 2000000000 | bytes 2000000 | tf_op jit(solution)/shard_map/radial_edge/pallas_call | solution.py:361
  77.6 2.6 %collective-permute-done.12 = bf16[256,512]{1,0:T(8,128)(2,1)S(1)} collective-permute-done((bf16[256,512]{1,0:T(8,128)(2,1)S(1)}, bf16[256,512]{1,0:T(8,128)(2,1)S(1)}, u32[]{:S(2)}, u32[]{:S(2)}) %collective-permute-start.12) | collective-permute-done | bytes 262176 | tf_op jit(solution)/shard_map/ppermute | solution.py:66
  80.3 1.0 %collective-permute-start.14 = (bf16[512,512]{1,0:T(8,128)(2,1)S(1)}, bf16[512,512]{1,0:T(8,128)(2,1)S(1)}, u32[]{:S(2)}, u32[]{:S(2)}) collective-permute-start(bf16[512,512]{1,0:T(8,128)(2,1)S(1)} %pad_maximum_fusion.coef), channel_id=1, source_target_pairs={{0,1},{1,0},{16,17},{17,16},{32,33},{33,32},{48,49},{49,48},{2,3},... | collective-permute-start | bytes 1572872 | tf_op jit(solution)/shard_map/ppermute | solution.py:66
  81.3 7.6 %collective-permute-done.15.block = bf16[4,144,256]{2,1,0:T(8,128)(2,1)S(1)} collective-permute-done((bf16[4,144,256]{2,1,0:T(8,128)(2,1)S(1)}, bf16[4,144,256]{2,1,0:T(8,128)(2,1)S(1)}, u32[]{:S(2)}, u32[]{:S(2)}) %collective-permute-start.15) | collective-permute-done | bytes 294944 | tf_op jit(solution)/shard_map/ppermute | solution.py:524
  88.8 1.4 %radial_edge.7 = f32[8,128,256]{2,1,0:T(8,128)S(1)} custom-call(s32[4]{0:T(128)S(1)} %pad_add_fusion.1.sides, f32[8]{0:T(128)S(1)} %copy-done.9, f32[8,9]{1,0:T(8,128)S(1)} %get-tuple-element.61.live, bf16[8,256]{1,0:T(8,128)(2,1)S(1)} %copy-done.6, f32[8,3,128,128]{3,2,1,0:T(8,128)S(1)} %get-tuple-element.62.mine, ...), custom_call_target="tpu_custom_call", output_to_operand_aliasing={{}: (6, {})} | custom-call | flops 2000000000 | bytes 2000000 | tf_op jit(solution)/shard_map/radial_edge/pallas_call | solution.py:361
  92.2 2.4 %mix_and_network.1 = bf16[1024,256]{1,0:T(8,128)(2,1)} custom-call(bf16[1024,512]{1,0:T(8,128)(2,1)S(1)} %copy-done.14, bf16[1024,512]{1,0:T(8,128)(2,1)S(1)} %copy-done.15, bf16[512,512]{1,0:T(8,128)(2,1)S(1)} %collective-permute-done.14.coef, bf16[1024,256]{1,0:T(8,128)(2,1)S(1)} %bitcast.17, f32[1024,256]{1,0:T(8,128)S(1)} %recip_piece.5.acc, ...), custom_call_target="tpu_custom_call" | custom-call | flops 3000000000 | bytes 8000000 | tf_op jit(solution)/shard_map/mix_and_network/pallas_call | solution.py:421
  (79 shorter events, 5.6 us)
Async XLA Ops:
  0.2 12.6 %copy-start.16 = (s32[2,4]{1,0:T(2,128)S(1)}, s32[2,4]{1,0:T(2,128)}, u32[]{:S(2)}) copy-start(s32[2,4]{1,0:T(2,128)} %param.14) | copy-start | bytes 100
  0.2 12.6 %copy-start.3 = (s32[3,1024]{1,0:T(4,128)S(1)}, s32[3,1024]{1,0:T(4,128)}, u32[]{:S(2)}) copy-start(s32[3,1024]{1,0:T(4,128)} %miller.5) | copy-start | bytes 36868
  0.2 12.6 %copy-start.4 = (bf16[2,4,3,128]{3,1,2,0:T(4,128)(2,1)S(1)}, bf16[2,4,3,128]{3,1,2,0:T(4,128)(2,1)}, u32[]{:S(2)}) copy-start(bf16[2,4,3,128]{3,1,2,0:T(4,128)(2,1)} %param.12) | copy-start | bytes 18436
  4.4 11.2 %collective-permute-start = (bf16[512,512]{1,0:T(8,128)(2,1)S(1)}, bf16[512,512]{1,0:T(8,128)(2,1)S(1)}, u32[]{:S(2)}, u32[]{:S(2)}) collective-permute-start(bf16[512,512]{1,0:T(8,128)(2,1)S(1)} %get-tuple-element.53), channel_id=1, source_target_pairs={{0,1},{1,0},{16,17},{17,16},{32,33},{33,32},{48,49},{49,48},{2,3},... | collective-permute-start | bytes 1572872 | tf_op jit(solution)/shard_map/ppermute | solution.py:66
  7.7 32.5 %collective-permute-start.7 = (bf16[4,144,256]{2,1,0:T(8,128)(2,1)S(1)}, bf16[4,144,256]{2,1,0:T(8,128)(2,1)S(1)}, u32[]{:S(2)}, u32[]{:S(2)}) collective-permute-start(bf16[4,144,256]{2,1,0:T(8,128)(2,1)S(1)} %get-tuple-element.102), channel_id=1, source_target_pairs={{0,16},{16,0},{32,48},{48,32},{64,80},{80,64},{96,112},{112,96},{1... | collective-permute-start | bytes 884744 | tf_op jit(solution)/shard_map/ppermute | solution.py:470
  7.8 39.3 %collective-permute-start.9 = (bf16[4,144,256]{2,1,0:T(8,128)(2,1)S(1)}, bf16[4,144,256]{2,1,0:T(8,128)(2,1)S(1)}, u32[]{:S(2)}, u32[]{:S(2)}) collective-permute-start(bf16[4,144,256]{2,1,0:T(8,128)(2,1)S(1)} %get-tuple-element.101), channel_id=1, source_target_pairs={{0,240},{16,32},{32,16},{48,64},{64,48},{80,96},{96,80},{112,128},... | collective-permute-start | bytes 884744 | tf_op jit(solution)/shard_map/ppermute | solution.py:471
  15.6 5.6 %collective-permute-start.1 = (bf16[256,512]{1,0:T(8,128)(2,1)S(1)}, bf16[256,512]{1,0:T(8,128)(2,1)S(1)}, u32[]{:S(2)}, u32[]{:S(2)}) collective-permute-start(bf16[256,512]{1,0:T(8,128)(2,1)S(1)} %add_convert_fusion), channel_id=1, source_target_pairs={{0,64},{1,5},{16,80},{17,21},{32,96},{33,37},{48,112},{49,53},{2,6... | collective-permute-start | bytes 786440 | tf_op jit(solution)/shard_map/ppermute | solution.py:66
  17.0 2.6 %copy-start.5 = (s32[2,4,9]{2,1,0:T(4,128)S(1)}, s32[2,4,9]{2,1,0:T(4,128)}, u32[]{:S(2)}) copy-start(s32[2,4,9]{2,1,0:T(4,128)} %param.13) | copy-start | bytes 868
  17.0 2.6 %copy-start.7 = (bf16[4,256]{1,0:T(4,128)(2,1)S(1)}, bf16[4,256]{1,0:T(4,128)(2,1)}, u32[]{:S(2)}) copy-start(bf16[4,256]{1,0:T(4,128)(2,1)} %row_filter.1) | copy-start | bytes 6148
  20.9 3.2 %copy-start.6 = (bf16[8,256]{1,0:T(8,128)(2,1)S(1)}, bf16[8,256]{1,0:T(8,128)(2,1)}, u32[]{:S(2)}) copy-start(bf16[8,256]{1,0:T(8,128)(2,1)} %filters.15) | copy-start | bytes 12292
  20.9 3.2 %copy-start.9 = (f32[8]{0:T(128)S(1)}, f32[8]{0:T(128)}, u32[]{:S(2)}) copy-start(f32[8]{0:T(128)} %rates.15) | copy-start | bytes 100
  21.3 5.3 %collective-permute-start.2 = (bf16[128,512]{1,0:T(8,128)(2,1)S(1)}, bf16[128,512]{1,0:T(8,128)(2,1)S(1)}, u32[]{:S(2)}, u32[]{:S(2)}) collective-permute-start(bf16[128,512]{1,0:T(8,128)(2,1)S(1)} %get-tuple-element.60), channel_id=1, source_target_pairs={{0,192},{1,13},{16,208},{17,29},{32,224},{33,45},{48,240},{49,61},... | collective-permute-start | bytes 393224 | tf_op jit(solution)/shard_map/ppermute | solution.py:66
  26.6 3.2 %collective-permute-start.3 = (bf16[64,512]{1,0:T(8,128)(2,1)S(1)}, bf16[64,512]{1,0:T(8,128)(2,1)S(1)}, u32[]{:S(2)}, u32[]{:S(2)}) collective-permute-start(bf16[64,512]{1,0:T(8,128)(2,1)S(1)} %fusion.1), channel_id=1, source_target_pairs={{0,4},{1,65},{16,20},{17,81},{32,36},{33,97},{48,52},{49,113},{2,6... | collective-permute-start | bytes 196616 | tf_op jit(solution)/shard_map/ppermute | solution.py:66
  29.9 4.9 %collective-permute-start.4 = (bf16[64,768]{1,0:T(8,128)(2,1)S(1)}, bf16[64,768]{1,0:T(8,128)(2,1)S(1)}, u32[]{:S(2)}, u32[]{:S(2)}) collective-permute-start(bf16[64,768]{1,0:T(8,128)(2,1)S(1)} %convert_element_type.65), channel_id=1, source_target_pairs={{0,12},{1,193},{16,28},{17,209},{32,44},{33,225},{48,60},{49,241},... | collective-permute-start | bytes 294920 | tf_op jit(solution)/shard_map/ppermute | solution.py:66
  34.8 5.3 %collective-permute-start.5 = (bf16[64,768]{1,0:T(8,128)(2,1)S(1)}, bf16[64,768]{1,0:T(8,128)(2,1)S(1)}, u32[]{:S(2)}, u32[]{:S(2)}) collective-permute-start(bf16[64,768]{1,0:T(8,128)(2,1)S(1)} %convert_element_type.67), channel_id=1, source_target_pairs={{0,16},{1,51},{16,0},{17,33},{32,48},{33,17},{48,32},{49,3},{2,18}... | collective-permute-start | bytes 294920 | tf_op jit(solution)/shard_map/ppermute | solution.py:66
  40.2 3.6 %collective-permute-start.6 = (bf16[64,768]{1,0:T(8,128)(2,1)S(1)}, bf16[64,768]{1,0:T(8,128)(2,1)S(1)}, u32[]{:S(2)}, u32[]{:S(2)}) collective-permute-start(bf16[64,768]{1,0:T(8,128)(2,1)S(1)} %convert_element_type.69), channel_id=1, source_target_pairs={{0,50},{1,17},{16,32},{17,1},{32,16},{33,49},{48,2},{49,33},{2,48}... | collective-permute-start | bytes 294920 | tf_op jit(solution)/shard_map/ppermute | solution.py:66
  43.8 6.6 %collective-permute-start.8 = (bf16[64,768]{1,0:T(8,128)(2,1)S(1)}, bf16[64,768]{1,0:T(8,128)(2,1)S(1)}, u32[]{:S(2)}, u32[]{:S(2)}) collective-permute-start(bf16[64,768]{1,0:T(8,128)(2,1)S(1)} %convert_element_type.71), channel_id=1, source_target_pairs={{0,48},{1,19},{16,34},{17,3},{32,18},{33,51},{48,0},{49,35},{2,50}... | collective-permute-start | bytes 294920 | tf_op jit(solution)/shard_map/ppermute | solution.py:66
  48.9 25.2 %copy-start.12 = (bf16[1024,256]{1,0:T(8,128)(2,1)S(1)}, bf16[1024,256]{1,0:T(8,128)(2,1)}, u32[]{:S(2)}) copy-start(bf16[1024,256]{1,0:T(8,128)(2,1)} %get-tuple-element.83.cos_ref) | copy-start | bytes 1572868
  48.9 25.2 %copy-start.13 = (bf16[1024,256]{1,0:T(8,128)(2,1)S(1)}, bf16[1024,256]{1,0:T(8,128)(2,1)}, u32[]{:S(2)}) copy-start(bf16[1024,256]{1,0:T(8,128)(2,1)} %get-tuple-element.84.sin_ref) | copy-start | bytes 1572868
  50.4 3.2 %collective-permute-start.10 = (bf16[64,512]{1,0:T(8,128)(2,1)S(1)}, bf16[64,512]{1,0:T(8,128)(2,1)S(1)}, u32[]{:S(2)}, u32[]{:S(2)}) collective-permute-start(bf16[64,512]{1,0:T(8,128)(2,1)S(1)} %pad_maximum_fusion.6), channel_id=1, source_target_pairs={{0,4},{1,65},{16,20},{17,81},{32,36},{33,97},{48,52},{49,113},{2,6... | collective-permute-start | bytes 196616 | tf_op jit(solution)/shard_map/ppermute | solution.py:66
  53.6 22.1 %collective-permute-start.13 = (bf16[4,144,256]{2,1,0:T(8,128)(2,1)S(1)}, bf16[4,144,256]{2,1,0:T(8,128)(2,1)S(1)}, u32[]{:S(2)}, u32[]{:S(2)}) collective-permute-start(bf16[4,144,256]{2,1,0:T(8,128)(2,1)S(1)} %get-tuple-element.87), channel_id=1, source_target_pairs={{0,1},{1,0},{2,3},{3,2},{4,5},{5,4},{6,7},{7,6},{8,9},{9,8},{10,11... | collective-permute-start | bytes 884744 | tf_op jit(solution)/shard_map/ppermute | solution.py:528
  67.9 6.7 %collective-permute-start.11 = (bf16[128,512]{1,0:T(8,128)(2,1)S(1)}, bf16[128,512]{1,0:T(8,128)(2,1)S(1)}, u32[]{:S(2)}, u32[]{:S(2)}) collective-permute-start(bf16[128,512]{1,0:T(8,128)(2,1)S(1)} %pad_maximum_fusion.5.coef), channel_id=1, source_target_pairs={{0,192},{1,13},{16,208},{17,29},{32,224},{33,45},{48,240},{49,61},... | collective-permute-start | bytes 393224 | tf_op jit(solution)/shard_map/ppermute | solution.py:66
  70.7 18.2 %collective-permute-start.15 = (bf16[4,144,256]{2,1,0:T(8,128)(2,1)S(1)}, bf16[4,144,256]{2,1,0:T(8,128)(2,1)S(1)}, u32[]{:S(2)}, u32[]{:S(2)}) collective-permute-start(bf16[4,144,256]{2,1,0:T(8,128)(2,1)S(1)} %get-tuple-element.95), channel_id=1, source_target_pairs={{0,15},{1,2},{2,1},{3,4},{4,3},{5,6},{6,5},{7,8},{8,7},{9,10},{10,... | collective-permute-start | bytes 884744 | tf_op jit(solution)/shard_map/ppermute | solution.py:524
  74.6 5.6 %collective-permute-start.12 = (bf16[256,512]{1,0:T(8,128)(2,1)S(1)}, bf16[256,512]{1,0:T(8,128)(2,1)S(1)}, u32[]{:S(2)}, u32[]{:S(2)}) collective-permute-start(bf16[256,512]{1,0:T(8,128)(2,1)S(1)} %pad_maximum_fusion.3.coef), channel_id=1, source_target_pairs={{0,64},{1,5},{16,80},{17,21},{32,96},{33,37},{48,112},{49,53},{2,6... | collective-permute-start | bytes 786440 | tf_op jit(solution)/shard_map/ppermute | solution.py:66
  80.3 10.0 %copy-start.10 = (bf16[1024,256]{1,0:T(8,128)(2,1)S(1)}, bf16[1024,256]{1,0:T(8,128)(2,1)}, u32[]{:S(2)}) copy-start(bf16[1024,256]{1,0:T(8,128)(2,1)} %get-tuple-element.90.cos_ref) | copy-start | bytes 1572868
  80.3 10.0 %copy-start.11 = (bf16[1024,256]{1,0:T(8,128)(2,1)S(1)}, bf16[1024,256]{1,0:T(8,128)(2,1)}, u32[]{:S(2)}) copy-start(bf16[1024,256]{1,0:T(8,128)(2,1)} %get-tuple-element.91.sin_ref) | copy-start | bytes 1572868
  80.3 10.6 %collective-permute-start.14 = (bf16[512,512]{1,0:T(8,128)(2,1)S(1)}, bf16[512,512]{1,0:T(8,128)(2,1)S(1)}, u32[]{:S(2)}, u32[]{:S(2)}) collective-permute-start(bf16[512,512]{1,0:T(8,128)(2,1)S(1)} %pad_maximum_fusion.coef), channel_id=1, source_target_pairs={{0,1},{1,0},{16,17},{17,16},{32,33},{33,32},{48,49},{49,48},{2,3},... | collective-permute-start | bytes 1572872 | tf_op jit(solution)/shard_map/ppermute | solution.py:66
  90.3 1.1 %copy-start.1 = (bf16[256,512]{1,0:T(8,128)(2,1)S(1)}, bf16[256,512]{1,0:T(8,128)(2,1)}, u32[]{:S(2)}) copy-start(bf16[256,512]{1,0:T(8,128)(2,1)} %w_in.1) | copy-start | bytes 786436
  90.3 1.2 %copy-start.2 = (bf16[512,256]{1,0:T(8,128)(2,1)S(1)}, bf16[512,256]{1,0:T(8,128)(2,1)}, u32[]{:S(2)}) copy-start(bf16[512,256]{1,0:T(8,128)(2,1)} %w_out.1) | copy-start | bytes 786436
  90.3 1.2 %copy-start.8 = (f32[256]{0:T(256)S(1)}, f32[256]{0:T(256)}, u32[]{:S(2)}) copy-start(f32[256]{0:T(256)} %param.19) | copy-start | bytes 3076
  90.4 1.5 %copy-start.14 = (bf16[1024,512]{1,0:T(8,128)(2,1)S(1)}, bf16[1024,512]{1,0:T(8,128)(2,1)}, u32[]{:S(2)}) copy-start(bf16[1024,512]{1,0:T(8,128)(2,1)} %get-tuple-element.49.cos_ref) | copy-start | bytes 3145732
  90.4 1.8 %copy-start.15 = (bf16[1024,512]{1,0:T(8,128)(2,1)S(1)}, bf16[1024,512]{1,0:T(8,128)(2,1)}, u32[]{:S(2)}) copy-start(bf16[1024,512]{1,0:T(8,128)(2,1)} %get-tuple-element.50.sin_ref) | copy-start | bytes 3145732
  (1 other events, 1.0 us)

commit v7 on v6

--- a/solution.py
+++ b/solution.py
@@ -39,11 +39,16 @@
     return x, y, z, 1 - core
 
 
-def flip_plane(first, second):
+def flip_x(first, second):
     def step(x, y, z, core):
-        if core == 0:
-            return x ^ first, y ^ second, z, core
-        return x ^ second, y ^ first, z, core
+        return x ^ (second if core else first), y, z, core
+
+    return step
+
+
+def flip_y(first, second):
+    def step(x, y, z, core):
+        return x, y ^ (second if core else first), z, core
 
     return step
 
@@ -57,8 +62,8 @@
     return step
 
 
-HALVING = (flip_core, flip_plane(1, 0), flip_plane(3, 0), flip_plane(0, 1))
-DOUBLING = (flip_plane(0, 3), flip_z(0), flip_z(1), flip_z(2))
+HALVING = (flip_core, flip_y(1, 3), flip_y(3, 1), flip_x(1, 3))
+DOUBLING = (flip_x(3, 1), flip_z(0), flip_z(1), flip_z(2))
 CHUNK = 64
 
 
@@ -81,12 +86,9 @@
     b2 = (pos // 128) % 2
     b1 = (pos // 256) % 2
     owner = core ^ (pos // 512)
-    main = jnp.where(owner == 0, x, y) ^ b1 ^ (3 * b2)
-    other = jnp.where(owner == 0, y, x)
-    coset = (other ^ (other >> 1)) & 1
-    side = (coset ^ b3) ^ (3 * mb)
-    ox = jnp.where(owner == 0, main, side)
-    oy = jnp.where(owner == 0, side, main)
+    oy = y ^ jnp.where(owner == 0, b1 ^ (3 * b2), (3 * b1) ^ b2)
+    coset = jnp.where(owner == 0, (x ^ (x >> 1)) & 1, x >> 1) ^ b3
+    ox = jnp.where(owner == 0, coset ^ (3 * mb), 2 * coset + mb)
     return linear(ox, oy, mz, owner) * 4 + rest
 
 
@@ -222,8 +224,7 @@
         for d in range(3):
             mine[c, d] = jnp.broadcast_to(columns[:, d : d + 1], (ATOMS, ATOMS))
     x, z = place[0] // 4, place[0] % 4 + 4 * ((place[1] // 2) % 2)
-    y, core = place[1] // 4, place[1] % 2
-    member = (jnp.where(core == 0, y, x) // 2) * 8 + z
+    member = jnp.where(place[1] % 2 == 0, x // 2, x % 2) * 8 + z
     whole = jnp.concatenate([row_filter[...].astype(F32)] * (CHUNK // 4), axis=0)
     slots = lax.broadcasted_iota(jnp.int32, (CHUNK, WIDTH), 0) // 4
     filters[...] = jnp.where(slots == member, whole, 0.0)
@@ -485,8 +486,21 @@
         if step == 2:
             send, live, mine, filters = barrier((send, live, mine, filters))
         elif step == 3:
-            send, acc = barrier((send, acc))
+            send, acc, row_a, row_b = barrier((send, acc, row_a, row_b))
         fresh = permute(send, HALVING[step])
+        if step == 3:
+            ends = [
+                (jnp.where(even_x, row_b[b : b + 1], row_a[b : b + 1]), jnp.where(even_x, row_a[b : b + 1], row_b[b : b + 1]))
+                for b in (0, CY - 1)
+            ]
+            left, right = (
+                jnp.concatenate([low, upper[b : b + 1], lower[b : b + 1], high], axis=0)
+                for b, (low, high) in zip((0, CY - 1), ends)
+            )
+            far_send, near_send = jnp.where(even_y, left, right), jnp.where(even_y, right, left)
+            far_send, near_send, acc = barrier((far_send, near_send, acc))
+            column_b = lax.ppermute(far_send, "gy", column_pairs(False))
+            column_a = lax.ppermute(near_send, "gy", column_pairs(True))
         if step == 1:
             across, place, send = barrier((across, place, send))
             cos_near, sin_near, keep = waves(place, turned, miller, order[:, :256], across, False)
@@ -500,6 +514,8 @@
     total = jnp.concatenate([keep + got.astype(F32), filters], axis=1)
     for step in range(4):
         total, acc = barrier((total, acc))
+        if step == 1:
+            total, column_a, column_b = barrier((total, column_a, column_b))
         fresh = permute(total.astype(BF16), DOUBLING[step])
         if step < 2:
             acc = own_piece(step + 2, acc)
@@ -508,25 +524,10 @@
         total = total + fresh.astype(F32)
     scale = total[:, 2 * WIDTH :]
     chunk = jnp.concatenate([total[:, :WIDTH] * scale, total[:, WIDTH : 2 * WIDTH] * scale], axis=1).astype(BF16)
-    chunk, row_a, row_b = barrier((chunk, row_a, row_b))
     for step, low_at, high_at in ((3, 0, 0), (2, 0, 128), (1, 128, 256), (0, 256, 512)):
         chunk, acc = barrier((chunk, acc))
         fresh = permute(chunk, HALVING[step])
-        if step == 3:
-            ends = [
-                (jnp.where(even_x, row_b[b : b + 1], row_a[b : b + 1]), jnp.where(even_x, row_a[b : b + 1], row_b[b : b + 1]))
-                for b in (0, CY - 1)
-            ]
-            left, right = (
-                jnp.concatenate([low, upper[b : b + 1], lower[b : b + 1], high], axis=0)
-                for b, (low, high) in zip((0, CY - 1), ends)
-            )
-            column_b = lax.ppermute(jnp.where(even_y, left, right), "gy", column_pairs(False))
-            near_send = jnp.where(even_y, right, left)
-        elif step == 2:
-            near_send, chunk = barrier((near_send, chunk))
-            column_a = lax.ppermute(near_send, "gy", column_pairs(True))
-        elif step == 1:
+        if step == 1:
             acc = beyond(False, 2, column_a, acc)
         elif step == 0:
             acc = beyond(False, 3, column_b, acc)

time: 94.9 us -> 94.7 us (level)
  waiting for transfers between devices: 21.3 us -> 18.4 us
  starting transfers between devices: 42.9 us -> 45.3 us
    ppermute x12, starting transfers between devices: 20.1 us -> 34.5 us  [permute(): return lax.ppermute(value, AXES, partner_list(step))]
    ppermute x1, starting transfers between devices: 14.3 us -> 1.65 us  [per_device(): column_a = lax.ppermute(near_send, 'gy', column_pairs(True))]
    ppermute x1, waiting for transfers between devices: 7.56 us -> 5.29 us  [per_device(): column_b = lax.ppermute(far_send, 'gy', column_pairs(False))]
  transfers between devices with their start and end apart: 16 -> 16, of which waited for: 10 -> 9; matrix products, arithmetic and copies ran while one was open for 1% -> 1% of each run, Pallas kernels for 22% -> 22%
where the time goes in v7:
time: 94.7 us; the launch traced here: 94.6 us
  starting transfers between devices  45.3 us (48%)
  Pallas kernels  27.6 us (29%)
  waiting for transfers between devices  18.4 us (19%)
  local copies, waits for them, and re-layouts  1.86 us (2%)
    ppermute x12, starting transfers between devices, permute(): return lax.ppermute(value, AXES, partner_list(step))  34.5 us
    ppermute x12, waiting for transfers between devices, permute(): return lax.ppermute(value, AXES, partner_list(step))  13.1 us
    pallas_call x3, Pallas kernels, waves(): pl.pallas_call(functools.partial(wave_kernel, first), out_shape=out_shape...  9.35 us
    pallas_call x4, Pallas kernels, radial_piece(): pl.pallas_call(functools.partial(radial_kernel, near_cells, fresh), out_s...  6.73 us
    pallas_call x4, Pallas kernels, edge_piece(): pl.pallas_call(functools.partial(edge_kernel, along_x, which), out_shape=...  6.49 us
    ppermute x1, waiting for transfers between devices, per_device(): column_b = lax.ppermute(far_send, 'gy', column_pairs(False))  5.29 us
    ppermute x1, starting transfers between devices, per_device(): lax.ppermute(jnp.where(even_x, upper, lower), 'gx', row_pairs(False))  4.89 us
    ppermute x1, starting transfers between devices, per_device(): column_b = lax.ppermute(far_send, 'gy', column_pairs(False))  4.2 us
  transfers between devices with their start and end apart: 16, of which 9 were waited for; matrix products, arithmetic and copies ran while one was open for 1% of the time, Pallas kernels for 22%

profile of v7, /device:TPU:1, one launch (start us, length us, event | category | flops | bytes accessed | tf_op | source)
XLA Modules:
  0.0 94.6 jit_solution(11349611852621692272)
XLA Ops:
  0.2 4.2 %wave_tables.3 = (bf16[1024,512]{1,0:T(8,128)(2,1)}, bf16[1024,512]{1,0:T(8,128)(2,1)}, bf16[512,512]{1,0:T(8,128)(2,1)S(1)}, bf16[256,1024]{1,0:T(8,128)(2,1)S(...) custom-call(s32[2]{0:T(128)S(1)} %pad_add_fusion.place, bf16[2,3,4,128]{3,2,1,0:T(4,128)(2,1)} %bitcast.18, ...), custom_call_target="tpu_custom_call" | custom-call | flops 2048000000 | bytes 3000000 | tf_op jit(solution)/shard_map/wave_tables/pallas_call | solution.py:195
  4.4 3.3 %collective-permute-start = (bf16[512,512]{1,0:T(8,128)(2,1)S(1)}, bf16[512,512]{1,0:T(8,128)(2,1)S(1)}, u32[]{:S(2)}, u32[]{:S(2)}) collective-permute-start(bf16[512,512]{1,0:T(8,128)(2,1)S(1)} %get-tuple-element.56), channel_id=1, source_target_pairs={{0,1},{1,0},{16,17},{17,16},{32,33},{33,32},{48,49},{49,48},{2,3},... | collective-permute-start | bytes 1572872 | tf_op jit(solution)/shard_map/ppermute | solution.py:71
  7.7 4.9 %collective-permute-start.4 = (bf16[4,144,256]{2,1,0:T(8,128)(2,1)S(1)}, bf16[4,144,256]{2,1,0:T(8,128)(2,1)S(1)}, u32[]{:S(2)}, u32[]{:S(2)}) collective-permute-start(bf16[4,144,256]{2,1,0:T(8,128)(2,1)S(1)} %get-tuple-element.107), channel_id=1, source_target_pairs={{0,240},{16,32},{32,16},{48,64},{64,48},{80,96},{96,80},{112,128},... | collective-permute-start | bytes 884744 | tf_op jit(solution)/shard_map/ppermute | solution.py:472
  12.7 2.6 %wave_tables.4 = (bf16[1024,256]{1,0:T(8,128)(2,1)}, bf16[1024,256]{1,0:T(8,128)(2,1)}, f32[256,512]{1,0:T(8,128)S(1)}) custom-call(s32[2]{0:T(128)S(1)} %pad_add_fusion.place, bf16[2,3,4,128]{3,2,1,0:T(4,128)(2,1)S(1)} %bitcast.19, s32[3,1024]{1,0:T(4,128)S(1)} %copy-done.3, s32[1,256]{1,0:T(1,128)S(1)} %get-tuple-element.116.order, ...), custom_call_target="tpu_custom_call" | custom-call | flops 1024000000 | bytes 3000000 | tf_op jit(solution)/shard_map/wave_tables/pallas_call | solution.py:195
  15.5 2.8 %collective-permute-start.1 = (bf16[256,512]{1,0:T(8,128)(2,1)S(1)}, bf16[256,512]{1,0:T(8,128)(2,1)S(1)}, u32[]{:S(2)}, u32[]{:S(2)}) collective-permute-start(bf16[256,512]{1,0:T(8,128)(2,1)S(1)} %add_convert_fusion), channel_id=1, source_target_pairs={{0,4},{1,13},{16,20},{17,29},{32,36},{33,45},{48,52},{49,61},{2,6}... | collective-permute-start | bytes 786440 | tf_op jit(solution)/shard_map/ppermute | solution.py:71
  18.4 2.6 %wave_tables.5 = (bf16[1024,256]{1,0:T(8,128)(2,1)}, bf16[1024,256]{1,0:T(8,128)(2,1)}, f32[256,512]{1,0:T(8,128)S(1)}) custom-call(s32[2]{0:T(128)S(1)} %pad_add_fusion.place, bf16[2,3,4,128]{3,2,1,0:T(4,128)(2,1)S(1)} %bitcast.20, s32[3,1024]{1,0:T(4,128)S(1)} %copy-done.3, s32[1,256]{1,0:T(1,128)S(1)} %get-tuple-element.115.order, ...), custom_call_target="tpu_custom_call" | custom-call | flops 1024000000 | bytes 3000000 | tf_op jit(solution)/shard_map/wave_tables/pallas_call | solution.py:195
  21.0 1.3 %radial_prepare.1 = (f32[8,9]{1,0:T(8,128)S(1)}, f32[8,3,128,128]{3,2,1,0:T(8,128)S(1)}, f32[64,256]{1,0:T(8,128)S(1)}) custom-call(s32[2]{0:T(128)S(1)} %pad_add_fusion.place, s32[8]{0:T(128)S(1)} %reshape.729.near_count, s32[8,9]{1,0:T(8,128)S(1)} %bitcast.22, bf16[2,3,4,128]{3,2,1,0:T(4,128)(2,1)S(1)} %bitcast.21, bf16[4,256]{1,0:T(4,128)(2,1)S(1)} %copy-done.7), custom_call_target="tpu_custom_call" | custom-call | flops 500000000 | bytes 100000 | tf_op jit(solution)/shard_map/radial_prepare/pallas_call | solution.py:236
  22.9 1.4 %radial_piece.4.rest_2_ = f32[8,128,256]{2,1,0:T(8,128)S(1)} custom-call(f32[8]{0:T(128)S(1)} %copy-done.9, f32[8,9]{1,0:T(8,128)S(1)} %get-tuple-element.64.live, bf16[8,256]{1,0:T(8,128)(2,1)S(1)} %copy-done.6, f32[8,3,128,128]{3,2,1,0:T(8,128)S(1)} %get-tuple-element.65.mine, bf16[4,144,256]{2,1,0:T(8,128)(2,1)S(1)} %get-tuple-element.66.rest_0_, ...), custom_call_target="tpu_custom_call" | custom-call | flops 2000000000 | bytes 2000000 | tf_op jit(solution)/shard_map/radial_piece/pallas_call | solution.py:291
  24.3 2.0 %collective-permute-done.2 = bf16[128,512]{1,0:T(8,128)(2,1)S(1)} collective-permute-done((bf16[128,512]{1,0:T(8,128)(2,1)S(1)}, bf16[128,512]{1,0:T(8,128)(2,1)S(1)}, u32[]{:S(2)}, u32[]{:S(2)}) %collective-permute-start.2) | collective-permute-done | bytes 131104 | tf_op jit(solution)/shard_map/ppermute | solution.py:71
  27.5 1.9 %radial_piece.5.rest_2_ = f32[8,128,256]{2,1,0:T(8,128)S(1)} custom-call(f32[8]{0:T(128)S(1)} %copy-done.9, f32[8,9]{1,0:T(8,128)S(1)} %get-tuple-element.64.live, bf16[8,256]{1,0:T(8,128)(2,1)S(1)} %copy-done.6, f32[8,3,128,128]{3,2,1,0:T(8,128)S(1)} %get-tuple-element.65.mine, ...), custom_call_target="tpu_custom_call", output_to_operand_aliasing={{}: (6, {})} | custom-call | flops 2000000000 | bytes 2000000 | tf_op jit(solution)/shard_map/radial_piece/pallas_call | solution.py:291
  29.4 1.7 %collective-permute-start.7 = (bf16[4,144,256]{2,1,0:T(8,128)(2,1)S(1)}, bf16[4,144,256]{2,1,0:T(8,128)(2,1)S(1)}, u32[]{:S(2)}, u32[]{:S(2)}) collective-permute-start(bf16[4,144,256]{2,1,0:T(8,128)(2,1)S(1)} %get-tuple-element.77), channel_id=1, source_target_pairs={{0,1},{1,0},{2,3},{3,2},{4,5},{5,4},{6,7},{7,6},{8,9},{9,8},{10,11... | collective-permute-start | bytes 884744 | tf_op jit(solution)/shard_map/ppermute | solution.py:503
  31.1 4.2 %collective-permute-start.8 = (bf16[4,144,256]{2,1,0:T(8,128)(2,1)S(1)}, bf16[4,144,256]{2,1,0:T(8,128)(2,1)S(1)}, u32[]{:S(2)}, u32[]{:S(2)}) collective-permute-start(bf16[4,144,256]{2,1,0:T(8,128)(2,1)S(1)} %get-tuple-element.78), channel_id=1, source_target_pairs={{0,15},{1,2},{2,1},{3,4},{4,3},{5,6},{6,5},{7,8},{8,7},{9,10},{10,... | collective-permute-start | bytes 884744 | tf_op jit(solution)/shard_map/ppermute | solution.py:502
  35.3 1.8 %collective-permute-start.6 = (bf16[64,768]{1,0:T(8,128)(2,1)S(1)}, bf16[64,768]{1,0:T(8,128)(2,1)S(1)}, u32[]{:S(2)}, u32[]{:S(2)}) collective-permute-start(bf16[64,768]{1,0:T(8,128)(2,1)S(1)} %convert_element_type.65), channel_id=1, source_target_pairs={{0,192},{1,65},{16,208},{17,81},{32,224},{33,97},{48,240},{49,113}... | collective-permute-start | bytes 294920 | tf_op jit(solution)/shard_map/ppermute | solution.py:71
  37.2 1.9 %radial_piece.6.rest_2_ = f32[8,128,256]{2,1,0:T(8,128)S(1)} custom-call(f32[8]{0:T(128)S(1)} %copy-done.9, f32[8,9]{1,0:T(8,128)S(1)} %get-tuple-element.64.live, bf16[8,256]{1,0:T(8,128)(2,1)S(1)} %copy-done.6, f32[8,3,128,128]{3,2,1,0:T(8,128)S(1)} %get-tuple-element.65.mine, ...), custom_call_target="tpu_custom_call", output_to_operand_aliasing={{}: (6, {})} | custom-call | flops 2000000000 | bytes 2000000 | tf_op jit(solution)/shard_map/radial_piece/pallas_call | solution.py:291
  39.2 5.3 %collective-permute-done.8.block = bf16[4,144,256]{2,1,0:T(8,128)(2,1)S(1)} collective-permute-done((bf16[4,144,256]{2,1,0:T(8,128)(2,1)S(1)}, bf16[4,144,256]{2,1,0:T(8,128)(2,1)S(1)}, u32[]{:S(2)}, u32[]{:S(2)}) %collective-permute-start.8) | collective-permute-done | bytes 294944 | tf_op jit(solution)/shard_map/ppermute | solution.py:502
  44.5 2.8 %collective-permute-start.9 = (bf16[64,768]{1,0:T(8,128)(2,1)S(1)}, bf16[64,768]{1,0:T(8,128)(2,1)S(1)}, u32[]{:S(2)}, u32[]{:S(2)}) collective-permute-start(bf16[64,768]{1,0:T(8,128)(2,1)S(1)} %convert_element_type.67), channel_id=1, source_target_pairs={{0,16},{1,51},{16,0},{17,33},{32,48},{33,17},{48,32},{49,3},{2,18}... | collective-permute-start | bytes 294920 | tf_op jit(solution)/shard_map/ppermute | solution.py:71
  47.3 1.6 %radial_piece.7.start = f32[8,128,256]{2,1,0:T(8,128)S(1)} custom-call(f32[8]{0:T(128)S(1)} %copy-done.9, f32[8,9]{1,0:T(8,128)S(1)} %get-tuple-element.64.live, bf16[8,256]{1,0:T(8,128)(2,1)S(1)} %copy-done.6, f32[8,3,128,128]{3,2,1,0:T(8,128)S(1)} %get-tuple-element.65.mine, ...), custom_call_target="tpu_custom_call", output_to_operand_aliasing={{}: (6, {})} | custom-call | flops 2000000000 | bytes 2000000 | tf_op jit(solution)/shard_map/radial_piece/pallas_call | solution.py:291
  48.9 2.0 %collective-permute-done.9 = bf16[64,768]{1,0:T(8,128)(2,1)S(1)} collective-permute-done((bf16[64,768]{1,0:T(8,128)(2,1)S(1)}, bf16[64,768]{1,0:T(8,128)(2,1)S(1)}, u32[]{:S(2)}, u32[]{:S(2)}) %collective-permute-start.9) | collective-permute-done | bytes 98336 | tf_op jit(solution)/shard_map/ppermute | solution.py:71
  51.0 3.7 %collective-permute-start.10 = (bf16[64,768]{1,0:T(8,128)(2,1)S(1)}, bf16[64,768]{1,0:T(8,128)(2,1)S(1)}, u32[]{:S(2)}, u32[]{:S(2)}) collective-permute-start(bf16[64,768]{1,0:T(8,128)(2,1)S(1)} %convert_element_type.69), channel_id=1, source_target_pairs={{0,50},{1,17},{16,32},{17,1},{32,16},{33,49},{48,2},{49,33},{2,48}... | collective-permute-start | bytes 294920 | tf_op jit(solution)/shard_map/ppermute | solution.py:71
  54.7 1.8 %radial_edge.4.start = f32[8,128,256]{2,1,0:T(8,128)S(1)} custom-call(s32[4]{0:T(128)S(1)} %pad_add_fusion.1.sides, f32[8]{0:T(128)S(1)} %copy-done.9, f32[8,9]{1,0:T(8,128)S(1)} %get-tuple-element.64.live, bf16[8,256]{1,0:T(8,128)(2,1)S(1)} %copy-done.6, f32[8,3,128,128]{3,2,1,0:T(8,128)S(1)} %get-tuple-element.65.mine, ...), custom_call_target="tpu_custom_call", output_to_operand_aliasing={{}: (6, {})} | custom-call | flops 2000000000 | bytes 2000000 | tf_op jit(solution)/shard_map/radial_edge/pallas_call | solution.py:362
  57.2 5.1 %collective-permute-start.11 = (bf16[64,768]{1,0:T(8,128)(2,1)S(1)}, bf16[64,768]{1,0:T(8,128)(2,1)S(1)}, u32[]{:S(2)}, u32[]{:S(2)}) collective-permute-start(bf16[64,768]{1,0:T(8,128)(2,1)S(1)} %convert_element_type.71), channel_id=1, source_target_pairs={{0,48},{1,19},{16,34},{17,3},{32,18},{33,51},{48,0},{49,35},{2,50}... | collective-permute-start | bytes 294920 | tf_op jit(solution)/shard_map/ppermute | solution.py:71
  62.3 1.8 %radial_edge.5 = f32[8,128,256]{2,1,0:T(8,128)S(1)} custom-call(s32[4]{0:T(128)S(1)} %pad_add_fusion.1.sides, f32[8]{0:T(128)S(1)} %copy-done.9, f32[8,9]{1,0:T(8,128)S(1)} %get-tuple-element.64.live, bf16[8,256]{1,0:T(8,128)(2,1)S(1)} %copy-done.6, f32[8,3,128,128]{3,2,1,0:T(8,128)S(1)} %get-tuple-element.65.mine, ...), custom_call_target="tpu_custom_call", output_to_operand_aliasing={{}: (6, {})} | custom-call | flops 2000000000 | bytes 2000000 | tf_op jit(solution)/shard_map/radial_edge/pallas_call | solution.py:362
  64.5 2.2 %collective-permute-start.12 = (bf16[64,512]{1,0:T(8,128)(2,1)S(1)}, bf16[64,512]{1,0:T(8,128)(2,1)S(1)}, u32[]{:S(2)}, u32[]{:S(2)}) collective-permute-start(bf16[64,512]{1,0:T(8,128)(2,1)S(1)} %pad_maximum_fusion.6), channel_id=1, source_target_pairs={{0,64},{1,193},{16,80},{17,209},{32,96},{33,225},{48,112},{49,241}... | collective-permute-start | bytes 196616 | tf_op jit(solution)/shard_map/ppermute | solution.py:71
  66.6 2.5 %collective-permute-done.12 = bf16[64,512]{1,0:T(8,128)(2,1)S(1)} collective-permute-done((bf16[64,512]{1,0:T(8,128)(2,1)S(1)}, bf16[64,512]{1,0:T(8,128)(2,1)S(1)}, u32[]{:S(2)}, u32[]{:S(2)}) %collective-permute-start.12) | collective-permute-done | bytes 65568 | tf_op jit(solution)/shard_map/ppermute | solution.py:71
  69.2 1.8 %collective-permute-start.13 = (bf16[128,512]{1,0:T(8,128)(2,1)S(1)}, bf16[128,512]{1,0:T(8,128)(2,1)S(1)}, u32[]{:S(2)}, u32[]{:S(2)}) collective-permute-start(bf16[128,512]{1,0:T(8,128)(2,1)S(1)} %pad_maximum_fusion.5.coef), channel_id=1, source_target_pairs={{0,12},{1,5},{16,28},{17,21},{32,44},{33,37},{48,60},{49,53},{2,14... | collective-permute-start | bytes 393224 | tf_op jit(solution)/shard_map/ppermute | solution.py:71
  71.4 2.2 %collective-permute-done.13 = bf16[128,512]{1,0:T(8,128)(2,1)S(1)} collective-permute-done((bf16[128,512]{1,0:T(8,128)(2,1)S(1)}, bf16[128,512]{1,0:T(8,128)(2,1)S(1)}, u32[]{:S(2)}, u32[]{:S(2)}) %collective-permute-start.13) | collective-permute-done | bytes 131104 | tf_op jit(solution)/shard_map/ppermute | solution.py:71
  73.6 2.7 %collective-permute-start.14 = (bf16[256,512]{1,0:T(8,128)(2,1)S(1)}, bf16[256,512]{1,0:T(8,128)(2,1)S(1)}, u32[]{:S(2)}, u32[]{:S(2)}) collective-permute-start(bf16[256,512]{1,0:T(8,128)(2,1)S(1)} %pad_maximum_fusion.3.coef), channel_id=1, source_target_pairs={{0,4},{1,13},{16,20},{17,29},{32,36},{33,45},{48,52},{49,61},{2,6}... | collective-permute-start | bytes 786440 | tf_op jit(solution)/shard_map/ppermute | solution.py:71
  76.3 1.4 %radial_edge.6 = f32[8,128,256]{2,1,0:T(8,128)S(1)} custom-call(s32[4]{0:T(128)S(1)} %pad_add_fusion.1.sides, f32[8]{0:T(128)S(1)} %copy-done.9, f32[8,9]{1,0:T(8,128)S(1)} %get-tuple-element.64.live, bf16[8,256]{1,0:T(8,128)(2,1)S(1)} %copy-done.6, f32[8,3,128,128]{3,2,1,0:T(8,128)S(1)} %get-tuple-element.65.mine, ...), custom_call_target="tpu_custom_call", output_to_operand_aliasing={{}: (6, {})} | custom-call | flops 2000000000 | bytes 2000000 | tf_op jit(solution)/shard_map/radial_edge/pallas_call | solution.py:362
  78.2 3.3 %collective-permute-done.14 = bf16[256,512]{1,0:T(8,128)(2,1)S(1)} collective-permute-done((bf16[256,512]{1,0:T(8,128)(2,1)S(1)}, bf16[256,512]{1,0:T(8,128)(2,1)S(1)}, u32[]{:S(2)}, u32[]{:S(2)}) %collective-permute-start.14) | collective-permute-done | bytes 262176 | tf_op jit(solution)/shard_map/ppermute | solution.py:71
  81.6 7.0 %collective-permute-start.15 = (bf16[512,512]{1,0:T(8,128)(2,1)S(1)}, bf16[512,512]{1,0:T(8,128)(2,1)S(1)}, u32[]{:S(2)}, u32[]{:S(2)}) collective-permute-start(bf16[512,512]{1,0:T(8,128)(2,1)S(1)} %pad_maximum_fusion.coef), channel_id=1, source_target_pairs={{0,1},{1,0},{16,17},{17,16},{32,33},{33,32},{48,49},{49,48},{2,3},... | collective-permute-start | bytes 1572872 | tf_op jit(solution)/shard_map/ppermute | solution.py:71
  88.6 1.4 %radial_edge.7 = f32[8,128,256]{2,1,0:T(8,128)S(1)} custom-call(s32[4]{0:T(128)S(1)} %pad_add_fusion.1.sides, f32[8]{0:T(128)S(1)} %copy-done.9, f32[8,9]{1,0:T(8,128)S(1)} %get-tuple-element.64.live, bf16[8,256]{1,0:T(8,128)(2,1)S(1)} %copy-done.6, f32[8,3,128,128]{3,2,1,0:T(8,128)S(1)} %get-tuple-element.65.mine, ...), custom_call_target="tpu_custom_call", output_to_operand_aliasing={{}: (6, {})} | custom-call | flops 2000000000 | bytes 2000000 | tf_op jit(solution)/shard_map/radial_edge/pallas_call | solution.py:362
  92.0 2.4 %mix_and_network.1 = bf16[1024,256]{1,0:T(8,128)(2,1)} custom-call(bf16[1024,512]{1,0:T(8,128)(2,1)S(1)} %copy-done.14, bf16[1024,512]{1,0:T(8,128)(2,1)S(1)} %copy-done.15, bf16[512,512]{1,0:T(8,128)(2,1)S(1)} %collective-permute-done.15.coef, bf16[1024,256]{1,0:T(8,128)(2,1)S(1)} %bitcast.17, f32[1024,256]{1,0:T(8,128)S(1)} %recip_piece.5.acc, ...), custom_call_target="tpu_custom_call" | custom-call | flops 3000000000 | bytes 8000000 | tf_op jit(solution)/shard_map/mix_and_network/pallas_call | solution.py:422
  (79 shorter events, 6.3 us)
Async XLA Ops:
  0.2 12.5 %copy-start.16 = (s32[2,4]{1,0:T(2,128)S(1)}, s32[2,4]{1,0:T(2,128)}, u32[]{:S(2)}) copy-start(s32[2,4]{1,0:T(2,128)} %param.14) | copy-start | bytes 100
  0.2 12.5 %copy-start.3 = (s32[3,1024]{1,0:T(4,128)S(1)}, s32[3,1024]{1,0:T(4,128)}, u32[]{:S(2)}) copy-start(s32[3,1024]{1,0:T(4,128)} %miller.5) | copy-start | bytes 36868
  0.2 12.5 %copy-start.4 = (bf16[2,4,3,128]{3,1,2,0:T(4,128)(2,1)S(1)}, bf16[2,4,3,128]{3,1,2,0:T(4,128)(2,1)}, u32[]{:S(2)}) copy-start(bf16[2,4,3,128]{3,1,2,0:T(4,128)(2,1)} %param.12) | copy-start | bytes 18436
  4.4 11.1 %collective-permute-start = (bf16[512,512]{1,0:T(8,128)(2,1)S(1)}, bf16[512,512]{1,0:T(8,128)(2,1)S(1)}, u32[]{:S(2)}, u32[]{:S(2)}) collective-permute-start(bf16[512,512]{1,0:T(8,128)(2,1)S(1)} %get-tuple-element.56), channel_id=1, source_target_pairs={{0,1},{1,0},{16,17},{17,16},{32,33},{33,32},{48,49},{49,48},{2,3},... | collective-permute-start | bytes 1572872 | tf_op jit(solution)/shard_map/ppermute | solution.py:71
  7.7 18.6 %collective-permute-start.4 = (bf16[4,144,256]{2,1,0:T(8,128)(2,1)S(1)}, bf16[4,144,256]{2,1,0:T(8,128)(2,1)S(1)}, u32[]{:S(2)}, u32[]{:S(2)}) collective-permute-start(bf16[4,144,256]{2,1,0:T(8,128)(2,1)S(1)} %get-tuple-element.107), channel_id=1, source_target_pairs={{0,240},{16,32},{32,16},{48,64},{64,48},{80,96},{96,80},{112,128},... | collective-permute-start | bytes 884744 | tf_op jit(solution)/shard_map/ppermute | solution.py:472
  12.6 13.7 %collective-permute-start.3 = (bf16[4,144,256]{2,1,0:T(8,128)(2,1)S(1)}, bf16[4,144,256]{2,1,0:T(8,128)(2,1)S(1)}, u32[]{:S(2)}, u32[]{:S(2)}) collective-permute-start(bf16[4,144,256]{2,1,0:T(8,128)(2,1)S(1)} %get-tuple-element.108), channel_id=1, source_target_pairs={{0,16},{16,0},{32,48},{48,32},{64,80},{80,64},{96,112},{112,96},{1... | collective-permute-start | bytes 884744 | tf_op jit(solution)/shard_map/ppermute | solution.py:471
  15.5 6.8 %collective-permute-start.1 = (bf16[256,512]{1,0:T(8,128)(2,1)S(1)}, bf16[256,512]{1,0:T(8,128)(2,1)S(1)}, u32[]{:S(2)}, u32[]{:S(2)}) collective-permute-start(bf16[256,512]{1,0:T(8,128)(2,1)S(1)} %add_convert_fusion), channel_id=1, source_target_pairs={{0,4},{1,13},{16,20},{17,29},{32,36},{33,45},{48,52},{49,61},{2,6}... | collective-permute-start | bytes 786440 | tf_op jit(solution)/shard_map/ppermute | solution.py:71
  18.3 2.6 %copy-start.5 = (s32[2,4,9]{2,1,0:T(4,128)S(1)}, s32[2,4,9]{2,1,0:T(4,128)}, u32[]{:S(2)}) copy-start(s32[2,4,9]{2,1,0:T(4,128)} %param.13) | copy-start | bytes 868
  18.4 2.6 %copy-start.7 = (bf16[4,256]{1,0:T(4,128)(2,1)S(1)}, bf16[4,256]{1,0:T(4,128)(2,1)}, u32[]{:S(2)}) copy-start(bf16[4,256]{1,0:T(4,128)(2,1)} %row_filter.1) | copy-start | bytes 6148
  22.2 0.7 copy-start.6
  22.4 3.9 %collective-permute-start.2 = (bf16[128,512]{1,0:T(8,128)(2,1)S(1)}, bf16[128,512]{1,0:T(8,128)(2,1)S(1)}, u32[]{:S(2)}, u32[]{:S(2)}) collective-permute-start(bf16[128,512]{1,0:T(8,128)(2,1)S(1)} %get-tuple-element.63), channel_id=1, source_target_pairs={{0,12},{1,5},{16,28},{17,21},{32,44},{33,37},{48,60},{49,53},{2,14... | collective-permute-start | bytes 393224 | tf_op jit(solution)/shard_map/ppermute | solution.py:71
  26.4 8.9 %collective-permute-start.5 = (bf16[64,512]{1,0:T(8,128)(2,1)S(1)}, bf16[64,512]{1,0:T(8,128)(2,1)S(1)}, u32[]{:S(2)}, u32[]{:S(2)}) collective-permute-start(bf16[64,512]{1,0:T(8,128)(2,1)S(1)} %fusion.1), channel_id=1, source_target_pairs={{0,64},{1,193},{16,80},{17,209},{32,96},{33,225},{48,112},{49,241}... | collective-permute-start | bytes 196616 | tf_op jit(solution)/shard_map/ppermute | solution.py:71
  29.4 9.8 %collective-permute-start.7 = (bf16[4,144,256]{2,1,0:T(8,128)(2,1)S(1)}, bf16[4,144,256]{2,1,0:T(8,128)(2,1)S(1)}, u32[]{:S(2)}, u32[]{:S(2)}) collective-permute-start(bf16[4,144,256]{2,1,0:T(8,128)(2,1)S(1)} %get-tuple-element.77), channel_id=1, source_target_pairs={{0,1},{1,0},{2,3},{3,2},{4,5},{5,4},{6,7},{7,6},{8,9},{9,8},{10,11... | collective-permute-start | bytes 884744 | tf_op jit(solution)/shard_map/ppermute | solution.py:503
  31.1 13.4 %collective-permute-start.8 = (bf16[4,144,256]{2,1,0:T(8,128)(2,1)S(1)}, bf16[4,144,256]{2,1,0:T(8,128)(2,1)S(1)}, u32[]{:S(2)}, u32[]{:S(2)}) collective-permute-start(bf16[4,144,256]{2,1,0:T(8,128)(2,1)S(1)} %get-tuple-element.78), channel_id=1, source_target_pairs={{0,15},{1,2},{2,1},{3,4},{4,3},{5,6},{6,5},{7,8},{8,7},{9,10},{10,... | collective-permute-start | bytes 884744 | tf_op jit(solution)/shard_map/ppermute | solution.py:502
  35.3 3.8 %collective-permute-start.6 = (bf16[64,768]{1,0:T(8,128)(2,1)S(1)}, bf16[64,768]{1,0:T(8,128)(2,1)S(1)}, u32[]{:S(2)}, u32[]{:S(2)}) collective-permute-start(bf16[64,768]{1,0:T(8,128)(2,1)S(1)} %convert_element_type.65), channel_id=1, source_target_pairs={{0,192},{1,65},{16,208},{17,81},{32,224},{33,97},{48,240},{49,113}... | collective-permute-start | bytes 294920 | tf_op jit(solution)/shard_map/ppermute | solution.py:71
  44.5 6.4 %collective-permute-start.9 = (bf16[64,768]{1,0:T(8,128)(2,1)S(1)}, bf16[64,768]{1,0:T(8,128)(2,1)S(1)}, u32[]{:S(2)}, u32[]{:S(2)}) collective-permute-start(bf16[64,768]{1,0:T(8,128)(2,1)S(1)} %convert_element_type.67), channel_id=1, source_target_pairs={{0,16},{1,51},{16,0},{17,33},{32,48},{33,17},{48,32},{49,3},{2,18}... | collective-permute-start | bytes 294920 | tf_op jit(solution)/shard_map/ppermute | solution.py:71
  51.0 6.1 %collective-permute-start.10 = (bf16[64,768]{1,0:T(8,128)(2,1)S(1)}, bf16[64,768]{1,0:T(8,128)(2,1)S(1)}, u32[]{:S(2)}, u32[]{:S(2)}) collective-permute-start(bf16[64,768]{1,0:T(8,128)(2,1)S(1)} %convert_element_type.69), channel_id=1, source_target_pairs={{0,50},{1,17},{16,32},{17,1},{32,16},{33,49},{48,2},{49,33},{2,48}... | collective-permute-start | bytes 294920 | tf_op jit(solution)/shard_map/ppermute | solution.py:71
  57.1 13.8 %copy-start.12 = (bf16[1024,256]{1,0:T(8,128)(2,1)S(1)}, bf16[1024,256]{1,0:T(8,128)(2,1)}, u32[]{:S(2)}) copy-start(bf16[1024,256]{1,0:T(8,128)(2,1)} %get-tuple-element.88.cos_ref) | copy-start | bytes 1572868
  57.1 13.8 %copy-start.13 = (bf16[1024,256]{1,0:T(8,128)(2,1)S(1)}, bf16[1024,256]{1,0:T(8,128)(2,1)}, u32[]{:S(2)}) copy-start(bf16[1024,256]{1,0:T(8,128)(2,1)} %get-tuple-element.89.sin_ref) | copy-start | bytes 1572868
  57.2 7.2 %collective-permute-start.11 = (bf16[64,768]{1,0:T(8,128)(2,1)S(1)}, bf16[64,768]{1,0:T(8,128)(2,1)S(1)}, u32[]{:S(2)}, u32[]{:S(2)}) collective-permute-start(bf16[64,768]{1,0:T(8,128)(2,1)S(1)} %convert_element_type.71), channel_id=1, source_target_pairs={{0,48},{1,19},{16,34},{17,3},{32,18},{33,51},{48,0},{49,35},{2,50}... | collective-permute-start | bytes 294920 | tf_op jit(solution)/shard_map/ppermute | solution.py:71
  64.5 4.7 %collective-permute-start.12 = (bf16[64,512]{1,0:T(8,128)(2,1)S(1)}, bf16[64,512]{1,0:T(8,128)(2,1)S(1)}, u32[]{:S(2)}, u32[]{:S(2)}) collective-permute-start(bf16[64,512]{1,0:T(8,128)(2,1)S(1)} %pad_maximum_fusion.6), channel_id=1, source_target_pairs={{0,64},{1,193},{16,80},{17,209},{32,96},{33,225},{48,112},{49,241}... | collective-permute-start | bytes 196616 | tf_op jit(solution)/shard_map/ppermute | solution.py:71
  69.2 4.4 %collective-permute-start.13 = (bf16[128,512]{1,0:T(8,128)(2,1)S(1)}, bf16[128,512]{1,0:T(8,128)(2,1)S(1)}, u32[]{:S(2)}, u32[]{:S(2)}) collective-permute-start(bf16[128,512]{1,0:T(8,128)(2,1)S(1)} %pad_maximum_fusion.5.coef), channel_id=1, source_target_pairs={{0,12},{1,5},{16,28},{17,21},{32,44},{33,37},{48,60},{49,53},{2,14... | collective-permute-start | bytes 393224 | tf_op jit(solution)/shard_map/ppermute | solution.py:71
  73.6 7.9 %collective-permute-start.14 = (bf16[256,512]{1,0:T(8,128)(2,1)S(1)}, bf16[256,512]{1,0:T(8,128)(2,1)S(1)}, u32[]{:S(2)}, u32[]{:S(2)}) collective-permute-start(bf16[256,512]{1,0:T(8,128)(2,1)S(1)} %pad_maximum_fusion.3.coef), channel_id=1, source_target_pairs={{0,4},{1,13},{16,20},{17,29},{32,36},{33,45},{48,52},{49,61},{2,6}... | collective-permute-start | bytes 786440 | tf_op jit(solution)/shard_map/ppermute | solution.py:71
  81.6 8.5 %copy-start.10 = (bf16[1024,256]{1,0:T(8,128)(2,1)S(1)}, bf16[1024,256]{1,0:T(8,128)(2,1)}, u32[]{:S(2)}) copy-start(bf16[1024,256]{1,0:T(8,128)(2,1)} %get-tuple-element.95.cos_ref) | copy-start | bytes 1572868
  81.6 8.5 %copy-start.11 = (bf16[1024,256]{1,0:T(8,128)(2,1)S(1)}, bf16[1024,256]{1,0:T(8,128)(2,1)}, u32[]{:S(2)}) copy-start(bf16[1024,256]{1,0:T(8,128)(2,1)} %get-tuple-element.96.sin_ref) | copy-start | bytes 1572868
  81.6 9.0 %collective-permute-start.15 = (bf16[512,512]{1,0:T(8,128)(2,1)S(1)}, bf16[512,512]{1,0:T(8,128)(2,1)S(1)}, u32[]{:S(2)}, u32[]{:S(2)}) collective-permute-start(bf16[512,512]{1,0:T(8,128)(2,1)S(1)} %pad_maximum_fusion.coef), channel_id=1, source_target_pairs={{0,1},{1,0},{16,17},{17,16},{32,33},{33,32},{48,49},{49,48},{2,3},... | collective-permute-start | bytes 1572872 | tf_op jit(solution)/shard_map/ppermute | solution.py:71
  90.1 1.0 %copy-start = (bf16[2,4,128,256]{3,2,1,0:T(8,128)(2,1)S(1)}, bf16[2,4,128,256]{3,2,1,0:T(8,128)(2,1)}, u32[]{:S(2)}) copy-start(bf16[2,4,128,256]{3,2,1,0:T(8,128)(2,1)} %param.11) | copy-start | bytes 1572868
  90.1 1.1 %copy-start.1 = (bf16[256,512]{1,0:T(8,128)(2,1)S(1)}, bf16[256,512]{1,0:T(8,128)(2,1)}, u32[]{:S(2)}) copy-start(bf16[256,512]{1,0:T(8,128)(2,1)} %w_in.1) | copy-start | bytes 786436
  90.1 1.2 %copy-start.2 = (bf16[512,256]{1,0:T(8,128)(2,1)S(1)}, bf16[512,256]{1,0:T(8,128)(2,1)}, u32[]{:S(2)}) copy-start(bf16[512,256]{1,0:T(8,128)(2,1)} %w_out.1) | copy-start | bytes 786436
  90.1 1.2 %copy-start.8 = (f32[256]{0:T(256)S(1)}, f32[256]{0:T(256)}, u32[]{:S(2)}) copy-start(f32[256]{0:T(256)} %param.19) | copy-start | bytes 3076
  90.1 1.5 %copy-start.14 = (bf16[1024,512]{1,0:T(8,128)(2,1)S(1)}, bf16[1024,512]{1,0:T(8,128)(2,1)}, u32[]{:S(2)}) copy-start(bf16[1024,512]{1,0:T(8,128)(2,1)} %get-tuple-element.52.cos_ref) | copy-start | bytes 3145732
  90.1 1.8 %copy-start.15 = (bf16[1024,512]{1,0:T(8,128)(2,1)S(1)}, bf16[1024,512]{1,0:T(8,128)(2,1)}, u32[]{:S(2)}) copy-start(bf16[1024,512]{1,0:T(8,128)(2,1)} %get-tuple-element.53.sin_ref) | copy-start | bytes 3145732
  (1 other events, 0.7 us)

commit v8 on v6

--- a/solution.py
+++ b/solution.py
@@ -39,11 +39,16 @@
     return x, y, z, 1 - core
 
 
-def flip_plane(first, second):
+def flip_x(first, second):
     def step(x, y, z, core):
-        if core == 0:
-            return x ^ first, y ^ second, z, core
-        return x ^ second, y ^ first, z, core
+        return x ^ (second if core else first), y, z, core
+
+    return step
+
+
+def flip_y(first, second):
+    def step(x, y, z, core):
+        return x, y ^ (second if core else first), z, core
 
     return step
 
@@ -57,8 +62,8 @@
     return step
 
 
-HALVING = (flip_core, flip_plane(1, 0), flip_plane(3, 0), flip_plane(0, 1))
-DOUBLING = (flip_plane(0, 3), flip_z(0), flip_z(1), flip_z(2))
+HALVING = (flip_core, flip_y(1, 3), flip_y(3, 1), flip_x(1, 3))
+DOUBLING = (flip_x(3, 1), flip_z(0), flip_z(1), flip_z(2))
 CHUNK = 64
 
 
@@ -81,12 +86,9 @@
     b2 = (pos // 128) % 2
     b1 = (pos // 256) % 2
     owner = core ^ (pos // 512)
-    main = jnp.where(owner == 0, x, y) ^ b1 ^ (3 * b2)
-    other = jnp.where(owner == 0, y, x)
-    coset = (other ^ (other >> 1)) & 1
-    side = (coset ^ b3) ^ (3 * mb)
-    ox = jnp.where(owner == 0, main, side)
-    oy = jnp.where(owner == 0, side, main)
+    oy = y ^ jnp.where(owner == 0, b1 ^ (3 * b2), (3 * b1) ^ b2)
+    coset = jnp.where(owner == 0, (x ^ (x >> 1)) & 1, x >> 1) ^ b3
+    ox = jnp.where(owner == 0, coset ^ (3 * mb), 2 * coset + mb)
     return linear(ox, oy, mz, owner) * 4 + rest
 
 
@@ -222,8 +224,7 @@
         for d in range(3):
             mine[c, d] = jnp.broadcast_to(columns[:, d : d + 1], (ATOMS, ATOMS))
     x, z = place[0] // 4, place[0] % 4 + 4 * ((place[1] // 2) % 2)
-    y, core = place[1] // 4, place[1] % 2
-    member = (jnp.where(core == 0, y, x) // 2) * 8 + z
+    member = jnp.where(place[1] % 2 == 0, x // 2, x % 2) * 8 + z
     whole = jnp.concatenate([row_filter[...].astype(F32)] * (CHUNK // 4), axis=0)
     slots = lax.broadcasted_iota(jnp.int32, (CHUNK, WIDTH), 0) // 4
     filters[...] = jnp.where(slots == member, whole, 0.0)
@@ -366,7 +367,7 @@
         scratch_shapes=[VMEM((2, 8 * ATOMS, WIDTH), BF16)],
         input_output_aliases={6: 0},
         compiler_params=pltpu.CompilerParams(vmem_limit_bytes=10 * 1024 * 1024),
-        cost_estimate=pl.CostEstimate(flops=2_000_000_000, bytes_accessed=2_000_000, transcendentals=0),
+        cost_estimate=pl.CostEstimate(flops=20_000_000_000, bytes_accessed=2_000_000, transcendentals=0),
         name="radial_edge",
     )(sides, gammas, live, filters, mine, block, acc)
 
@@ -392,7 +393,7 @@
         out_specs=vm,
         input_output_aliases={3: 0},
         compiler_params=pltpu.CompilerParams(vmem_limit_bytes=10 * 1024 * 1024),
-        cost_estimate=pl.CostEstimate(flops=1_000_000_000, bytes_accessed=2_000_000, transcendentals=0),
+        cost_estimate=pl.CostEstimate(flops=10_000_000_000, bytes_accessed=2_000_000, transcendentals=0),
         name="recip_piece",
     )(cos_table, sin_table, coef, acc)
 
@@ -521,8 +522,8 @@
                 jnp.concatenate([low, upper[b : b + 1], lower[b : b + 1], high], axis=0)
                 for b, (low, high) in zip((0, CY - 1), ends)
             )
-            column_b = lax.ppermute(jnp.where(even_y, left, right), "gy", column_pairs(False))
-            near_send = jnp.where(even_y, right, left)
+            far_send, near_send = jnp.where(even_y, left, right), jnp.where(even_y, right, left)
+            column_b = lax.ppermute(far_send, "gy", column_pairs(False))
         elif step == 2:
             near_send, chunk = barrier((near_send, chunk))
             column_a = lax.ppermute(near_send, "gy", column_pairs(True))

time: 94.9 us -> 82.7 us (0.87)
  starting transfers between devices: 42.9 us -> 34.6 us
  waiting for transfers between devices: 21.3 us -> 17 us
    ppermute x1, starting transfers between devices: 14.3 us -> 2.1 us  [per_device(): column_a = lax.ppermute(near_send, 'gy', column_pairs(True))]
    ppermute x1, waiting for transfers between devices: 7.56 us -> 0.01 us  [per_device(): column_b = lax.ppermute(far_send, 'gy', column_pairs(False))]
    ppermute x1, starting transfers between devices: 3.48 us -> 10.4 us  [per_device(): column_b = lax.ppermute(far_send, 'gy', column_pairs(False))]
    ppermute x12, waiting for transfers between devices: 13.8 us -> 17 us  [permute(): return lax.ppermute(value, AXES, partner_list(step))]
    ppermute x12, starting transfers between devices: 20.1 us -> 17.1 us  [permute(): return lax.ppermute(value, AXES, partner_list(step))]
  transfers between devices with their start and end apart: 16 -> 16, of which waited for: 10 -> 9; matrix products, arithmetic and copies ran while one was open for 1% -> 1% of each run, Pallas kernels for 22% -> 25%
where the time goes in v8:
time: 82.7 us; the launch traced here: 82.5 us
  starting transfers between devices  34.6 us (42%)
  Pallas kernels  27.6 us (33%)
  waiting for transfers between devices  17 us (21%)
  local copies, waits for them, and re-layouts  1.85 us (2%)
  other arithmetic  0.88 us (1%)
    ppermute x12, starting transfers between devices, permute(): return lax.ppermute(value, AXES, partner_list(step))  17.1 us
    ppermute x12, waiting for transfers between devices, permute(): return lax.ppermute(value, AXES, partner_list(step))  17 us
    ppermute x1, starting transfers between devices, per_device(): column_b = lax.ppermute(far_send, 'gy', column_pairs(False))  10.4 us
    pallas_call x3, Pallas kernels, waves(): pl.pallas_call(functools.partial(wave_kernel, first), out_shape=out_shape...  9.36 us
    pallas_call x4, Pallas kernels, radial_piece(): pl.pallas_call(functools.partial(radial_kernel, near_cells, fresh), out_s...  6.73 us
    pallas_call x4, Pallas kernels, edge_piece(): pl.pallas_call(functools.partial(edge_kernel, along_x, which), out_shape=...  6.49 us
    ppermute x1, starting transfers between devices, per_device(): lax.ppermute(jnp.where(even_x, upper, lower), 'gx', row_pairs(False))  4.89 us
    pallas_call x1, Pallas kernels, final(): pl.pallas_call(final_kernel, out_shape=pltpu.MemorySpace.HBM((1024, WIDTH...  2.42 us
  transfers between devices with their start and end apart: 16, of which 9 were waited for; matrix products, arithmetic and copies ran while one was open for 1% of the time, Pallas kernels for 25%

profile of v8, /device:TPU:1, one launch (start us, length us, event | category | flops | bytes accessed | tf_op | source)
XLA Modules:
  0.0 82.5 jit_solution(9195330342308786278)
XLA Ops:
  0.2 4.2 %wave_tables.3 = (bf16[1024,512]{1,0:T(8,128)(2,1)}, bf16[1024,512]{1,0:T(8,128)(2,1)}, bf16[512,512]{1,0:T(8,128)(2,1)S(1)}, bf16[256,1024]{1,0:T(8,128)(2,1)S(...) custom-call(s32[2]{0:T(128)S(1)} %pad_add_fusion.place, bf16[2,3,4,128]{3,2,1,0:T(4,128)(2,1)} %bitcast.18, ...), custom_call_target="tpu_custom_call" | custom-call | flops 2048000000 | bytes 3000000 | tf_op jit(solution)/shard_map/wave_tables/pallas_call | solution.py:195
  4.4 3.3 %collective-permute-start = (bf16[512,512]{1,0:T(8,128)(2,1)S(1)}, bf16[512,512]{1,0:T(8,128)(2,1)S(1)}, u32[]{:S(2)}, u32[]{:S(2)}) collective-permute-start(bf16[512,512]{1,0:T(8,128)(2,1)S(1)} %get-tuple-element.53), channel_id=1, source_target_pairs={{0,1},{1,0},{16,17},{17,16},{32,33},{33,32},{48,49},{49,48},{2,3},... | collective-permute-start | bytes 1572872 | tf_op jit(solution)/shard_map/ppermute | solution.py:71
  7.8 4.9 %collective-permute-start.9 = (bf16[4,144,256]{2,1,0:T(8,128)(2,1)S(1)}, bf16[4,144,256]{2,1,0:T(8,128)(2,1)S(1)}, u32[]{:S(2)}, u32[]{:S(2)}) collective-permute-start(bf16[4,144,256]{2,1,0:T(8,128)(2,1)S(1)} %get-tuple-element.101), channel_id=1, source_target_pairs={{0,240},{16,32},{32,16},{48,64},{64,48},{80,96},{96,80},{112,128},... | collective-permute-start | bytes 884744 | tf_op jit(solution)/shard_map/ppermute | solution.py:472
  12.8 2.6 %wave_tables.4 = (bf16[1024,256]{1,0:T(8,128)(2,1)}, bf16[1024,256]{1,0:T(8,128)(2,1)}, f32[256,512]{1,0:T(8,128)S(1)}) custom-call(s32[2]{0:T(128)S(1)} %pad_add_fusion.place, bf16[2,3,4,128]{3,2,1,0:T(4,128)(2,1)S(1)} %bitcast.19, s32[3,1024]{1,0:T(4,128)S(1)} %copy-done.3, s32[1,256]{1,0:T(1,128)S(1)} %get-tuple-element.110.order, ...), custom_call_target="tpu_custom_call" | custom-call | flops 1024000000 | bytes 3000000 | tf_op jit(solution)/shard_map/wave_tables/pallas_call | solution.py:195
  15.6 2.8 %collective-permute-start.1 = (bf16[256,512]{1,0:T(8,128)(2,1)S(1)}, bf16[256,512]{1,0:T(8,128)(2,1)S(1)}, u32[]{:S(2)}, u32[]{:S(2)}) collective-permute-start(bf16[256,512]{1,0:T(8,128)(2,1)S(1)} %add_convert_fusion), channel_id=1, source_target_pairs={{0,4},{1,13},{16,20},{17,29},{32,36},{33,45},{48,52},{49,61},{2,6}... | collective-permute-start | bytes 786440 | tf_op jit(solution)/shard_map/ppermute | solution.py:71
  18.4 2.6 %wave_tables.5 = (bf16[1024,256]{1,0:T(8,128)(2,1)}, bf16[1024,256]{1,0:T(8,128)(2,1)}, f32[256,512]{1,0:T(8,128)S(1)}) custom-call(s32[2]{0:T(128)S(1)} %pad_add_fusion.place, bf16[2,3,4,128]{3,2,1,0:T(4,128)(2,1)S(1)} %bitcast.20, s32[3,1024]{1,0:T(4,128)S(1)} %copy-done.3, s32[1,256]{1,0:T(1,128)S(1)} %get-tuple-element.109.order, ...), custom_call_target="tpu_custom_call" | custom-call | flops 1024000000 | bytes 3000000 | tf_op jit(solution)/shard_map/wave_tables/pallas_call | solution.py:195
  21.1 1.3 %radial_prepare.1 = (f32[8,9]{1,0:T(8,128)S(1)}, f32[8,3,128,128]{3,2,1,0:T(8,128)S(1)}, f32[64,256]{1,0:T(8,128)S(1)}) custom-call(s32[2]{0:T(128)S(1)} %pad_add_fusion.place, s32[8]{0:T(128)S(1)} %reshape.729.near_count, s32[8,9]{1,0:T(8,128)S(1)} %bitcast.22, bf16[2,3,4,128]{3,2,1,0:T(4,128)(2,1)S(1)} %bitcast.21, bf16[4,256]{1,0:T(4,128)(2,1)S(1)} %copy-done.7), custom_call_target="tpu_custom_call" | custom-call | flops 500000000 | bytes 100000 | tf_op jit(solution)/shard_map/radial_prepare/pallas_call | solution.py:236
  23.0 1.4 %radial_piece.4.rest_2_ = f32[8,128,256]{2,1,0:T(8,128)S(1)} custom-call(f32[8]{0:T(128)S(1)} %copy-done.9, f32[8,9]{1,0:T(8,128)S(1)} %get-tuple-element.61.live, bf16[8,256]{1,0:T(8,128)(2,1)S(1)} %copy-done.6, f32[8,3,128,128]{3,2,1,0:T(8,128)S(1)} %get-tuple-element.62.mine, bf16[4,144,256]{2,1,0:T(8,128)(2,1)S(1)} %get-tuple-element.63.rest_0_, ...), custom_call_target="tpu_custom_call" | custom-call | flops 2000000000 | bytes 2000000 | tf_op jit(solution)/shard_map/radial_piece/pallas_call | solution.py:291
  24.4 2.2 %collective-permute-done.2 = bf16[128,512]{1,0:T(8,128)(2,1)S(1)} collective-permute-done((bf16[128,512]{1,0:T(8,128)(2,1)S(1)}, bf16[128,512]{1,0:T(8,128)(2,1)S(1)}, u32[]{:S(2)}, u32[]{:S(2)}) %collective-permute-start.2) | collective-permute-done | bytes 131104 | tf_op jit(solution)/shard_map/ppermute | solution.py:71
  26.6 0.6 collective-permute-start.3
  27.2 1.9 %radial_piece.5.rest_2_ = f32[8,128,256]{2,1,0:T(8,128)S(1)} custom-call(f32[8]{0:T(128)S(1)} %copy-done.9, f32[8,9]{1,0:T(8,128)S(1)} %get-tuple-element.61.live, bf16[8,256]{1,0:T(8,128)(2,1)S(1)} %copy-done.6, f32[8,3,128,128]{3,2,1,0:T(8,128)S(1)} %get-tuple-element.62.mine, ...), custom_call_target="tpu_custom_call", output_to_operand_aliasing={{}: (6, {})} | custom-call | flops 2000000000 | bytes 2000000 | tf_op jit(solution)/shard_map/radial_piece/pallas_call | solution.py:291
  29.1 1.9 %collective-permute-done.3 = bf16[64,512]{1,0:T(8,128)(2,1)S(1)} collective-permute-done((bf16[64,512]{1,0:T(8,128)(2,1)S(1)}, bf16[64,512]{1,0:T(8,128)(2,1)S(1)}, u32[]{:S(2)}, u32[]{:S(2)}) %collective-permute-start.3) | collective-permute-done | bytes 65568 | tf_op jit(solution)/shard_map/ppermute | solution.py:71
  31.3 1.9 %radial_piece.6.rest_2_ = f32[8,128,256]{2,1,0:T(8,128)S(1)} custom-call(f32[8]{0:T(128)S(1)} %copy-done.9, f32[8,9]{1,0:T(8,128)S(1)} %get-tuple-element.61.live, bf16[8,256]{1,0:T(8,128)(2,1)S(1)} %copy-done.6, f32[8,3,128,128]{3,2,1,0:T(8,128)S(1)} %get-tuple-element.62.mine, ...), custom_call_target="tpu_custom_call", output_to_operand_aliasing={{}: (6, {})} | custom-call | flops 2000000000 | bytes 2000000 | tf_op jit(solution)/shard_map/radial_piece/pallas_call | solution.py:291
  33.3 1.5 %collective-permute-done.4 = bf16[64,768]{1,0:T(8,128)(2,1)S(1)} collective-permute-done((bf16[64,768]{1,0:T(8,128)(2,1)S(1)}, bf16[64,768]{1,0:T(8,128)(2,1)S(1)}, u32[]{:S(2)}, u32[]{:S(2)}) %collective-permute-start.4) | collective-permute-done | bytes 98336 | tf_op jit(solution)/shard_map/ppermute | solution.py:71
  34.8 2.4 %collective-permute-start.5 = (bf16[64,768]{1,0:T(8,128)(2,1)S(1)}, bf16[64,768]{1,0:T(8,128)(2,1)S(1)}, u32[]{:S(2)}, u32[]{:S(2)}) collective-permute-start(bf16[64,768]{1,0:T(8,128)(2,1)S(1)} %convert_element_type.67), channel_id=1, source_target_pairs={{0,16},{1,51},{16,0},{17,33},{32,48},{33,17},{48,32},{49,3},{2,18}... | collective-permute-start | bytes 294920 | tf_op jit(solution)/shard_map/ppermute | solution.py:71
  37.2 1.6 %radial_piece.7.start = f32[8,128,256]{2,1,0:T(8,128)S(1)} custom-call(f32[8]{0:T(128)S(1)} %copy-done.9, f32[8,9]{1,0:T(8,128)S(1)} %get-tuple-element.61.live, bf16[8,256]{1,0:T(8,128)(2,1)S(1)} %copy-done.6, f32[8,3,128,128]{3,2,1,0:T(8,128)S(1)} %get-tuple-element.62.mine, ...), custom_call_target="tpu_custom_call", output_to_operand_aliasing={{}: (6, {})} | custom-call | flops 2000000000 | bytes 2000000 | tf_op jit(solution)/shard_map/radial_piece/pallas_call | solution.py:291
  38.8 0.8 collective-permute-done.5
  39.8 1.8 %radial_edge.4.start = f32[8,128,256]{2,1,0:T(8,128)S(1)} custom-call(s32[4]{0:T(128)S(1)} %pad_add_fusion.1.sides, f32[8]{0:T(128)S(1)} %copy-done.9, f32[8,9]{1,0:T(8,128)S(1)} %get-tuple-element.61.live, bf16[8,256]{1,0:T(8,128)(2,1)S(1)} %copy-done.6, f32[8,3,128,128]{3,2,1,0:T(8,128)S(1)} %get-tuple-element.62.mine, ...), custom_call_target="tpu_custom_call", output_to_operand_aliasing={{}: (6, {})} | custom-call | flops 20000000000 | bytes 2000000 | tf_op jit(solution)/shard_map/radial_edge/pallas_call | solution.py:362
  41.6 2.9 %collective-permute-done.6 = bf16[64,768]{1,0:T(8,128)(2,1)S(1)} collective-permute-done((bf16[64,768]{1,0:T(8,128)(2,1)S(1)}, bf16[64,768]{1,0:T(8,128)(2,1)S(1)}, u32[]{:S(2)}, u32[]{:S(2)}) %collective-permute-start.6) | collective-permute-done | bytes 98336 | tf_op jit(solution)/shard_map/ppermute | solution.py:71
  44.5 3.9 %collective-permute-start.8 = (bf16[64,768]{1,0:T(8,128)(2,1)S(1)}, bf16[64,768]{1,0:T(8,128)(2,1)S(1)}, u32[]{:S(2)}, u32[]{:S(2)}) collective-permute-start(bf16[64,768]{1,0:T(8,128)(2,1)S(1)} %convert_element_type.71), channel_id=1, source_target_pairs={{0,48},{1,19},{16,34},{17,3},{32,18},{33,51},{48,0},{49,35},{2,50}... | collective-permute-start | bytes 294920 | tf_op jit(solution)/shard_map/ppermute | solution.py:71
  48.4 1.8 %radial_edge.5 = f32[8,128,256]{2,1,0:T(8,128)S(1)} custom-call(s32[4]{0:T(128)S(1)} %pad_add_fusion.1.sides, f32[8]{0:T(128)S(1)} %copy-done.9, f32[8,9]{1,0:T(8,128)S(1)} %get-tuple-element.61.live, bf16[8,256]{1,0:T(8,128)(2,1)S(1)} %copy-done.6, f32[8,3,128,128]{3,2,1,0:T(8,128)S(1)} %get-tuple-element.62.mine, ...), custom_call_target="tpu_custom_call", output_to_operand_aliasing={{}: (6, {})} | custom-call | flops 20000000000 | bytes 2000000 | tf_op jit(solution)/shard_map/radial_edge/pallas_call | solution.py:362
  50.3 2.9 %collective-permute-done.8 = bf16[64,768]{1,0:T(8,128)(2,1)S(1)} collective-permute-done((bf16[64,768]{1,0:T(8,128)(2,1)S(1)}, bf16[64,768]{1,0:T(8,128)(2,1)S(1)}, u32[]{:S(2)}, u32[]{:S(2)}) %collective-permute-start.8) | collective-permute-done | bytes 98336 | tf_op jit(solution)/shard_map/ppermute | solution.py:71
  53.4 10.4 %collective-permute-start.15 = (bf16[4,144,256]{2,1,0:T(8,128)(2,1)S(1)}, bf16[4,144,256]{2,1,0:T(8,128)(2,1)S(1)}, u32[]{:S(2)}, u32[]{:S(2)}) collective-permute-start(bf16[4,144,256]{2,1,0:T(8,128)(2,1)S(1)} %get-tuple-element.95), channel_id=1, source_target_pairs={{0,15},{1,2},{2,1},{3,4},{4,3},{5,6},{6,5},{7,8},{8,7},{9,10},{10,... | collective-permute-start | bytes 884744 | tf_op jit(solution)/shard_map/ppermute | solution.py:526
  63.9 2.1 %collective-permute-start.13 = (bf16[4,144,256]{2,1,0:T(8,128)(2,1)S(1)}, bf16[4,144,256]{2,1,0:T(8,128)(2,1)S(1)}, u32[]{:S(2)}, u32[]{:S(2)}) collective-permute-start(bf16[4,144,256]{2,1,0:T(8,128)(2,1)S(1)} %get-tuple-element.87), channel_id=1, source_target_pairs={{0,1},{1,0},{2,3},{3,2},{4,5},{5,4},{6,7},{7,6},{8,9},{9,8},{10,11... | collective-permute-start | bytes 884744 | tf_op jit(solution)/shard_map/ppermute | solution.py:529
  66.5 1.5 %collective-permute-done.11 = bf16[128,512]{1,0:T(8,128)(2,1)S(1)} collective-permute-done((bf16[128,512]{1,0:T(8,128)(2,1)S(1)}, bf16[128,512]{1,0:T(8,128)(2,1)S(1)}, u32[]{:S(2)}, u32[]{:S(2)}) %collective-permute-start.11) | collective-permute-done | bytes 131104 | tf_op jit(solution)/shard_map/ppermute | solution.py:71
  68.0 2.8 %collective-permute-start.12 = (bf16[256,512]{1,0:T(8,128)(2,1)S(1)}, bf16[256,512]{1,0:T(8,128)(2,1)S(1)}, u32[]{:S(2)}, u32[]{:S(2)}) collective-permute-start(bf16[256,512]{1,0:T(8,128)(2,1)S(1)} %pad_maximum_fusion.3.coef), channel_id=1, source_target_pairs={{0,4},{1,13},{16,20},{17,29},{32,36},{33,45},{48,52},{49,61},{2,6}... | collective-permute-start | bytes 786440 | tf_op jit(solution)/shard_map/ppermute | solution.py:71
  70.9 1.4 %radial_edge.6 = f32[8,128,256]{2,1,0:T(8,128)S(1)} custom-call(s32[4]{0:T(128)S(1)} %pad_add_fusion.1.sides, f32[8]{0:T(128)S(1)} %copy-done.9, f32[8,9]{1,0:T(8,128)S(1)} %get-tuple-element.61.live, bf16[8,256]{1,0:T(8,128)(2,1)S(1)} %copy-done.6, f32[8,3,128,128]{3,2,1,0:T(8,128)S(1)} %get-tuple-element.62.mine, ...), custom_call_target="tpu_custom_call", output_to_operand_aliasing={{}: (6, {})} | custom-call | flops 20000000000 | bytes 2000000 | tf_op jit(solution)/shard_map/radial_edge/pallas_call | solution.py:362
  72.8 3.3 %collective-permute-done.12 = bf16[256,512]{1,0:T(8,128)(2,1)S(1)} collective-permute-done((bf16[256,512]{1,0:T(8,128)(2,1)S(1)}, bf16[256,512]{1,0:T(8,128)(2,1)S(1)}, u32[]{:S(2)}, u32[]{:S(2)}) %collective-permute-start.12) | collective-permute-done | bytes 262176 | tf_op jit(solution)/shard_map/ppermute | solution.py:71
  76.6 1.4 %radial_edge.7 = f32[8,128,256]{2,1,0:T(8,128)S(1)} custom-call(s32[4]{0:T(128)S(1)} %pad_add_fusion.1.sides, f32[8]{0:T(128)S(1)} %copy-done.9, f32[8,9]{1,0:T(8,128)S(1)} %get-tuple-element.61.live, bf16[8,256]{1,0:T(8,128)(2,1)S(1)} %copy-done.6, f32[8,3,128,128]{3,2,1,0:T(8,128)S(1)} %get-tuple-element.62.mine, ...), custom_call_target="tpu_custom_call", output_to_operand_aliasing={{}: (6, {})} | custom-call | flops 20000000000 | bytes 2000000 | tf_op jit(solution)/shard_map/radial_edge/pallas_call | solution.py:362
  78.1 0.5 recip_piece.5.acc
  78.6 0.5 copy-done
  79.9 2.4 %mix_and_network.1 = bf16[1024,256]{1,0:T(8,128)(2,1)} custom-call(bf16[1024,512]{1,0:T(8,128)(2,1)S(1)} %copy-done.14, bf16[1024,512]{1,0:T(8,128)(2,1)S(1)} %copy-done.15, bf16[512,512]{1,0:T(8,128)(2,1)S(1)} %collective-permute-done.14.coef, bf16[1024,256]{1,0:T(8,128)(2,1)S(1)} %bitcast.17, f32[1024,256]{1,0:T(8,128)S(1)} %recip_piece.5.acc, ...), custom_call_target="tpu_custom_call" | custom-call | flops 3000000000 | bytes 8000000 | tf_op jit(solution)/shard_map/mix_and_network/pallas_call | solution.py:422
  (79 shorter events, 4.5 us)
Async XLA Ops:
  0.2 12.6 %copy-start.16 = (s32[2,4]{1,0:T(2,128)S(1)}, s32[2,4]{1,0:T(2,128)}, u32[]{:S(2)}) copy-start(s32[2,4]{1,0:T(2,128)} %param.14) | copy-start | bytes 100
  0.2 12.6 %copy-start.3 = (s32[3,1024]{1,0:T(4,128)S(1)}, s32[3,1024]{1,0:T(4,128)}, u32[]{:S(2)}) copy-start(s32[3,1024]{1,0:T(4,128)} %miller.5) | copy-start | bytes 36868
  0.2 12.6 %copy-start.4 = (bf16[2,4,3,128]{3,1,2,0:T(4,128)(2,1)S(1)}, bf16[2,4,3,128]{3,1,2,0:T(4,128)(2,1)}, u32[]{:S(2)}) copy-start(bf16[2,4,3,128]{3,1,2,0:T(4,128)(2,1)} %param.12) | copy-start | bytes 18436
  4.4 11.2 %collective-permute-start = (bf16[512,512]{1,0:T(8,128)(2,1)S(1)}, bf16[512,512]{1,0:T(8,128)(2,1)S(1)}, u32[]{:S(2)}, u32[]{:S(2)}) collective-permute-start(bf16[512,512]{1,0:T(8,128)(2,1)S(1)} %get-tuple-element.53), channel_id=1, source_target_pairs={{0,1},{1,0},{16,17},{17,16},{32,33},{33,32},{48,49},{49,48},{2,3},... | collective-permute-start | bytes 1572872 | tf_op jit(solution)/shard_map/ppermute | solution.py:71
  7.7 32.0 %collective-permute-start.7 = (bf16[4,144,256]{2,1,0:T(8,128)(2,1)S(1)}, bf16[4,144,256]{2,1,0:T(8,128)(2,1)S(1)}, u32[]{:S(2)}, u32[]{:S(2)}) collective-permute-start(bf16[4,144,256]{2,1,0:T(8,128)(2,1)S(1)} %get-tuple-element.102), channel_id=1, source_target_pairs={{0,16},{16,0},{32,48},{48,32},{64,80},{80,64},{96,112},{112,96},{1... | collective-permute-start | bytes 884744 | tf_op jit(solution)/shard_map/ppermute | solution.py:471
  7.8 40.6 %collective-permute-start.9 = (bf16[4,144,256]{2,1,0:T(8,128)(2,1)S(1)}, bf16[4,144,256]{2,1,0:T(8,128)(2,1)S(1)}, u32[]{:S(2)}, u32[]{:S(2)}) collective-permute-start(bf16[4,144,256]{2,1,0:T(8,128)(2,1)S(1)} %get-tuple-element.101), channel_id=1, source_target_pairs={{0,240},{16,32},{32,16},{48,64},{64,48},{80,96},{96,80},{112,128},... | collective-permute-start | bytes 884744 | tf_op jit(solution)/shard_map/ppermute | solution.py:472
  15.6 6.9 %collective-permute-start.1 = (bf16[256,512]{1,0:T(8,128)(2,1)S(1)}, bf16[256,512]{1,0:T(8,128)(2,1)S(1)}, u32[]{:S(2)}, u32[]{:S(2)}) collective-permute-start(bf16[256,512]{1,0:T(8,128)(2,1)S(1)} %add_convert_fusion), channel_id=1, source_target_pairs={{0,4},{1,13},{16,20},{17,29},{32,36},{33,45},{48,52},{49,61},{2,6}... | collective-permute-start | bytes 786440 | tf_op jit(solution)/shard_map/ppermute | solution.py:71
  18.4 2.6 %copy-start.5 = (s32[2,4,9]{2,1,0:T(4,128)S(1)}, s32[2,4,9]{2,1,0:T(4,128)}, u32[]{:S(2)}) copy-start(s32[2,4,9]{2,1,0:T(4,128)} %param.13) | copy-start | bytes 868
  18.4 2.6 %copy-start.7 = (bf16[4,256]{1,0:T(4,128)(2,1)S(1)}, bf16[4,256]{1,0:T(4,128)(2,1)}, u32[]{:S(2)}) copy-start(bf16[4,256]{1,0:T(4,128)(2,1)} %row_filter.1) | copy-start | bytes 6148
  22.3 0.7 copy-start.6
  22.6 4.0 %collective-permute-start.2 = (bf16[128,512]{1,0:T(8,128)(2,1)S(1)}, bf16[128,512]{1,0:T(8,128)(2,1)S(1)}, u32[]{:S(2)}, u32[]{:S(2)}) collective-permute-start(bf16[128,512]{1,0:T(8,128)(2,1)S(1)} %get-tuple-element.60), channel_id=1, source_target_pairs={{0,12},{1,5},{16,28},{17,21},{32,44},{33,37},{48,60},{49,53},{2,14... | collective-permute-start | bytes 393224 | tf_op jit(solution)/shard_map/ppermute | solution.py:71
  26.6 4.4 %collective-permute-start.3 = (bf16[64,512]{1,0:T(8,128)(2,1)S(1)}, bf16[64,512]{1,0:T(8,128)(2,1)S(1)}, u32[]{:S(2)}, u32[]{:S(2)}) collective-permute-start(bf16[64,512]{1,0:T(8,128)(2,1)S(1)} %fusion.1), channel_id=1, source_target_pairs={{0,64},{1,193},{16,80},{17,209},{32,96},{33,225},{48,112},{49,241}... | collective-permute-start | bytes 196616 | tf_op jit(solution)/shard_map/ppermute | solution.py:71
  31.1 3.7 %collective-permute-start.4 = (bf16[64,768]{1,0:T(8,128)(2,1)S(1)}, bf16[64,768]{1,0:T(8,128)(2,1)S(1)}, u32[]{:S(2)}, u32[]{:S(2)}) collective-permute-start(bf16[64,768]{1,0:T(8,128)(2,1)S(1)} %convert_element_type.65), channel_id=1, source_target_pairs={{0,192},{1,65},{16,208},{17,81},{32,224},{33,97},{48,240},{49,113}... | collective-permute-start | bytes 294920 | tf_op jit(solution)/shard_map/ppermute | solution.py:71
  34.8 4.8 %collective-permute-start.5 = (bf16[64,768]{1,0:T(8,128)(2,1)S(1)}, bf16[64,768]{1,0:T(8,128)(2,1)S(1)}, u32[]{:S(2)}, u32[]{:S(2)}) collective-permute-start(bf16[64,768]{1,0:T(8,128)(2,1)S(1)} %convert_element_type.67), channel_id=1, source_target_pairs={{0,16},{1,51},{16,0},{17,33},{32,48},{33,17},{48,32},{49,3},{2,18}... | collective-permute-start | bytes 294920 | tf_op jit(solution)/shard_map/ppermute | solution.py:71
  39.7 4.8 %collective-permute-start.6 = (bf16[64,768]{1,0:T(8,128)(2,1)S(1)}, bf16[64,768]{1,0:T(8,128)(2,1)S(1)}, u32[]{:S(2)}, u32[]{:S(2)}) collective-permute-start(bf16[64,768]{1,0:T(8,128)(2,1)S(1)} %convert_element_type.69), channel_id=1, source_target_pairs={{0,50},{1,17},{16,32},{17,1},{32,16},{33,49},{48,2},{49,33},{2,48}... | collective-permute-start | bytes 294920 | tf_op jit(solution)/shard_map/ppermute | solution.py:71
  44.5 8.7 %collective-permute-start.8 = (bf16[64,768]{1,0:T(8,128)(2,1)S(1)}, bf16[64,768]{1,0:T(8,128)(2,1)S(1)}, u32[]{:S(2)}, u32[]{:S(2)}) collective-permute-start(bf16[64,768]{1,0:T(8,128)(2,1)S(1)} %convert_element_type.71), channel_id=1, source_target_pairs={{0,48},{1,19},{16,34},{17,3},{32,18},{33,51},{48,0},{49,35},{2,50}... | collective-permute-start | bytes 294920 | tf_op jit(solution)/shard_map/ppermute | solution.py:71
  50.2 15.8 %copy-start.12 = (bf16[1024,256]{1,0:T(8,128)(2,1)S(1)}, bf16[1024,256]{1,0:T(8,128)(2,1)}, u32[]{:S(2)}) copy-start(bf16[1024,256]{1,0:T(8,128)(2,1)} %get-tuple-element.83.cos_ref) | copy-start | bytes 1572868
  50.3 15.8 %copy-start.13 = (bf16[1024,256]{1,0:T(8,128)(2,1)S(1)}, bf16[1024,256]{1,0:T(8,128)(2,1)}, u32[]{:S(2)}) copy-start(bf16[1024,256]{1,0:T(8,128)(2,1)} %get-tuple-element.84.sin_ref) | copy-start | bytes 1572868
  53.2 10.6 %collective-permute-start.10 = (bf16[64,512]{1,0:T(8,128)(2,1)S(1)}, bf16[64,512]{1,0:T(8,128)(2,1)S(1)}, u32[]{:S(2)}, u32[]{:S(2)}) collective-permute-start(bf16[64,512]{1,0:T(8,128)(2,1)S(1)} %pad_maximum_fusion.6), channel_id=1, source_target_pairs={{0,64},{1,193},{16,80},{17,209},{32,96},{33,225},{48,112},{49,241}... | collective-permute-start | bytes 196616 | tf_op jit(solution)/shard_map/ppermute | solution.py:71
  53.4 23.1 %collective-permute-start.15 = (bf16[4,144,256]{2,1,0:T(8,128)(2,1)S(1)}, bf16[4,144,256]{2,1,0:T(8,128)(2,1)S(1)}, u32[]{:S(2)}, u32[]{:S(2)}) collective-permute-start(bf16[4,144,256]{2,1,0:T(8,128)(2,1)S(1)} %get-tuple-element.95), channel_id=1, source_target_pairs={{0,15},{1,2},{2,1},{3,4},{4,3},{5,6},{6,5},{7,8},{8,7},{9,10},{10,... | collective-permute-start | bytes 884744 | tf_op jit(solution)/shard_map/ppermute | solution.py:526
  63.8 4.2 %collective-permute-start.11 = (bf16[128,512]{1,0:T(8,128)(2,1)S(1)}, bf16[128,512]{1,0:T(8,128)(2,1)S(1)}, u32[]{:S(2)}, u32[]{:S(2)}) collective-permute-start(bf16[128,512]{1,0:T(8,128)(2,1)S(1)} %pad_maximum_fusion.5.coef), channel_id=1, source_target_pairs={{0,12},{1,5},{16,28},{17,21},{32,44},{33,37},{48,60},{49,53},{2,14... | collective-permute-start | bytes 393224 | tf_op jit(solution)/shard_map/ppermute | solution.py:71
  63.9 6.9 %collective-permute-start.13 = (bf16[4,144,256]{2,1,0:T(8,128)(2,1)S(1)}, bf16[4,144,256]{2,1,0:T(8,128)(2,1)S(1)}, u32[]{:S(2)}, u32[]{:S(2)}) collective-permute-start(bf16[4,144,256]{2,1,0:T(8,128)(2,1)S(1)} %get-tuple-element.87), channel_id=1, source_target_pairs={{0,1},{1,0},{2,3},{3,2},{4,5},{5,4},{6,7},{7,6},{8,9},{9,8},{10,11... | collective-permute-start | bytes 884744 | tf_op jit(solution)/shard_map/ppermute | solution.py:529
  68.0 8.0 %collective-permute-start.12 = (bf16[256,512]{1,0:T(8,128)(2,1)S(1)}, bf16[256,512]{1,0:T(8,128)(2,1)S(1)}, u32[]{:S(2)}, u32[]{:S(2)}) collective-permute-start(bf16[256,512]{1,0:T(8,128)(2,1)S(1)} %pad_maximum_fusion.3.coef), channel_id=1, source_target_pairs={{0,4},{1,13},{16,20},{17,29},{32,36},{33,45},{48,52},{49,61},{2,6}... | collective-permute-start | bytes 786440 | tf_op jit(solution)/shard_map/ppermute | solution.py:71
  76.1 1.9 %copy-start.10 = (bf16[1024,256]{1,0:T(8,128)(2,1)S(1)}, bf16[1024,256]{1,0:T(8,128)(2,1)}, u32[]{:S(2)}) copy-start(bf16[1024,256]{1,0:T(8,128)(2,1)} %get-tuple-element.90.cos_ref) | copy-start | bytes 1572868
  76.1 1.9 %copy-start.11 = (bf16[1024,256]{1,0:T(8,128)(2,1)S(1)}, bf16[1024,256]{1,0:T(8,128)(2,1)}, u32[]{:S(2)}) copy-start(bf16[1024,256]{1,0:T(8,128)(2,1)} %get-tuple-element.91.sin_ref) | copy-start | bytes 1572868
  76.1 2.5 %collective-permute-start.14 = (bf16[512,512]{1,0:T(8,128)(2,1)S(1)}, bf16[512,512]{1,0:T(8,128)(2,1)S(1)}, u32[]{:S(2)}, u32[]{:S(2)}) collective-permute-start(bf16[512,512]{1,0:T(8,128)(2,1)S(1)} %pad_maximum_fusion.coef), channel_id=1, source_target_pairs={{0,1},{1,0},{16,17},{17,16},{32,33},{33,32},{48,49},{49,48},{2,3},... | collective-permute-start | bytes 1572872 | tf_op jit(solution)/shard_map/ppermute | solution.py:71
  78.0 1.0 %copy-start = (bf16[2,4,128,256]{3,2,1,0:T(8,128)(2,1)S(1)}, bf16[2,4,128,256]{3,2,1,0:T(8,128)(2,1)}, u32[]{:S(2)}) copy-start(bf16[2,4,128,256]{3,2,1,0:T(8,128)(2,1)} %param.11) | copy-start | bytes 1572868
  78.0 1.1 %copy-start.1 = (bf16[256,512]{1,0:T(8,128)(2,1)S(1)}, bf16[256,512]{1,0:T(8,128)(2,1)}, u32[]{:S(2)}) copy-start(bf16[256,512]{1,0:T(8,128)(2,1)} %w_in.1) | copy-start | bytes 786436
  78.1 1.2 %copy-start.2 = (bf16[512,256]{1,0:T(8,128)(2,1)S(1)}, bf16[512,256]{1,0:T(8,128)(2,1)}, u32[]{:S(2)}) copy-start(bf16[512,256]{1,0:T(8,128)(2,1)} %w_out.1) | copy-start | bytes 786436
  78.1 1.2 %copy-start.8 = (f32[256]{0:T(256)S(1)}, f32[256]{0:T(256)}, u32[]{:S(2)}) copy-start(f32[256]{0:T(256)} %param.19) | copy-start | bytes 3076
  78.1 1.5 %copy-start.14 = (bf16[1024,512]{1,0:T(8,128)(2,1)S(1)}, bf16[1024,512]{1,0:T(8,128)(2,1)}, u32[]{:S(2)}) copy-start(bf16[1024,512]{1,0:T(8,128)(2,1)} %get-tuple-element.49.cos_ref) | copy-start | bytes 3145732
  78.1 1.8 %copy-start.15 = (bf16[1024,512]{1,0:T(8,128)(2,1)S(1)}, bf16[1024,512]{1,0:T(8,128)(2,1)}, u32[]{:S(2)}) copy-start(bf16[1024,512]{1,0:T(8,128)(2,1)} %get-tuple-element.50.sin_ref) | copy-start | bytes 3145732
  (1 other events, 0.7 us)

commit v9 on v8

--- a/solution.py
+++ b/solution.py
@@ -82,8 +82,8 @@
     rest = pos % 4
     mz = (pos // 4) % 8
     mb = (pos // 32) % 2
-    b3 = (pos // 64) % 2
-    b2 = (pos // 128) % 2
+    b2 = (pos // 64) % 2
+    b3 = (pos // 128) % 2
     b1 = (pos // 256) % 2
     owner = core ^ (pos // 512)
     oy = y ^ jnp.where(owner == 0, b1 ^ (3 * b2), (3 * b1) ^ b2)
@@ -96,16 +96,16 @@
 
 
 def wave_kernel(first, place, coords, miller, order, source, cos_out, sin_out, sums, *rest):
-    cos_ref, sin_ref, sems = rest[-3:]
+    cos_ref, sin_ref, copies = cos_out, sin_out, []
     if first:
         turned, packed, features = rest[0], rest[1:3], rest[3]
         coords_in, miller_in = coords, miller
-        coords, miller = rest[4:6]
+        coords, miller, cos_ref, sin_ref, sems, table_sems = rest[4:]
         fetch = [
-            pltpu.make_async_copy(coords_in, coords, sems.at[2, 1]),
-            pltpu.make_async_copy(miller_in, miller, sems.at[2, 2]),
+            pltpu.make_async_copy(coords_in, coords, sems.at[1]),
+            pltpu.make_async_copy(miller_in, miller, sems.at[2]),
         ]
-        load = pltpu.make_async_copy(source, features, sems.at[2, 0])
+        load = pltpu.make_async_copy(source, features, sems.at[0])
         for copy in fetch + [load]:
             copy.start()
         for copy in fetch:
@@ -119,9 +119,9 @@
     pick = jnp.where(natural == order[...], 1.0, 0.0).astype(BF16)
     placed = jnp.dot(five, pick, preferred_element_type=F32).astype(BF16)
     ones = jnp.ones((1, ATOMS), F32)
-    copies = []
 
     for cell in range(CX * CY):
+        rows_at = pl.ds(cell * ATOMS, ATOMS)
         ia, ib = cell // CY, cell % CY
         block = [coords[ia, d, ib : ib + 1, :].astype(F32) for d in range(3)]
         along = (place[0] * CX + ia).astype(F32) / 32.0
@@ -137,11 +137,10 @@
             ],
             axis=0,
         )
-        columns = rows.T.astype(BF16)
-        rows_at = pl.ds(cell * ATOMS, ATOMS)
+        at = rows.T.astype(BF16)
         for j in range(size // 256):
             lanes = slice(j * 256, (j + 1) * 256)
-            angle = jnp.dot(columns, placed[:, lanes], preferred_element_type=F32)
+            angle = jnp.dot(at, placed[:, lanes], preferred_element_type=F32)
             r = angle - jnp.round(angle)
             s = r * r
             sine = SIN_COEF[3]
@@ -153,10 +152,12 @@
             double = sine + sine
             cos_ref[rows_at, lanes] = (1.0 - double * sine).astype(BF16)
             sin_ref[rows_at, lanes] = (double * cosine).astype(BF16)
-        for i, (source, target) in enumerate(((cos_ref, cos_out), (sin_ref, sin_out))):
-            copy = pltpu.make_async_copy(source.at[rows_at], target.at[rows_at], sems.at[i, cell])
-            copy.start()
-            copies.append(copy)
+
+        if first:
+            for i, (table, target) in enumerate(((cos_ref, cos_out), (sin_ref, sin_out))):
+                copy = pltpu.make_async_copy(table.at[rows_at], target.at[rows_at], table_sems.at[i, cell])
+                copy.start()
+                copies.append(copy)
 
     if first:
         load.wait()
@@ -180,23 +181,24 @@
     place_of = hbm if first else vm
     size = order.shape[1]
     out_shape = [
-        pltpu.MemorySpace.HBM((1024, size), BF16),
-        pltpu.MemorySpace.HBM((1024, size), BF16),
+        (pltpu.MemorySpace.HBM if first else pltpu.MemorySpace.VMEM)((1024, size), BF16),
+        (pltpu.MemorySpace.HBM if first else pltpu.MemorySpace.VMEM)((1024, size), BF16),
         jax.ShapeDtypeStruct((size, 2 * WIDTH), BF16 if first else F32),
     ]
-    scratch = [VMEM((1024, size), BF16), VMEM((1024, size), BF16), pltpu.SemaphoreType.DMA((3, CX * CY))]
+    scratch = []
     if first:
         source, coords, miller = (
             pltpu.with_memory_space_constraint(value, pltpu.MemorySpace.HBM) for value in (source, coords, miller)
         )
         out_shape.append(jax.ShapeDtypeStruct((WIDTH, 1024), BF16))
         out_shape += [jax.ShapeDtypeStruct((CY, PACK, WIDTH), BF16)] * CX
-        scratch = [VMEM((1024, WIDTH), BF16), VMEM(coords.shape, BF16), VMEM(miller.shape, jnp.int32)] + scratch
+        scratch = [VMEM((1024, WIDTH), BF16), VMEM(coords.shape, BF16), VMEM(miller.shape, jnp.int32)]
+        scratch += [VMEM((1024, size), BF16)] * 2 + [pltpu.SemaphoreType.DMA((3,)), pltpu.SemaphoreType.DMA((2, CX * CY))]
     return pl.pallas_call(
         functools.partial(wave_kernel, first),
         out_shape=out_shape,
         in_specs=[pl.BlockSpec(memory_space=pltpu.SMEM), place_of, place_of, vm, place_of],
-        out_specs=[hbm, hbm] + [vm] * (len(out_shape) - 2),
+        out_specs=[place_of, place_of] + [vm] * (len(out_shape) - 2),
         scratch_shapes=scratch,
         compiler_params=pltpu.CompilerParams(vmem_limit_bytes=14 * 1024 * 1024),
         cost_estimate=pl.CostEstimate(flops=size * 4_000_000, bytes_accessed=3_000_000, transcendentals=0),
@@ -357,6 +359,7 @@
 
 
 def edge_piece(along_x, which, sides, gammas, live, filters, mine, block, acc):
+    flops = 20_000_000_000
     vm = pl.BlockSpec(memory_space=VMEM)
     sm = pl.BlockSpec(memory_space=pltpu.SMEM)
     return pl.pallas_call(
@@ -367,44 +370,49 @@
         scratch_shapes=[VMEM((2, 8 * ATOMS, WIDTH), BF16)],
         input_output_aliases={6: 0},
         compiler_params=pltpu.CompilerParams(vmem_limit_bytes=10 * 1024 * 1024),
-        cost_estimate=pl.CostEstimate(flops=20_000_000_000, bytes_accessed=2_000_000, transcendentals=0),
+        cost_estimate=pl.CostEstimate(flops=flops, bytes_accessed=2_000_000, transcendentals=0),
         name="radial_edge",
     )(sides, gammas, live, filters, mine, block, acc)
 
 
-def recip_kernel(low, high, cos_ref, sin_ref, coef, start, acc):
-    at = slice(low, high)
-    lanes = slice(low % 256, (high - 1) % 256 + 1)
+def recip_kernel(spots, *refs):
+    coef, start, acc = refs[-3:]
     for row in range(4):
         rows = slice(row * 256, row * 256 + 256)
-        acc[rows] = (
-            start[rows]
-            + jnp.dot(cos_ref[rows, lanes], coef[at, 0:WIDTH], preferred_element_type=F32)
-            + jnp.dot(sin_ref[rows, lanes], coef[at, WIDTH:], preferred_element_type=F32)
-        )
-
-
-def recip_piece(low, high, cos_table, sin_table, coef, acc):
+        total = start[rows]
+        for i, (column, at) in enumerate(spots):
+            lanes, span = slice(column, column + 128), slice(at, at + 128)
+            total += jnp.dot(refs[2 * i][rows, lanes], coef[span, 0:WIDTH], preferred_element_type=F32)
+            total += jnp.dot(refs[2 * i + 1][rows, lanes], coef[span, WIDTH:], preferred_element_type=F32)
+        acc[rows] = total
+
+
+def recip_piece(parts, far, coef, acc):
     vm = pl.BlockSpec(memory_space=VMEM)
+    tables = [table for part in parts for table in part[:2]] + list(far)
     return pl.pallas_call(
-        functools.partial(recip_kernel, low, high),
+        functools.partial(recip_kernel, tuple(part[2:] for part in parts)),
         out_shape=jax.ShapeDtypeStruct((1024, WIDTH), F32),
-        in_specs=[vm] * 4,
+        in_specs=[vm] * (len(tables) + 2),
         out_specs=vm,
-        input_output_aliases={3: 0},
+        input_output_aliases={len(tables) + 1: 0},
         compiler_params=pltpu.CompilerParams(vmem_limit_bytes=10 * 1024 * 1024),
         cost_estimate=pl.CostEstimate(flops=10_000_000_000, bytes_accessed=2_000_000, transcendentals=0),
         name="recip_piece",
-    )(cos_table, sin_table, coef, acc)
-
-
-def final_kernel(cos_ref, sin_ref, coef, features, acc, gain, w_in, w_out, out, result, sems):
+    )(*tables, coef, acc)
+
+
+def final_kernel(cos_ref, sin_ref, coef_in, upper, lower, acc, gain, w_in, w_out, out, coef, result, sems):
+    for block, source in enumerate((0, 2, 1, 3)):
+        coef[block * 128 : block * 128 + 128, :] = coef_in[source * 128 : source * 128 + 128, :]
     copies = []
     for block in range(4):
         rows = pl.ds(block * 256, 256)
         recip = jnp.dot(cos_ref[rows, :], coef[:, 0:WIDTH], preferred_element_type=F32)
         recip += jnp.dot(sin_ref[rows, :], coef[:, WIDTH:], preferred_element_type=F32)
-        mixed = features[rows, :].astype(F32) + acc[rows, :] + recip
+        cells = (upper, lower)[block // 2]
+        features = jnp.concatenate([cells[block % 2 * 2 + i, 0:ATOMS, :] for i in range(2)], axis=0)
+        mixed = features.astype(F32) + acc[rows, :] + recip
         power = jnp.mean(mixed * mixed, axis=-1, keepdims=True)
         normed = (mixed * lax.rsqrt(power + epsilon) * gain[...]).astype(BF16)
         v = jnp.dot(normed, w_in[...], preferred_element_type=F32)
@@ -417,18 +425,18 @@
         copy.wait()
 
 
-def final(cos_table, sin_table, coef, features, acc, gain, w_in, w_out):
+def final(cos_table, sin_table, coef, upper, lower, acc, gain, w_in, w_out):
     whole = pl.BlockSpec(memory_space=VMEM)
     return pl.pallas_call(
         final_kernel,
         out_shape=pltpu.MemorySpace.HBM((1024, WIDTH), BF16),
-        in_specs=[whole] * 8,
+        in_specs=[whole] * 9,
         out_specs=pl.BlockSpec(memory_space=pl.ANY),
-        scratch_shapes=[VMEM((1024, WIDTH), BF16), pltpu.SemaphoreType.DMA((4,))],
+        scratch_shapes=[VMEM((HALF, 2 * WIDTH), BF16), VMEM((1024, WIDTH), BF16), pltpu.SemaphoreType.DMA((4,))],
         compiler_params=pltpu.CompilerParams(vmem_limit_bytes=14 * 1024 * 1024),
         cost_estimate=pl.CostEstimate(flops=3_000_000_000, bytes_accessed=8_000_000, transcendentals=0),
         name="mix_and_network",
-    )(cos_table, sin_table, coef, features, acc, gain, w_in, w_out)
+    )(cos_table, sin_table, coef, upper, lower, acc, gain, w_in, w_out)
 
 
 def row_pairs(first):
@@ -440,6 +448,14 @@
 
 def column_pairs(first):
     return row_pairs(first)
+
+
+def first_blocks(rows):
+    return jnp.concatenate([rows[0:64], rows[128:192]], axis=0)
+
+
+def second_blocks(rows):
+    return jnp.concatenate([rows[64:128], rows[192:256]], axis=0)
 
 
 def per_device(
@@ -482,7 +498,10 @@
         return edge_piece(along_x, which, sides, gammas, live, radial_filter, mine, block, acc)
 
     for step, height in ((1, 256), (2, 128), (3, 64)):
-        send = ((keep_next if step == 1 else keep[height:]) + got[height:].astype(F32)).astype(BF16)
+        if step == 2:
+            send = (second_blocks(keep) + second_blocks(got).astype(F32)).astype(BF16)
+        else:
+            send = ((keep_next if step == 1 else keep[height:]) + got[height:].astype(F32)).astype(BF16)
         if step == 2:
             send, live, mine, filters = barrier((send, live, mine, filters))
         elif step == 3:
@@ -496,7 +515,10 @@
             )
         else:
             acc = own_piece(step - 2, acc)
-        keep = keep[:height] + got[:height].astype(F32)
+        if step == 2:
+            keep = first_blocks(keep) + first_blocks(got).astype(F32)
+        else:
+            keep = keep[:height] + got[:height].astype(F32)
         got = fresh
     total = jnp.concatenate([keep + got.astype(F32), filters], axis=1)
     for step in range(4):
@@ -510,10 +532,10 @@
     scale = total[:, 2 * WIDTH :]
     chunk = jnp.concatenate([total[:, :WIDTH] * scale, total[:, WIDTH : 2 * WIDTH] * scale], axis=1).astype(BF16)
     chunk, row_a, row_b = barrier((chunk, row_a, row_b))
-    for step, low_at, high_at in ((3, 0, 0), (2, 0, 128), (1, 128, 256), (0, 256, 512)):
+    for turn, step in enumerate((2, 1, 3, 0)):
         chunk, acc = barrier((chunk, acc))
         fresh = permute(chunk, HALVING[step])
-        if step == 3:
+        if turn == 0:
             ends = [
                 (jnp.where(even_x, row_b[b : b + 1], row_a[b : b + 1]), jnp.where(even_x, row_a[b : b + 1], row_b[b : b + 1]))
                 for b in (0, CY - 1)
@@ -524,22 +546,28 @@
             )
             far_send, near_send = jnp.where(even_y, left, right), jnp.where(even_y, right, left)
             column_b = lax.ppermute(far_send, "gy", column_pairs(False))
-        elif step == 2:
+        elif turn == 1:
             near_send, chunk = barrier((near_send, chunk))
             column_a = lax.ppermute(near_send, "gy", column_pairs(True))
-        elif step == 1:
+        elif turn == 2:
             acc = beyond(False, 2, column_a, acc)
-        elif step == 0:
+        elif turn == 3:
             acc = beyond(False, 3, column_b, acc)
-        if high_at:
-            tables = (cos_near, sin_near) if high_at <= 256 else (cos_next, sin_next)
-            acc = recip_piece(low_at, high_at, *tables, chunk, acc.reshape(1024, WIDTH)).reshape(CX * CY, ATOMS, WIDTH)
+        parts = (
+            (),
+            ((cos_near, sin_near, 0, 0),),
+            ((cos_next, sin_next, 0, 128),),
+            ((cos_near, sin_near, 128, 256), (cos_next, sin_next, 128, 384)),
+        )[turn]
+        if parts:
+            far = (cos_far, sin_far, w_in, w_out) if turn > 1 else ()
+            acc = recip_piece(parts, far, chunk, acc.reshape(1024, WIDTH)).reshape(CX * CY, ATOMS, WIDTH)
         if step:
             chunk = jnp.concatenate([chunk, fresh], axis=0)
     acc = acc.reshape(1024, WIDTH)
 
     out = final(
-        cos_far, sin_far, fresh, own_rows, acc, norm_gain.reshape(1, WIDTH), w_in, w_out
+        cos_far, sin_far, fresh, upper, lower, acc, norm_gain.reshape(1, WIDTH), w_in, w_out
     )
     return out.reshape(CX, CY, ATOMS, WIDTH)
 

time: 82.7 us -> 83.2 us (level)
  waiting for transfers between devices: 17 us -> 21.4 us
  local copies, waits for them, and re-layouts: 1.85 us -> 0.22 us
  starting transfers between devices: 34.6 us -> 33.1 us
    ppermute x12, waiting for transfers between devices: 17 us -> 21.4 us  [permute(): return lax.ppermute(value, AXES, partner_list(step))]
    ppermute x1, starting transfers between devices: 10.4 us -> 13.3 us  [per_device(): column_b = lax.ppermute(far_send, 'gy', column_pairs(False))]
    ppermute x12, starting transfers between devices: 17.1 us -> 14.7 us  [permute(): return lax.ppermute(value, AXES, partner_list(step))]
    ppermute x1, starting transfers between devices: 2.1 us -> 0.09 us  [per_device(): column_a = lax.ppermute(near_send, 'gy', column_pairs(True))]
    unnamed x34 -> x24, local copies, waits for them, and re-layouts: 1.74 us -> 0.06 us
    pallas_call x3, Pallas kernels: 9.36 us -> 8.33 us  [waves(): pl.pallas_call(functools.partial(wave_kernel, first), out_shape=out_shape...]
where the time goes in v9:
time: 83.2 us; the launch traced here: 83.1 us
  starting transfers between devices  33.1 us (40%)
  Pallas kernels  26.9 us (32%)
  waiting for transfers between devices  21.4 us (26%)
  other arithmetic  0.9 us (1%)
    ppermute x12, waiting for transfers between devices, permute(): return lax.ppermute(value, AXES, partner_list(step))  21.4 us
    ppermute x12, starting transfers between devices, permute(): return lax.ppermute(value, AXES, partner_list(step))  14.7 us
    ppermute x1, starting transfers between devices, per_device(): column_b = lax.ppermute(far_send, 'gy', column_pairs(False))  13.3 us
    pallas_call x3, Pallas kernels, waves(): pl.pallas_call(functools.partial(wave_kernel, first), out_shape=out_shape...  8.33 us
    pallas_call x4, Pallas kernels, radial_piece(): pl.pallas_call(functools.partial(radial_kernel, near_cells, fresh), out_s...  6.82 us
    pallas_call x4, Pallas kernels, edge_piece(): pl.pallas_call(functools.partial(edge_kernel, along_x, which), out_shape=...  6.53 us
    ppermute x1, starting transfers between devices, per_device(): lax.ppermute(jnp.where(even_x, upper, lower), 'gx', row_pairs(False))  4.89 us
    pallas_call x1, Pallas kernels, final(): pl.pallas_call(final_kernel, out_shape=pltpu.MemorySpace.HBM((1024, WIDTH...  2.44 us
  transfers between devices with their start and end apart: 16, of which 9 were waited for; matrix products, arithmetic and copies ran while one was open for 1% of the time, Pallas kernels for 25%

profile of v9, /device:TPU:1, one launch (start us, length us, event | category | flops | bytes accessed | tf_op | source)
XLA Modules:
  0.0 83.1 jit_solution(5216846855159487475)
XLA Ops:
  0.2 4.1 %wave_tables.3 = (bf16[1024,512]{1,0:T(8,128)(2,1)}, bf16[1024,512]{1,0:T(8,128)(2,1)}, bf16[512,512]{1,0:T(8,128)(2,1)S(1)}, bf16[256,1024]{1,0:T(8,128)(2,1)S(...) custom-call(s32[2]{0:T(128)S(1)} %pad_add_fusion.place, bf16[2,3,4,128]{3,2,1,0:T(4,128)(2,1)} %bitcast.16, ...), custom_call_target="tpu_custom_call" | custom-call | flops 2048000000 | bytes 3000000 | tf_op jit(solution)/shard_map/wave_tables/pallas_call | solution.py:197
  4.3 3.3 %collective-permute-start = (bf16[512,512]{1,0:T(8,128)(2,1)S(1)}, bf16[512,512]{1,0:T(8,128)(2,1)S(1)}, u32[]{:S(2)}, u32[]{:S(2)}) collective-permute-start(bf16[512,512]{1,0:T(8,128)(2,1)S(1)} %get-tuple-element.53), channel_id=1, source_target_pairs={{0,1},{1,0},{16,17},{17,16},{32,33},{33,32},{48,49},{49,48},{2,3},... | collective-permute-start | bytes 1572872 | tf_op jit(solution)/shard_map/ppermute | solution.py:71
  7.8 4.9 %collective-permute-start.9 = (bf16[4,144,256]{2,1,0:T(8,128)(2,1)S(1)}, bf16[4,144,256]{2,1,0:T(8,128)(2,1)S(1)}, u32[]{:S(2)}, u32[]{:S(2)}) collective-permute-start(bf16[4,144,256]{2,1,0:T(8,128)(2,1)S(1)} %get-tuple-element.99), channel_id=1, source_target_pairs={{0,240},{16,32},{32,16},{48,64},{64,48},{80,96},{96,80},{112,128},... | collective-permute-start | bytes 884744 | tf_op jit(solution)/shard_map/ppermute | solution.py:488
  12.8 2.1 %wave_tables.4 = (bf16[1024,256]{1,0:T(8,128)(2,1)S(1)}, bf16[1024,256]{1,0:T(8,128)(2,1)S(1)}, f32[256,512]{1,0:T(8,128)S(1)}) custom-call(s32[2]{0:T(128)S(1)} %pad_add_fusion.place, bf16[2,3,4,128]{3,2,1,0:T(4,128)(2,1)S(1)} %bitcast.17, s32[3,1024]{1,0:T(4,128)S(1)} %copy-done.2, s32[1,256]{1,0:T(1,128)S(1)} %get-tuple-element.116.order, ...), custom_call_target="tpu_custom_call" | custom-call | flops 1024000000 | bytes 3000000 | tf_op jit(solution)/shard_map/wave_tables/pallas_call | solution.py:197
  15.1 2.8 %collective-permute-start.1 = (bf16[256,512]{1,0:T(8,128)(2,1)S(1)}, bf16[256,512]{1,0:T(8,128)(2,1)S(1)}, u32[]{:S(2)}, u32[]{:S(2)}) collective-permute-start(bf16[256,512]{1,0:T(8,128)(2,1)S(1)} %add_convert_fusion), channel_id=1, source_target_pairs={{0,4},{1,13},{16,20},{17,29},{32,36},{33,45},{48,52},{49,61},{2,6}... | collective-permute-start | bytes 786440 | tf_op jit(solution)/shard_map/ppermute | solution.py:71
  17.9 2.1 %wave_tables.5 = (bf16[1024,256]{1,0:T(8,128)(2,1)S(1)}, bf16[1024,256]{1,0:T(8,128)(2,1)S(1)}, f32[256,512]{1,0:T(8,128)S(1)}) custom-call(s32[2]{0:T(128)S(1)} %pad_add_fusion.place, bf16[2,3,4,128]{3,2,1,0:T(4,128)(2,1)S(1)} %bitcast.18, s32[3,1024]{1,0:T(4,128)S(1)} %copy-done.2, s32[1,256]{1,0:T(1,128)S(1)} %get-tuple-element.115.order, ...), custom_call_target="tpu_custom_call" | custom-call | flops 1024000000 | bytes 3000000 | tf_op jit(solution)/shard_map/wave_tables/pallas_call | solution.py:197
  20.1 1.3 %radial_prepare.1 = (f32[8,9]{1,0:T(8,128)S(1)}, f32[8,3,128,128]{3,2,1,0:T(8,128)S(1)}, f32[64,256]{1,0:T(8,128)S(1)}) custom-call(s32[2]{0:T(128)S(1)} %pad_add_fusion.place, s32[8]{0:T(128)S(1)} %reshape.729.near_count, s32[8,9]{1,0:T(8,128)S(1)} %bitcast.20, bf16[2,3,4,128]{3,2,1,0:T(4,128)(2,1)S(1)} %bitcast.19, bf16[4,256]{1,0:T(4,128)(2,1)S(1)} %copy-done.6), custom_call_target="tpu_custom_call" | custom-call | flops 500000000 | bytes 100000 | tf_op jit(solution)/shard_map/radial_prepare/pallas_call | solution.py:238
  21.4 0.5 collective-permute-done.1
  22.1 1.4 %radial_piece.4.rest_2_ = f32[8,128,256]{2,1,0:T(8,128)S(1)} custom-call(f32[8]{0:T(128)S(1)} %copy-done.8, f32[8,9]{1,0:T(8,128)S(1)} %get-tuple-element.61.live, bf16[8,256]{1,0:T(8,128)(2,1)S(1)} %copy-done.5, f32[8,3,128,128]{3,2,1,0:T(8,128)S(1)} %get-tuple-element.62.mine, bf16[4,144,256]{2,1,0:T(8,128)(2,1)S(1)} %get-tuple-element.63.rest_0_.upper, ...), custom_call_target="tpu_custom_call" | custom-call | flops 2000000000 | bytes 2000000 | tf_op jit(solution)/shard_map/radial_piece/pallas_call | solution.py:293
  23.6 2.7 %collective-permute-done.2 = bf16[128,512]{1,0:T(8,128)(2,1)S(1)} collective-permute-done((bf16[128,512]{1,0:T(8,128)(2,1)S(1)}, bf16[128,512]{1,0:T(8,128)(2,1)S(1)}, u32[]{:S(2)}, u32[]{:S(2)}) %collective-permute-start.2) | collective-permute-done | bytes 131104 | tf_op jit(solution)/shard_map/ppermute | solution.py:71
  26.2 0.6 collective-permute-start.3
  26.9 1.9 %radial_piece.5.rest_2_ = f32[8,128,256]{2,1,0:T(8,128)S(1)} custom-call(f32[8]{0:T(128)S(1)} %copy-done.8, f32[8,9]{1,0:T(8,128)S(1)} %get-tuple-element.61.live, bf16[8,256]{1,0:T(8,128)(2,1)S(1)} %copy-done.5, f32[8,3,128,128]{3,2,1,0:T(8,128)S(1)} %get-tuple-element.62.mine, ...), custom_call_target="tpu_custom_call", output_to_operand_aliasing={{}: (6, {})} | custom-call | flops 2000000000 | bytes 2000000 | tf_op jit(solution)/shard_map/radial_piece/pallas_call | solution.py:293
  28.8 1.8 %collective-permute-done.3 = bf16[64,512]{1,0:T(8,128)(2,1)S(1)} collective-permute-done((bf16[64,512]{1,0:T(8,128)(2,1)S(1)}, bf16[64,512]{1,0:T(8,128)(2,1)S(1)}, u32[]{:S(2)}, u32[]{:S(2)}) %collective-permute-start.3) | collective-permute-done | bytes 65568 | tf_op jit(solution)/shard_map/ppermute | solution.py:71
  31.0 1.9 %radial_piece.6.rest_2_ = f32[8,128,256]{2,1,0:T(8,128)S(1)} custom-call(f32[8]{0:T(128)S(1)} %copy-done.8, f32[8,9]{1,0:T(8,128)S(1)} %get-tuple-element.61.live, bf16[8,256]{1,0:T(8,128)(2,1)S(1)} %copy-done.5, f32[8,3,128,128]{3,2,1,0:T(8,128)S(1)} %get-tuple-element.62.mine, ...), custom_call_target="tpu_custom_call", output_to_operand_aliasing={{}: (6, {})} | custom-call | flops 2000000000 | bytes 2000000 | tf_op jit(solution)/shard_map/radial_piece/pallas_call | solution.py:293
  32.9 1.5 %collective-permute-done.4 = bf16[64,768]{1,0:T(8,128)(2,1)S(1)} collective-permute-done((bf16[64,768]{1,0:T(8,128)(2,1)S(1)}, bf16[64,768]{1,0:T(8,128)(2,1)S(1)}, u32[]{:S(2)}, u32[]{:S(2)}) %collective-permute-start.4) | collective-permute-done | bytes 98336 | tf_op jit(solution)/shard_map/ppermute | solution.py:71
  34.5 2.3 %collective-permute-start.5 = (bf16[64,768]{1,0:T(8,128)(2,1)S(1)}, bf16[64,768]{1,0:T(8,128)(2,1)S(1)}, u32[]{:S(2)}, u32[]{:S(2)}) collective-permute-start(bf16[64,768]{1,0:T(8,128)(2,1)S(1)} %convert_element_type.67), channel_id=1, source_target_pairs={{0,16},{1,51},{16,0},{17,33},{32,48},{33,17},{48,32},{49,3},{2,18}... | collective-permute-start | bytes 294920 | tf_op jit(solution)/shard_map/ppermute | solution.py:71
  36.8 1.6 %radial_piece.7.start = f32[8,128,256]{2,1,0:T(8,128)S(1)} custom-call(f32[8]{0:T(128)S(1)} %copy-done.8, f32[8,9]{1,0:T(8,128)S(1)} %get-tuple-element.61.live, bf16[8,256]{1,0:T(8,128)(2,1)S(1)} %copy-done.5, f32[8,3,128,128]{3,2,1,0:T(8,128)S(1)} %get-tuple-element.62.mine, ...), custom_call_target="tpu_custom_call", output_to_operand_aliasing={{}: (6, {})} | custom-call | flops 2000000000 | bytes 2000000 | tf_op jit(solution)/shard_map/radial_piece/pallas_call | solution.py:293
  38.4 0.9 %collective-permute-done.5 = bf16[64,768]{1,0:T(8,128)(2,1)S(1)} collective-permute-done((bf16[64,768]{1,0:T(8,128)(2,1)S(1)}, bf16[64,768]{1,0:T(8,128)(2,1)S(1)}, u32[]{:S(2)}, u32[]{:S(2)}) %collective-permute-start.5) | collective-permute-done | bytes 98336 | tf_op jit(solution)/shard_map/ppermute | solution.py:71
  39.4 1.8 %radial_edge.4.start = f32[8,128,256]{2,1,0:T(8,128)S(1)} custom-call(s32[4]{0:T(128)S(1)} %pad_add_fusion.1.sides, f32[8]{0:T(128)S(1)} %copy-done.8, f32[8,9]{1,0:T(8,128)S(1)} %get-tuple-element.61.live, bf16[8,256]{1,0:T(8,128)(2,1)S(1)} %copy-done.5, f32[8,3,128,128]{3,2,1,0:T(8,128)S(1)} %get-tuple-element.62.mine, ...), custom_call_target="tpu_custom_call", output_to_operand_aliasing={{}: (6, {})} | custom-call | flops 20000000000 | bytes 2000000 | tf_op jit(solution)/shard_map/radial_edge/pallas_call | solution.py:365
  41.3 2.8 %collective-permute-done.6 = bf16[64,768]{1,0:T(8,128)(2,1)S(1)} collective-permute-done((bf16[64,768]{1,0:T(8,128)(2,1)S(1)}, bf16[64,768]{1,0:T(8,128)(2,1)S(1)}, u32[]{:S(2)}, u32[]{:S(2)}) %collective-permute-start.6) | collective-permute-done | bytes 98336 | tf_op jit(solution)/shard_map/ppermute | solution.py:71
  44.1 3.7 %collective-permute-start.8 = (bf16[64,768]{1,0:T(8,128)(2,1)S(1)}, bf16[64,768]{1,0:T(8,128)(2,1)S(1)}, u32[]{:S(2)}, u32[]{:S(2)}) collective-permute-start(bf16[64,768]{1,0:T(8,128)(2,1)S(1)} %convert_element_type.71), channel_id=1, source_target_pairs={{0,48},{1,19},{16,34},{17,3},{32,18},{33,51},{48,0},{49,35},{2,50}... | collective-permute-start | bytes 294920 | tf_op jit(solution)/shard_map/ppermute | solution.py:71
  47.8 1.8 %radial_edge.5 = f32[8,128,256]{2,1,0:T(8,128)S(1)} custom-call(s32[4]{0:T(128)S(1)} %pad_add_fusion.1.sides, f32[8]{0:T(128)S(1)} %copy-done.8, f32[8,9]{1,0:T(8,128)S(1)} %get-tuple-element.61.live, bf16[8,256]{1,0:T(8,128)(2,1)S(1)} %copy-done.5, f32[8,3,128,128]{3,2,1,0:T(8,128)S(1)} %get-tuple-element.62.mine, ...), custom_call_target="tpu_custom_call", output_to_operand_aliasing={{}: (6, {})} | custom-call | flops 20000000000 | bytes 2000000 | tf_op jit(solution)/shard_map/radial_edge/pallas_call | solution.py:365
  49.6 2.9 %collective-permute-done.8 = bf16[64,768]{1,0:T(8,128)(2,1)S(1)} collective-permute-done((bf16[64,768]{1,0:T(8,128)(2,1)S(1)}, bf16[64,768]{1,0:T(8,128)(2,1)S(1)}, u32[]{:S(2)}, u32[]{:S(2)}) %collective-permute-start.8) | collective-permute-done | bytes 98336 | tf_op jit(solution)/shard_map/ppermute | solution.py:71
  52.9 13.3 %collective-permute-start.15 = (bf16[4,144,256]{2,1,0:T(8,128)(2,1)S(1)}, bf16[4,144,256]{2,1,0:T(8,128)(2,1)S(1)}, u32[]{:S(2)}, u32[]{:S(2)}) collective-permute-start(bf16[4,144,256]{2,1,0:T(8,128)(2,1)S(1)} %get-tuple-element.93), channel_id=1, source_target_pairs={{0,15},{1,2},{2,1},{3,4},{4,3},{5,6},{6,5},{7,8},{8,7},{9,10},{10,... | collective-permute-start | bytes 884744 | tf_op jit(solution)/shard_map/ppermute | solution.py:548
  66.9 4.5 %collective-permute-done.11 = bf16[128,512]{1,0:T(8,128)(2,1)S(1)} collective-permute-done((bf16[128,512]{1,0:T(8,128)(2,1)S(1)}, bf16[128,512]{1,0:T(8,128)(2,1)S(1)}, u32[]{:S(2)}, u32[]{:S(2)}) %collective-permute-start.11) | collective-permute-done | bytes 131104 | tf_op jit(solution)/shard_map/ppermute | solution.py:71
  71.4 0.8 collective-permute-start.12
  72.2 1.4 %radial_edge.6 = f32[8,128,256]{2,1,0:T(8,128)S(1)} custom-call(s32[4]{0:T(128)S(1)} %pad_add_fusion.1.sides, f32[8]{0:T(128)S(1)} %copy-done.8, f32[8,9]{1,0:T(8,128)S(1)} %get-tuple-element.61.live, bf16[8,256]{1,0:T(8,128)(2,1)S(1)} %copy-done.5, f32[8,3,128,128]{3,2,1,0:T(8,128)S(1)} %get-tuple-element.62.mine, ...), custom_call_target="tpu_custom_call", output_to_operand_aliasing={{}: (6, {})} | custom-call | flops 20000000000 | bytes 2000000 | tf_op jit(solution)/shard_map/radial_edge/pallas_call | solution.py:365
  73.7 0.4 recip_piece.4
  74.1 3.8 %collective-permute-done.12 = bf16[256,512]{1,0:T(8,128)(2,1)S(1)} collective-permute-done((bf16[256,512]{1,0:T(8,128)(2,1)S(1)}, bf16[256,512]{1,0:T(8,128)(2,1)S(1)}, u32[]{:S(2)}, u32[]{:S(2)}) %collective-permute-start.12) | collective-permute-done | bytes 262176 | tf_op jit(solution)/shard_map/ppermute | solution.py:71
  78.3 1.4 %radial_edge.7 = f32[8,128,256]{2,1,0:T(8,128)S(1)} custom-call(s32[4]{0:T(128)S(1)} %pad_add_fusion.1.sides, f32[8]{0:T(128)S(1)} %copy-done.8, f32[8,9]{1,0:T(8,128)S(1)} %get-tuple-element.61.live, bf16[8,256]{1,0:T(8,128)(2,1)S(1)} %copy-done.5, f32[8,3,128,128]{3,2,1,0:T(8,128)S(1)} %get-tuple-element.62.mine, ...), custom_call_target="tpu_custom_call", output_to_operand_aliasing={{}: (6, {})} | custom-call | flops 20000000000 | bytes 2000000 | tf_op jit(solution)/shard_map/radial_edge/pallas_call | solution.py:365
  79.8 0.7 recip_piece.5.acc
  80.5 2.4 %mix_and_network.1 = bf16[1024,256]{1,0:T(8,128)(2,1)} custom-call(bf16[1024,512]{1,0:T(8,128)(2,1)S(1)} %copy-done.9, bf16[1024,512]{1,0:T(8,128)(2,1)S(1)} %copy-done.10, bf16[512,512]{1,0:T(8,128)(2,1)S(1)} %collective-permute-done.14.coef_in, bf16[4,144,256]{2,1,0:T(8,128)(2,1)S(1)} %get-tuple-element.63.rest_0_.upper, ...), custom_call_target="tpu_custom_call" | custom-call | flops 3000000000 | bytes 8000000 | tf_op jit(solution)/shard_map/mix_and_network/pallas_call | solution.py:430
  (72 shorter events, 2.9 us)
Async XLA Ops:
  0.2 12.5 %copy-start.11 = (s32[2,4]{1,0:T(2,128)S(1)}, s32[2,4]{1,0:T(2,128)}, u32[]{:S(2)}) copy-start(s32[2,4]{1,0:T(2,128)} %param.14) | copy-start | bytes 100
  0.2 12.6 %copy-start.2 = (s32[3,1024]{1,0:T(4,128)S(1)}, s32[3,1024]{1,0:T(4,128)}, u32[]{:S(2)}) copy-start(s32[3,1024]{1,0:T(4,128)} %miller.5) | copy-start | bytes 36868
  0.2 12.6 %copy-start.3 = (bf16[2,4,3,128]{3,1,2,0:T(4,128)(2,1)S(1)}, bf16[2,4,3,128]{3,1,2,0:T(4,128)(2,1)}, u32[]{:S(2)}) copy-start(bf16[2,4,3,128]{3,1,2,0:T(4,128)(2,1)} %param.12) | copy-start | bytes 18436
  4.3 10.7 %collective-permute-start = (bf16[512,512]{1,0:T(8,128)(2,1)S(1)}, bf16[512,512]{1,0:T(8,128)(2,1)S(1)}, u32[]{:S(2)}, u32[]{:S(2)}) collective-permute-start(bf16[512,512]{1,0:T(8,128)(2,1)S(1)} %get-tuple-element.53), channel_id=1, source_target_pairs={{0,1},{1,0},{16,17},{17,16},{32,33},{33,32},{48,49},{49,48},{2,3},... | collective-permute-start | bytes 1572872 | tf_op jit(solution)/shard_map/ppermute | solution.py:71
  7.7 31.7 %collective-permute-start.7 = (bf16[4,144,256]{2,1,0:T(8,128)(2,1)S(1)}, bf16[4,144,256]{2,1,0:T(8,128)(2,1)S(1)}, u32[]{:S(2)}, u32[]{:S(2)}) collective-permute-start(bf16[4,144,256]{2,1,0:T(8,128)(2,1)S(1)} %get-tuple-element.100), channel_id=1, source_target_pairs={{0,16},{16,0},{32,48},{48,32},{64,80},{80,64},{96,112},{112,96},{1... | collective-permute-start | bytes 884744 | tf_op jit(solution)/shard_map/ppermute | solution.py:487
  7.8 40.0 %collective-permute-start.9 = (bf16[4,144,256]{2,1,0:T(8,128)(2,1)S(1)}, bf16[4,144,256]{2,1,0:T(8,128)(2,1)S(1)}, u32[]{:S(2)}, u32[]{:S(2)}) collective-permute-start(bf16[4,144,256]{2,1,0:T(8,128)(2,1)S(1)} %get-tuple-element.99), channel_id=1, source_target_pairs={{0,240},{16,32},{32,16},{48,64},{64,48},{80,96},{96,80},{112,128},... | collective-permute-start | bytes 884744 | tf_op jit(solution)/shard_map/ppermute | solution.py:488
  15.1 6.9 %collective-permute-start.1 = (bf16[256,512]{1,0:T(8,128)(2,1)S(1)}, bf16[256,512]{1,0:T(8,128)(2,1)S(1)}, u32[]{:S(2)}, u32[]{:S(2)}) collective-permute-start(bf16[256,512]{1,0:T(8,128)(2,1)S(1)} %add_convert_fusion), channel_id=1, source_target_pairs={{0,4},{1,13},{16,20},{17,29},{32,36},{33,45},{48,52},{49,61},{2,6}... | collective-permute-start | bytes 786440 | tf_op jit(solution)/shard_map/ppermute | solution.py:71
  17.9 2.2 %copy-start.4 = (s32[2,4,9]{2,1,0:T(4,128)S(1)}, s32[2,4,9]{2,1,0:T(4,128)}, u32[]{:S(2)}) copy-start(s32[2,4,9]{2,1,0:T(4,128)} %param.13) | copy-start | bytes 868
  17.9 2.2 %copy-start.6 = (bf16[4,256]{1,0:T(4,128)(2,1)S(1)}, bf16[4,256]{1,0:T(4,128)(2,1)}, u32[]{:S(2)}) copy-start(bf16[4,256]{1,0:T(4,128)(2,1)} %row_filter.1) | copy-start | bytes 6148
  20.1 2.0 %copy-start.5 = (bf16[8,256]{1,0:T(8,128)(2,1)S(1)}, bf16[8,256]{1,0:T(8,128)(2,1)}, u32[]{:S(2)}) copy-start(bf16[8,256]{1,0:T(8,128)(2,1)} %filters.15) | copy-start | bytes 12292
  20.1 2.0 %copy-start.8 = (f32[8]{0:T(128)S(1)}, f32[8]{0:T(128)}, u32[]{:S(2)}) copy-start(f32[8]{0:T(128)} %rates.15) | copy-start | bytes 100
  22.0 4.2 %collective-permute-start.2 = (bf16[128,512]{1,0:T(8,128)(2,1)S(1)}, bf16[128,512]{1,0:T(8,128)(2,1)S(1)}, u32[]{:S(2)}, u32[]{:S(2)}) collective-permute-start(bf16[128,512]{1,0:T(8,128)(2,1)S(1)} %fusion), channel_id=1, source_target_pairs={{0,12},{1,5},{16,28},{17,21},{32,44},{33,37},{48,60},{49,53},{2,14... | collective-permute-start | bytes 393224 | tf_op jit(solution)/shard_map/ppermute | solution.py:71
  26.2 4.4 %collective-permute-start.3 = (bf16[64,512]{1,0:T(8,128)(2,1)S(1)}, bf16[64,512]{1,0:T(8,128)(2,1)S(1)}, u32[]{:S(2)}, u32[]{:S(2)}) collective-permute-start(bf16[64,512]{1,0:T(8,128)(2,1)S(1)} %fusion.1), channel_id=1, source_target_pairs={{0,64},{1,193},{16,80},{17,209},{32,96},{33,225},{48,112},{49,241}... | collective-permute-start | bytes 196616 | tf_op jit(solution)/shard_map/ppermute | solution.py:71
  30.7 3.7 %collective-permute-start.4 = (bf16[64,768]{1,0:T(8,128)(2,1)S(1)}, bf16[64,768]{1,0:T(8,128)(2,1)S(1)}, u32[]{:S(2)}, u32[]{:S(2)}) collective-permute-start(bf16[64,768]{1,0:T(8,128)(2,1)S(1)} %convert_element_type.65), channel_id=1, source_target_pairs={{0,192},{1,65},{16,208},{17,81},{32,224},{33,97},{48,240},{49,113}... | collective-permute-start | bytes 294920 | tf_op jit(solution)/shard_map/ppermute | solution.py:71
  34.5 4.8 %collective-permute-start.5 = (bf16[64,768]{1,0:T(8,128)(2,1)S(1)}, bf16[64,768]{1,0:T(8,128)(2,1)S(1)}, u32[]{:S(2)}, u32[]{:S(2)}) collective-permute-start(bf16[64,768]{1,0:T(8,128)(2,1)S(1)} %convert_element_type.67), channel_id=1, source_target_pairs={{0,16},{1,51},{16,0},{17,33},{32,48},{33,17},{48,32},{49,3},{2,18}... | collective-permute-start | bytes 294920 | tf_op jit(solution)/shard_map/ppermute | solution.py:71
  39.3 4.7 %collective-permute-start.6 = (bf16[64,768]{1,0:T(8,128)(2,1)S(1)}, bf16[64,768]{1,0:T(8,128)(2,1)S(1)}, u32[]{:S(2)}, u32[]{:S(2)}) collective-permute-start(bf16[64,768]{1,0:T(8,128)(2,1)S(1)} %convert_element_type.69), channel_id=1, source_target_pairs={{0,50},{1,17},{16,32},{17,1},{32,16},{33,49},{48,2},{49,33},{2,48}... | collective-permute-start | bytes 294920 | tf_op jit(solution)/shard_map/ppermute | solution.py:71
  44.1 8.4 %collective-permute-start.8 = (bf16[64,768]{1,0:T(8,128)(2,1)S(1)}, bf16[64,768]{1,0:T(8,128)(2,1)S(1)}, u32[]{:S(2)}, u32[]{:S(2)}) collective-permute-start(bf16[64,768]{1,0:T(8,128)(2,1)S(1)} %convert_element_type.71), channel_id=1, source_target_pairs={{0,48},{1,19},{16,34},{17,3},{32,18},{33,51},{48,0},{49,35},{2,50}... | collective-permute-start | bytes 294920 | tf_op jit(solution)/shard_map/ppermute | solution.py:71
  52.6 13.6 %collective-permute-start.10 = (bf16[64,512]{1,0:T(8,128)(2,1)S(1)}, bf16[64,512]{1,0:T(8,128)(2,1)S(1)}, u32[]{:S(2)}, u32[]{:S(2)}) collective-permute-start(bf16[64,512]{1,0:T(8,128)(2,1)S(1)} %pad_maximum_fusion.6), channel_id=1, source_target_pairs={{0,12},{1,5},{16,28},{17,21},{32,44},{33,37},{48,60},{49,53},{2,14... | collective-permute-start | bytes 196616 | tf_op jit(solution)/shard_map/ppermute | solution.py:71
  52.9 25.4 %collective-permute-start.15 = (bf16[4,144,256]{2,1,0:T(8,128)(2,1)S(1)}, bf16[4,144,256]{2,1,0:T(8,128)(2,1)S(1)}, u32[]{:S(2)}, u32[]{:S(2)}) collective-permute-start(bf16[4,144,256]{2,1,0:T(8,128)(2,1)S(1)} %get-tuple-element.93), channel_id=1, source_target_pairs={{0,15},{1,2},{2,1},{3,4},{4,3},{5,6},{6,5},{7,8},{8,7},{9,10},{10,... | collective-permute-start | bytes 884744 | tf_op jit(solution)/shard_map/ppermute | solution.py:548
  66.2 5.1 %collective-permute-start.11 = (bf16[128,512]{1,0:T(8,128)(2,1)S(1)}, bf16[128,512]{1,0:T(8,128)(2,1)S(1)}, u32[]{:S(2)}, u32[]{:S(2)}) collective-permute-start(bf16[128,512]{1,0:T(8,128)(2,1)S(1)} %pad_maximum_fusion.5.refs_2_), channel_id=1, source_target_pairs={{0,4},{1,13},{16,20},{17,29},{32,36},{33,45},{48,52},{49,61},{2,6}... | collective-permute-start | bytes 393224 | tf_op jit(solution)/shard_map/ppermute | solution.py:71
  66.3 5.8 %collective-permute-start.13 = (bf16[4,144,256]{2,1,0:T(8,128)(2,1)S(1)}, bf16[4,144,256]{2,1,0:T(8,128)(2,1)S(1)}, u32[]{:S(2)}, u32[]{:S(2)}) collective-permute-start(bf16[4,144,256]{2,1,0:T(8,128)(2,1)S(1)} %get-tuple-element.89), channel_id=1, source_target_pairs={{0,1},{1,0},{2,3},{3,2},{4,5},{5,4},{6,7},{7,6},{8,9},{9,8},{10,11... | collective-permute-start | bytes 884744 | tf_op jit(solution)/shard_map/ppermute | solution.py:551
  71.4 2.3 %copy-start = (bf16[256,512]{1,0:T(8,128)(2,1)S(1)}, bf16[256,512]{1,0:T(8,128)(2,1)}, u32[]{:S(2)}) copy-start(bf16[256,512]{1,0:T(8,128)(2,1)} %w_in.1) | copy-start | bytes 786436
  71.4 2.3 %copy-start.1 = (bf16[512,256]{1,0:T(8,128)(2,1)S(1)}, bf16[512,256]{1,0:T(8,128)(2,1)}, u32[]{:S(2)}) copy-start(bf16[512,256]{1,0:T(8,128)(2,1)} %w_out.1) | copy-start | bytes 786436
  71.4 2.3 %copy-start.9 = (bf16[1024,512]{1,0:T(8,128)(2,1)S(1)}, bf16[1024,512]{1,0:T(8,128)(2,1)}, u32[]{:S(2)}) copy-start(bf16[1024,512]{1,0:T(8,128)(2,1)} %get-tuple-element.49.refs_2_.refs_4_.cos_ref) | copy-start | bytes 3145732
  71.4 2.3 %copy-start.10 = (bf16[1024,512]{1,0:T(8,128)(2,1)S(1)}, bf16[1024,512]{1,0:T(8,128)(2,1)}, u32[]{:S(2)}) copy-start(bf16[1024,512]{1,0:T(8,128)(2,1)} %get-tuple-element.50.refs_3_.refs_5_.sin_ref) | copy-start | bytes 3145732
  71.4 6.5 %collective-permute-start.12 = (bf16[256,512]{1,0:T(8,128)(2,1)S(1)}, bf16[256,512]{1,0:T(8,128)(2,1)S(1)}, u32[]{:S(2)}, u32[]{:S(2)}) collective-permute-start(bf16[256,512]{1,0:T(8,128)(2,1)S(1)} %pad_maximum_fusion.3.refs_6_), channel_id=1, source_target_pairs={{0,64},{1,193},{16,80},{17,209},{32,96},{33,225},{48,112},{49,241}... | collective-permute-start | bytes 786440 | tf_op jit(solution)/shard_map/ppermute | solution.py:71
  78.0 2.5 %collective-permute-start.14 = (bf16[512,512]{1,0:T(8,128)(2,1)S(1)}, bf16[512,512]{1,0:T(8,128)(2,1)S(1)}, u32[]{:S(2)}, u32[]{:S(2)}) collective-permute-start(bf16[512,512]{1,0:T(8,128)(2,1)S(1)} %pad_maximum_fusion.refs_8_), channel_id=1, source_target_pairs={{0,1},{1,0},{16,17},{17,16},{32,33},{33,32},{48,49},{49,48},{2,3},... | collective-permute-start | bytes 1572872 | tf_op jit(solution)/shard_map/ppermute | solution.py:71
  79.8 0.7 copy-start.7

commit v10 on v9

--- a/solution.py
+++ b/solution.py
@@ -92,6 +92,19 @@
     return linear(ox, oy, mz, owner) * 4 + rest
 
 
+def z_sources():
+    table = []
+    for core in range(2):
+        for own in range(8):
+            for b in range(8):
+                z = own
+                for which in (2, 1, 0):
+                    if b >> which & 1:
+                        z = flip_z(which)(0, 0, z, core)[2]
+                table.append(z)
+    return jnp.asarray(table, jnp.int32)
+
+
 HALF = 512
 
 
@@ -108,15 +121,15 @@
         load = pltpu.make_async_copy(source, features, sems.at[0])
         for copy in fetch + [load]:
             copy.start()
-        for copy in fetch:
-            copy.wait()
     else:
-        turned = source
-    number = miller[...].astype(F32)
-    five = jnp.concatenate([number, number[0:2], jnp.zeros((3, 1024), F32)], axis=0).astype(BF16)
+        turned, fetch = source, ()
     size = order.shape[1]
     natural = lax.broadcasted_iota(jnp.int32, (1024, size), 0)
     pick = jnp.where(natural == order[...], 1.0, 0.0).astype(BF16)
+    for copy in fetch:
+        copy.wait()
+    number = miller[...].astype(F32)
+    five = jnp.concatenate([number, number[0:2], jnp.zeros((3, 1024), F32)], axis=0).astype(BF16)
     placed = jnp.dot(five, pick, preferred_element_type=F32).astype(BF16)
     ones = jnp.ones((1, ATOMS), F32)
 
@@ -206,7 +219,17 @@
     )(place, coords, miller, order, source)
 
 
-def prepare_kernel(place, near_count, near_list, coords, row_filter, live, mine, filters):
+def prepare_kernel(place, near_count, sources, near_list, coords, live, mine, placement):
+    row = lax.broadcasted_iota(jnp.int32, (CHUNK, 32), 0)
+    at = lax.broadcasted_iota(jnp.int32, (CHUNK, 32), 1)
+    core, x, z = place[1] % 2, place[0] // 4, place[0] % 4 + 4 * ((place[1] // 2) % 2)
+    from_z = jnp.zeros((CHUNK, 32), jnp.int32)
+    for b in range(8):
+        from_z = jnp.where(at // 4 == b, sources[(core * 8 + z) * 8 + b], from_z)
+    half = jnp.where(core == 0, x // 2, x % 2)
+    member = (half ^ (at // 2 % 2)) * 8 + from_z
+    placement[...] = jnp.where((row // 4 == member) & (row % 4 // 2 == at % 2), 1.0, 0.0)
+
     shape = (CX * CY, 9)
     cell = lax.broadcasted_iota(jnp.int32, shape, 0)
     slot = lax.broadcasted_iota(jnp.int32, shape, 1)
@@ -225,14 +248,10 @@
         columns = jnp.concatenate(rows + [jnp.zeros((5, ATOMS), F32)], axis=0).T
         for d in range(3):
             mine[c, d] = jnp.broadcast_to(columns[:, d : d + 1], (ATOMS, ATOMS))
-    x, z = place[0] // 4, place[0] % 4 + 4 * ((place[1] // 2) % 2)
-    member = jnp.where(place[1] % 2 == 0, x // 2, x % 2) * 8 + z
-    whole = jnp.concatenate([row_filter[...].astype(F32)] * (CHUNK // 4), axis=0)
-    slots = lax.broadcasted_iota(jnp.int32, (CHUNK, WIDTH), 0) // 4
-    filters[...] = jnp.where(slots == member, whole, 0.0)
-
-
-def prepare(place, near_count, near_list, coords, row_filter):
+
+
+def prepare(place, near_count, near_list, coords):
+    sources = z_sources()
     vm = pl.BlockSpec(memory_space=VMEM)
     sm = pl.BlockSpec(memory_space=pltpu.SMEM)
     return pl.pallas_call(
@@ -240,14 +259,14 @@
         out_shape=(
             jax.ShapeDtypeStruct((CX * CY, 9), F32),
             jax.ShapeDtypeStruct((CX * CY, 3, ATOMS, ATOMS), F32),
-            jax.ShapeDtypeStruct((CHUNK, WIDTH), F32),
+            jax.ShapeDtypeStruct((CHUNK, 32), F32),
         ),
-        in_specs=[sm, sm, vm, vm, vm],
+        in_specs=[sm, sm, sm, vm, vm],
         out_specs=(vm, vm, vm),
         compiler_params=pltpu.CompilerParams(vmem_limit_bytes=6 * 1024 * 1024),
         cost_estimate=pl.CostEstimate(flops=500_000_000, bytes_accessed=100_000, transcendentals=0),
         name="radial_prepare",
-    )(place, near_count, near_list, coords, row_filter)
+    )(place, near_count, sources, near_list, coords)
 
 
 def radial_kernel(near_cells, fresh, rates, live, filters, mine, *rest):
@@ -375,6 +394,29 @@
     )(sides, gammas, live, filters, mine, block, acc)
 
 
+def coefficient_kernel(total, rows, fresh, placement, out):
+    gathered = jnp.concatenate([rows[...], fresh[CHUNK:, :]], axis=0)
+    placed = jnp.dot(placement[...].astype(BF16), gathered, preferred_element_type=F32)
+    odd = lax.broadcasted_iota(jnp.int32, (CHUNK, WIDTH), 0) % 2 == 1
+    scale = jnp.where(odd, placed[:, WIDTH:], placed[:, :WIDTH])
+    sums = total[...] + fresh[0:CHUNK, :].astype(F32)
+    out[:, :WIDTH] = (sums[:, :WIDTH] * scale).astype(BF16)
+    out[:, WIDTH:] = (sums[:, WIDTH:] * scale).astype(BF16)
+
+
+def coefficients(total, rows, fresh, placement):
+    vm = pl.BlockSpec(memory_space=VMEM)
+    return pl.pallas_call(
+        coefficient_kernel,
+        out_shape=jax.ShapeDtypeStruct((CHUNK, 2 * WIDTH), BF16),
+        in_specs=[vm] * 4,
+        out_specs=vm,
+        compiler_params=pltpu.CompilerParams(vmem_limit_bytes=4 * 1024 * 1024),
+        cost_estimate=pl.CostEstimate(flops=100_000_000, bytes_accessed=200_000, transcendentals=0),
+        name="coefficients",
+    )(total, rows, fresh, placement)
+
+
 def recip_kernel(spots, *refs):
     coef, start, acc = refs[-3:]
     for row in range(4):
@@ -503,16 +545,14 @@
         else:
             send = ((keep_next if step == 1 else keep[height:]) + got[height:].astype(F32)).astype(BF16)
         if step == 2:
-            send, live, mine, filters = barrier((send, live, mine, filters))
+            send, live, mine, placement = barrier((send, live, mine, placement))
         elif step == 3:
             send, acc = barrier((send, acc))
         fresh = permute(send, HALVING[step])
         if step == 1:
             across, place, send = barrier((across, place, send))
             cos_near, sin_near, keep = waves(place, turned, miller, order[:, :256], across, False)
-            live, mine, filters = prepare(
-                place, nbr_count.reshape(8), nbr_cells.reshape(8, 9), turned, reciprocal_filter
-            )
+            live, mine, placement = prepare(place, nbr_count.reshape(8), nbr_cells.reshape(8, 9), turned)
         else:
             acc = own_piece(step - 2, acc)
         if step == 2:
@@ -520,17 +560,19 @@
         else:
             keep = keep[:height] + got[:height].astype(F32)
         got = fresh
-    total = jnp.concatenate([keep + got.astype(F32), filters], axis=1)
+    total = keep + got.astype(F32)
+    rows = reciprocal_filter.reshape(2, 2 * WIDTH)
     for step in range(4):
         total, acc = barrier((total, acc))
-        fresh = permute(total.astype(BF16), DOUBLING[step])
+        fresh = permute(jnp.concatenate([total.astype(BF16), rows], axis=0), DOUBLING[step])
         if step < 2:
             acc = own_piece(step + 2, acc)
         else:
             acc = beyond(True, step - 2, row_a if step == 2 else row_b, acc)
-        total = total + fresh.astype(F32)
-    scale = total[:, 2 * WIDTH :]
-    chunk = jnp.concatenate([total[:, :WIDTH] * scale, total[:, WIDTH : 2 * WIDTH] * scale], axis=1).astype(BF16)
+        if step < 3:
+            total = total + fresh[:CHUNK].astype(F32)
+            rows = jnp.concatenate([rows, fresh[CHUNK:]], axis=0)
+    chunk = coefficients(total, rows, fresh, placement)
     chunk, row_a, row_b = barrier((chunk, row_a, row_b))
     for turn, step in enumerate((2, 1, 3, 0)):
         chunk, acc = barrier((chunk, acc))

time: 83.2 us -> 87.2 us (1.048)
  waiting for transfers between devices: 21.4 us -> 15.5 us
  local copies, waits for them, and re-layouts: 0.22 us -> 5.05 us
  other arithmetic: 0.9 us -> 4.39 us
  starting transfers between devices: 33.1 us -> 34.2 us
    ppermute x12, waiting for transfers between devices: 21.4 us -> 15 us  [permute(): return lax.ppermute(value, AXES, partner_list(step))]
    concatenate x0 -> x1, local copies, waits for them, and re-layouts: none -> 2.67 us  [per_device(): jnp.concatenate([total.astype(BF16), rows], axis=0)]
    ppermute x12, starting transfers between devices: 14.7 us -> 16.2 us  [permute(): return lax.ppermute(value, AXES, partner_list(step))]
    unnamed x24 -> x46, local copies, waits for them, and re-layouts: 0.06 us -> 1.51 us
    add x1, other arithmetic: 0.08 us -> 1.23 us  [per_device(): keep = keep[:height] + got[:height].astype(F32)]
    convert_element_type x2, other arithmetic: 0.09 us -> 1.03 us  [per_device(): ((keep_next if step == 1 else keep[height:]) + got[height:].astype(F32))....]
  transfers between devices with their start and end apart: 16 -> 16, of which waited for: 9 -> 8; matrix products, arithmetic and copies ran while one was open for 1% -> 9% of each run, Pallas kernels for 25% -> 23%
where the time goes in v10:
time: 87.2 us; the launch traced here: 86.9 us
  starting transfers between devices  34.2 us (39%)
  Pallas kernels  27 us (31%)
  waiting for transfers between devices  15.5 us (18%)
  local copies, waits for them, and re-layouts  5.05 us (6%)
  other arithmetic  4.39 us (5%)
    ppermute x12, starting transfers between devices, permute(): return lax.ppermute(value, AXES, partner_list(step))  16.2 us
    ppermute x12, waiting for transfers between devices, permute(): return lax.ppermute(value, AXES, partner_list(step))  15 us
    ppermute x1, starting transfers between devices, per_device(): column_b = lax.ppermute(far_send, 'gy', column_pairs(False))  13.2 us
    pallas_call x3, Pallas kernels, waves(): pl.pallas_call(functools.partial(wave_kernel, first), out_shape=out_shape...  8.3 us
    pallas_call x4, Pallas kernels, radial_piece(): pl.pallas_call(functools.partial(radial_kernel, near_cells, fresh), out_s...  6.82 us
    pallas_call x4, Pallas kernels, edge_piece(): pl.pallas_call(functools.partial(edge_kernel, along_x, which), out_shape=...  6.51 us
    ppermute x1, starting transfers between devices, per_device(): lax.ppermute(jnp.where(even_x, upper, lower), 'gx', row_pairs(False))  4.8 us
    concatenate x1, local copies, waits for them, and re-layouts, per_device(): jnp.concatenate([total.astype(BF16), rows], axis=0)  2.67 us
  transfers between devices with their start and end apart: 16, of which 8 were waited for; matrix products, arithmetic and copies ran while one was open for 9% of the time, Pallas kernels for 23%

profile of v10, /device:TPU:1, one launch (start us, length us, event | category | flops | bytes accessed | tf_op | source)
XLA Modules:
  0.0 86.9 jit_solution(11216336644096353600)
XLA Ops:
  0.2 4.1 %wave_tables.3 = (bf16[1024,512]{1,0:T(8,128)(2,1)}, bf16[1024,512]{1,0:T(8,128)(2,1)}, bf16[512,512]{1,0:T(8,128)(2,1)S(1)}, bf16[256,1024]{1,0:T(8,128)(2,1)S(...) custom-call(s32[2]{0:T(128)S(1)} %pad_add_fusion.place, bf16[2,3,4,128]{3,2,1,0:T(4,128)(2,1)} %bitcast.16, ...), custom_call_target="tpu_custom_call" | custom-call | flops 2048000000 | bytes 3000000 | tf_op jit(solution)/shard_map/wave_tables/pallas_call | solution.py:210
  4.3 3.3 %collective-permute-start = (bf16[512,512]{1,0:T(8,128)(2,1)S(1)}, bf16[512,512]{1,0:T(8,128)(2,1)}, u32[]{:S(2)}, u32[]{:S(2)}) collective-permute-start(bf16[512,512]{1,0:T(8,128)(2,1)S(1)} %get-tuple-element.53), channel_id=1, source_target_pairs={{0,1},{1,0},{16,17},{17,16},{32,33},{33,32},{48,49},{49,48},{2,3},... | collective-permute-start | bytes 1572872 | tf_op jit(solution)/shard_map/ppermute | solution.py:71
  7.6 0.9 broadcast_select_fusion
  8.5 4.8 %collective-permute-start.9 = (bf16[4,144,256]{2,1,0:T(8,128)(2,1)}, bf16[4,144,256]{2,1,0:T(8,128)(2,1)S(1)}, u32[]{:S(2)}, u32[]{:S(2)}) collective-permute-start(bf16[4,144,256]{2,1,0:T(8,128)(2,1)} %get-tuple-element.99), channel_id=1, source_target_pairs={{0,240},{16,32},{32,16},{48,64},{64,48},{80,96},{96,80},{112,128},... | collective-permute-start | bytes 884744 | tf_op jit(solution)/shard_map/ppermute | solution.py:530
  13.4 2.1 %wave_tables.4 = (bf16[1024,256]{1,0:T(8,128)(2,1)S(1)}, bf16[1024,256]{1,0:T(8,128)(2,1)S(1)}, f32[256,512]{1,0:T(8,128)S(1)}) custom-call(s32[2]{0:T(128)S(1)} %pad_add_fusion.place, bf16[2,3,4,128]{3,2,1,0:T(4,128)(2,1)S(1)} %bitcast.17, s32[3,1024]{1,0:T(4,128)S(1)} %copy-done.2, s32[1,256]{1,0:T(1,128)S(1)} %get-tuple-element.114.order, ...), custom_call_target="tpu_custom_call" | custom-call | flops 1024000000 | bytes 3000000 | tf_op jit(solution)/shard_map/wave_tables/pallas_call | solution.py:210
  16.3 1.0 %add_convert_fusion = bf16[256,512]{1,0:T(8,128)(2,1)S(1)} fusion(f32[256,512]{1,0:T(8,128)S(1)} %get-tuple-element.52, bf16[512,512]{1,0:T(8,128)(2,1)} %collective-permute-done), kind=kLoop, calls=%fused_computation.2 | loop fusion | flops 393216 | bytes 1048576 | tf_op jit(solution)/shard_map/convert_element_type | solution.py:546
  17.3 2.8 %collective-permute-start.1 = (bf16[256,512]{1,0:T(8,128)(2,1)S(1)}, bf16[256,512]{1,0:T(8,128)(2,1)S(1)}, u32[]{:S(2)}, u32[]{:S(2)}) collective-permute-start(bf16[256,512]{1,0:T(8,128)(2,1)S(1)} %add_convert_fusion), channel_id=1, source_target_pairs={{0,4},{1,13},{16,20},{17,29},{32,36},{33,45},{48,52},{49,61},{2,6}... | collective-permute-start | bytes 786440 | tf_op jit(solution)/shard_map/ppermute | solution.py:71
  20.1 2.1 %wave_tables.5 = (bf16[1024,256]{1,0:T(8,128)(2,1)S(1)}, bf16[1024,256]{1,0:T(8,128)(2,1)S(1)}, f32[256,512]{1,0:T(8,128)S(1)}) custom-call(s32[2]{0:T(128)S(1)} %pad_add_fusion.place, bf16[2,3,4,128]{3,2,1,0:T(4,128)(2,1)S(1)} %bitcast.18, s32[3,1024]{1,0:T(4,128)S(1)} %copy-done.2, s32[1,256]{1,0:T(1,128)S(1)} %get-tuple-element.113.order, ...), custom_call_target="tpu_custom_call" | custom-call | flops 1024000000 | bytes 3000000 | tf_op jit(solution)/shard_map/wave_tables/pallas_call | solution.py:210
  22.3 1.2 %convert_add_fusion = f32[256,512]{1,0:T(8,128)S(1)} fusion(f32[256,512]{1,0:T(8,128)S(1)} %get-tuple-element.56, bf16[512,512]{1,0:T(8,128)(2,1)} %collective-permute-done), kind=kLoop, calls=%fused_computation.1 | loop fusion | flops 262144 | bytes 1310720 | tf_op jit(solution)/shard_map/add | solution.py:561
  23.6 1.3 %radial_prepare.1 = (f32[8,9]{1,0:T(8,128)S(1)}, f32[8,3,128,128]{3,2,1,0:T(8,128)S(1)}, f32[64,32]{1,0:T(8,128)S(1)}) custom-call(s32[2]{0:T(128)S(1)} %pad_add_fusion.place, s32[8]{0:T(128)S(1)} %reshape.732.near_count, s32[128]{0:T(128)S(1)} %copy-done.8, s32[8,9]{1,0:T(8,128)S(1)} %bitcast.20, bf16[2,3,4,128]{3,2,1,0:T(4,128)(2,1)S(1)} %bitcast.19), custom_call_target="tpu_custom_call" | custom-call | flops 500000000 | bytes 100000 | tf_op jit(solution)/shard_map/radial_prepare/pallas_call | solution.py:257
  25.1 1.4 %radial_piece.4.rest_2_ = f32[8,128,256]{2,1,0:T(8,128)S(1)} custom-call(f32[8]{0:T(128)S(1)} %copy-done.7, f32[8,9]{1,0:T(8,128)S(1)} %get-tuple-element.61.live, bf16[8,256]{1,0:T(8,128)(2,1)S(1)} %copy-done.5, f32[8,3,128,128]{3,2,1,0:T(8,128)S(1)} %get-tuple-element.62.mine, bf16[4,144,256]{2,1,0:T(8,128)(2,1)S(1)} %get-tuple-element.63.rest_0_.upper, ...), custom_call_target="tpu_custom_call" | custom-call | flops 2000000000 | bytes 2000000 | tf_op jit(solution)/shard_map/radial_piece/pallas_call | solution.py:312
  26.5 2.7 %collective-permute-done.2 = bf16[128,512]{1,0:T(8,128)(2,1)S(1)} collective-permute-done((bf16[128,512]{1,0:T(8,128)(2,1)S(1)}, bf16[128,512]{1,0:T(8,128)(2,1)S(1)}, u32[]{:S(2)}, u32[]{:S(2)}) %collective-permute-start.2) | collective-permute-done | bytes 131104 | tf_op jit(solution)/shard_map/ppermute | solution.py:71
  29.8 1.9 %radial_piece.5.rest_2_ = f32[8,128,256]{2,1,0:T(8,128)S(1)} custom-call(f32[8]{0:T(128)S(1)} %copy-done.7, f32[8,9]{1,0:T(8,128)S(1)} %get-tuple-element.61.live, bf16[8,256]{1,0:T(8,128)(2,1)S(1)} %copy-done.5, f32[8,3,128,128]{3,2,1,0:T(8,128)S(1)} %get-tuple-element.62.mine, ...), custom_call_target="tpu_custom_call", output_to_operand_aliasing={{}: (6, {})} | custom-call | flops 2000000000 | bytes 2000000 | tf_op jit(solution)/shard_map/radial_piece/pallas_call | solution.py:312
  31.8 1.8 %collective-permute-done.3 = bf16[64,512]{1,0:T(8,128)(2,1)S(1)} collective-permute-done((bf16[64,512]{1,0:T(8,128)(2,1)S(1)}, bf16[64,512]{1,0:T(8,128)(2,1)S(1)}, u32[]{:S(2)}, u32[]{:S(2)}) %collective-permute-start.3) | collective-permute-done | bytes 65568 | tf_op jit(solution)/shard_map/ppermute | solution.py:71
  33.9 1.9 %radial_piece.6.rest_2_ = f32[8,128,256]{2,1,0:T(8,128)S(1)} custom-call(f32[8]{0:T(128)S(1)} %copy-done.7, f32[8,9]{1,0:T(8,128)S(1)} %get-tuple-element.61.live, bf16[8,256]{1,0:T(8,128)(2,1)S(1)} %copy-done.5, f32[8,3,128,128]{3,2,1,0:T(8,128)S(1)} %get-tuple-element.62.mine, ...), custom_call_target="tpu_custom_call", output_to_operand_aliasing={{}: (6, {})} | custom-call | flops 2000000000 | bytes 2000000 | tf_op jit(solution)/shard_map/radial_piece/pallas_call | solution.py:312
  35.9 1.2 %collective-permute-done.4 = bf16[66,512]{1,0:T(8,128)(2,1)S(1)} collective-permute-done((bf16[66,512]{1,0:T(8,128)(2,1)S(1)}, bf16[66,512]{1,0:T(8,128)(2,1)S(1)}, u32[]{:S(2)}, u32[]{:S(2)}) %collective-permute-start.4) | collective-permute-done | bytes 67616 | tf_op jit(solution)/shard_map/ppermute | solution.py:71
  37.2 2.4 %collective-permute-start.5 = (bf16[68,512]{1,0:T(8,128)(2,1)S(1)}, bf16[68,512]{1,0:T(8,128)(2,1)S(1)}, u32[]{:S(2)}, u32[]{:S(2)}) collective-permute-start(bf16[68,512]{1,0:T(8,128)(2,1)S(1)} %pad_maximum_fusion.6), channel_id=1, source_target_pairs={{0,16},{1,51},{16,0},{17,33},{32,48},{33,17},{48,32},{49,3},{2,18}... | collective-permute-start | bytes 208904 | tf_op jit(solution)/shard_map/ppermute | solution.py:71
  39.6 1.6 %radial_piece.7.start = f32[8,128,256]{2,1,0:T(8,128)S(1)} custom-call(f32[8]{0:T(128)S(1)} %copy-done.7, f32[8,9]{1,0:T(8,128)S(1)} %get-tuple-element.61.live, bf16[8,256]{1,0:T(8,128)(2,1)S(1)} %copy-done.5, f32[8,3,128,128]{3,2,1,0:T(8,128)S(1)} %get-tuple-element.62.mine, ...), custom_call_target="tpu_custom_call", output_to_operand_aliasing={{}: (6, {})} | custom-call | flops 2000000000 | bytes 2000000 | tf_op jit(solution)/shard_map/radial_piece/pallas_call | solution.py:312
  41.9 1.8 %radial_edge.4.start = f32[8,128,256]{2,1,0:T(8,128)S(1)} custom-call(s32[4]{0:T(128)S(1)} %pad_add_fusion.1.sides, f32[8]{0:T(128)S(1)} %copy-done.7, f32[8,9]{1,0:T(8,128)S(1)} %get-tuple-element.61.live, bf16[8,256]{1,0:T(8,128)(2,1)S(1)} %copy-done.5, f32[8,3,128,128]{3,2,1,0:T(8,128)S(1)} %get-tuple-element.62.mine, ...), custom_call_target="tpu_custom_call", output_to_operand_aliasing={{}: (6, {})} | custom-call | flops 20000000000 | bytes 2000000 | tf_op jit(solution)/shard_map/radial_edge/pallas_call | solution.py:384
  43.7 1.7 %collective-permute-done.6 = bf16[72,512]{1,0:T(8,128)(2,1)S(1)} collective-permute-done((bf16[72,512]{1,0:T(8,128)(2,1)S(1)}, bf16[72,512]{1,0:T(8,128)(2,1)S(1)}, u32[]{:S(2)}, u32[]{:S(2)}) %collective-permute-start.6) | collective-permute-done | bytes 73760 | tf_op jit(solution)/shard_map/ppermute | solution.py:71
  46.1 2.7 %concatenate.57 = bf16[80,512]{1,0:T(8,128)(2,1)} concatenate(bf16[64,512]{1,0:T(8,128)(2,1)} %convert_element_type.67, bf16[2,512]{1,0:T(2,128)(2,1)S(1)} %reshape.734, bf16[2,512]{1,0:T(2,128)(2,1)S(1)} %slice.146, bf16[4,512]{1,0:T(4,128)(2,1)S(1)} %slice.148, bf16[8,512]{1,0:T(8,128)(2,1)S(1)} %slice.150), dimensions={0} | concatenate | bytes 163840 | tf_op jit(solution)/shard_map/concatenate | solution.py:567
  48.7 3.6 %collective-permute-start.8 = (bf16[80,512]{1,0:T(8,128)(2,1)}, bf16[80,512]{1,0:T(8,128)(2,1)S(1)}, u32[]{:S(2)}, u32[]{:S(2)}) collective-permute-start(bf16[80,512]{1,0:T(8,128)(2,1)} %concatenate.57), channel_id=1, source_target_pairs={{0,48},{1,19},{16,34},{17,3},{32,18},{33,51},{48,0},{49,35},{2,50}... | collective-permute-start | bytes 245768 | tf_op jit(solution)/shard_map/ppermute | solution.py:71
  52.4 1.4 %copy-done.10 = f32[8,3,128,128]{3,2,1,0:T(8,128)S(1)} copy-done((f32[8,3,128,128]{3,2,1,0:T(8,128)S(1)}, f32[8,3,128,128]{3,2,1,0:T(8,128)}, u32[]{:S(2)}) %copy-start.10) | copy-done | bytes 1572888
  53.8 1.8 %radial_edge.5 = f32[8,128,256]{2,1,0:T(8,128)S(1)} custom-call(s32[4]{0:T(128)S(1)} %pad_add_fusion.1.sides, f32[8]{0:T(128)S(1)} %copy-done.7, f32[8,9]{1,0:T(8,128)S(1)} %get-tuple-element.61.live, bf16[8,256]{1,0:T(8,128)(2,1)S(1)} %copy-done.5, f32[8,3,128,128]{3,2,1,0:T(8,128)S(1)} %copy-done.10, ...), custom_call_target="tpu_custom_call", output_to_operand_aliasing={{}: (6, {})} | custom-call | flops 20000000000 | bytes 2000000 | tf_op jit(solution)/shard_map/radial_edge/pallas_call | solution.py:384
  56.1 13.2 %collective-permute-start.15 = (bf16[4,144,256]{2,1,0:T(8,128)(2,1)S(1)}, bf16[4,144,256]{2,1,0:T(8,128)(2,1)S(1)}, u32[]{:S(2)}, u32[]{:S(2)}) collective-permute-start(bf16[4,144,256]{2,1,0:T(8,128)(2,1)S(1)} %get-tuple-element.93), channel_id=1, source_target_pairs={{0,15},{1,2},{2,1},{3,4},{4,3},{5,6},{6,5},{7,8},{8,7},{9,10},{10,... | collective-permute-start | bytes 884744 | tf_op jit(solution)/shard_map/ppermute | solution.py:590
  70.2 4.2 %collective-permute-done.11 = bf16[128,512]{1,0:T(8,128)(2,1)S(1)} collective-permute-done((bf16[128,512]{1,0:T(8,128)(2,1)S(1)}, bf16[128,512]{1,0:T(8,128)(2,1)S(1)}, u32[]{:S(2)}, u32[]{:S(2)}) %collective-permute-start.11) | collective-permute-done | bytes 131104 | tf_op jit(solution)/shard_map/ppermute | solution.py:71
  74.5 2.0 %collective-permute-start.12 = (bf16[256,512]{1,0:T(8,128)(2,1)S(1)}, bf16[256,512]{1,0:T(8,128)(2,1)S(1)}, u32[]{:S(2)}, u32[]{:S(2)}) collective-permute-start(bf16[256,512]{1,0:T(8,128)(2,1)S(1)} %pad_maximum_fusion.3.refs_6_), channel_id=1, source_target_pairs={{0,64},{1,193},{16,80},{17,209},{32,96},{33,225},{48,112},{49,241}... | collective-permute-start | bytes 786440 | tf_op jit(solution)/shard_map/ppermute | solution.py:71
  76.5 1.4 %radial_edge.6 = f32[8,128,256]{2,1,0:T(8,128)S(1)} custom-call(s32[4]{0:T(128)S(1)} %pad_add_fusion.1.sides, f32[8]{0:T(128)S(1)} %copy-done.7, f32[8,9]{1,0:T(8,128)S(1)} %get-tuple-element.61.live, bf16[8,256]{1,0:T(8,128)(2,1)S(1)} %copy-done.5, f32[8,3,128,128]{3,2,1,0:T(8,128)S(1)} %copy-done.11, ...), custom_call_target="tpu_custom_call", output_to_operand_aliasing={{}: (6, {})} | custom-call | flops 20000000000 | bytes 2000000 | tf_op jit(solution)/shard_map/radial_edge/pallas_call | solution.py:384
  78.5 2.9 %collective-permute-done.12 = bf16[256,512]{1,0:T(8,128)(2,1)S(1)} collective-permute-done((bf16[256,512]{1,0:T(8,128)(2,1)S(1)}, bf16[256,512]{1,0:T(8,128)(2,1)S(1)}, u32[]{:S(2)}, u32[]{:S(2)}) %collective-permute-start.12) | collective-permute-done | bytes 262176 | tf_op jit(solution)/shard_map/ppermute | solution.py:71
  82.1 1.4 %radial_edge.7 = f32[8,128,256]{2,1,0:T(8,128)S(1)} custom-call(s32[4]{0:T(128)S(1)} %pad_add_fusion.1.sides, f32[8]{0:T(128)S(1)} %copy-done.7, f32[8,9]{1,0:T(8,128)S(1)} %get-tuple-element.61.live, bf16[8,256]{1,0:T(8,128)(2,1)S(1)} %copy-done.5, f32[8,3,128,128]{3,2,1,0:T(8,128)S(1)} %copy-done.11, ...), custom_call_target="tpu_custom_call", output_to_operand_aliasing={{}: (6, {})} | custom-call | flops 20000000000 | bytes 2000000 | tf_op jit(solution)/shard_map/radial_edge/pallas_call | solution.py:384
  83.6 0.7 recip_piece.5.acc
  84.3 2.4 %mix_and_network.1 = bf16[1024,256]{1,0:T(8,128)(2,1)} custom-call(bf16[1024,512]{1,0:T(8,128)(2,1)S(1)} %copy-done.16, bf16[1024,512]{1,0:T(8,128)(2,1)S(1)} %copy-done.17, bf16[512,512]{1,0:T(8,128)(2,1)S(1)} %collective-permute-done.14.coef_in, bf16[4,144,256]{2,1,0:T(8,128)(2,1)S(1)} %get-tuple-element.63.rest_0_.upper, ...), custom_call_target="tpu_custom_call" | custom-call | flops 3000000000 | bytes 8000000 | tf_op jit(solution)/shard_map/mix_and_network/pallas_call | solution.py:472
  (100 shorter events, 6.3 us)
Async XLA Ops:
  0.2 13.1 %copy-start.22 = (s32[2,4]{1,0:T(2,128)S(1)}, s32[2,4]{1,0:T(2,128)}, u32[]{:S(2)}) copy-start(s32[2,4]{1,0:T(2,128)} %param.15) | copy-start | bytes 100
  0.2 13.2 %copy-start.21 = (bf16[4,256]{1,0:T(4,128)(2,1)S(1)}, bf16[4,256]{1,0:T(4,128)(2,1)}, u32[]{:S(2)}) copy-start(bf16[4,256]{1,0:T(4,128)(2,1)} %param.19) | copy-start | bytes 6148
  0.2 13.2 %copy-start.2 = (s32[3,1024]{1,0:T(4,128)S(1)}, s32[3,1024]{1,0:T(4,128)}, u32[]{:S(2)}) copy-start(s32[3,1024]{1,0:T(4,128)} %miller.5) | copy-start | bytes 36868
  0.2 13.2 %copy-start.3 = (bf16[2,4,3,128]{3,1,2,0:T(4,128)(2,1)S(1)}, bf16[2,4,3,128]{3,1,2,0:T(4,128)(2,1)}, u32[]{:S(2)}) copy-start(bf16[2,4,3,128]{3,1,2,0:T(4,128)(2,1)} %param.13) | copy-start | bytes 18436
  4.3 12.0 %collective-permute-start = (bf16[512,512]{1,0:T(8,128)(2,1)S(1)}, bf16[512,512]{1,0:T(8,128)(2,1)}, u32[]{:S(2)}, u32[]{:S(2)}) collective-permute-start(bf16[512,512]{1,0:T(8,128)(2,1)S(1)} %get-tuple-element.53), channel_id=1, source_target_pairs={{0,1},{1,0},{16,17},{17,16},{32,33},{33,32},{48,49},{49,48},{2,3},... | collective-permute-start | bytes 1572872 | tf_op jit(solution)/shard_map/ppermute | solution.py:71
  8.5 33.4 %collective-permute-start.7 = (bf16[4,144,256]{2,1,0:T(8,128)(2,1)}, bf16[4,144,256]{2,1,0:T(8,128)(2,1)S(1)}, u32[]{:S(2)}, u32[]{:S(2)}) collective-permute-start(bf16[4,144,256]{2,1,0:T(8,128)(2,1)} %get-tuple-element.100), channel_id=1, source_target_pairs={{0,16},{16,0},{32,48},{48,32},{64,80},{80,64},{96,112},{112,96},{1... | collective-permute-start | bytes 884744 | tf_op jit(solution)/shard_map/ppermute | solution.py:529
  8.5 43.9 %collective-permute-start.9 = (bf16[4,144,256]{2,1,0:T(8,128)(2,1)}, bf16[4,144,256]{2,1,0:T(8,128)(2,1)S(1)}, u32[]{:S(2)}, u32[]{:S(2)}) collective-permute-start(bf16[4,144,256]{2,1,0:T(8,128)(2,1)} %get-tuple-element.99), channel_id=1, source_target_pairs={{0,240},{16,32},{32,16},{48,64},{64,48},{80,96},{96,80},{112,128},... | collective-permute-start | bytes 884744 | tf_op jit(solution)/shard_map/ppermute | solution.py:530
  17.3 7.6 %collective-permute-start.1 = (bf16[256,512]{1,0:T(8,128)(2,1)S(1)}, bf16[256,512]{1,0:T(8,128)(2,1)S(1)}, u32[]{:S(2)}, u32[]{:S(2)}) collective-permute-start(bf16[256,512]{1,0:T(8,128)(2,1)S(1)} %add_convert_fusion), channel_id=1, source_target_pairs={{0,4},{1,13},{16,20},{17,29},{32,36},{33,45},{48,52},{49,61},{2,6}... | collective-permute-start | bytes 786440 | tf_op jit(solution)/shard_map/ppermute | solution.py:71
  20.1 3.4 %copy-start.4 = (s32[2,4,9]{2,1,0:T(4,128)S(1)}, s32[2,4,9]{2,1,0:T(4,128)}, u32[]{:S(2)}) copy-start(s32[2,4,9]{2,1,0:T(4,128)} %param.14) | copy-start | bytes 868
  20.1 3.4 %copy-start.8 = (s32[128]{0:T(128)S(1)}, s32[128]{0:T(128)}, u32[]{:S(2)}) copy-start(s32[128]{0:T(128)} %constant.187.clone.sources) | copy-start | bytes 1540
  22.2 2.6 %copy-start.12 = (bf16[1024,256]{1,0:T(8,128)(2,1)}, bf16[1024,256]{1,0:T(8,128)(2,1)S(1)}, u32[]{:S(2)}) copy-start(bf16[1024,256]{1,0:T(8,128)(2,1)S(1)} %get-tuple-element.83.refs_0_) | copy-start | bytes 1572868
  22.3 2.6 %copy-start.14 = (bf16[1024,256]{1,0:T(8,128)(2,1)}, bf16[1024,256]{1,0:T(8,128)(2,1)S(1)}, u32[]{:S(2)}) copy-start(bf16[1024,256]{1,0:T(8,128)(2,1)S(1)} %get-tuple-element.84.refs_1_) | copy-start | bytes 1572868
  24.8 17.1 %copy-start.9 = (f32[8,3,128,128]{3,2,1,0:T(8,128)}, f32[8,3,128,128]{3,2,1,0:T(8,128)S(1)}, u32[]{:S(2)}) copy-start(f32[8,3,128,128]{3,2,1,0:T(8,128)S(1)} %get-tuple-element.62.mine) | copy-start | bytes 4718596
  25.0 4.2 %collective-permute-start.2 = (bf16[128,512]{1,0:T(8,128)(2,1)S(1)}, bf16[128,512]{1,0:T(8,128)(2,1)S(1)}, u32[]{:S(2)}, u32[]{:S(2)}) collective-permute-start(bf16[128,512]{1,0:T(8,128)(2,1)S(1)} %fusion), channel_id=1, source_target_pairs={{0,12},{1,5},{16,28},{17,21},{32,44},{33,37},{48,60},{49,53},{2,14... | collective-permute-start | bytes 393224 | tf_op jit(solution)/shard_map/ppermute | solution.py:71
  29.2 4.4 %collective-permute-start.3 = (bf16[64,512]{1,0:T(8,128)(2,1)S(1)}, bf16[64,512]{1,0:T(8,128)(2,1)S(1)}, u32[]{:S(2)}, u32[]{:S(2)}) collective-permute-start(bf16[64,512]{1,0:T(8,128)(2,1)S(1)} %fusion.1), channel_id=1, source_target_pairs={{0,64},{1,193},{16,80},{17,209},{32,96},{33,225},{48,112},{49,241}... | collective-permute-start | bytes 196616 | tf_op jit(solution)/shard_map/ppermute | solution.py:71
  33.7 3.5 %collective-permute-start.4 = (bf16[66,512]{1,0:T(8,128)(2,1)S(1)}, bf16[66,512]{1,0:T(8,128)(2,1)S(1)}, u32[]{:S(2)}, u32[]{:S(2)}) collective-permute-start(bf16[66,512]{1,0:T(8,128)(2,1)S(1)} %pad_maximum_fusion.5), channel_id=1, source_target_pairs={{0,192},{1,65},{16,208},{17,81},{32,224},{33,97},{48,240},{49,113}... | collective-permute-start | bytes 202760 | tf_op jit(solution)/shard_map/ppermute | solution.py:71
  37.2 4.5 %collective-permute-start.5 = (bf16[68,512]{1,0:T(8,128)(2,1)S(1)}, bf16[68,512]{1,0:T(8,128)(2,1)S(1)}, u32[]{:S(2)}, u32[]{:S(2)}) collective-permute-start(bf16[68,512]{1,0:T(8,128)(2,1)S(1)} %pad_maximum_fusion.6), channel_id=1, source_target_pairs={{0,16},{1,51},{16,0},{17,33},{32,48},{33,17},{48,32},{49,3},{2,18}... | collective-permute-start | bytes 208904 | tf_op jit(solution)/shard_map/ppermute | solution.py:71
  41.8 3.6 %collective-permute-start.6 = (bf16[72,512]{1,0:T(8,128)(2,1)S(1)}, bf16[72,512]{1,0:T(8,128)(2,1)S(1)}, u32[]{:S(2)}, u32[]{:S(2)}) collective-permute-start(bf16[72,512]{1,0:T(8,128)(2,1)S(1)} %pad_maximum_fusion.7), channel_id=1, source_target_pairs={{0,50},{1,17},{16,32},{17,1},{32,16},{33,49},{48,2},{49,33},{2,48}... | collective-permute-start | bytes 221192 | tf_op jit(solution)/shard_map/ppermute | solution.py:71
  48.7 6.9 %collective-permute-start.8 = (bf16[80,512]{1,0:T(8,128)(2,1)}, bf16[80,512]{1,0:T(8,128)(2,1)S(1)}, u32[]{:S(2)}, u32[]{:S(2)}) collective-permute-start(bf16[80,512]{1,0:T(8,128)(2,1)} %concatenate.57), channel_id=1, source_target_pairs={{0,48},{1,19},{16,34},{17,3},{32,18},{33,51},{48,0},{49,35},{2,50}... | collective-permute-start | bytes 245768 | tf_op jit(solution)/shard_map/ppermute | solution.py:71
  55.6 14.2 %copy-start.13 = (bf16[1024,256]{1,0:T(8,128)(2,1)S(1)}, bf16[1024,256]{1,0:T(8,128)(2,1)}, u32[]{:S(2)}) copy-start(bf16[1024,256]{1,0:T(8,128)(2,1)} %copy-done.12) | copy-start | bytes 1572868
  55.6 14.2 %copy-start.15 = (bf16[1024,256]{1,0:T(8,128)(2,1)S(1)}, bf16[1024,256]{1,0:T(8,128)(2,1)}, u32[]{:S(2)}) copy-start(bf16[1024,256]{1,0:T(8,128)(2,1)} %copy-done.14) | copy-start | bytes 1572868
  55.8 13.5 %collective-permute-start.10 = (bf16[64,512]{1,0:T(8,128)(2,1)S(1)}, bf16[64,512]{1,0:T(8,128)(2,1)S(1)}, u32[]{:S(2)}, u32[]{:S(2)}) collective-permute-start(bf16[64,512]{1,0:T(8,128)(2,1)S(1)} %coefficients.1), channel_id=1, source_target_pairs={{0,12},{1,5},{16,28},{17,21},{32,44},{33,37},{48,60},{49,53},{2,14... | collective-permute-start | bytes 196616 | tf_op jit(solution)/shard_map/ppermute | solution.py:71
  56.1 26.0 %collective-permute-start.15 = (bf16[4,144,256]{2,1,0:T(8,128)(2,1)S(1)}, bf16[4,144,256]{2,1,0:T(8,128)(2,1)S(1)}, u32[]{:S(2)}, u32[]{:S(2)}) collective-permute-start(bf16[4,144,256]{2,1,0:T(8,128)(2,1)S(1)} %get-tuple-element.93), channel_id=1, source_target_pairs={{0,15},{1,2},{2,1},{3,4},{4,3},{5,6},{6,5},{7,8},{8,7},{9,10},{10,... | collective-permute-start | bytes 884744 | tf_op jit(solution)/shard_map/ppermute | solution.py:590
  69.3 5.1 %collective-permute-start.11 = (bf16[128,512]{1,0:T(8,128)(2,1)S(1)}, bf16[128,512]{1,0:T(8,128)(2,1)S(1)}, u32[]{:S(2)}, u32[]{:S(2)}) collective-permute-start(bf16[128,512]{1,0:T(8,128)(2,1)S(1)} %pad_maximum_fusion.4.refs_2_), channel_id=1, source_target_pairs={{0,4},{1,13},{16,20},{17,29},{32,36},{33,45},{48,52},{49,61},{2,6}... | collective-permute-start | bytes 393224 | tf_op jit(solution)/shard_map/ppermute | solution.py:71
  69.8 6.7 %collective-permute-start.13 = (bf16[4,144,256]{2,1,0:T(8,128)(2,1)S(1)}, bf16[4,144,256]{2,1,0:T(8,128)(2,1)S(1)}, u32[]{:S(2)}, u32[]{:S(2)}) collective-permute-start(bf16[4,144,256]{2,1,0:T(8,128)(2,1)S(1)} %get-tuple-element.89), channel_id=1, source_target_pairs={{0,1},{1,0},{2,3},{3,2},{4,5},{5,4},{6,7},{7,6},{8,9},{9,8},{10,11... | collective-permute-start | bytes 884744 | tf_op jit(solution)/shard_map/ppermute | solution.py:593
  69.8 6.7 %copy-start.11 = (f32[8,3,128,128]{3,2,1,0:T(8,128)S(1)}, f32[8,3,128,128]{3,2,1,0:T(8,128)}, u32[]{:S(2)}) copy-start(f32[8,3,128,128]{3,2,1,0:T(8,128)} %copy-done.9) | copy-start | bytes 4718596
  74.5 3.5 %copy-start = (bf16[256,512]{1,0:T(8,128)(2,1)S(1)}, bf16[256,512]{1,0:T(8,128)(2,1)}, u32[]{:S(2)}) copy-start(bf16[256,512]{1,0:T(8,128)(2,1)} %w_in.1) | copy-start | bytes 786436
  74.5 3.5 %copy-start.1 = (bf16[512,256]{1,0:T(8,128)(2,1)S(1)}, bf16[512,256]{1,0:T(8,128)(2,1)}, u32[]{:S(2)}) copy-start(bf16[512,256]{1,0:T(8,128)(2,1)} %w_out.1) | copy-start | bytes 786436
  74.5 3.5 %copy-start.16 = (bf16[1024,512]{1,0:T(8,128)(2,1)S(1)}, bf16[1024,512]{1,0:T(8,128)(2,1)}, u32[]{:S(2)}) copy-start(bf16[1024,512]{1,0:T(8,128)(2,1)} %get-tuple-element.49.refs_2_.refs_4_.cos_ref) | copy-start | bytes 3145732
  74.5 3.5 %copy-start.17 = (bf16[1024,512]{1,0:T(8,128)(2,1)S(1)}, bf16[1024,512]{1,0:T(8,128)(2,1)}, u32[]{:S(2)}) copy-start(bf16[1024,512]{1,0:T(8,128)(2,1)} %get-tuple-element.50.refs_3_.refs_5_.sin_ref) | copy-start | bytes 3145732
  74.5 6.8 %collective-permute-start.12 = (bf16[256,512]{1,0:T(8,128)(2,1)S(1)}, bf16[256,512]{1,0:T(8,128)(2,1)S(1)}, u32[]{:S(2)}, u32[]{:S(2)}) collective-permute-start(bf16[256,512]{1,0:T(8,128)(2,1)S(1)} %pad_maximum_fusion.3.refs_6_), channel_id=1, source_target_pairs={{0,64},{1,193},{16,80},{17,209},{32,96},{33,225},{48,112},{49,241}... | collective-permute-start | bytes 786440 | tf_op jit(solution)/shard_map/ppermute | solution.py:71
  81.4 3.0 %collective-permute-start.14 = (bf16[512,512]{1,0:T(8,128)(2,1)S(1)}, bf16[512,512]{1,0:T(8,128)(2,1)S(1)}, u32[]{:S(2)}, u32[]{:S(2)}) collective-permute-start(bf16[512,512]{1,0:T(8,128)(2,1)S(1)} %pad_maximum_fusion.refs_8_), channel_id=1, source_target_pairs={{0,1},{1,0},{16,17},{17,16},{32,33},{33,32},{48,49},{49,48},{2,3},... | collective-permute-start | bytes 1572872 | tf_op jit(solution)/shard_map/ppermute | solution.py:71
  (7 other events, 11.9 us)

commit v11 on v9

--- a/solution.py
+++ b/solution.py
@@ -108,15 +108,15 @@
         load = pltpu.make_async_copy(source, features, sems.at[0])
         for copy in fetch + [load]:
             copy.start()
-        for copy in fetch:
-            copy.wait()
     else:
-        turned = source
-    number = miller[...].astype(F32)
-    five = jnp.concatenate([number, number[0:2], jnp.zeros((3, 1024), F32)], axis=0).astype(BF16)
+        turned, fetch = source, ()
     size = order.shape[1]
     natural = lax.broadcasted_iota(jnp.int32, (1024, size), 0)
     pick = jnp.where(natural == order[...], 1.0, 0.0).astype(BF16)
+    for copy in fetch:
+        copy.wait()
+    number = miller[...].astype(F32)
+    five = jnp.concatenate([number, number[0:2], jnp.zeros((3, 1024), F32)], axis=0).astype(BF16)
     placed = jnp.dot(five, pick, preferred_element_type=F32).astype(BF16)
     ones = jnp.ones((1, ATOMS), F32)
 

time: 83.2 us -> 83.2 us (level)
  no operation moved by 1% of the time
where the time goes in v11:
time: 83.2 us; the launch traced here: 83.1 us
  starting transfers between devices  33 us (40%)
  Pallas kernels  26.9 us (32%)
  waiting for transfers between devices  21.4 us (26%)
  other arithmetic  0.9 us (1%)
    ppermute x12, waiting for transfers between devices, permute(): return lax.ppermute(value, AXES, partner_list(step))  21.4 us
    ppermute x12, starting transfers between devices, permute(): return lax.ppermute(value, AXES, partner_list(step))  14.7 us
    ppermute x1, starting transfers between devices, per_device(): column_b = lax.ppermute(far_send, 'gy', column_pairs(False))  13.3 us
    pallas_call x3, Pallas kernels, waves(): pl.pallas_call(functools.partial(wave_kernel, first), out_shape=out_shape...  8.29 us
    pallas_call x4, Pallas kernels, radial_piece(): pl.pallas_call(functools.partial(radial_kernel, near_cells, fresh), out_s...  6.81 us
    pallas_call x4, Pallas kernels, edge_piece(): pl.pallas_call(functools.partial(edge_kernel, along_x, which), out_shape=...  6.54 us
    ppermute x1, starting transfers between devices, per_device(): lax.ppermute(jnp.where(even_x, upper, lower), 'gx', row_pairs(False))  4.88 us
    pallas_call x1, Pallas kernels, final(): pl.pallas_call(final_kernel, out_shape=pltpu.MemorySpace.HBM((1024, WIDTH...  2.44 us
  transfers between devices with their start and end apart: 16, of which 9 were waited for; matrix products, arithmetic and copies ran while one was open for 1% of the time, Pallas kernels for 25%

profile of v11, /device:TPU:1, one launch (start us, length us, event | category | flops | bytes accessed | tf_op | source)
XLA Modules:
  0.0 83.1 jit_solution(5035098324362607682)
XLA Ops:
  0.2 4.1 %wave_tables.3 = (bf16[1024,512]{1,0:T(8,128)(2,1)}, bf16[1024,512]{1,0:T(8,128)(2,1)}, bf16[512,512]{1,0:T(8,128)(2,1)S(1)}, bf16[256,1024]{1,0:T(8,128)(2,1)S(...) custom-call(s32[2]{0:T(128)S(1)} %pad_add_fusion.place, bf16[2,3,4,128]{3,2,1,0:T(4,128)(2,1)} %bitcast.16, ...), custom_call_target="tpu_custom_call" | custom-call | flops 2048000000 | bytes 3000000 | tf_op jit(solution)/shard_map/wave_tables/pallas_call | solution.py:197
  4.3 3.3 %collective-permute-start = (bf16[512,512]{1,0:T(8,128)(2,1)S(1)}, bf16[512,512]{1,0:T(8,128)(2,1)S(1)}, u32[]{:S(2)}, u32[]{:S(2)}) collective-permute-start(bf16[512,512]{1,0:T(8,128)(2,1)S(1)} %get-tuple-element.53), channel_id=1, source_target_pairs={{0,1},{1,0},{16,17},{17,16},{32,33},{33,32},{48,49},{49,48},{2,3},... | collective-permute-start | bytes 1572872 | tf_op jit(solution)/shard_map/ppermute | solution.py:71
  7.8 4.9 %collective-permute-start.9 = (bf16[4,144,256]{2,1,0:T(8,128)(2,1)S(1)}, bf16[4,144,256]{2,1,0:T(8,128)(2,1)S(1)}, u32[]{:S(2)}, u32[]{:S(2)}) collective-permute-start(bf16[4,144,256]{2,1,0:T(8,128)(2,1)S(1)} %get-tuple-element.99), channel_id=1, source_target_pairs={{0,240},{16,32},{32,16},{48,64},{64,48},{80,96},{96,80},{112,128},... | collective-permute-start | bytes 884744 | tf_op jit(solution)/shard_map/ppermute | solution.py:488
  12.7 2.1 %wave_tables.4 = (bf16[1024,256]{1,0:T(8,128)(2,1)S(1)}, bf16[1024,256]{1,0:T(8,128)(2,1)S(1)}, f32[256,512]{1,0:T(8,128)S(1)}) custom-call(s32[2]{0:T(128)S(1)} %pad_add_fusion.place, bf16[2,3,4,128]{3,2,1,0:T(4,128)(2,1)S(1)} %bitcast.17, s32[3,1024]{1,0:T(4,128)S(1)} %copy-done.2, s32[1,256]{1,0:T(1,128)S(1)} %get-tuple-element.116.order, ...), custom_call_target="tpu_custom_call" | custom-call | flops 1024000000 | bytes 3000000 | tf_op jit(solution)/shard_map/wave_tables/pallas_call | solution.py:197
  15.0 2.8 %collective-permute-start.1 = (bf16[256,512]{1,0:T(8,128)(2,1)S(1)}, bf16[256,512]{1,0:T(8,128)(2,1)S(1)}, u32[]{:S(2)}, u32[]{:S(2)}) collective-permute-start(bf16[256,512]{1,0:T(8,128)(2,1)S(1)} %add_convert_fusion), channel_id=1, source_target_pairs={{0,4},{1,13},{16,20},{17,29},{32,36},{33,45},{48,52},{49,61},{2,6}... | collective-permute-start | bytes 786440 | tf_op jit(solution)/shard_map/ppermute | solution.py:71
  17.9 2.1 %wave_tables.5 = (bf16[1024,256]{1,0:T(8,128)(2,1)S(1)}, bf16[1024,256]{1,0:T(8,128)(2,1)S(1)}, f32[256,512]{1,0:T(8,128)S(1)}) custom-call(s32[2]{0:T(128)S(1)} %pad_add_fusion.place, bf16[2,3,4,128]{3,2,1,0:T(4,128)(2,1)S(1)} %bitcast.18, s32[3,1024]{1,0:T(4,128)S(1)} %copy-done.2, s32[1,256]{1,0:T(1,128)S(1)} %get-tuple-element.115.order, ...), custom_call_target="tpu_custom_call" | custom-call | flops 1024000000 | bytes 3000000 | tf_op jit(solution)/shard_map/wave_tables/pallas_call | solution.py:197
  20.1 1.3 %radial_prepare.1 = (f32[8,9]{1,0:T(8,128)S(1)}, f32[8,3,128,128]{3,2,1,0:T(8,128)S(1)}, f32[64,256]{1,0:T(8,128)S(1)}) custom-call(s32[2]{0:T(128)S(1)} %pad_add_fusion.place, s32[8]{0:T(128)S(1)} %reshape.729.near_count, s32[8,9]{1,0:T(8,128)S(1)} %bitcast.20, bf16[2,3,4,128]{3,2,1,0:T(4,128)(2,1)S(1)} %bitcast.19, bf16[4,256]{1,0:T(4,128)(2,1)S(1)} %copy-done.6), custom_call_target="tpu_custom_call" | custom-call | flops 500000000 | bytes 100000 | tf_op jit(solution)/shard_map/radial_prepare/pallas_call | solution.py:238
  21.4 0.5 collective-permute-done.1
  22.1 1.4 %radial_piece.4.rest_2_ = f32[8,128,256]{2,1,0:T(8,128)S(1)} custom-call(f32[8]{0:T(128)S(1)} %copy-done.8, f32[8,9]{1,0:T(8,128)S(1)} %get-tuple-element.61.live, bf16[8,256]{1,0:T(8,128)(2,1)S(1)} %copy-done.5, f32[8,3,128,128]{3,2,1,0:T(8,128)S(1)} %get-tuple-element.62.mine, bf16[4,144,256]{2,1,0:T(8,128)(2,1)S(1)} %get-tuple-element.63.rest_0_.upper, ...), custom_call_target="tpu_custom_call" | custom-call | flops 2000000000 | bytes 2000000 | tf_op jit(solution)/shard_map/radial_piece/pallas_call | solution.py:293
  23.5 2.7 %collective-permute-done.2 = bf16[128,512]{1,0:T(8,128)(2,1)S(1)} collective-permute-done((bf16[128,512]{1,0:T(8,128)(2,1)S(1)}, bf16[128,512]{1,0:T(8,128)(2,1)S(1)}, u32[]{:S(2)}, u32[]{:S(2)}) %collective-permute-start.2) | collective-permute-done | bytes 131104 | tf_op jit(solution)/shard_map/ppermute | solution.py:71
  26.2 0.6 collective-permute-start.3
  26.8 1.9 %radial_piece.5.rest_2_ = f32[8,128,256]{2,1,0:T(8,128)S(1)} custom-call(f32[8]{0:T(128)S(1)} %copy-done.8, f32[8,9]{1,0:T(8,128)S(1)} %get-tuple-element.61.live, bf16[8,256]{1,0:T(8,128)(2,1)S(1)} %copy-done.5, f32[8,3,128,128]{3,2,1,0:T(8,128)S(1)} %get-tuple-element.62.mine, ...), custom_call_target="tpu_custom_call", output_to_operand_aliasing={{}: (6, {})} | custom-call | flops 2000000000 | bytes 2000000 | tf_op jit(solution)/shard_map/radial_piece/pallas_call | solution.py:293
  28.8 1.8 %collective-permute-done.3 = bf16[64,512]{1,0:T(8,128)(2,1)S(1)} collective-permute-done((bf16[64,512]{1,0:T(8,128)(2,1)S(1)}, bf16[64,512]{1,0:T(8,128)(2,1)S(1)}, u32[]{:S(2)}, u32[]{:S(2)}) %collective-permute-start.3) | collective-permute-done | bytes 65568 | tf_op jit(solution)/shard_map/ppermute | solution.py:71
  31.0 1.9 %radial_piece.6.rest_2_ = f32[8,128,256]{2,1,0:T(8,128)S(1)} custom-call(f32[8]{0:T(128)S(1)} %copy-done.8, f32[8,9]{1,0:T(8,128)S(1)} %get-tuple-element.61.live, bf16[8,256]{1,0:T(8,128)(2,1)S(1)} %copy-done.5, f32[8,3,128,128]{3,2,1,0:T(8,128)S(1)} %get-tuple-element.62.mine, ...), custom_call_target="tpu_custom_call", output_to_operand_aliasing={{}: (6, {})} | custom-call | flops 2000000000 | bytes 2000000 | tf_op jit(solution)/shard_map/radial_piece/pallas_call | solution.py:293
  32.9 1.5 %collective-permute-done.4 = bf16[64,768]{1,0:T(8,128)(2,1)S(1)} collective-permute-done((bf16[64,768]{1,0:T(8,128)(2,1)S(1)}, bf16[64,768]{1,0:T(8,128)(2,1)S(1)}, u32[]{:S(2)}, u32[]{:S(2)}) %collective-permute-start.4) | collective-permute-done | bytes 98336 | tf_op jit(solution)/shard_map/ppermute | solution.py:71
  34.5 2.3 %collective-permute-start.5 = (bf16[64,768]{1,0:T(8,128)(2,1)S(1)}, bf16[64,768]{1,0:T(8,128)(2,1)S(1)}, u32[]{:S(2)}, u32[]{:S(2)}) collective-permute-start(bf16[64,768]{1,0:T(8,128)(2,1)S(1)} %convert_element_type.67), channel_id=1, source_target_pairs={{0,16},{1,51},{16,0},{17,33},{32,48},{33,17},{48,32},{49,3},{2,18}... | collective-permute-start | bytes 294920 | tf_op jit(solution)/shard_map/ppermute | solution.py:71
  36.8 1.6 %radial_piece.7.start = f32[8,128,256]{2,1,0:T(8,128)S(1)} custom-call(f32[8]{0:T(128)S(1)} %copy-done.8, f32[8,9]{1,0:T(8,128)S(1)} %get-tuple-element.61.live, bf16[8,256]{1,0:T(8,128)(2,1)S(1)} %copy-done.5, f32[8,3,128,128]{3,2,1,0:T(8,128)S(1)} %get-tuple-element.62.mine, ...), custom_call_target="tpu_custom_call", output_to_operand_aliasing={{}: (6, {})} | custom-call | flops 2000000000 | bytes 2000000 | tf_op jit(solution)/shard_map/radial_piece/pallas_call | solution.py:293
  38.3 0.9 %collective-permute-done.5 = bf16[64,768]{1,0:T(8,128)(2,1)S(1)} collective-permute-done((bf16[64,768]{1,0:T(8,128)(2,1)S(1)}, bf16[64,768]{1,0:T(8,128)(2,1)S(1)}, u32[]{:S(2)}, u32[]{:S(2)}) %collective-permute-start.5) | collective-permute-done | bytes 98336 | tf_op jit(solution)/shard_map/ppermute | solution.py:71
  39.4 1.8 %radial_edge.4.start = f32[8,128,256]{2,1,0:T(8,128)S(1)} custom-call(s32[4]{0:T(128)S(1)} %pad_add_fusion.1.sides, f32[8]{0:T(128)S(1)} %copy-done.8, f32[8,9]{1,0:T(8,128)S(1)} %get-tuple-element.61.live, bf16[8,256]{1,0:T(8,128)(2,1)S(1)} %copy-done.5, f32[8,3,128,128]{3,2,1,0:T(8,128)S(1)} %get-tuple-element.62.mine, ...), custom_call_target="tpu_custom_call", output_to_operand_aliasing={{}: (6, {})} | custom-call | flops 20000000000 | bytes 2000000 | tf_op jit(solution)/shard_map/radial_edge/pallas_call | solution.py:365
  41.2 2.8 %collective-permute-done.6 = bf16[64,768]{1,0:T(8,128)(2,1)S(1)} collective-permute-done((bf16[64,768]{1,0:T(8,128)(2,1)S(1)}, bf16[64,768]{1,0:T(8,128)(2,1)S(1)}, u32[]{:S(2)}, u32[]{:S(2)}) %collective-permute-start.6) | collective-permute-done | bytes 98336 | tf_op jit(solution)/shard_map/ppermute | solution.py:71
  44.1 3.7 %collective-permute-start.8 = (bf16[64,768]{1,0:T(8,128)(2,1)S(1)}, bf16[64,768]{1,0:T(8,128)(2,1)S(1)}, u32[]{:S(2)}, u32[]{:S(2)}) collective-permute-start(bf16[64,768]{1,0:T(8,128)(2,1)S(1)} %convert_element_type.71), channel_id=1, source_target_pairs={{0,48},{1,19},{16,34},{17,3},{32,18},{33,51},{48,0},{49,35},{2,50}... | collective-permute-start | bytes 294920 | tf_op jit(solution)/shard_map/ppermute | solution.py:71
  47.8 1.8 %radial_edge.5 = f32[8,128,256]{2,1,0:T(8,128)S(1)} custom-call(s32[4]{0:T(128)S(1)} %pad_add_fusion.1.sides, f32[8]{0:T(128)S(1)} %copy-done.8, f32[8,9]{1,0:T(8,128)S(1)} %get-tuple-element.61.live, bf16[8,256]{1,0:T(8,128)(2,1)S(1)} %copy-done.5, f32[8,3,128,128]{3,2,1,0:T(8,128)S(1)} %get-tuple-element.62.mine, ...), custom_call_target="tpu_custom_call", output_to_operand_aliasing={{}: (6, {})} | custom-call | flops 20000000000 | bytes 2000000 | tf_op jit(solution)/shard_map/radial_edge/pallas_call | solution.py:365
  49.6 2.9 %collective-permute-done.8 = bf16[64,768]{1,0:T(8,128)(2,1)S(1)} collective-permute-done((bf16[64,768]{1,0:T(8,128)(2,1)S(1)}, bf16[64,768]{1,0:T(8,128)(2,1)S(1)}, u32[]{:S(2)}, u32[]{:S(2)}) %collective-permute-start.8) | collective-permute-done | bytes 98336 | tf_op jit(solution)/shard_map/ppermute | solution.py:71
  52.9 13.3 %collective-permute-start.15 = (bf16[4,144,256]{2,1,0:T(8,128)(2,1)S(1)}, bf16[4,144,256]{2,1,0:T(8,128)(2,1)S(1)}, u32[]{:S(2)}, u32[]{:S(2)}) collective-permute-start(bf16[4,144,256]{2,1,0:T(8,128)(2,1)S(1)} %get-tuple-element.93), channel_id=1, source_target_pairs={{0,15},{1,2},{2,1},{3,4},{4,3},{5,6},{6,5},{7,8},{8,7},{9,10},{10,... | collective-permute-start | bytes 884744 | tf_op jit(solution)/shard_map/ppermute | solution.py:548
  66.4 0.4 recip_piece.3
  66.8 4.5 %collective-permute-done.11 = bf16[128,512]{1,0:T(8,128)(2,1)S(1)} collective-permute-done((bf16[128,512]{1,0:T(8,128)(2,1)S(1)}, bf16[128,512]{1,0:T(8,128)(2,1)S(1)}, u32[]{:S(2)}, u32[]{:S(2)}) %collective-permute-start.11) | collective-permute-done | bytes 131104 | tf_op jit(solution)/shard_map/ppermute | solution.py:71
  71.4 0.8 collective-permute-start.12
  72.1 1.4 %radial_edge.6 = f32[8,128,256]{2,1,0:T(8,128)S(1)} custom-call(s32[4]{0:T(128)S(1)} %pad_add_fusion.1.sides, f32[8]{0:T(128)S(1)} %copy-done.8, f32[8,9]{1,0:T(8,128)S(1)} %get-tuple-element.61.live, bf16[8,256]{1,0:T(8,128)(2,1)S(1)} %copy-done.5, f32[8,3,128,128]{3,2,1,0:T(8,128)S(1)} %get-tuple-element.62.mine, ...), custom_call_target="tpu_custom_call", output_to_operand_aliasing={{}: (6, {})} | custom-call | flops 20000000000 | bytes 2000000 | tf_op jit(solution)/shard_map/radial_edge/pallas_call | solution.py:365
  74.1 3.8 %collective-permute-done.12 = bf16[256,512]{1,0:T(8,128)(2,1)S(1)} collective-permute-done((bf16[256,512]{1,0:T(8,128)(2,1)S(1)}, bf16[256,512]{1,0:T(8,128)(2,1)S(1)}, u32[]{:S(2)}, u32[]{:S(2)}) %collective-permute-start.12) | collective-permute-done | bytes 262176 | tf_op jit(solution)/shard_map/ppermute | solution.py:71
  78.3 1.4 %radial_edge.7 = f32[8,128,256]{2,1,0:T(8,128)S(1)} custom-call(s32[4]{0:T(128)S(1)} %pad_add_fusion.1.sides, f32[8]{0:T(128)S(1)} %copy-done.8, f32[8,9]{1,0:T(8,128)S(1)} %get-tuple-element.61.live, bf16[8,256]{1,0:T(8,128)(2,1)S(1)} %copy-done.5, f32[8,3,128,128]{3,2,1,0:T(8,128)S(1)} %get-tuple-element.62.mine, ...), custom_call_target="tpu_custom_call", output_to_operand_aliasing={{}: (6, {})} | custom-call | flops 20000000000 | bytes 2000000 | tf_op jit(solution)/shard_map/radial_edge/pallas_call | solution.py:365
  79.7 0.7 recip_piece.5.acc
  80.5 2.4 %mix_and_network.1 = bf16[1024,256]{1,0:T(8,128)(2,1)} custom-call(bf16[1024,512]{1,0:T(8,128)(2,1)S(1)} %copy-done.9, bf16[1024,512]{1,0:T(8,128)(2,1)S(1)} %copy-done.10, bf16[512,512]{1,0:T(8,128)(2,1)S(1)} %collective-permute-done.14.coef_in, bf16[4,144,256]{2,1,0:T(8,128)(2,1)S(1)} %get-tuple-element.63.rest_0_.upper, ...), custom_call_target="tpu_custom_call" | custom-call | flops 3000000000 | bytes 8000000 | tf_op jit(solution)/shard_map/mix_and_network/pallas_call | solution.py:430
  (72 shorter events, 2.9 us)
Async XLA Ops:
  0.2 12.5 %copy-start.11 = (s32[2,4]{1,0:T(2,128)S(1)}, s32[2,4]{1,0:T(2,128)}, u32[]{:S(2)}) copy-start(s32[2,4]{1,0:T(2,128)} %param.14) | copy-start | bytes 100
  0.2 12.6 %copy-start.2 = (s32[3,1024]{1,0:T(4,128)S(1)}, s32[3,1024]{1,0:T(4,128)}, u32[]{:S(2)}) copy-start(s32[3,1024]{1,0:T(4,128)} %miller.5) | copy-start | bytes 36868
  0.2 12.6 %copy-start.3 = (bf16[2,4,3,128]{3,1,2,0:T(4,128)(2,1)S(1)}, bf16[2,4,3,128]{3,1,2,0:T(4,128)(2,1)}, u32[]{:S(2)}) copy-start(bf16[2,4,3,128]{3,1,2,0:T(4,128)(2,1)} %param.12) | copy-start | bytes 18436
  4.3 10.7 %collective-permute-start = (bf16[512,512]{1,0:T(8,128)(2,1)S(1)}, bf16[512,512]{1,0:T(8,128)(2,1)S(1)}, u32[]{:S(2)}, u32[]{:S(2)}) collective-permute-start(bf16[512,512]{1,0:T(8,128)(2,1)S(1)} %get-tuple-element.53), channel_id=1, source_target_pairs={{0,1},{1,0},{16,17},{17,16},{32,33},{33,32},{48,49},{49,48},{2,3},... | collective-permute-start | bytes 1572872 | tf_op jit(solution)/shard_map/ppermute | solution.py:71
  7.7 31.7 %collective-permute-start.7 = (bf16[4,144,256]{2,1,0:T(8,128)(2,1)S(1)}, bf16[4,144,256]{2,1,0:T(8,128)(2,1)S(1)}, u32[]{:S(2)}, u32[]{:S(2)}) collective-permute-start(bf16[4,144,256]{2,1,0:T(8,128)(2,1)S(1)} %get-tuple-element.100), channel_id=1, source_target_pairs={{0,16},{16,0},{32,48},{48,32},{64,80},{80,64},{96,112},{112,96},{1... | collective-permute-start | bytes 884744 | tf_op jit(solution)/shard_map/ppermute | solution.py:487
  7.8 40.0 %collective-permute-start.9 = (bf16[4,144,256]{2,1,0:T(8,128)(2,1)S(1)}, bf16[4,144,256]{2,1,0:T(8,128)(2,1)S(1)}, u32[]{:S(2)}, u32[]{:S(2)}) collective-permute-start(bf16[4,144,256]{2,1,0:T(8,128)(2,1)S(1)} %get-tuple-element.99), channel_id=1, source_target_pairs={{0,240},{16,32},{32,16},{48,64},{64,48},{80,96},{96,80},{112,128},... | collective-permute-start | bytes 884744 | tf_op jit(solution)/shard_map/ppermute | solution.py:488
  15.0 6.9 %collective-permute-start.1 = (bf16[256,512]{1,0:T(8,128)(2,1)S(1)}, bf16[256,512]{1,0:T(8,128)(2,1)S(1)}, u32[]{:S(2)}, u32[]{:S(2)}) collective-permute-start(bf16[256,512]{1,0:T(8,128)(2,1)S(1)} %add_convert_fusion), channel_id=1, source_target_pairs={{0,4},{1,13},{16,20},{17,29},{32,36},{33,45},{48,52},{49,61},{2,6}... | collective-permute-start | bytes 786440 | tf_op jit(solution)/shard_map/ppermute | solution.py:71
  17.9 2.2 %copy-start.4 = (s32[2,4,9]{2,1,0:T(4,128)S(1)}, s32[2,4,9]{2,1,0:T(4,128)}, u32[]{:S(2)}) copy-start(s32[2,4,9]{2,1,0:T(4,128)} %param.13) | copy-start | bytes 868
  17.9 2.2 %copy-start.6 = (bf16[4,256]{1,0:T(4,128)(2,1)S(1)}, bf16[4,256]{1,0:T(4,128)(2,1)}, u32[]{:S(2)}) copy-start(bf16[4,256]{1,0:T(4,128)(2,1)} %row_filter.1) | copy-start | bytes 6148
  20.1 2.0 %copy-start.5 = (bf16[8,256]{1,0:T(8,128)(2,1)S(1)}, bf16[8,256]{1,0:T(8,128)(2,1)}, u32[]{:S(2)}) copy-start(bf16[8,256]{1,0:T(8,128)(2,1)} %filters.15) | copy-start | bytes 12292
  20.1 2.0 %copy-start.8 = (f32[8]{0:T(128)S(1)}, f32[8]{0:T(128)}, u32[]{:S(2)}) copy-start(f32[8]{0:T(128)} %rates.15) | copy-start | bytes 100
  22.0 4.2 %collective-permute-start.2 = (bf16[128,512]{1,0:T(8,128)(2,1)S(1)}, bf16[128,512]{1,0:T(8,128)(2,1)S(1)}, u32[]{:S(2)}, u32[]{:S(2)}) collective-permute-start(bf16[128,512]{1,0:T(8,128)(2,1)S(1)} %fusion), channel_id=1, source_target_pairs={{0,12},{1,5},{16,28},{17,21},{32,44},{33,37},{48,60},{49,53},{2,14... | collective-permute-start | bytes 393224 | tf_op jit(solution)/shard_map/ppermute | solution.py:71
  26.2 4.4 %collective-permute-start.3 = (bf16[64,512]{1,0:T(8,128)(2,1)S(1)}, bf16[64,512]{1,0:T(8,128)(2,1)S(1)}, u32[]{:S(2)}, u32[]{:S(2)}) collective-permute-start(bf16[64,512]{1,0:T(8,128)(2,1)S(1)} %fusion.1), channel_id=1, source_target_pairs={{0,64},{1,193},{16,80},{17,209},{32,96},{33,225},{48,112},{49,241}... | collective-permute-start | bytes 196616 | tf_op jit(solution)/shard_map/ppermute | solution.py:71
  30.7 3.7 %collective-permute-start.4 = (bf16[64,768]{1,0:T(8,128)(2,1)S(1)}, bf16[64,768]{1,0:T(8,128)(2,1)S(1)}, u32[]{:S(2)}, u32[]{:S(2)}) collective-permute-start(bf16[64,768]{1,0:T(8,128)(2,1)S(1)} %convert_element_type.65), channel_id=1, source_target_pairs={{0,192},{1,65},{16,208},{17,81},{32,224},{33,97},{48,240},{49,113}... | collective-permute-start | bytes 294920 | tf_op jit(solution)/shard_map/ppermute | solution.py:71
  34.5 4.8 %collective-permute-start.5 = (bf16[64,768]{1,0:T(8,128)(2,1)S(1)}, bf16[64,768]{1,0:T(8,128)(2,1)S(1)}, u32[]{:S(2)}, u32[]{:S(2)}) collective-permute-start(bf16[64,768]{1,0:T(8,128)(2,1)S(1)} %convert_element_type.67), channel_id=1, source_target_pairs={{0,16},{1,51},{16,0},{17,33},{32,48},{33,17},{48,32},{49,3},{2,18}... | collective-permute-start | bytes 294920 | tf_op jit(solution)/shard_map/ppermute | solution.py:71
  39.3 4.7 %collective-permute-start.6 = (bf16[64,768]{1,0:T(8,128)(2,1)S(1)}, bf16[64,768]{1,0:T(8,128)(2,1)S(1)}, u32[]{:S(2)}, u32[]{:S(2)}) collective-permute-start(bf16[64,768]{1,0:T(8,128)(2,1)S(1)} %convert_element_type.69), channel_id=1, source_target_pairs={{0,50},{1,17},{16,32},{17,1},{32,16},{33,49},{48,2},{49,33},{2,48}... | collective-permute-start | bytes 294920 | tf_op jit(solution)/shard_map/ppermute | solution.py:71
  44.1 8.4 %collective-permute-start.8 = (bf16[64,768]{1,0:T(8,128)(2,1)S(1)}, bf16[64,768]{1,0:T(8,128)(2,1)S(1)}, u32[]{:S(2)}, u32[]{:S(2)}) collective-permute-start(bf16[64,768]{1,0:T(8,128)(2,1)S(1)} %convert_element_type.71), channel_id=1, source_target_pairs={{0,48},{1,19},{16,34},{17,3},{32,18},{33,51},{48,0},{49,35},{2,50}... | collective-permute-start | bytes 294920 | tf_op jit(solution)/shard_map/ppermute | solution.py:71
  52.5 13.6 %collective-permute-start.10 = (bf16[64,512]{1,0:T(8,128)(2,1)S(1)}, bf16[64,512]{1,0:T(8,128)(2,1)S(1)}, u32[]{:S(2)}, u32[]{:S(2)}) collective-permute-start(bf16[64,512]{1,0:T(8,128)(2,1)S(1)} %pad_maximum_fusion.6), channel_id=1, source_target_pairs={{0,12},{1,5},{16,28},{17,21},{32,44},{33,37},{48,60},{49,53},{2,14... | collective-permute-start | bytes 196616 | tf_op jit(solution)/shard_map/ppermute | solution.py:71
  52.9 25.4 %collective-permute-start.15 = (bf16[4,144,256]{2,1,0:T(8,128)(2,1)S(1)}, bf16[4,144,256]{2,1,0:T(8,128)(2,1)S(1)}, u32[]{:S(2)}, u32[]{:S(2)}) collective-permute-start(bf16[4,144,256]{2,1,0:T(8,128)(2,1)S(1)} %get-tuple-element.93), channel_id=1, source_target_pairs={{0,15},{1,2},{2,1},{3,4},{4,3},{5,6},{6,5},{7,8},{8,7},{9,10},{10,... | collective-permute-start | bytes 884744 | tf_op jit(solution)/shard_map/ppermute | solution.py:548
  66.2 5.1 %collective-permute-start.11 = (bf16[128,512]{1,0:T(8,128)(2,1)S(1)}, bf16[128,512]{1,0:T(8,128)(2,1)S(1)}, u32[]{:S(2)}, u32[]{:S(2)}) collective-permute-start(bf16[128,512]{1,0:T(8,128)(2,1)S(1)} %pad_maximum_fusion.5.refs_2_), channel_id=1, source_target_pairs={{0,4},{1,13},{16,20},{17,29},{32,36},{33,45},{48,52},{49,61},{2,6}... | collective-permute-start | bytes 393224 | tf_op jit(solution)/shard_map/ppermute | solution.py:71
  66.3 5.8 %collective-permute-start.13 = (bf16[4,144,256]{2,1,0:T(8,128)(2,1)S(1)}, bf16[4,144,256]{2,1,0:T(8,128)(2,1)S(1)}, u32[]{:S(2)}, u32[]{:S(2)}) collective-permute-start(bf16[4,144,256]{2,1,0:T(8,128)(2,1)S(1)} %get-tuple-element.89), channel_id=1, source_target_pairs={{0,1},{1,0},{2,3},{3,2},{4,5},{5,4},{6,7},{7,6},{8,9},{9,8},{10,11... | collective-permute-start | bytes 884744 | tf_op jit(solution)/shard_map/ppermute | solution.py:551
  71.3 2.3 %copy-start = (bf16[256,512]{1,0:T(8,128)(2,1)S(1)}, bf16[256,512]{1,0:T(8,128)(2,1)}, u32[]{:S(2)}) copy-start(bf16[256,512]{1,0:T(8,128)(2,1)} %w_in.1) | copy-start | bytes 786436
  71.3 2.3 %copy-start.1 = (bf16[512,256]{1,0:T(8,128)(2,1)S(1)}, bf16[512,256]{1,0:T(8,128)(2,1)}, u32[]{:S(2)}) copy-start(bf16[512,256]{1,0:T(8,128)(2,1)} %w_out.1) | copy-start | bytes 786436
  71.4 2.3 %copy-start.9 = (bf16[1024,512]{1,0:T(8,128)(2,1)S(1)}, bf16[1024,512]{1,0:T(8,128)(2,1)}, u32[]{:S(2)}) copy-start(bf16[1024,512]{1,0:T(8,128)(2,1)} %get-tuple-element.49.refs_2_.refs_4_.cos_ref) | copy-start | bytes 3145732
  71.4 2.3 %copy-start.10 = (bf16[1024,512]{1,0:T(8,128)(2,1)S(1)}, bf16[1024,512]{1,0:T(8,128)(2,1)}, u32[]{:S(2)}) copy-start(bf16[1024,512]{1,0:T(8,128)(2,1)} %get-tuple-element.50.refs_3_.refs_5_.sin_ref) | copy-start | bytes 3145732
  71.4 6.5 %collective-permute-start.12 = (bf16[256,512]{1,0:T(8,128)(2,1)S(1)}, bf16[256,512]{1,0:T(8,128)(2,1)S(1)}, u32[]{:S(2)}, u32[]{:S(2)}) collective-permute-start(bf16[256,512]{1,0:T(8,128)(2,1)S(1)} %pad_maximum_fusion.3.refs_6_), channel_id=1, source_target_pairs={{0,64},{1,193},{16,80},{17,209},{32,96},{33,225},{48,112},{49,241}... | collective-permute-start | bytes 786440 | tf_op jit(solution)/shard_map/ppermute | solution.py:71
  77.9 2.5 %collective-permute-start.14 = (bf16[512,512]{1,0:T(8,128)(2,1)S(1)}, bf16[512,512]{1,0:T(8,128)(2,1)S(1)}, u32[]{:S(2)}, u32[]{:S(2)}) collective-permute-start(bf16[512,512]{1,0:T(8,128)(2,1)S(1)} %pad_maximum_fusion.refs_8_), channel_id=1, source_target_pairs={{0,1},{1,0},{16,17},{17,16},{32,33},{33,32},{48,49},{49,48},{2,3},... | collective-permute-start | bytes 1572872 | tf_op jit(solution)/shard_map/ppermute | solution.py:71
  79.7 0.7 copy-start.7

commit v12 on v11

--- a/solution.py
+++ b/solution.py
@@ -551,8 +551,6 @@
             column_a = lax.ppermute(near_send, "gy", column_pairs(True))
         elif turn == 2:
             acc = beyond(False, 2, column_a, acc)
-        elif turn == 3:
-            acc = beyond(False, 3, column_b, acc)
         parts = (
             (),
             ((cos_near, sin_near, 0, 0),),
@@ -562,6 +560,8 @@
         if parts:
             far = (cos_far, sin_far, w_in, w_out) if turn > 1 else ()
             acc = recip_piece(parts, far, chunk, acc.reshape(1024, WIDTH)).reshape(CX * CY, ATOMS, WIDTH)
+        if turn == 2:
+            acc = beyond(False, 3, column_b, acc)
         if step:
             chunk = jnp.concatenate([chunk, fresh], axis=0)
     acc = acc.reshape(1024, WIDTH)

time: 83.2 us -> 83.8 us (level)
    ppermute x1, waiting for transfers between devices: 0.01 us -> 3.28 us  [per_device(): column_b = lax.ppermute(far_send, 'gy', column_pairs(False))]
    ppermute x12, waiting for transfers between devices: 21.4 us -> 18.5 us  [permute(): return lax.ppermute(value, AXES, partner_list(step))]
  transfers between devices with their start and end apart: 16 -> 16, of which waited for: 9 -> 10; matrix products, arithmetic and copies ran while one was open for 1% -> 1% of each run, Pallas kernels for 25% -> 24%
where the time goes in v12:
time: 83.8 us; the launch traced here: 83.7 us
  starting transfers between devices  33.1 us (39%)
  Pallas kernels  27 us (32%)
  waiting for transfers between devices  21.8 us (26%)
  other arithmetic  0.87 us (1%)
    ppermute x12, waiting for transfers between devices, permute(): return lax.ppermute(value, AXES, partner_list(step))  18.5 us
    ppermute x12, starting transfers between devices, permute(): return lax.ppermute(value, AXES, partner_list(step))  14.8 us
    ppermute x1, starting transfers between devices, per_device(): column_b = lax.ppermute(far_send, 'gy', column_pairs(False))  13.3 us
    pallas_call x3, Pallas kernels, waves(): pl.pallas_call(functools.partial(wave_kernel, first), out_shape=out_shape...  8.29 us
    pallas_call x4, Pallas kernels, radial_piece(): pl.pallas_call(functools.partial(radial_kernel, near_cells, fresh), out_s...  6.72 us
    pallas_call x4, Pallas kernels, edge_piece(): pl.pallas_call(functools.partial(edge_kernel, along_x, which), out_shape=...  6.7 us
    ppermute x1, starting transfers between devices, per_device(): lax.ppermute(jnp.where(even_x, upper, lower), 'gx', row_pairs(False))  4.88 us
    ppermute x1, waiting for transfers between devices, per_device(): column_b = lax.ppermute(far_send, 'gy', column_pairs(False))  3.28 us
  transfers between devices with their start and end apart: 16, of which 10 were waited for; matrix products, arithmetic and copies ran while one was open for 1% of the time, Pallas kernels for 24%

profile of v12, /device:TPU:1, one launch (start us, length us, event | category | flops | bytes accessed | tf_op | source)
XLA Modules:
  0.0 83.7 jit_solution(7747470561132025998)
XLA Ops:
  0.2 4.1 %wave_tables.3 = (bf16[1024,512]{1,0:T(8,128)(2,1)}, bf16[1024,512]{1,0:T(8,128)(2,1)}, bf16[512,512]{1,0:T(8,128)(2,1)S(1)}, bf16[256,1024]{1,0:T(8,128)(2,1)S(...) custom-call(s32[2]{0:T(128)S(1)} %pad_add_fusion.place, bf16[2,3,4,128]{3,2,1,0:T(4,128)(2,1)} %bitcast.16, ...), custom_call_target="tpu_custom_call" | custom-call | flops 2048000000 | bytes 3000000 | tf_op jit(solution)/shard_map/wave_tables/pallas_call | solution.py:197
  4.3 3.3 %collective-permute-start = (bf16[512,512]{1,0:T(8,128)(2,1)S(1)}, bf16[512,512]{1,0:T(8,128)(2,1)S(1)}, u32[]{:S(2)}, u32[]{:S(2)}) collective-permute-start(bf16[512,512]{1,0:T(8,128)(2,1)S(1)} %get-tuple-element.53), channel_id=1, source_target_pairs={{0,1},{1,0},{16,17},{17,16},{32,33},{33,32},{48,49},{49,48},{2,3},... | collective-permute-start | bytes 1572872 | tf_op jit(solution)/shard_map/ppermute | solution.py:71
  7.8 4.9 %collective-permute-start.9 = (bf16[4,144,256]{2,1,0:T(8,128)(2,1)S(1)}, bf16[4,144,256]{2,1,0:T(8,128)(2,1)S(1)}, u32[]{:S(2)}, u32[]{:S(2)}) collective-permute-start(bf16[4,144,256]{2,1,0:T(8,128)(2,1)S(1)} %get-tuple-element.99), channel_id=1, source_target_pairs={{0,240},{16,32},{32,16},{48,64},{64,48},{80,96},{96,80},{112,128},... | collective-permute-start | bytes 884744 | tf_op jit(solution)/shard_map/ppermute | solution.py:488
  12.7 2.1 %wave_tables.4 = (bf16[1024,256]{1,0:T(8,128)(2,1)S(1)}, bf16[1024,256]{1,0:T(8,128)(2,1)S(1)}, f32[256,512]{1,0:T(8,128)S(1)}) custom-call(s32[2]{0:T(128)S(1)} %pad_add_fusion.place, bf16[2,3,4,128]{3,2,1,0:T(4,128)(2,1)S(1)} %bitcast.17, s32[3,1024]{1,0:T(4,128)S(1)} %copy-done.2, s32[1,256]{1,0:T(1,128)S(1)} %get-tuple-element.116.order, ...), custom_call_target="tpu_custom_call" | custom-call | flops 1024000000 | bytes 3000000 | tf_op jit(solution)/shard_map/wave_tables/pallas_call | solution.py:197
  15.0 2.8 %collective-permute-start.1 = (bf16[256,512]{1,0:T(8,128)(2,1)S(1)}, bf16[256,512]{1,0:T(8,128)(2,1)S(1)}, u32[]{:S(2)}, u32[]{:S(2)}) collective-permute-start(bf16[256,512]{1,0:T(8,128)(2,1)S(1)} %add_convert_fusion), channel_id=1, source_target_pairs={{0,4},{1,13},{16,20},{17,29},{32,36},{33,45},{48,52},{49,61},{2,6}... | collective-permute-start | bytes 786440 | tf_op jit(solution)/shard_map/ppermute | solution.py:71
  17.9 2.1 %wave_tables.5 = (bf16[1024,256]{1,0:T(8,128)(2,1)S(1)}, bf16[1024,256]{1,0:T(8,128)(2,1)S(1)}, f32[256,512]{1,0:T(8,128)S(1)}) custom-call(s32[2]{0:T(128)S(1)} %pad_add_fusion.place, bf16[2,3,4,128]{3,2,1,0:T(4,128)(2,1)S(1)} %bitcast.18, s32[3,1024]{1,0:T(4,128)S(1)} %copy-done.2, s32[1,256]{1,0:T(1,128)S(1)} %get-tuple-element.115.order, ...), custom_call_target="tpu_custom_call" | custom-call | flops 1024000000 | bytes 3000000 | tf_op jit(solution)/shard_map/wave_tables/pallas_call | solution.py:197
  20.1 1.3 %radial_prepare.1 = (f32[8,9]{1,0:T(8,128)S(1)}, f32[8,3,128,128]{3,2,1,0:T(8,128)S(1)}, f32[64,256]{1,0:T(8,128)S(1)}) custom-call(s32[2]{0:T(128)S(1)} %pad_add_fusion.place, s32[8]{0:T(128)S(1)} %reshape.729.near_count, s32[8,9]{1,0:T(8,128)S(1)} %bitcast.20, bf16[2,3,4,128]{3,2,1,0:T(4,128)(2,1)S(1)} %bitcast.19, bf16[4,256]{1,0:T(4,128)(2,1)S(1)} %copy-done.6), custom_call_target="tpu_custom_call" | custom-call | flops 500000000 | bytes 100000 | tf_op jit(solution)/shard_map/radial_prepare/pallas_call | solution.py:238
  21.4 0.5 collective-permute-done.1
  22.1 1.4 %radial_piece.4.rest_2_ = f32[8,128,256]{2,1,0:T(8,128)S(1)} custom-call(f32[8]{0:T(128)S(1)} %copy-done.8, f32[8,9]{1,0:T(8,128)S(1)} %get-tuple-element.61.live, bf16[8,256]{1,0:T(8,128)(2,1)S(1)} %copy-done.5, f32[8,3,128,128]{3,2,1,0:T(8,128)S(1)} %get-tuple-element.62.mine, bf16[4,144,256]{2,1,0:T(8,128)(2,1)S(1)} %get-tuple-element.63.rest_0_.upper, ...), custom_call_target="tpu_custom_call" | custom-call | flops 2000000000 | bytes 2000000 | tf_op jit(solution)/shard_map/radial_piece/pallas_call | solution.py:293
  23.5 2.7 %collective-permute-done.2 = bf16[128,512]{1,0:T(8,128)(2,1)S(1)} collective-permute-done((bf16[128,512]{1,0:T(8,128)(2,1)S(1)}, bf16[128,512]{1,0:T(8,128)(2,1)S(1)}, u32[]{:S(2)}, u32[]{:S(2)}) %collective-permute-start.2) | collective-permute-done | bytes 131104 | tf_op jit(solution)/shard_map/ppermute | solution.py:71
  26.2 0.6 collective-permute-start.3
  26.8 1.9 %radial_piece.5.rest_2_ = f32[8,128,256]{2,1,0:T(8,128)S(1)} custom-call(f32[8]{0:T(128)S(1)} %copy-done.8, f32[8,9]{1,0:T(8,128)S(1)} %get-tuple-element.61.live, bf16[8,256]{1,0:T(8,128)(2,1)S(1)} %copy-done.5, f32[8,3,128,128]{3,2,1,0:T(8,128)S(1)} %get-tuple-element.62.mine, ...), custom_call_target="tpu_custom_call", output_to_operand_aliasing={{}: (6, {})} | custom-call | flops 2000000000 | bytes 2000000 | tf_op jit(solution)/shard_map/radial_piece/pallas_call | solution.py:293
  28.7 1.9 %collective-permute-done.3 = bf16[64,512]{1,0:T(8,128)(2,1)S(1)} collective-permute-done((bf16[64,512]{1,0:T(8,128)(2,1)S(1)}, bf16[64,512]{1,0:T(8,128)(2,1)S(1)}, u32[]{:S(2)}, u32[]{:S(2)}) %collective-permute-start.3) | collective-permute-done | bytes 65568 | tf_op jit(solution)/shard_map/ppermute | solution.py:71
  31.0 1.9 %radial_piece.6.rest_2_ = f32[8,128,256]{2,1,0:T(8,128)S(1)} custom-call(f32[8]{0:T(128)S(1)} %copy-done.8, f32[8,9]{1,0:T(8,128)S(1)} %get-tuple-element.61.live, bf16[8,256]{1,0:T(8,128)(2,1)S(1)} %copy-done.5, f32[8,3,128,128]{3,2,1,0:T(8,128)S(1)} %get-tuple-element.62.mine, ...), custom_call_target="tpu_custom_call", output_to_operand_aliasing={{}: (6, {})} | custom-call | flops 2000000000 | bytes 2000000 | tf_op jit(solution)/shard_map/radial_piece/pallas_call | solution.py:293
  32.9 1.5 %collective-permute-done.4 = bf16[64,768]{1,0:T(8,128)(2,1)S(1)} collective-permute-done((bf16[64,768]{1,0:T(8,128)(2,1)S(1)}, bf16[64,768]{1,0:T(8,128)(2,1)S(1)}, u32[]{:S(2)}, u32[]{:S(2)}) %collective-permute-start.4) | collective-permute-done | bytes 98336 | tf_op jit(solution)/shard_map/ppermute | solution.py:71
  34.5 2.3 %collective-permute-start.5 = (bf16[64,768]{1,0:T(8,128)(2,1)S(1)}, bf16[64,768]{1,0:T(8,128)(2,1)S(1)}, u32[]{:S(2)}, u32[]{:S(2)}) collective-permute-start(bf16[64,768]{1,0:T(8,128)(2,1)S(1)} %convert_element_type.67), channel_id=1, source_target_pairs={{0,16},{1,51},{16,0},{17,33},{32,48},{33,17},{48,32},{49,3},{2,18}... | collective-permute-start | bytes 294920 | tf_op jit(solution)/shard_map/ppermute | solution.py:71
  36.8 1.6 %radial_piece.7.start = f32[8,128,256]{2,1,0:T(8,128)S(1)} custom-call(f32[8]{0:T(128)S(1)} %copy-done.8, f32[8,9]{1,0:T(8,128)S(1)} %get-tuple-element.61.live, bf16[8,256]{1,0:T(8,128)(2,1)S(1)} %copy-done.5, f32[8,3,128,128]{3,2,1,0:T(8,128)S(1)} %get-tuple-element.62.mine, ...), custom_call_target="tpu_custom_call", output_to_operand_aliasing={{}: (6, {})} | custom-call | flops 2000000000 | bytes 2000000 | tf_op jit(solution)/shard_map/radial_piece/pallas_call | solution.py:293
  38.3 0.9 %collective-permute-done.5 = bf16[64,768]{1,0:T(8,128)(2,1)S(1)} collective-permute-done((bf16[64,768]{1,0:T(8,128)(2,1)S(1)}, bf16[64,768]{1,0:T(8,128)(2,1)S(1)}, u32[]{:S(2)}, u32[]{:S(2)}) %collective-permute-start.5) | collective-permute-done | bytes 98336 | tf_op jit(solution)/shard_map/ppermute | solution.py:71
  39.4 1.8 %radial_edge.4.start = f32[8,128,256]{2,1,0:T(8,128)S(1)} custom-call(s32[4]{0:T(128)S(1)} %pad_add_fusion.1.sides, f32[8]{0:T(128)S(1)} %copy-done.8, f32[8,9]{1,0:T(8,128)S(1)} %get-tuple-element.61.live, bf16[8,256]{1,0:T(8,128)(2,1)S(1)} %copy-done.5, f32[8,3,128,128]{3,2,1,0:T(8,128)S(1)} %get-tuple-element.62.mine, ...), custom_call_target="tpu_custom_call", output_to_operand_aliasing={{}: (6, {})} | custom-call | flops 20000000000 | bytes 2000000 | tf_op jit(solution)/shard_map/radial_edge/pallas_call | solution.py:365
  41.2 2.8 %collective-permute-done.6 = bf16[64,768]{1,0:T(8,128)(2,1)S(1)} collective-permute-done((bf16[64,768]{1,0:T(8,128)(2,1)S(1)}, bf16[64,768]{1,0:T(8,128)(2,1)S(1)}, u32[]{:S(2)}, u32[]{:S(2)}) %collective-permute-start.6) | collective-permute-done | bytes 98336 | tf_op jit(solution)/shard_map/ppermute | solution.py:71
  44.1 3.7 %collective-permute-start.8 = (bf16[64,768]{1,0:T(8,128)(2,1)S(1)}, bf16[64,768]{1,0:T(8,128)(2,1)S(1)}, u32[]{:S(2)}, u32[]{:S(2)}) collective-permute-start(bf16[64,768]{1,0:T(8,128)(2,1)S(1)} %convert_element_type.71), channel_id=1, source_target_pairs={{0,48},{1,19},{16,34},{17,3},{32,18},{33,51},{48,0},{49,35},{2,50}... | collective-permute-start | bytes 294920 | tf_op jit(solution)/shard_map/ppermute | solution.py:71
  47.8 1.8 %radial_edge.5 = f32[8,128,256]{2,1,0:T(8,128)S(1)} custom-call(s32[4]{0:T(128)S(1)} %pad_add_fusion.1.sides, f32[8]{0:T(128)S(1)} %copy-done.8, f32[8,9]{1,0:T(8,128)S(1)} %get-tuple-element.61.live, bf16[8,256]{1,0:T(8,128)(2,1)S(1)} %copy-done.5, f32[8,3,128,128]{3,2,1,0:T(8,128)S(1)} %get-tuple-element.62.mine, ...), custom_call_target="tpu_custom_call", output_to_operand_aliasing={{}: (6, {})} | custom-call | flops 20000000000 | bytes 2000000 | tf_op jit(solution)/shard_map/radial_edge/pallas_call | solution.py:365
  49.6 2.9 %collective-permute-done.8 = bf16[64,768]{1,0:T(8,128)(2,1)S(1)} collective-permute-done((bf16[64,768]{1,0:T(8,128)(2,1)S(1)}, bf16[64,768]{1,0:T(8,128)(2,1)S(1)}, u32[]{:S(2)}, u32[]{:S(2)}) %collective-permute-start.8) | collective-permute-done | bytes 98336 | tf_op jit(solution)/shard_map/ppermute | solution.py:71
  52.9 13.3 %collective-permute-start.13 = (bf16[4,144,256]{2,1,0:T(8,128)(2,1)S(1)}, bf16[4,144,256]{2,1,0:T(8,128)(2,1)S(1)}, u32[]{:S(2)}, u32[]{:S(2)}) collective-permute-start(bf16[4,144,256]{2,1,0:T(8,128)(2,1)S(1)} %get-tuple-element.93), channel_id=1, source_target_pairs={{0,15},{1,2},{2,1},{3,4},{4,3},{5,6},{6,5},{7,8},{8,7},{9,10},{10,... | collective-permute-start | bytes 884744 | tf_op jit(solution)/shard_map/ppermute | solution.py:548
  66.8 4.5 %collective-permute-done.11 = bf16[128,512]{1,0:T(8,128)(2,1)S(1)} collective-permute-done((bf16[128,512]{1,0:T(8,128)(2,1)S(1)}, bf16[128,512]{1,0:T(8,128)(2,1)S(1)}, u32[]{:S(2)}, u32[]{:S(2)}) %collective-permute-start.11) | collective-permute-done | bytes 131104 | tf_op jit(solution)/shard_map/ppermute | solution.py:71
  71.4 0.8 collective-permute-start.12
  72.1 1.4 %radial_edge.6 = f32[8,128,256]{2,1,0:T(8,128)S(1)} custom-call(s32[4]{0:T(128)S(1)} %pad_add_fusion.1.sides, f32[8]{0:T(128)S(1)} %copy-done.8, f32[8,9]{1,0:T(8,128)S(1)} %get-tuple-element.61.live, bf16[8,256]{1,0:T(8,128)(2,1)S(1)} %copy-done.5, f32[8,3,128,128]{3,2,1,0:T(8,128)S(1)} %get-tuple-element.62.mine, ...), custom_call_target="tpu_custom_call", output_to_operand_aliasing={{}: (6, {})} | custom-call | flops 20000000000 | bytes 2000000 | tf_op jit(solution)/shard_map/radial_edge/pallas_call | solution.py:365
  74.1 3.3 %collective-permute-done.13.block = bf16[4,144,256]{2,1,0:T(8,128)(2,1)S(1)} collective-permute-done((bf16[4,144,256]{2,1,0:T(8,128)(2,1)S(1)}, bf16[4,144,256]{2,1,0:T(8,128)(2,1)S(1)}, u32[]{:S(2)}, u32[]{:S(2)}) %collective-permute-start.13) | collective-permute-done | bytes 294944 | tf_op jit(solution)/shard_map/ppermute | solution.py:548
  77.3 1.7 %radial_edge.7 = f32[8,128,256]{2,1,0:T(8,128)S(1)} custom-call(s32[4]{0:T(128)S(1)} %pad_add_fusion.1.sides, f32[8]{0:T(128)S(1)} %copy-done.8, f32[8,9]{1,0:T(8,128)S(1)} %get-tuple-element.61.live, bf16[8,256]{1,0:T(8,128)(2,1)S(1)} %copy-done.5, f32[8,3,128,128]{3,2,1,0:T(8,128)S(1)} %get-tuple-element.62.mine, ...), custom_call_target="tpu_custom_call", output_to_operand_aliasing={{}: (6, {})} | custom-call | flops 20000000000 | bytes 2000000 | tf_op jit(solution)/shard_map/radial_edge/pallas_call | solution.py:365
  79.5 0.7 recip_piece.5.acc
  80.2 0.9 %collective-permute-done.15.coef_in = bf16[512,512]{1,0:T(8,128)(2,1)S(1)} collective-permute-done((bf16[512,512]{1,0:T(8,128)(2,1)S(1)}, bf16[512,512]{1,0:T(8,128)(2,1)S(1)}, u32[]{:S(2)}, u32[]{:S(2)}) %collective-permute-start.15) | collective-permute-done | bytes 524320 | tf_op jit(solution)/shard_map/ppermute | solution.py:71
  81.0 2.4 %mix_and_network.1 = bf16[1024,256]{1,0:T(8,128)(2,1)} custom-call(bf16[1024,512]{1,0:T(8,128)(2,1)S(1)} %copy-done.9, bf16[1024,512]{1,0:T(8,128)(2,1)S(1)} %copy-done.10, bf16[512,512]{1,0:T(8,128)(2,1)S(1)} %collective-permute-done.15.coef_in, bf16[4,144,256]{2,1,0:T(8,128)(2,1)S(1)} %get-tuple-element.63.rest_0_.upper, ...), custom_call_target="tpu_custom_call" | custom-call | flops 3000000000 | bytes 8000000 | tf_op jit(solution)/shard_map/mix_and_network/pallas_call | solution.py:430
  (72 shorter events, 3.4 us)
Async XLA Ops:
  0.2 12.5 %copy-start.11 = (s32[2,4]{1,0:T(2,128)S(1)}, s32[2,4]{1,0:T(2,128)}, u32[]{:S(2)}) copy-start(s32[2,4]{1,0:T(2,128)} %param.14) | copy-start | bytes 100
  0.2 12.6 %copy-start.2 = (s32[3,1024]{1,0:T(4,128)S(1)}, s32[3,1024]{1,0:T(4,128)}, u32[]{:S(2)}) copy-start(s32[3,1024]{1,0:T(4,128)} %miller.5) | copy-start | bytes 36868
  0.2 12.6 %copy-start.3 = (bf16[2,4,3,128]{3,1,2,0:T(4,128)(2,1)S(1)}, bf16[2,4,3,128]{3,1,2,0:T(4,128)(2,1)}, u32[]{:S(2)}) copy-start(bf16[2,4,3,128]{3,1,2,0:T(4,128)(2,1)} %param.12) | copy-start | bytes 18436
  4.3 10.7 %collective-permute-start = (bf16[512,512]{1,0:T(8,128)(2,1)S(1)}, bf16[512,512]{1,0:T(8,128)(2,1)S(1)}, u32[]{:S(2)}, u32[]{:S(2)}) collective-permute-start(bf16[512,512]{1,0:T(8,128)(2,1)S(1)} %get-tuple-element.53), channel_id=1, source_target_pairs={{0,1},{1,0},{16,17},{17,16},{32,33},{33,32},{48,49},{49,48},{2,3},... | collective-permute-start | bytes 1572872 | tf_op jit(solution)/shard_map/ppermute | solution.py:71
  7.7 31.7 %collective-permute-start.7 = (bf16[4,144,256]{2,1,0:T(8,128)(2,1)S(1)}, bf16[4,144,256]{2,1,0:T(8,128)(2,1)S(1)}, u32[]{:S(2)}, u32[]{:S(2)}) collective-permute-start(bf16[4,144,256]{2,1,0:T(8,128)(2,1)S(1)} %get-tuple-element.100), channel_id=1, source_target_pairs={{0,16},{16,0},{32,48},{48,32},{64,80},{80,64},{96,112},{112,96},{1... | collective-permute-start | bytes 884744 | tf_op jit(solution)/shard_map/ppermute | solution.py:487
  7.8 40.0 %collective-permute-start.9 = (bf16[4,144,256]{2,1,0:T(8,128)(2,1)S(1)}, bf16[4,144,256]{2,1,0:T(8,128)(2,1)S(1)}, u32[]{:S(2)}, u32[]{:S(2)}) collective-permute-start(bf16[4,144,256]{2,1,0:T(8,128)(2,1)S(1)} %get-tuple-element.99), channel_id=1, source_target_pairs={{0,240},{16,32},{32,16},{48,64},{64,48},{80,96},{96,80},{112,128},... | collective-permute-start | bytes 884744 | tf_op jit(solution)/shard_map/ppermute | solution.py:488
  15.0 6.9 %collective-permute-start.1 = (bf16[256,512]{1,0:T(8,128)(2,1)S(1)}, bf16[256,512]{1,0:T(8,128)(2,1)S(1)}, u32[]{:S(2)}, u32[]{:S(2)}) collective-permute-start(bf16[256,512]{1,0:T(8,128)(2,1)S(1)} %add_convert_fusion), channel_id=1, source_target_pairs={{0,4},{1,13},{16,20},{17,29},{32,36},{33,45},{48,52},{49,61},{2,6}... | collective-permute-start | bytes 786440 | tf_op jit(solution)/shard_map/ppermute | solution.py:71
  17.9 2.2 %copy-start.4 = (s32[2,4,9]{2,1,0:T(4,128)S(1)}, s32[2,4,9]{2,1,0:T(4,128)}, u32[]{:S(2)}) copy-start(s32[2,4,9]{2,1,0:T(4,128)} %param.13) | copy-start | bytes 868
  17.9 2.2 %copy-start.6 = (bf16[4,256]{1,0:T(4,128)(2,1)S(1)}, bf16[4,256]{1,0:T(4,128)(2,1)}, u32[]{:S(2)}) copy-start(bf16[4,256]{1,0:T(4,128)(2,1)} %row_filter.1) | copy-start | bytes 6148
  20.1 2.0 %copy-start.5 = (bf16[8,256]{1,0:T(8,128)(2,1)S(1)}, bf16[8,256]{1,0:T(8,128)(2,1)}, u32[]{:S(2)}) copy-start(bf16[8,256]{1,0:T(8,128)(2,1)} %filters.15) | copy-start | bytes 12292
  20.1 2.0 %copy-start.8 = (f32[8]{0:T(128)S(1)}, f32[8]{0:T(128)}, u32[]{:S(2)}) copy-start(f32[8]{0:T(128)} %rates.15) | copy-start | bytes 100
  22.0 4.2 %collective-permute-start.2 = (bf16[128,512]{1,0:T(8,128)(2,1)S(1)}, bf16[128,512]{1,0:T(8,128)(2,1)S(1)}, u32[]{:S(2)}, u32[]{:S(2)}) collective-permute-start(bf16[128,512]{1,0:T(8,128)(2,1)S(1)} %fusion), channel_id=1, source_target_pairs={{0,12},{1,5},{16,28},{17,21},{32,44},{33,37},{48,60},{49,53},{2,14... | collective-permute-start | bytes 393224 | tf_op jit(solution)/shard_map/ppermute | solution.py:71
  26.2 4.4 %collective-permute-start.3 = (bf16[64,512]{1,0:T(8,128)(2,1)S(1)}, bf16[64,512]{1,0:T(8,128)(2,1)S(1)}, u32[]{:S(2)}, u32[]{:S(2)}) collective-permute-start(bf16[64,512]{1,0:T(8,128)(2,1)S(1)} %fusion.1), channel_id=1, source_target_pairs={{0,64},{1,193},{16,80},{17,209},{32,96},{33,225},{48,112},{49,241}... | collective-permute-start | bytes 196616 | tf_op jit(solution)/shard_map/ppermute | solution.py:71
  30.7 3.7 %collective-permute-start.4 = (bf16[64,768]{1,0:T(8,128)(2,1)S(1)}, bf16[64,768]{1,0:T(8,128)(2,1)S(1)}, u32[]{:S(2)}, u32[]{:S(2)}) collective-permute-start(bf16[64,768]{1,0:T(8,128)(2,1)S(1)} %convert_element_type.65), channel_id=1, source_target_pairs={{0,192},{1,65},{16,208},{17,81},{32,224},{33,97},{48,240},{49,113}... | collective-permute-start | bytes 294920 | tf_op jit(solution)/shard_map/ppermute | solution.py:71
  34.5 4.8 %collective-permute-start.5 = (bf16[64,768]{1,0:T(8,128)(2,1)S(1)}, bf16[64,768]{1,0:T(8,128)(2,1)S(1)}, u32[]{:S(2)}, u32[]{:S(2)}) collective-permute-start(bf16[64,768]{1,0:T(8,128)(2,1)S(1)} %convert_element_type.67), channel_id=1, source_target_pairs={{0,16},{1,51},{16,0},{17,33},{32,48},{33,17},{48,32},{49,3},{2,18}... | collective-permute-start | bytes 294920 | tf_op jit(solution)/shard_map/ppermute | solution.py:71
  39.3 4.8 %collective-permute-start.6 = (bf16[64,768]{1,0:T(8,128)(2,1)S(1)}, bf16[64,768]{1,0:T(8,128)(2,1)S(1)}, u32[]{:S(2)}, u32[]{:S(2)}) collective-permute-start(bf16[64,768]{1,0:T(8,128)(2,1)S(1)} %convert_element_type.69), channel_id=1, source_target_pairs={{0,50},{1,17},{16,32},{17,1},{32,16},{33,49},{48,2},{49,33},{2,48}... | collective-permute-start | bytes 294920 | tf_op jit(solution)/shard_map/ppermute | solution.py:71
  44.1 8.4 %collective-permute-start.8 = (bf16[64,768]{1,0:T(8,128)(2,1)S(1)}, bf16[64,768]{1,0:T(8,128)(2,1)S(1)}, u32[]{:S(2)}, u32[]{:S(2)}) collective-permute-start(bf16[64,768]{1,0:T(8,128)(2,1)S(1)} %convert_element_type.71), channel_id=1, source_target_pairs={{0,48},{1,19},{16,34},{17,3},{32,18},{33,51},{48,0},{49,35},{2,50}... | collective-permute-start | bytes 294920 | tf_op jit(solution)/shard_map/ppermute | solution.py:71
  52.5 13.6 %collective-permute-start.10 = (bf16[64,512]{1,0:T(8,128)(2,1)S(1)}, bf16[64,512]{1,0:T(8,128)(2,1)S(1)}, u32[]{:S(2)}, u32[]{:S(2)}) collective-permute-start(bf16[64,512]{1,0:T(8,128)(2,1)S(1)} %pad_maximum_fusion.6), channel_id=1, source_target_pairs={{0,12},{1,5},{16,28},{17,21},{32,44},{33,37},{48,60},{49,53},{2,14... | collective-permute-start | bytes 196616 | tf_op jit(solution)/shard_map/ppermute | solution.py:71
  52.9 24.4 %collective-permute-start.13 = (bf16[4,144,256]{2,1,0:T(8,128)(2,1)S(1)}, bf16[4,144,256]{2,1,0:T(8,128)(2,1)S(1)}, u32[]{:S(2)}, u32[]{:S(2)}) collective-permute-start(bf16[4,144,256]{2,1,0:T(8,128)(2,1)S(1)} %get-tuple-element.93), channel_id=1, source_target_pairs={{0,15},{1,2},{2,1},{3,4},{4,3},{5,6},{6,5},{7,8},{8,7},{9,10},{10,... | collective-permute-start | bytes 884744 | tf_op jit(solution)/shard_map/ppermute | solution.py:548
  66.2 5.1 %collective-permute-start.11 = (bf16[128,512]{1,0:T(8,128)(2,1)S(1)}, bf16[128,512]{1,0:T(8,128)(2,1)S(1)}, u32[]{:S(2)}, u32[]{:S(2)}) collective-permute-start(bf16[128,512]{1,0:T(8,128)(2,1)S(1)} %pad_maximum_fusion.5.refs_2_), channel_id=1, source_target_pairs={{0,4},{1,13},{16,20},{17,29},{32,36},{33,45},{48,52},{49,61},{2,6}... | collective-permute-start | bytes 393224 | tf_op jit(solution)/shard_map/ppermute | solution.py:71
  66.3 5.8 %collective-permute-start.14 = (bf16[4,144,256]{2,1,0:T(8,128)(2,1)S(1)}, bf16[4,144,256]{2,1,0:T(8,128)(2,1)S(1)}, u32[]{:S(2)}, u32[]{:S(2)}) collective-permute-start(bf16[4,144,256]{2,1,0:T(8,128)(2,1)S(1)} %get-tuple-element.89), channel_id=1, source_target_pairs={{0,1},{1,0},{2,3},{3,2},{4,5},{5,4},{6,7},{7,6},{8,9},{9,8},{10,11... | collective-permute-start | bytes 884744 | tf_op jit(solution)/shard_map/ppermute | solution.py:551
  71.3 2.3 %copy-start = (bf16[256,512]{1,0:T(8,128)(2,1)S(1)}, bf16[256,512]{1,0:T(8,128)(2,1)}, u32[]{:S(2)}) copy-start(bf16[256,512]{1,0:T(8,128)(2,1)} %w_in.1) | copy-start | bytes 786436
  71.3 2.3 %copy-start.1 = (bf16[512,256]{1,0:T(8,128)(2,1)S(1)}, bf16[512,256]{1,0:T(8,128)(2,1)}, u32[]{:S(2)}) copy-start(bf16[512,256]{1,0:T(8,128)(2,1)} %w_out.1) | copy-start | bytes 786436
  71.3 2.3 %copy-start.9 = (bf16[1024,512]{1,0:T(8,128)(2,1)S(1)}, bf16[1024,512]{1,0:T(8,128)(2,1)}, u32[]{:S(2)}) copy-start(bf16[1024,512]{1,0:T(8,128)(2,1)} %get-tuple-element.49.refs_2_.refs_4_.cos_ref) | copy-start | bytes 3145732
  71.4 2.3 %copy-start.10 = (bf16[1024,512]{1,0:T(8,128)(2,1)S(1)}, bf16[1024,512]{1,0:T(8,128)(2,1)}, u32[]{:S(2)}) copy-start(bf16[1024,512]{1,0:T(8,128)(2,1)} %get-tuple-element.50.refs_3_.refs_5_.sin_ref) | copy-start | bytes 3145732
  71.4 7.6 %collective-permute-start.12 = (bf16[256,512]{1,0:T(8,128)(2,1)S(1)}, bf16[256,512]{1,0:T(8,128)(2,1)S(1)}, u32[]{:S(2)}, u32[]{:S(2)}) collective-permute-start(bf16[256,512]{1,0:T(8,128)(2,1)S(1)} %pad_maximum_fusion.3.refs_6_), channel_id=1, source_target_pairs={{0,64},{1,193},{16,80},{17,209},{32,96},{33,225},{48,112},{49,241}... | collective-permute-start | bytes 786440 | tf_op jit(solution)/shard_map/ppermute | solution.py:71
  79.0 2.0 %collective-permute-start.15 = (bf16[512,512]{1,0:T(8,128)(2,1)S(1)}, bf16[512,512]{1,0:T(8,128)(2,1)S(1)}, u32[]{:S(2)}, u32[]{:S(2)}) collective-permute-start(bf16[512,512]{1,0:T(8,128)(2,1)S(1)} %pad_maximum_fusion.refs_8_), channel_id=1, source_target_pairs={{0,1},{1,0},{16,17},{17,16},{32,33},{33,32},{48,49},{49,48},{2,3},... | collective-permute-start | bytes 1572872 | tf_op jit(solution)/shard_map/ppermute | solution.py:71
  79.5 1.6 %copy-start.7 = (f32[256]{0:T(256)S(1)}, f32[256]{0:T(256)}, u32[]{:S(2)}) copy-start(f32[256]{0:T(256)} %param.19) | copy-start | bytes 3076
